TPU v7x, 32 devices: a whole 2x2x4 slice. The times are simulated.
32 devices in a mesh: crop: 2 (over x), row: 8 (over z, y), col: 2 (over core).
Axes of the slice: x: 2, y: 2, z: 4, core: 2. Of those that a mesh axis runs over, the one named last changes fastest.
Arguments:
- pair_rep: bfloat16 [96, 48, 128], P(('crop', 'row'), 'col'), parts along dimension 0, may hold values from -6 to 6
- cotangent: bfloat16 [96, 48, 128], P(('crop', 'row'), 'col'), parts along dimension 0, may hold values from -6 to 6
- norm_gain: float32 [128], replicated, may hold values from 0.5 to 1.5
- norm_bias: float32 [128], replicated, may hold values from -3 to 3
- proj_weight: bfloat16 [128, 512], replicated, may hold values from -0.5 to 0.5
- gate_weight: bfloat16 [128, 128], replicated, may hold values from -0.5 to 0.5
- tri_gain: float32 [128], replicated, may hold values from 0.5 to 1.5
- tri_bias: float32 [128], replicated, may hold values from -3 to 3
- out_weight: bfloat16 [128, 128], replicated, may hold values from -0.5 to 0.5
Outputs:
- block_out: bfloat16 [96, 48, 128], P(('crop', 'row'), 'col'), parts along dimension 0
- pair_grad: float32 [96, 48, 128], P(('crop', 'row'), 'col'), parts along dimension 0
- proj_grad: float32 [256, 512], P('crop'), parts along dimension 0
- gate_grad: float32 [256, 128], P('crop'), parts along dimension 0
- out_grad: float32 [256, 128], P('crop'), parts along dimension 0
There are 2 independent parts, one for each index of `crop`. A program takes and returns all parts, laid end to end along the dimension named above; an argument that names none is the same for every part. Nothing has to cross between parts.
All inputs are finite; a program needn't handle non-finite values.
Results may differ from a plain program's by a relative error of at most 0.0066.
Values may be sent and summed in bfloat16 or wider, within the bound.
No kernel may reach another device: no remote copies, remote signals or barrier semaphores. Data moves between devices by JAX's collectives and lax.ppermute only.
A program may use at most 128 MiB of HBM per device.

v0:
```python
import jax
import jax.numpy as jnp
from jax import lax
from jax.sharding import PartitionSpec as P


def layer_norm(values, gain, bias):
    centred = values - jnp.mean(values, axis=-1, keepdims=True)
    inverse = lax.rsqrt(jnp.mean(centred * centred, axis=-1, keepdims=True) + 1e-05)
    scaled = centred * inverse
    return (scaled * gain + bias, scaled, inverse)


def norm_back(grads, gain, scaled, inverse):
    weighted = grads * gain
    first = jnp.mean(weighted, axis=-1, keepdims=True)
    second = jnp.mean(weighted * scaled, axis=-1, keepdims=True)
    return inverse * (weighted - first - scaled * second)


def local(
    pair_rep,
    cotangent,
    norm_gain,
    norm_bias,
    proj_weight,
    gate_weight,
    tri_gain,
    tri_bias,
    out_weight,
):
    f32 = jnp.float32
    bf16 = jnp.bfloat16
    hidden = tri_gain.shape[0]
    channels = norm_gain.shape[0]
    row_count = pair_rep.shape[0]
    col_count = pair_rep.shape[1]
    crop_len = row_count * lax.axis_size("row")
    normed_f, pair_hat, pair_inv = layer_norm(pair_rep.astype(f32), norm_gain, norm_bias)
    normed = normed_f.astype(bf16)
    projected = jnp.einsum("ijc,cd->ijd", normed, proj_weight, preferred_element_type=f32)
    sig_left = jax.nn.sigmoid(projected[..., 0:hidden])
    val_left = projected[..., hidden : 2 * hidden]
    sig_right = jax.nn.sigmoid(projected[..., 2 * hidden : 3 * hidden])
    val_right = projected[..., 3 * hidden : 4 * hidden]
    left_edge = (sig_left * val_left).astype(bf16)
    right_edge = (sig_right * val_right).astype(bf16)
    out_gate = jax.nn.sigmoid(
        jnp.einsum("ijc,cd->ijd", normed, gate_weight, preferred_element_type=f32)
    )
    right_all = lax.all_gather(right_edge, "row", axis=0, tiled=True)
    block = right_all
    triangle = lax.psum_scatter(
        jnp.einsum("ikc,jkc->jic", left_edge, block, preferred_element_type=f32),
        "col",
        scatter_dimension=0,
        tiled=True,
    ).transpose(1, 0, 2)
    tri_f, tri_hat, tri_inv = layer_norm(triangle, tri_gain, tri_bias)
    tri_norm = tri_f.astype(bf16)
    update = jnp.einsum("ijh,hc->ijc", tri_norm, out_weight, preferred_element_type=f32)
    block_out = (out_gate * update).astype(bf16)
    cot = cotangent.astype(f32)
    d_update = (cot * out_gate).astype(bf16)
    d_gate = (cot * update * out_gate * (1.0 - out_gate)).astype(bf16)
    d_norm = jnp.einsum("ijc,hc->ijh", d_update, out_weight, preferred_element_type=f32)
    d_triangle = norm_back(d_norm, tri_gain, tri_hat, tri_inv).astype(bf16)
    tri_rows = lax.all_gather(d_triangle, "col", axis=1, tiled=True)
    d_left = jnp.einsum("ijc,jkc->ikc", tri_rows, right_all, preferred_element_type=f32)
    tri_cols = lax.all_to_all(tri_rows, "row", split_axis=1, concat_axis=0, tiled=True)
    block = tri_cols
    d_right = jnp.einsum(
        "ijc,ikc->jkc",
        block,
        lax.all_gather(left_edge, "row", axis=0, tiled=True),
        preferred_element_type=f32,
    )
    d_proj = jnp.concatenate(
        [
            d_left * val_left * sig_left * (1.0 - sig_left),
            d_left * sig_left,
            d_right * val_right * sig_right * (1.0 - sig_right),
            d_right * sig_right,
        ],
        axis=-1,
    ).astype(bf16)
    d_normed = jnp.einsum(
        "ijd,cd->ijc", d_proj, proj_weight, preferred_element_type=f32
    ) + jnp.einsum("ijd,cd->ijc", d_gate, gate_weight, preferred_element_type=f32)
    pair_grad = norm_back(d_normed, norm_gain, pair_hat, pair_inv)
    cells = row_count * col_count
    flat_norm = normed.reshape(cells, channels)
    local_proj = (
        jnp.dot(flat_norm.T, d_proj.reshape(cells, 4 * hidden), preferred_element_type=f32)
        / crop_len
    )
    local_gate = (
        jnp.dot(flat_norm.T, d_gate.reshape(cells, channels), preferred_element_type=f32) / crop_len
    )
    local_out = (
        jnp.dot(
            tri_norm.reshape(cells, hidden).T,
            d_update.reshape(cells, channels),
            preferred_element_type=f32,
        )
        / crop_len
    )
    proj_grad, gate_grad, out_grad = lax.psum((local_proj, local_gate, local_out), ("row", "col"))
    return (block_out, pair_grad, proj_grad, gate_grad, out_grad)


def solution(mesh):
    return jax.shard_map(
        local,
        mesh=mesh,
        in_specs=(
            P(("crop", "row"), "col", None),
            P(("crop", "row"), "col", None),
            P(),
            P(),
            P(),
            P(),
            P(),
            P(),
            P(),
        ),
        out_specs=(
            P(("crop", "row"), "col", None),
            P(("crop", "row"), "col", None),
            P("crop", None),
            P("crop", None),
            P("crop", None),
        ),
        check_vma=False,
    )
```

profile of v0, /device:TPU:0, one launch (start us, length us, event | category | flops | bytes accessed | tf_op | source)
XLA Modules:
  0.0 210.8 jit_solution(7040037834363857959)
XLA Ops:
  7.2 0.9 convert_reduce_fusion
  8.1 0.9 fusion.21
  9.1 1.0 fusion.9
  10.2 0.6 copy-done.2
  10.8 32.6 %all_gather.9 = bf16[48,24,128]{2,1,0:T(8,128)(2,1)S(1)} all-gather(bf16[6,24,128]{2,1,0:T(8,128)(2,1)S(1)} %get-tuple-element.19), channel_id=1, replica_groups=mesh['crop'=2,'row'=8,'col'=2] {'row'}, dimensions={0}, use_global_device_ids=true | all-gather | bytes 331776 | tf_op jit(solution)/shard_map/all_gather | solution.py:51
  43.4 0.9 copy.36
  44.5 0.9 convolution_bitcast_fusion
  45.5 0.9 copy.38
  46.4 32.9 %all_gather.11 = bf16[48,24,128]{2,1,0:T(8,128)(2,1)} all-gather(bf16[6,24,128]{2,1,0:T(8,128)(2,1)S(1)} %get-tuple-element.18), channel_id=1, replica_groups=mesh['crop'=2,'row'=8,'col'=2] {'row'}, dimensions={0}, use_global_device_ids=true | all-gather | bytes 331776 | tf_op jit(solution)/shard_map/all_gather | solution.py:75
  79.3 1.8 copy.46
  81.2 1.0 bitcast_reduce_fusion
  82.2 1.1 multiply_reduce_fusion.1
  83.3 1.1 fusion.42
  84.4 1.6 fusion.25
  86.0 1.2 fusion.55
  87.3 1.0 multiply_convert_fusion
  88.3 1.9 all_gather.10
  90.2 0.9 copy.41
  91.0 0.7 copy.43
  91.7 2.3 %fusion.56 = f32[128,24,6]{1,2,0:T(8,128)} fusion(bf16[48,24,128]{1,0,2:T(8,128)(2,1)S(1)} %copy.36, bf16[6,48,128]{1,0,2:T(8,128)(2,1)} %copy.41), kind=kOutput, calls=%fused_computation.85 | convolution fusion | flops 1769472 | bytes 442368 | tf_op jit(solution)/shard_map/ijc,jkc->ikc/dot_general | solution.py:69
  94.0 1.2 copy.42
  95.2 5.6 %all-to-all-start = ((bf16[6,48,128]{2,0,1:T(8,128)(2,1)}), bf16[6,48,128]{2,0,1:T(8,128)(2,1)S(1)}, u32[]{:S(2)}, u32[]{:S(2)}) async-start(bf16[6,48,128]{2,0,1:T(8,128)(2,1)} %copy.43), calls=%async_computation.1 | async-start | bytes 196608 | tf_op jit(solution)/shard_map/all_to_all | solution.py:70
  100.8 0.9 fusion.5
  101.8 1.7 fusion.6
  103.4 4.5 %all-to-all-done = bf16[6,48,128]{2,0,1:T(8,128)(2,1)S(1)} async-done(((bf16[6,48,128]{2,0,1:T(8,128)(2,1)}), bf16[6,48,128]{2,0,1:T(8,128)(2,1)S(1)}, u32[]{:S(2)}, u32[]{:S(2)}) %all-to-all-start) | async-done | bytes 73760 | tf_op jit(solution)/shard_map/all_to_all | solution.py:70
  108.2 0.5 fusion.57
  109.2 1.0 fusion
  110.6 0.8 fusion.20
  111.3 88.0 %all-reduce.3.cloned.1.call-done = (f32[128,512]{1,0:T(8,128)}, f32[128,128]{1,0:T(8,128)}, f32[128,128]{1,0:T(8,128)}) async-done(((f32[128,512]{1,0:T(8,128)}, f32[128,128]{1,0:T(8,128)}, f32[128,128]{1,0:T(8,128)}), (f32[128,512]{1,0:T(8,128)}, f32[128,128]{1,0:T(8,128)}, f32[128,128]{1,0:T(8,128)})) %all-reduce.3.cloned.1.call-update) | async-done | bytes 393232 | tf_op jit(solution)/shard_map/psum | solution.py:108
  199.4 1.7 copy.61
  201.0 1.5 copy.62
  202.5 1.5 copy.63
  (46 shorter events, 1.5 us)
Async XLA Ops:
  7.2 1.9 copy-start
  7.2 74.0 %reduce-scatter.2.cloned.1.call-start = ((), (), s32[]{:S(2)}) async-start(), calls=%async_computation.2 | async-start | bytes 294912 | tf_op jit(solution)/shard_map/reduce_scatter | solution.py:53
  10.1 0.7 copy-start.2
  45.5 37.8 %copy-start.6 = (bf16[128,128]{1,0:T(8,128)(2,1)S(1)}, bf16[128,128]{1,0:T(8,128)(2,1)}, u32[]{:S(2)}) copy-start(bf16[128,128]{1,0:T(8,128)(2,1)} %param.17) | copy-start | bytes 98308
  45.5 37.8 %copy-start.9 = (f32[128]{0:T(128)S(1)}, f32[128]{0:T(128)}, u32[]{:S(2)}) copy-start(f32[128]{0:T(128)} %param.15) | copy-start | bytes 1540
  45.5 37.8 %copy-start.10 = (f32[128]{0:T(128)S(1)}, f32[128]{0:T(128)}, u32[]{:S(2)}) copy-start(f32[128]{0:T(128)} %param.16) | copy-start | bytes 1540
  46.4 38.0 %copy-start.4 = (bf16[6,24,128]{2,1,0:T(8,128)(2,1)S(1)}, bf16[6,24,128]{2,1,0:T(8,128)(2,1)}, u32[]{:S(2)}) copy-start(bf16[6,24,128]{2,1,0:T(8,128)(2,1)} %param.9) | copy-start | bytes 110596
  46.4 38.0 %copy-start.5 = (bf16[6,24,128]{2,1,0:T(8,128)(2,1)S(1)}, bf16[6,24,128]{2,1,0:T(8,128)(2,1)}, u32[]{:S(2)}) copy-start(bf16[6,24,128]{2,1,0:T(8,128)(2,1)} %param.10) | copy-start | bytes 110596
  46.4 38.0 %copy-start.11 = (f32[128]{0:T(128)S(1)}, f32[128]{0:T(128)}, u32[]{:S(2)}) copy-start(f32[128]{0:T(128)} %param.11) | copy-start | bytes 1540
  46.4 38.0 %copy-start.12 = (f32[128]{0:T(128)S(1)}, f32[128]{0:T(128)}, u32[]{:S(2)}) copy-start(f32[128]{0:T(128)} %param.12) | copy-start | bytes 1540
  91.7 9.1 %copy-start.1 = (f32[24,6,128]{2,1,0:T(8,128)S(1)}, f32[24,6,128]{2,1,0:T(8,128)}, u32[]{:S(2)}) copy-start(f32[24,6,128]{2,1,0:T(8,128)} %reduce-scatter.2.cloned.1.call-done) | copy-start | bytes 221188
  95.2 12.7 %all-to-all-start = ((bf16[6,48,128]{2,0,1:T(8,128)(2,1)}), bf16[6,48,128]{2,0,1:T(8,128)(2,1)S(1)}, u32[]{:S(2)}, u32[]{:S(2)}) async-start(bf16[6,48,128]{2,0,1:T(8,128)(2,1)} %copy.43), calls=%async_computation.1 | async-start | bytes 196608 | tf_op jit(solution)/shard_map/all_to_all | solution.py:70
  100.8 98.6 %all-reduce.3.cloned.1.call-start = ((), (), s32[]{:S(2)}) async-start(), calls=%async_computation.3 | async-start | bytes 786432 | tf_op jit(solution)/shard_map/psum | solution.py:108
  108.0 1.0 copy-start.3
  108.7 1.5 copy-start.7
  108.7 1.5 copy-start.8
Sparse Core Ops, SparseCore 0:
  46.5 8.5 reduce-scatter.1
  110.7 88.6 all-reduce.2
where the time goes:
time: 212 us; the launch traced here: 211 us
  waiting for transfers between devices  92.5 us (44%)
  blocking collectives  67.4 us (32%)
  between operations  14.3 us (7%)
  matrix products  12.8 us (6%)
  local copies, waits for them, and re-layouts  12.3 us (6%)
  other arithmetic  5.82 us (3%)
  starting transfers between devices  5.69 us (3%)
    psum x1, waiting for transfers between devices, local(): lax.psum((local_proj, local_gate, local_out), ('row', 'col'))  88 us
    all_gather x1, blocking collectives, local(): lax.all_gather(left_edge, 'row', axis=0, tiled=True)  32.9 us
    all_gather x1, blocking collectives, local(): right_all = lax.all_gather(right_edge, 'row', axis=0, tiled=True)  32.6 us
    all_to_all x1, starting transfers between devices, local(): lax.all_to_all(tri_rows, 'row', split_axis=1, concat_axis=0, tiled=True)  5.61 us
    unnamed x29, local copies, waits for them, and re-layouts  5.38 us
    all_to_all x1, waiting for transfers between devices, local(): lax.all_to_all(tri_rows, 'row', split_axis=1, concat_axis=0, tiled=True)  4.46 us
  transfers between devices with their start and end apart: 3, of which 2 were waited for; matrix products, arithmetic and copies ran while one was open for 2% of the time, Pallas kernels for 0%

commit v1 on v0

--- a/solution.py
+++ b/solution.py
@@ -1,7 +1,15 @@
+import functools
+
 import jax
 import jax.numpy as jnp
 from jax import lax
+from jax.experimental import pallas as pl
+from jax.experimental.pallas import tpu as pltpu
 from jax.sharding import PartitionSpec as P
+
+F32 = jnp.float32
+BF16 = jnp.bfloat16
+VMEM_BUDGET = 40 * 2**20
 
 
 def layer_norm(values, gain, bias):
@@ -18,7 +26,353 @@
     return inverse * (weighted - first - scaled * second)
 
 
-def local(
+def sigmoid(values):
+    return 0.5 * jnp.tanh(0.5 * values) + 0.5
+
+
+def dot(a, b, contract=((1,), (0,))):
+    return lax.dot_general(a, b, (contract, ((), ())), preferred_element_type=F32)
+
+
+def at(index, size):
+    return pl.ds(pl.multiple_of(index * size, size), size)
+
+
+def forward_kernel(
+    sizes,
+    pair_z,
+    pair_y,
+    mate_z,
+    mate_y,
+    cot_z,
+    cot_y,
+    norm_gain,
+    norm_bias,
+    proj_weight,
+    gate_weight,
+    tri_gain,
+    tri_bias,
+    out_weight,
+    block_out,
+    d_tri,
+    normed_out,
+    d_gate_out,
+    out_grad,
+    left_own,
+    right_own,
+    left_mate,
+    right_mate,
+    tri,
+    cot,
+    tri_norm_s,
+    d_update_s,
+    block_s,
+):
+    rows, cols, groups = sizes
+    total = rows * groups
+    cells = rows * cols
+    hidden = tri_gain.shape[-1]
+    me = lax.axis_index("row")
+    half = lax.axis_index("col")
+
+    def slot_row(ref_index, slot):
+        return lax.bitwise_xor(me, 2 * slot + ref_index)
+
+    for source, is_own in ((pair_z, True), (pair_y, True), (mate_z, False), (mate_y, False)):
+        parity = 0 if source is pair_z or source is mate_z else 1
+        left, right = (left_own, right_own) if is_own else (left_mate, right_mate)
+        values = source[...].astype(F32)
+        normed = layer_norm(values, norm_gain[...], norm_bias[...])[0].astype(BF16)
+        projected = dot(normed, proj_weight[...])
+        left_edge = sigmoid(projected[:, :hidden]) * projected[:, hidden : 2 * hidden]
+        right_edge = sigmoid(projected[:, 2 * hidden : 3 * hidden]) * projected[:, 3 * hidden :]
+        left_edge = left_edge.astype(BF16).astype(F32)
+        right_edge = right_edge.astype(BF16).astype(F32)
+        for slot in range(groups // 2):
+            place = at(slot_row(parity, slot), cells)
+            part = slice(slot * cells, (slot + 1) * cells)
+            left[place, :] = left_edge[part]
+            right[place, :] = right_edge[part]
+            if is_own:
+                normed_out[place, :] = normed[part]
+                cot[place, :] = (cot_z, cot_y)[parity][part, :]
+
+    def tri_block(block, carry):
+        first = block * rows
+
+        def step(k, sums):
+            new = list(sums)
+            for left, right in ((left_own, right_own), (left_mate, right_mate)):
+                tiles = [
+                    right[pl.ds(half * cols * cols + tile * 8 * cols + k, 8, stride=cols), :]
+                    for tile in range(cols // 8)
+                ]
+                for a in range(rows):
+                    row = left[pl.ds((first + a) * cols + k, 1), :]
+                    for t, tile in enumerate(tiles):
+                        new[a * len(tiles) + t] += row * tile
+            return tuple(new)
+
+        zero = jnp.zeros((8, hidden), F32)
+        sums = lax.fori_loop(0, cols, step, (zero,) * (rows * cols // 8), unroll=4)
+        for t, value in enumerate(sums):
+            tri[pl.ds(pl.multiple_of(block * cells + t * 8, 8), 8), :] = value
+        return carry
+
+    lax.fori_loop(0, groups, tri_block, 0)
+
+    def cell_block(block, carry):
+        place = at(block, 2 * cells)
+        tri_f, tri_hat, tri_inv = layer_norm(tri[place, :], tri_gain[...], tri_bias[...])
+        tri_norm = tri_f.astype(BF16)
+        update = dot(tri_norm, out_weight[...])
+        out_gate = sigmoid(dot(normed_out[place, :], gate_weight[...]))
+        block_s[place, :] = (out_gate * update).astype(BF16)
+        cotangent = cot[place, :].astype(F32)
+        gated = cotangent * out_gate
+        d_update = gated.astype(BF16)
+        d_gate_out[place, :] = (gated * update * (1.0 - out_gate)).astype(BF16)
+        d_norm = dot(d_update, out_weight[...], ((1,), (1,)))
+        d_tri[place, :] = norm_back(d_norm, tri_gain[...], tri_hat, tri_inv).astype(BF16)
+        tri_norm_s[place, :] = tri_norm
+        d_update_s[place, :] = d_update
+        return carry
+
+    lax.fori_loop(0, groups // 2, cell_block, 0)
+    block_out[...] = block_s[at(me, cells), :]
+    out_grad[...] = dot(tri_norm_s[...], d_update_s[...], ((0,), (0,))) * (1.0 / total)
+
+
+def backward_kernel(
+    sizes,
+    pair,
+    d_tri_own,
+    d_tri_mate,
+    normed_ref,
+    d_gate,
+    out_grad,
+    norm_gain,
+    norm_bias,
+    proj_weight,
+    gate_weight,
+    pair_grad,
+    weight_grads,
+    tri_own,
+    tri_mate,
+    left,
+    right,
+    left_gate,
+    left_value,
+    right_gate,
+    right_value,
+    d_proj_s,
+):
+    rows, cols, groups = sizes
+    total = rows * groups
+    cells = rows * cols
+    channels = norm_gain.shape[-1]
+    hidden = left.shape[-1]
+    me = lax.axis_index("row")
+    half = lax.axis_index("col")
+
+    def project(block, carry):
+        place = at(block, 2 * cells)
+        projected = dot(normed_ref[place, :], proj_weight[...])
+        for gate_s, value_s, edge_s, start in (
+            (left_gate, left_value, left, 0),
+            (right_gate, right_value, right, 2 * hidden),
+        ):
+            gate = sigmoid(projected[:, start : start + hidden])
+            value = projected[:, start + hidden : start + 2 * hidden]
+            edge = gate * value
+            gate_s[place, :] = gate
+            value_s[place, :] = edge * (1.0 - gate)
+            edge_s[place, :] = edge.astype(BF16).astype(F32)
+        tri_own[place, :] = d_tri_own[place, :].astype(F32)
+        tri_mate[place, :] = d_tri_mate[place, :].astype(F32)
+        return carry
+
+    lax.fori_loop(0, groups // 2, project, 0)
+    zero = jnp.zeros((8, hidden), F32)
+    tiles = cols // 8
+
+    def finish(sums, block_start, gate_s, value_s, column):
+        for t, value in enumerate(sums):
+            place = pl.ds(pl.multiple_of(block_start + t * 8, 8), 8)
+            d_proj_s[place, column : column + hidden] = value * value_s[place, :]
+            d_proj_s[place, column + hidden : column + 2 * hidden] = value * gate_s[place, :]
+
+    def left_block(block, carry):
+        first = block * rows
+
+        def step(j, sums):
+            new = list(sums)
+            for source, side in ((tri_own, half), (tri_mate, 1 - half)):
+                start = (side * cols + j) * cols
+                operand = [
+                    right[pl.ds(pl.multiple_of(start + t * 8, 8), 8), :] for t in range(tiles)
+                ]
+                for a in range(rows):
+                    row = source[pl.ds((first + a) * cols + j, 1), :]
+                    for t in range(tiles):
+                        new[a * tiles + t] += row * operand[t]
+            return tuple(new)
+
+        sums = lax.fori_loop(0, cols, step, (zero,) * (rows * tiles), unroll=4)
+        finish(sums, block * cells, left_gate, left_value, 0)
+        return carry
+
+    lax.fori_loop(0, groups, left_block, 0)
+
+    for source, side in ((tri_own, half), (tri_mate, 1 - half)):
+
+        def right_block(block, carry, source=source, side=side):
+            first = block * rows
+
+            def step(i, sums):
+                new = list(sums)
+                operand = [
+                    left[pl.ds(pl.multiple_of(i * cols + t * 8, 8), 8), :] for t in range(tiles)
+                ]
+                for a in range(rows):
+                    row = source[pl.ds(i * cols + first + a, 1), :]
+                    for t in range(tiles):
+                        new[a * tiles + t] += row * operand[t]
+                return tuple(new)
+
+            sums = lax.fori_loop(0, total, step, (zero,) * (rows * tiles), unroll=8)
+            finish(
+                sums, (side * cols + first) * cols, right_gate, right_value, 2 * hidden
+            )
+            return carry
+
+        lax.fori_loop(0, cols // rows, right_block, 0)
+
+    scale = 1.0 / total
+    width = 4 * hidden
+    weight_grads[:, :width] = (
+        dot(normed_ref[...], d_proj_s[...].astype(BF16), ((0,), (0,))) * scale
+    )
+    weight_grads[:, width : width + channels] = (
+        dot(normed_ref[...], d_gate[...], ((0,), (0,))) * scale
+    )
+    weight_grads[:, width + channels :] = out_grad[...]
+    own = at(me, cells)
+    d_normed = dot(d_proj_s[own, :].astype(BF16), proj_weight[...], ((1,), (1,))) + dot(
+        d_gate[own, :], gate_weight[...], ((1,), (1,))
+    )
+    _, hat, inverse = layer_norm(pair[...].astype(F32), norm_gain[...], norm_bias[...])
+    pair_grad[...] = norm_back(d_normed, norm_gain[...], hat, inverse)
+
+
+def replicated(
+    pair_rep,
+    cotangent,
+    norm_gain,
+    norm_bias,
+    proj_weight,
+    gate_weight,
+    tri_gain,
+    tri_bias,
+    out_weight,
+):
+    rows, cols, channels = pair_rep.shape
+    hidden = tri_gain.shape[0]
+    groups = lax.axis_size("row")
+    cells = rows * cols
+    every = cells * groups
+    sizes = (rows, cols, groups)
+    norm_gain, norm_bias = norm_gain[None], norm_bias[None]
+    tri_gain, tri_bias = tri_gain[None], tri_bias[None]
+
+    def across(value, mask):
+        return lax.ppermute(value, "row", [(i, i ^ mask) for i in range(groups)])
+
+    pair = pair_rep.reshape(cells, channels)
+    own = jnp.stack([pair, cotangent.reshape(cells, channels)])
+    got = [own] + [across(own, 2 * s) for s in range(1, groups // 2)]
+    near = jnp.concatenate(got, axis=1)
+    far = across(near, 1)
+    pair_z, cot_z, pair_y, cot_y = near[0], near[1], far[0], far[1]
+    swap = [(0, 1), (1, 0)]
+    mate_z = lax.ppermute(pair_z, "col", swap)
+    mate_y = lax.ppermute(pair_y, "col", swap)
+
+    def vmem(*shape, dtype=F32):
+        return pltpu.VMEM(shape, dtype)
+
+    params = pltpu.CompilerParams(vmem_limit_bytes=VMEM_BUDGET)
+    shape = jax.ShapeDtypeStruct
+    block_out, d_tri, normed, d_gate, out_grad = pl.pallas_call(
+        functools.partial(forward_kernel, sizes),
+        out_shape=(
+            shape((cells, channels), BF16),
+            shape((every, hidden), BF16),
+            shape((every, channels), BF16),
+            shape((every, channels), BF16),
+            shape((hidden, channels), F32),
+        ),
+        scratch_shapes=[
+            vmem(every, hidden),
+            vmem(every, hidden),
+            vmem(every, hidden),
+            vmem(every, hidden),
+            vmem(every, hidden),
+            vmem(every, channels, dtype=BF16),
+            vmem(every, hidden, dtype=BF16),
+            vmem(every, channels, dtype=BF16),
+            vmem(every, channels, dtype=BF16),
+        ],
+        compiler_params=params,
+        name="forward",
+    )(
+        pair_z,
+        pair_y,
+        mate_z,
+        mate_y,
+        cot_z,
+        cot_y,
+        norm_gain,
+        norm_bias,
+        proj_weight,
+        gate_weight,
+        tri_gain,
+        tri_bias,
+        out_weight,
+    )
+    d_tri_mate = lax.ppermute(d_tri, "col", swap)
+    pair_grad, grads = pl.pallas_call(
+        functools.partial(backward_kernel, sizes),
+        out_shape=(
+            shape((cells, channels), F32),
+            shape((channels, 4 * hidden + channels + channels), F32),
+        ),
+        scratch_shapes=[vmem(every, hidden) for _ in range(8)] + [vmem(every, 4 * hidden)],
+        compiler_params=params,
+        name="backward",
+    )(
+        pair,
+        d_tri,
+        d_tri_mate,
+        normed,
+        d_gate,
+        out_grad,
+        norm_gain,
+        norm_bias,
+        proj_weight,
+        gate_weight,
+    )
+    grads = grads + lax.ppermute(grads, "col", swap)
+    return (
+        block_out.reshape(pair_rep.shape),
+        pair_grad.reshape(pair_rep.shape),
+        grads[:, : 4 * hidden],
+        grads[:, 4 * hidden : 4 * hidden + channels],
+        grads[:, 4 * hidden + channels :],
+    )
+
+
+def sharded(
     pair_rep,
     cotangent,
     norm_gain,
@@ -109,6 +463,17 @@
     return (block_out, pair_grad, proj_grad, gate_grad, out_grad)
 
 
+def local(pair_rep, *others):
+    rows, cols, channels = pair_rep.shape
+    groups = lax.axis_size("row")
+    every = rows * groups * cols
+    fits = 16 * every * channels * 4 <= VMEM_BUDGET
+    paired = lax.axis_size("col") == 2 and groups & (groups - 1) == 0 and groups >= 2
+    whole_tiles = cols % 8 == 0 and cols % rows == 0 and rows * cols % 16 == 0
+    plan = replicated if fits and paired and whole_tiles else sharded
+    return plan(pair_rep, *others)
+
+
 def solution(mesh):
     return jax.shard_map(
         local,

time: 212 us -> 42.1 us (0.20)
  waiting for transfers between devices: 92.5 us -> 16.6 us
  blocking collectives: 67.4 us -> 0 us
  Pallas kernels: 0 us -> 13.8 us
  between operations: 14.3 us -> 0.74 us
  matrix products: 12.8 us -> 0 us
  local copies, waits for them, and re-layouts: 12.3 us -> 2.1 us
  other arithmetic: 5.82 us -> 0.92 us
    psum x1 -> x0, waiting for transfers between devices: 88 us -> none  [local(): lax.psum((local_proj, local_gate, local_out), ('row', 'col'))]
    all_gather x3 -> x0, blocking collectives: 67.4 us -> none  [the longest x1 32.9 us: local(): lax.all_gather(left_edge, 'row', axis=0, tiled=True)]
    ppermute x0 -> x8, waiting for transfers between devices: none -> 16.6 us  [the longest x4 12.3 us: across(): return lax.ppermute(value, 'row', [(i, i ^ mask) for i in range(groups)])]
    pallas_call x0 -> x2, Pallas kernels: none -> 13.8 us  [the longest x1 6.9 us: replicated(): pl.pallas_call(functools.partial(forward_kernel, sizes), out_shape=(shape...]
    dot_general x12 -> x0, matrix products: 12.8 us -> none  [the longest x1 2.29 us: local(): jnp.einsum('ijc,jkc->ikc', tri_rows, right_all, preferred_element_type=f32)]
    ppermute x0 -> x8, starting transfers between devices: none -> 7.78 us  [the longest x4 7.34 us: across(): return lax.ppermute(value, 'row', [(i, i ^ mask) for i in range(groups)])]
    all_to_all x1 -> x0, starting transfers between devices: 5.61 us -> none  [local(): lax.all_to_all(tri_rows, 'row', split_axis=1, concat_axis=0, tiled=True)]
    unnamed x29 -> x18, local copies, waits for them, and re-layouts: 5.38 us -> 0.67 us
  transfers between devices with their start and end apart: 3 -> 8, of which waited for: 2 -> 6; matrix products, arithmetic and copies ran while one was open for 2% -> 0% of each run, Pallas kernels for 0% -> 0%
where the time goes in v1:
time: 42.1 us; the launch traced here: 42 us
  waiting for transfers between devices  16.6 us (39%)
  Pallas kernels  13.8 us (33%)
  starting transfers between devices  7.78 us (18%)
  local copies, waits for them, and re-layouts  2.1 us (5%)
  other arithmetic  0.92 us (2%)
  between operations  0.74 us (2%)
    ppermute x4, waiting for transfers between devices, across(): return lax.ppermute(value, 'row', [(i, i ^ mask) for i in range(groups)])  12.3 us
    ppermute x4, starting transfers between devices, across(): return lax.ppermute(value, 'row', [(i, i ^ mask) for i in range(groups)])  7.34 us
    pallas_call x1, Pallas kernels, replicated(): pl.pallas_call(functools.partial(forward_kernel, sizes), out_shape=(shape...  6.9 us
    pallas_call x1, Pallas kernels, replicated(): pl.pallas_call(functools.partial(backward_kernel, sizes), out_shape=(shap...  6.86 us
    ppermute x1, waiting for transfers between devices, replicated(): grads = grads + lax.ppermute(grads, 'col', swap)  1.57 us
    ppermute x1, waiting for transfers between devices, replicated(): d_tri_mate = lax.ppermute(d_tri, 'col', swap)  1.43 us
    ppermute x1, waiting for transfers between devices, replicated(): mate_y = lax.ppermute(pair_y, 'col', swap)  1.35 us
  transfers between devices with their start and end apart: 8, of which 6 were waited for; matrix products, arithmetic and copies ran while one was open for 0% of the time, Pallas kernels for 0%

profile of v1, /device:TPU:0, one launch (start us, length us, event | category | flops | bytes accessed | tf_op | source)
XLA Modules:
  0.0 42.0 jit_solution(8375545388856015082)
XLA Ops:
  0.6 0.0 copy-start.1
  0.6 0.0 copy-start.8
  0.7 0.8 %pad_maximum_fusion.1 = bf16[2,144,128]{2,1,0:T(8,128)(2,1)S(1)} fusion(bf16[1,144,128]{2,1,0:T(8,128)(2,1)} %bitcast.26, bf16[1,144,128]{2,1,0:T(8,128)(2,1)} %bitcast.17), kind=kLoop, calls=%fused_computation.5 | loop fusion | flops 36864 | bytes 147456 | tf_op jit(solution)/shard_map/stack | solution.py:292
  1.5 5.1 %collective-permute-start.2 = (bf16[2,144,128]{2,1,0:T(8,128)(2,1)S(1)}, bf16[2,144,128]{2,1,0:T(8,128)(2,1)S(1)}, u32[]{:S(2)}, u32[]{:S(2)}) collective-permute-start(bf16[2,144,128]{2,1,0:T(8,128)(2,1)S(1)} %pad_maximum_fusion.1), channel_id=1, source_target_pairs={{0,12},{2,14},{4,8},{6,10},{8,4},{10,6},{12,0},{14,2},{1,13},{3,15... | collective-permute-start | bytes 221192 | tf_op jit(solution)/shard_map/ppermute | solution.py:289
  6.6 0.0 collective-permute-start.1
  6.6 0.6 %collective-permute-start = (bf16[2,144,128]{2,1,0:T(8,128)(2,1)S(1)}, bf16[2,144,128]{2,1,0:T(8,128)(2,1)S(1)}, u32[]{:S(2)}, u32[]{:S(2)}) collective-permute-start(bf16[2,144,128]{2,1,0:T(8,128)(2,1)S(1)} %pad_maximum_fusion.1), channel_id=1, source_target_pairs={{0,4},{2,6},{4,0},{6,2},{8,12},{10,14},{12,8},{14,10},{1,5},{3,7},... | collective-permute-start | bytes 221192 | tf_op jit(solution)/shard_map/ppermute | solution.py:289
  7.3 2.1 %collective-permute-done.2 = bf16[2,144,128]{2,1,0:T(8,128)(2,1)S(1)} collective-permute-done((bf16[2,144,128]{2,1,0:T(8,128)(2,1)S(1)}, bf16[2,144,128]{2,1,0:T(8,128)(2,1)S(1)}, u32[]{:S(2)}, u32[]{:S(2)}) %collective-permute-start.2) | collective-permute-done | bytes 73760 | tf_op jit(solution)/shard_map/ppermute | solution.py:289
  9.4 3.5 %collective-permute-done.1 = bf16[2,144,128]{2,1,0:T(8,128)(2,1)S(1)} collective-permute-done((bf16[2,144,128]{2,1,0:T(8,128)(2,1)S(1)}, bf16[2,144,128]{2,1,0:T(8,128)(2,1)S(1)}, u32[]{:S(2)}, u32[]{:S(2)}) %collective-permute-start.1) | collective-permute-done | bytes 73760 | tf_op jit(solution)/shard_map/ppermute | solution.py:289
  12.8 0.0 collective-permute-done
  12.8 0.0 copy-done.1
  12.8 0.0 copy-done.8
  12.9 1.6 %collective-permute-start.3 = (bf16[2,576,128]{2,1,0:T(8,128)(2,1)S(1)}, bf16[2,576,128]{2,1,0:T(8,128)(2,1)S(1)}, u32[]{:S(2)}, u32[]{:S(2)}) collective-permute-start(bf16[2,576,128]{2,1,0:T(8,128)(2,1)S(1)} %pad_maximum_fusion), channel_id=1, source_target_pairs={{0,2},{2,0},{4,6},{6,4},{8,10},{10,8},{12,14},{14,12},{1,3},{3,1},... | collective-permute-start | bytes 884744 | tf_op jit(solution)/shard_map/ppermute | solution.py:289
  14.5 0.0 copy-start
  14.5 0.1 collective-permute-start.4
  14.6 6.7 %collective-permute-done.3 = bf16[2,576,128]{2,1,0:T(8,128)(2,1)S(1)} collective-permute-done((bf16[2,576,128]{2,1,0:T(8,128)(2,1)S(1)}, bf16[2,576,128]{2,1,0:T(8,128)(2,1)S(1)}, u32[]{:S(2)}, u32[]{:S(2)}) %collective-permute-start.3) | collective-permute-done | bytes 294944 | tf_op jit(solution)/shard_map/ppermute | solution.py:289
  21.3 0.1 collective-permute-start.5
  21.4 0.0 collective-permute-done.4.mate_z
  21.4 1.3 %collective-permute-done.5.mate_y = bf16[576,128]{1,0:T(8,128)(2,1)S(1)} collective-permute-done((bf16[576,128]{1,0:T(8,128)(2,1)S(1)}, bf16[576,128]{1,0:T(8,128)(2,1)S(1)}, u32[]{:S(2)}, u32[]{:S(2)}) %collective-permute-start.5) | collective-permute-done | bytes 147488 | tf_op jit(solution)/shard_map/ppermute | solution.py:299
  22.8 0.0 copy-done
  22.8 0.0 copy-done.2
  22.8 0.6 %copy-done.4 = f32[128]{0:T(128)S(1)} copy-done((f32[128]{0:T(128)S(1)}, f32[128]{0:T(128)}, u32[]{:S(2)}) %copy-start.4) | copy-done | bytes 536
  23.4 0.0 copy-done.5
  23.4 0.0 copy-done.6
  23.4 6.9 %forward.1 = (bf16[144,128]{1,0:T(8,128)(2,1)}, bf16[1152,128]{1,0:T(8,128)(2,1)S(1)}, bf16[1152,128]{1,0:T(8,128)(2,1)S(1)}, bf16[1152,128]{1,0:T(8,128)(2,1)S(1)}, f32[128,128]{1,0:T(8,128)S(1)}) custom-call(bf16[576,128]{1,0:T(8,128)(2,1)S(1)} %get-tuple-element.24.pair_z, bf16[576,128]{1,0:T(8,128)(2,1)S(1)} %get-tuple-element.22.pair_y, ...), custom_call_target="tpu_custom_call" | custom-call | tf_op jit(solution)/shard_map/forward/pallas_call | solution.py:306
  30.3 0.1 collective-permute-start.6
  30.5 1.4 %collective-permute-done.6.d_tri_mate = bf16[1152,128]{1,0:T(8,128)(2,1)S(1)} collective-permute-done((bf16[1152,128]{1,0:T(8,128)(2,1)S(1)}, bf16[1152,128]{1,0:T(8,128)(2,1)S(1)}, u32[]{:S(2)}, u32[]{:S(2)}) %collective-permute-start.6) | collective-permute-done | bytes 294944 | tf_op jit(solution)/shard_map/ppermute | solution.py:343
  31.9 6.9 %backward.1 = (f32[144,128]{1,0:T(8,128)}, f32[128,768]{1,0:T(8,128)S(1)}) custom-call(bf16[144,128]{1,0:T(8,128)(2,1)S(1)} %bitcast.19, bf16[1152,128]{1,0:T(8,128)(2,1)S(1)} %get-tuple-element.13.d_tri_own, bf16[1152,128]{1,0:T(8,128)(2,1)S(1)} %collective-permute-done.6.d_tri_mate, bf16[1152,128]{1,0:T(8,128)(2,1)S(1)} %get-tuple-element.14.normed_ref, ...), custom_call_target="tpu_custom_call" | custom-call | tf_op jit(solution)/shard_map/backward/pallas_call | solution.py:344
  38.8 0.1 collective-permute-start.7
  38.9 1.6 %collective-permute-done.7 = f32[128,768]{1,0:T(8,128)S(1)} collective-permute-done((f32[128,768]{1,0:T(8,128)S(1)}, f32[128,768]{1,0:T(8,128)S(1)}, u32[]{:S(2)}, u32[]{:S(2)}) %collective-permute-start.7) | collective-permute-done | bytes 393248 | tf_op jit(solution)/shard_map/ppermute | solution.py:365
  40.5 0.1 add.3
  40.6 0.7 %fusion = (f32[128,128]{1,0:T(8,128)}, f32[128,128]{1,0:T(8,128)}) fusion(f32[128,768]{1,0:T(8,128)S(1)} %add.3), kind=kLoop, calls=%fused_computation.6 | loop fusion | bytes 262144 | tf_op jit(solution)/shard_map/slice | solution.py:371
  41.2 0.7 %slice.32 = f32[128,512]{1,0:T(8,128)} slice(f32[128,768]{1,0:T(8,128)S(1)} %add.3), slice={[0:128], [0:512]} | slice | bytes 524288 | tf_op jit(solution)/shard_map/slice | solution.py:369
  (11 shorter events, 0.1 us)
Async XLA Ops:
  0.6 12.2 %copy-start.1 = (bf16[6,24,128]{2,1,0:T(8,128)(2,1)S(1)}, bf16[6,24,128]{2,1,0:T(8,128)(2,1)}, u32[]{:S(2)}) copy-start(bf16[6,24,128]{2,1,0:T(8,128)(2,1)} %param.9) | copy-start | bytes 110596
  0.6 12.2 %copy-start.8 = (bf16[6,24,128]{2,1,0:T(8,128)(2,1)S(1)}, bf16[6,24,128]{2,1,0:T(8,128)(2,1)}, u32[]{:S(2)}) copy-start(bf16[6,24,128]{2,1,0:T(8,128)(2,1)} %param.10) | copy-start | bytes 110596
  1.5 7.9 %collective-permute-start.2 = (bf16[2,144,128]{2,1,0:T(8,128)(2,1)S(1)}, bf16[2,144,128]{2,1,0:T(8,128)(2,1)S(1)}, u32[]{:S(2)}, u32[]{:S(2)}) collective-permute-start(bf16[2,144,128]{2,1,0:T(8,128)(2,1)S(1)} %pad_maximum_fusion.1), channel_id=1, source_target_pairs={{0,12},{2,14},{4,8},{6,10},{8,4},{10,6},{12,0},{14,2},{1,13},{3,15... | collective-permute-start | bytes 221192 | tf_op jit(solution)/shard_map/ppermute | solution.py:289
  6.6 6.2 %collective-permute-start.1 = (bf16[2,144,128]{2,1,0:T(8,128)(2,1)S(1)}, bf16[2,144,128]{2,1,0:T(8,128)(2,1)S(1)}, u32[]{:S(2)}, u32[]{:S(2)}) collective-permute-start(bf16[2,144,128]{2,1,0:T(8,128)(2,1)S(1)} %pad_maximum_fusion.1), channel_id=1, source_target_pairs={{0,8},{2,10},{4,12},{6,14},{8,0},{10,2},{12,4},{14,6},{1,9},{3,11}... | collective-permute-start | bytes 221192 | tf_op jit(solution)/shard_map/ppermute | solution.py:289
  6.6 6.2 %collective-permute-start = (bf16[2,144,128]{2,1,0:T(8,128)(2,1)S(1)}, bf16[2,144,128]{2,1,0:T(8,128)(2,1)S(1)}, u32[]{:S(2)}, u32[]{:S(2)}) collective-permute-start(bf16[2,144,128]{2,1,0:T(8,128)(2,1)S(1)} %pad_maximum_fusion.1), channel_id=1, source_target_pairs={{0,4},{2,6},{4,0},{6,2},{8,12},{10,14},{12,8},{14,10},{1,5},{3,7},... | collective-permute-start | bytes 221192 | tf_op jit(solution)/shard_map/ppermute | solution.py:289
  12.9 8.4 %collective-permute-start.3 = (bf16[2,576,128]{2,1,0:T(8,128)(2,1)S(1)}, bf16[2,576,128]{2,1,0:T(8,128)(2,1)S(1)}, u32[]{:S(2)}, u32[]{:S(2)}) collective-permute-start(bf16[2,576,128]{2,1,0:T(8,128)(2,1)S(1)} %pad_maximum_fusion), channel_id=1, source_target_pairs={{0,2},{2,0},{4,6},{6,4},{8,10},{10,8},{12,14},{14,12},{1,3},{3,1},... | collective-permute-start | bytes 884744 | tf_op jit(solution)/shard_map/ppermute | solution.py:289
  14.5 8.3 %copy-start = (bf16[128,512]{1,0:T(8,128)(2,1)S(1)}, bf16[128,512]{1,0:T(8,128)(2,1)}, u32[]{:S(2)}) copy-start(bf16[128,512]{1,0:T(8,128)(2,1)} %proj_weight.3) | copy-start | bytes 393220
  14.5 6.9 %collective-permute-start.4 = (bf16[576,128]{1,0:T(8,128)(2,1)S(1)}, bf16[576,128]{1,0:T(8,128)(2,1)S(1)}, u32[]{:S(2)}, u32[]{:S(2)}) collective-permute-start(bf16[576,128]{1,0:T(8,128)(2,1)S(1)} %get-tuple-element.24.pair_z), channel_id=1, source_target_pairs={{0,1},{1,0},{2,3},{3,2},{4,5},{5,4},{6,7},{7,6},{8,9},{9,8},{10,11... | collective-permute-start | bytes 442376 | tf_op jit(solution)/shard_map/ppermute | solution.py:298
  21.3 1.5 %copy-start.2 = (bf16[128,128]{1,0:T(8,128)(2,1)S(1)}, bf16[128,128]{1,0:T(8,128)(2,1)}, u32[]{:S(2)}) copy-start(bf16[128,128]{1,0:T(8,128)(2,1)} %gate_weight.3) | copy-start | bytes 98308
  21.3 1.5 %copy-start.3 = (bf16[128,128]{1,0:T(8,128)(2,1)S(1)}, bf16[128,128]{1,0:T(8,128)(2,1)}, u32[]{:S(2)}) copy-start(bf16[128,128]{1,0:T(8,128)(2,1)} %out_weight.1) | copy-start | bytes 98308
  21.3 1.5 %copy-start.7 = (f32[128]{0:T(128)S(1)}, f32[128]{0:T(128)}, u32[]{:S(2)}) copy-start(f32[128]{0:T(128)} %param.16) | copy-start | bytes 1540
  21.3 1.4 %collective-permute-start.5 = (bf16[576,128]{1,0:T(8,128)(2,1)S(1)}, bf16[576,128]{1,0:T(8,128)(2,1)S(1)}, u32[]{:S(2)}, u32[]{:S(2)}) collective-permute-start(bf16[576,128]{1,0:T(8,128)(2,1)S(1)} %get-tuple-element.22.pair_y), channel_id=1, source_target_pairs={{0,1},{1,0},{2,3},{3,2},{4,5},{5,4},{6,7},{7,6},{8,9},{9,8},{10,11... | collective-permute-start | bytes 442376 | tf_op jit(solution)/shard_map/ppermute | solution.py:299
  22.8 0.7 %copy-start.4 = (f32[128]{0:T(128)S(1)}, f32[128]{0:T(128)}, u32[]{:S(2)}) copy-start(f32[128]{0:T(128)} %param.11) | copy-start | bytes 1540
  22.8 0.7 %copy-start.5 = (f32[128]{0:T(128)S(1)}, f32[128]{0:T(128)}, u32[]{:S(2)}) copy-start(f32[128]{0:T(128)} %param.12) | copy-start | bytes 1540
  22.8 0.7 %copy-start.6 = (f32[128]{0:T(128)S(1)}, f32[128]{0:T(128)}, u32[]{:S(2)}) copy-start(f32[128]{0:T(128)} %param.15) | copy-start | bytes 1540
  30.3 1.6 %collective-permute-start.6 = (bf16[1152,128]{1,0:T(8,128)(2,1)S(1)}, bf16[1152,128]{1,0:T(8,128)(2,1)S(1)}, u32[]{:S(2)}, u32[]{:S(2)}) collective-permute-start(bf16[1152,128]{1,0:T(8,128)(2,1)S(1)} %get-tuple-element.13.d_tri_own), channel_id=1, source_target_pairs={{0,1},{1,0},{2,3},{3,2},{4,5},{5,4},{6,7},{7,6},{8,9},{9,8},{10,11... | collective-permute-start | bytes 884744 | tf_op jit(solution)/shard_map/ppermute | solution.py:343
  38.8 1.7 %collective-permute-start.7 = (f32[128,768]{1,0:T(8,128)S(1)}, f32[128,768]{1,0:T(8,128)S(1)}, u32[]{:S(2)}, u32[]{:S(2)}) collective-permute-start(f32[128,768]{1,0:T(8,128)S(1)} %get-tuple-element.18), channel_id=1, source_target_pairs={{0,1},{1,0},{2,3},{3,2},{4,5},{5,4},{6,7},{7,6},{8,9},{9,8},{10,11... | collective-permute-start | bytes 1179656 | tf_op jit(solution)/shard_map/ppermute | solution.py:365

commit v2 on v0

--- a/solution.py
+++ b/solution.py
@@ -1,7 +1,19 @@
+import functools
+
 import jax
 import jax.numpy as jnp
 from jax import lax
+from jax.experimental import pallas as pl
+from jax.experimental.pallas import tpu as pltpu
 from jax.sharding import PartitionSpec as P
+
+F32 = jnp.float32
+BF16 = jnp.bfloat16
+VMEM_BUDGET = 24 * 2**20
+SWAP = ((0, 1), (1, 0))
+NATIVE = ((1,), (0,))
+BY_ROWS = ((0,), (0,))
+TRANSPOSED = ((1,), (1,))
 
 
 def layer_norm(values, gain, bias):
@@ -18,7 +30,483 @@
     return inverse * (weighted - first - scaled * second)
 
 
-def local(
+def sigmoid(values):
+    return 0.5 * jnp.tanh(0.5 * values) + 0.5
+
+
+def dot(a, b, contract=NATIVE):
+    return lax.dot_general(a, b, (contract, ((), ())), preferred_element_type=F32)
+
+
+def at(index, size):
+    return pl.ds(pl.multiple_of(index * size, size), size)
+
+
+def tile(start):
+    return pl.ds(pl.multiple_of(start, 8), 8)
+
+
+def places(groups):
+    me = lax.axis_index("row")
+    return [lax.bitwise_xor(me // 2, t) for t in range(groups // 2)]
+
+
+def row_block(which, b):
+    me = lax.axis_index("row")
+    parity = lax.rem(me, 2)
+    return 2 * b + (parity if which == 0 else 1 - parity)
+
+
+def edges(values, norm_gain, norm_bias, proj_weight):
+    hidden = proj_weight.shape[1] // 4
+    normed = layer_norm(values.astype(F32), norm_gain, norm_bias)[0].astype(BF16)
+    projected = dot(normed, proj_weight)
+    sides = []
+    for start in (0, 2 * hidden):
+        gate = sigmoid(projected[:, start : start + hidden])
+        edge = gate * projected[:, start + hidden : start + 2 * hidden]
+        sides.append((edge.astype(BF16).astype(F32), gate, edge * (1.0 - gate)))
+    return normed, sides
+
+
+def own_edges_kernel(sizes, x, gain, bias, weight, normed_out, *outs):
+    rows, cols, groups = sizes
+    cells = rows * cols
+    normed, sides = edges(x[...], gain[...], bias[...], weight[...])
+    for t, b in enumerate(places(groups)):
+        part = slice(t * cells, (t + 1) * cells)
+        place = at(b, cells)
+        normed_out[place, :] = normed[part]
+        for out, value in zip(outs, sides[0] + sides[1], strict=True):
+            out[place, :] = value[part]
+
+
+def mate_edges_kernel(sizes, x, gain, bias, weight, left, right):
+    rows, cols, groups = sizes
+    cells = rows * cols
+    _, sides = edges(x[...], gain[...], bias[...], weight[...])
+    for t, b in enumerate(places(groups)):
+        part = slice(t * cells, (t + 1) * cells)
+        left[at(b, cells), :] = sides[0][0][part]
+        right[at(b, cells), :] = sides[1][0][part]
+
+
+def triangle_kernel(sizes, *refs):
+    rows, cols, groups = sizes
+    cells = rows * cols
+    lefts, rights, (tri,), picked = refs[:4], refs[4:8], refs[8:9], refs[9:]
+    hidden = tri.shape[-1]
+    half = lax.axis_index("col")
+    zero = jnp.zeros((8, hidden), F32)
+    count = cols // 8
+    blocks = cols // rows
+    for side in range(2):
+        for which in range(2):
+            for s in range(blocks // 2):
+                b = half * (blocks // 2) + s
+                p = row_block(which, b) - half * blocks
+                picked[side][at(p, cells), :] = rights[2 * side + which][at(b, cells), :]
+
+    for which in range(2):
+
+        def tri_block(b, carry, which=which):
+            def step(k, sums):
+                new = list(sums)
+                for side in range(2):
+                    left = lefts[2 * side + which]
+                    tiles = [
+                        picked[side][pl.ds(t * 8 * cols + k, 8, stride=cols), :]
+                        for t in range(count)
+                    ]
+                    for a in range(rows):
+                        row = left[pl.ds((b * rows + a) * cols + k, 1), :]
+                        for t in range(count):
+                            new[a * count + t] += row * tiles[t]
+                return tuple(new)
+
+            sums = lax.fori_loop(0, cols, step, (zero,) * (rows * count), unroll=4)
+            start = row_block(which, b) * cells
+            for t, value in enumerate(sums):
+                tri[tile(start + t * 8), :] = value
+            return carry
+
+        lax.fori_loop(0, groups // 2, tri_block, 0)
+
+
+def cells_kernel(
+    sizes,
+    tri,
+    normed_0,
+    normed_1,
+    cot_0,
+    cot_1,
+    gate_weight,
+    gain,
+    bias,
+    out_weight,
+    block_out,
+    d_tri,
+    d_gate,
+    tri_norm_out,
+    d_update_out,
+):
+    rows, cols, groups = sizes
+    cells = rows * cols
+    for which, normed, cot in ((0, normed_0, cot_0), (1, normed_1, cot_1)):
+        for t, b in enumerate(places(groups)):
+            place = at(row_block(which, b), cells)
+            tri_f, hat, inverse = layer_norm(tri[place, :], gain[...], bias[...])
+            tri_norm = tri_f.astype(BF16)
+            update = dot(tri_norm, out_weight[...])
+            out_gate = sigmoid(dot(normed[at(b, cells), :], gate_weight[...]))
+            if which == 0 and t == 0:
+                block_out[...] = (out_gate * update).astype(BF16)
+            gated = cot[t * cells : (t + 1) * cells, :].astype(F32) * out_gate
+            d_update = gated.astype(BF16)
+            d_gate[place, :] = (gated * update * (1.0 - out_gate)).astype(BF16)
+            d_norm = dot(d_update, out_weight[...], TRANSPOSED)
+            d_tri[place, :] = norm_back(d_norm, gain[...], hat, inverse).astype(BF16)
+            tri_norm_out[place, :] = tri_norm
+            d_update_out[place, :] = d_update
+
+
+def contract(rows, cols, count, unroll, start, source, row_at, operand, operand_at):
+    tiles = cols // 8
+
+    def step(term, sums):
+        new = list(sums)
+        loaded = [operand[tile(operand_at(term) + t * 8), :] for t in range(tiles)]
+        for a in range(rows):
+            row = source[pl.ds(row_at(a, term), 1), :]
+            for t in range(tiles):
+                new[a * tiles + t] += row * loaded[t]
+        return tuple(new)
+
+    return lax.fori_loop(0, count, step, start, unroll=unroll)
+
+
+def early_kernel(
+    sizes,
+    d_tri_ref,
+    d_gate,
+    tri_norm,
+    d_update,
+    normed_0,
+    normed_1,
+    left_0,
+    left_1,
+    right_0,
+    right_1,
+    left,
+    right,
+    normed,
+    d_left,
+    d_right,
+    small_grads,
+    source,
+):
+    rows, cols, groups = sizes
+    cells = rows * cols
+    hidden = left.shape[-1]
+    channels = normed.shape[-1]
+    half = lax.axis_index("col")
+    zeros = (jnp.zeros((8, hidden), F32),) * (rows * cols // 8)
+    source[...] = d_tri_ref[...].astype(F32)
+    for which, part_n, part_l, part_r in (
+        (0, normed_0, left_0, right_0),
+        (1, normed_1, left_1, right_1),
+    ):
+        for b in range(groups // 2):
+            place, part = at(row_block(which, b), cells), slice(b * cells, (b + 1) * cells)
+            normed[place, :] = part_n[part, :]
+            left[place, :] = part_l[part, :]
+            right[place, :] = part_r[part, :]
+
+    def left_block(p, carry):
+        sums = contract(
+            rows,
+            cols,
+            cols,
+            8,
+            zeros,
+            source,
+            lambda a, j: (p * rows + a) * cols + j,
+            right,
+            lambda j: (half * cols + j) * cols,
+        )
+        for t, value in enumerate(sums):
+            d_left[tile(p * cells + t * 8), :] = value
+        return carry
+
+    lax.fori_loop(0, groups, left_block, 0)
+
+    def right_block(p, carry):
+        sums = contract(
+            rows,
+            cols,
+            rows * groups,
+            8,
+            zeros,
+            source,
+            lambda a, i: i * cols + p * rows + a,
+            left,
+            lambda i: i * cols,
+        )
+        for t, value in enumerate(sums):
+            d_right[tile(p * cells + t * 8), :] = value
+        return carry
+
+    lax.fori_loop(0, cols // rows, right_block, 0)
+    scale = 1.0 / (rows * groups)
+    small_grads[:, :channels] = dot(normed[...], d_gate[...], BY_ROWS) * scale
+    small_grads[:, channels:] = dot(tri_norm[...], d_update[...], BY_ROWS) * scale
+
+
+def late_kernel(
+    sizes,
+    pair,
+    d_tri_ref,
+    d_gate,
+    left,
+    right,
+    normed,
+    d_left,
+    d_right,
+    left_gate_0,
+    left_gate_1,
+    left_value_0,
+    left_value_1,
+    right_gate_0,
+    right_gate_1,
+    right_value_0,
+    right_value_1,
+    norm_gain,
+    norm_bias,
+    proj_weight,
+    gate_weight,
+    pair_grad,
+    proj_grad,
+    source,
+    d_right_s,
+    d_proj,
+):
+    rows, cols, groups = sizes
+    cells = rows * cols
+    hidden = left.shape[-1]
+    half = lax.axis_index("col")
+    me = lax.axis_index("row")
+    zeros = (jnp.zeros((8, hidden), F32),) * (rows * cols // 8)
+    source[...] = d_tri_ref[...].astype(F32)
+    d_right_s[at(half, cols * cols), :] = d_right[...]
+
+    def right_block(p, carry):
+        sums = contract(
+            rows,
+            cols,
+            rows * groups,
+            8,
+            zeros,
+            source,
+            lambda a, i: i * cols + p * rows + a,
+            left,
+            lambda i: i * cols,
+        )
+        start = (1 - half) * cols * cols + p * cells
+        for t, value in enumerate(sums):
+            d_right_s[tile(start + t * 8), :] = value
+        return carry
+
+    lax.fori_loop(0, cols // rows, right_block, 0)
+
+    for which, left_gate, left_value, right_gate, right_value in (
+        (0, left_gate_0, left_value_0, right_gate_0, right_value_0),
+        (1, left_gate_1, left_value_1, right_gate_1, right_value_1),
+    ):
+
+        def left_block(
+            b,
+            carry,
+            which=which,
+            left_gate=left_gate,
+            left_value=left_value,
+            right_gate=right_gate,
+            right_value=right_value,
+        ):
+            p = row_block(which, b)
+            start = p * cells
+            sums = contract(
+                rows,
+                cols,
+                cols,
+                8,
+                tuple(d_left[tile(start + t * 8), :] for t in range(cells // 8)),
+                source,
+                lambda a, j: (p * rows + a) * cols + j,
+                right,
+                lambda j: ((1 - half) * cols + j) * cols,
+            )
+            part, place = at(b, cells), at(p, cells)
+            grads = jnp.concatenate(sums, axis=0)
+            d_proj[place, :hidden] = (grads * left_value[part, :]).astype(BF16)
+            d_proj[place, hidden : 2 * hidden] = (grads * left_gate[part, :]).astype(BF16)
+            grads = d_right_s[place, :]
+            d_proj[place, 2 * hidden : 3 * hidden] = (grads * right_value[part, :]).astype(BF16)
+            d_proj[place, 3 * hidden :] = (grads * right_gate[part, :]).astype(BF16)
+            return carry
+
+        lax.fori_loop(0, groups // 2, left_block, 0)
+
+    scale = 1.0 / (rows * groups)
+    proj_grad[...] = dot(normed[...], d_proj[...], BY_ROWS) * scale
+    own = at(me, cells)
+    d_normed = dot(d_proj[own, :], proj_weight[...], TRANSPOSED) + dot(
+        d_gate[own, :], gate_weight[...], TRANSPOSED
+    )
+    _, hat, inverse = layer_norm(pair[...].astype(F32), norm_gain[...], norm_bias[...])
+    pair_grad[...] = norm_back(d_normed, norm_gain[...], hat, inverse)
+
+
+def replicated(
+    pair_rep,
+    cotangent,
+    norm_gain,
+    norm_bias,
+    proj_weight,
+    gate_weight,
+    tri_gain,
+    tri_bias,
+    out_weight,
+):
+    rows, cols, channels = pair_rep.shape
+    hidden = tri_gain.shape[0]
+    groups = lax.axis_size("row")
+    cells = rows * cols
+    every = cells * groups
+    some = every // 2
+    sizes = (rows, cols, groups)
+    norm_gain, norm_bias = norm_gain[None], norm_bias[None]
+    tri_gain, tri_bias = tri_gain[None], tri_bias[None]
+
+    def call(kernel, outs, *args, scratch=(), name):
+        return pl.pallas_call(
+            functools.partial(kernel, sizes),
+            out_shape=[jax.ShapeDtypeStruct(*out) for out in outs],
+            scratch_shapes=[pltpu.VMEM(*one) for one in scratch],
+            compiler_params=pltpu.CompilerParams(vmem_limit_bytes=VMEM_BUDGET),
+            name=name,
+        )(*args)
+
+    def across(value, mask):
+        return lax.ppermute(value, "row", [(i, i ^ mask) for i in range(groups)])
+
+    def over(value):
+        return lax.ppermute(value, "col", SWAP)
+
+    def gather(value):
+        got = [value] + [across(value, 2 * s) for s in range(1, groups // 2)]
+        near = jnp.concatenate(got, axis=0)
+        return near, across(near, 1)
+
+    pair = pair_rep.reshape(cells, channels)
+    pairs = gather(pair)
+    cots = gather(cotangent.reshape(cells, channels))
+    mates = [over(part) for part in pairs]
+    weights = (norm_gain, norm_bias, proj_weight)
+
+    full, part = (every, hidden), (some, hidden)
+    own = [
+        call(
+            own_edges_kernel,
+            [((some, channels), BF16)] + [(part, F32)] * 6,
+            x,
+            *weights,
+            name="own_edges",
+        )
+        for x in pairs
+    ]
+    mate = [
+        call(mate_edges_kernel, [(part, F32)] * 2, x, *weights, name="mate_edges") for x in mates
+    ]
+    normed = [o[0] for o in own]
+    left, left_gate, left_value = ([o[n] for o in own] for n in (1, 2, 3))
+    right, right_gate, right_value = ([o[n] for o in own] for n in (4, 5, 6))
+    (tri,) = call(
+        triangle_kernel,
+        [(full, F32)],
+        *left,
+        *(m[0] for m in mate),
+        *right,
+        *(m[1] for m in mate),
+        scratch=[((cols * cols, hidden), F32)] * 2,
+        name="triangle",
+    )
+    block_out, d_tri, d_gate, tri_norm, d_update = call(
+        cells_kernel,
+        [((cells, channels), BF16)] + [(full, BF16)] * 4,
+        tri,
+        *normed,
+        *cots,
+        gate_weight,
+        tri_gain,
+        tri_bias,
+        out_weight,
+        name="cells",
+    )
+    d_tri_mate = over(d_tri)
+    left_all, right_all, normed_all, d_left, d_right, small_grads = call(
+        early_kernel,
+        [
+            (full, F32),
+            (full, F32),
+            ((every, channels), BF16),
+            (full, F32),
+            (part, F32),
+            ((channels, 2 * channels), F32),
+        ],
+        d_tri,
+        d_gate,
+        tri_norm,
+        d_update,
+        *normed,
+        *left,
+        *right,
+        scratch=[(full, F32)],
+        name="early",
+    )
+    small_mate = over(small_grads)
+    pair_grad, proj_grad = call(
+        late_kernel,
+        [((cells, channels), F32), ((channels, 4 * hidden), F32)],
+        pair,
+        d_tri_mate,
+        d_gate,
+        left_all,
+        right_all,
+        normed_all,
+        d_left,
+        d_right,
+        *left_gate,
+        *left_value,
+        *right_gate,
+        *right_value,
+        norm_gain,
+        norm_bias,
+        proj_weight,
+        gate_weight,
+        scratch=[(full, F32), (full, F32), ((every, 4 * hidden), BF16)],
+        name="late",
+    )
+    small = small_grads + small_mate
+    return (
+        block_out.reshape(pair_rep.shape),
+        pair_grad.reshape(pair_rep.shape),
+        proj_grad + over(proj_grad),
+        small[:, :channels],
+        small[:, channels:],
+    )
+
+
+def sharded(
     pair_rep,
     cotangent,
     norm_gain,
@@ -109,6 +597,18 @@
     return (block_out, pair_grad, proj_grad, gate_grad, out_grad)
 
 
+def local(pair_rep, *others):
+    rows, cols, channels = pair_rep.shape
+    hidden = others[7].shape[0]
+    groups = lax.axis_size("row")
+    every = rows * groups * cols
+    fits = 24 * every * channels * 4 <= VMEM_BUDGET and hidden == channels
+    paired = lax.axis_size("col") == 2 and groups & (groups - 1) == 0 and groups >= 2
+    whole_tiles = cols % 8 == 0 and cols % (2 * rows) == 0 and rows * cols % 16 == 0
+    plan = replicated if fits and paired and whole_tiles else sharded
+    return plan(pair_rep, *others)
+
+
 def solution(mesh):
     return jax.shard_map(
         local,

time: 212 us -> 40 us (0.19)
  waiting for transfers between devices: 92.5 us -> 8.7 us
  blocking collectives: 67.4 us -> 0 us
  between operations: 14.3 us -> 0.78 us
  Pallas kernels: 0 us -> 13.5 us
  matrix products: 12.8 us -> 0 us
  local copies, waits for them, and re-layouts: 12.3 us -> 1.99 us
  starting transfers between devices: 5.69 us -> 13.4 us
  other arithmetic: 5.82 us -> 1.55 us
    psum x1 -> x0, waiting for transfers between devices: 88 us -> none  [local(): lax.psum((local_proj, local_gate, local_out), ('row', 'col'))]
    all_gather x3 -> x0, blocking collectives: 67.4 us -> none  [the longest x1 32.9 us: local(): lax.all_gather(left_edge, 'row', axis=0, tiled=True)]
    pallas_call x0 -> x8, Pallas kernels: none -> 13.5 us  [call(): pl.pallas_call(functools.partial(kernel, sizes), out_shape=[jax.ShapeDtyp...]
    ppermute x0 -> x13, starting transfers between devices: none -> 13.4 us  [the longest x8 12.2 us: across(): return lax.ppermute(value, 'row', [(i, i ^ mask) for i in range(groups)])]
    dot_general x12 -> x0, matrix products: 12.8 us -> none  [the longest x1 2.29 us: local(): jnp.einsum('ijc,jkc->ikc', tri_rows, right_all, preferred_element_type=f32)]
    ppermute x0 -> x13, waiting for transfers between devices: none -> 8.7 us  [the longest x8 7.88 us: across(): return lax.ppermute(value, 'row', [(i, i ^ mask) for i in range(groups)])]
    all_to_all x1 -> x0, starting transfers between devices: 5.61 us -> none  [local(): lax.all_to_all(tri_rows, 'row', split_axis=1, concat_axis=0, tiled=True)]
    all_to_all x1 -> x0, waiting for transfers between devices: 4.46 us -> none  [local(): lax.all_to_all(tri_rows, 'row', split_axis=1, concat_axis=0, tiled=True)]
  transfers between devices with their start and end apart: 3 -> 13, of which waited for: 2 -> 4; matrix products, arithmetic and copies ran while one was open for 2% -> 2% of each run, Pallas kernels for 0% -> 29%
where the time goes in v2:
time: 40 us; the launch traced here: 39.8 us
  Pallas kernels  13.5 us (34%)
  starting transfers between devices  13.4 us (34%)
  waiting for transfers between devices  8.7 us (22%)
  local copies, waits for them, and re-layouts  1.99 us (5%)
  other arithmetic  1.55 us (4%)
  between operations  0.78 us (2%)
    pallas_call x8, Pallas kernels, call(): pl.pallas_call(functools.partial(kernel, sizes), out_shape=[jax.ShapeDtyp...  13.5 us
    ppermute x8, starting transfers between devices, across(): return lax.ppermute(value, 'row', [(i, i ^ mask) for i in range(groups)])  12.2 us
    ppermute x8, waiting for transfers between devices, across(): return lax.ppermute(value, 'row', [(i, i ^ mask) for i in range(groups)])  7.88 us
    unnamed x18, local copies, waits for them, and re-layouts  1.33 us
    ppermute x5, starting transfers between devices, over(): return lax.ppermute(value, 'col', SWAP)  1.13 us
    ppermute x5, waiting for transfers between devices, over(): return lax.ppermute(value, 'col', SWAP)  0.82 us
  transfers between devices with their start and end apart: 13, of which 4 were waited for; matrix products, arithmetic and copies ran while one was open for 2% of the time, Pallas kernels for 29%

profile of v2, /device:TPU:0, one launch (start us, length us, event | category | flops | bytes accessed | tf_op | source)
XLA Modules:
  0.0 39.8 jit_solution(9927347979106761296)
XLA Ops:
  0.6 3.1 %collective-permute-start = (bf16[144,128]{1,0:T(8,128)(2,1)}, bf16[144,128]{1,0:T(8,128)(2,1)S(1)}, u32[]{:S(2)}, u32[]{:S(2)}) collective-permute-start(bf16[144,128]{1,0:T(8,128)(2,1)} %bitcast.8), channel_id=1, source_target_pairs={{0,4},{2,6},{4,0},{6,2},{8,12},{10,14},{12,8},{14,10},{1,5},{3,7},... | collective-permute-start | bytes 110600 | tf_op jit(solution)/shard_map/ppermute | solution.py:400
  3.7 2.6 %collective-permute-start.1 = (bf16[144,128]{1,0:T(8,128)(2,1)}, bf16[144,128]{1,0:T(8,128)(2,1)S(1)}, u32[]{:S(2)}, u32[]{:S(2)}) collective-permute-start(bf16[144,128]{1,0:T(8,128)(2,1)} %bitcast.9), channel_id=1, source_target_pairs={{0,8},{2,10},{4,12},{6,14},{8,0},{10,2},{12,4},{14,6},{1,9},{3,11}... | collective-permute-start | bytes 110600 | tf_op jit(solution)/shard_map/ppermute | solution.py:400
  6.3 3.1 %collective-permute-done.1 = bf16[144,128]{1,0:T(8,128)(2,1)S(1)} collective-permute-done((bf16[144,128]{1,0:T(8,128)(2,1)}, bf16[144,128]{1,0:T(8,128)(2,1)S(1)}, u32[]{:S(2)}, u32[]{:S(2)}) %collective-permute-start.1) | collective-permute-done | bytes 36896 | tf_op jit(solution)/shard_map/ppermute | solution.py:400
  9.5 2.8 %collective-permute-done.2 = bf16[144,128]{1,0:T(8,128)(2,1)S(1)} collective-permute-done((bf16[144,128]{1,0:T(8,128)(2,1)}, bf16[144,128]{1,0:T(8,128)(2,1)S(1)}, u32[]{:S(2)}, u32[]{:S(2)}) %collective-permute-start.2) | collective-permute-done | bytes 36896 | tf_op jit(solution)/shard_map/ppermute | solution.py:400
  12.3 0.8 %pad_maximum_fusion.x = bf16[576,128]{1,0:T(8,128)(2,1)S(1)} fusion(bf16[144,128]{1,0:T(8,128)(2,1)S(1)} %collective-permute-done.2, bf16[144,128]{1,0:T(8,128)(2,1)S(1)} %collective-permute-done.1, bf16[144,128]{1,0:T(8,128)(2,1)S(1)} %collective-permute-done, bf16[144,128]{1,0:T(8,128)(2,1)} %bitcast.11), kind=kLoop, calls=%fused_computation | loop fusion | flops 589824 | bytes 294912 | tf_op jit(solution)/shard_map/concatenate | solution.py:407
  13.1 1.6 %collective-permute-start.3 = (bf16[576,128]{1,0:T(8,128)(2,1)S(1)}, bf16[576,128]{1,0:T(8,128)(2,1)S(1)}, u32[]{:S(2)}, u32[]{:S(2)}) collective-permute-start(bf16[576,128]{1,0:T(8,128)(2,1)S(1)} %pad_maximum_fusion.x), channel_id=1, source_target_pairs={{0,2},{2,0},{4,6},{6,4},{8,10},{10,8},{12,14},{14,12},{1,3},{3,1},... | collective-permute-start | bytes 442376 | tf_op jit(solution)/shard_map/ppermute | solution.py:400
  14.7 1.1 %collective-permute-start.7 = (bf16[144,128]{1,0:T(8,128)(2,1)S(1)}, bf16[144,128]{1,0:T(8,128)(2,1)S(1)}, u32[]{:S(2)}, u32[]{:S(2)}) collective-permute-start(bf16[144,128]{1,0:T(8,128)(2,1)S(1)} %bitcast.26), channel_id=1, source_target_pairs={{0,8},{2,10},{4,12},{6,14},{8,0},{10,2},{12,4},{14,6},{1,9},{3,11}... | collective-permute-start | bytes 110600 | tf_op jit(solution)/shard_map/ppermute | solution.py:400
  15.7 3.3 %collective-permute-start.8 = (bf16[144,128]{1,0:T(8,128)(2,1)S(1)}, bf16[144,128]{1,0:T(8,128)(2,1)S(1)}, u32[]{:S(2)}, u32[]{:S(2)}) collective-permute-start(bf16[144,128]{1,0:T(8,128)(2,1)S(1)} %bitcast.27), channel_id=1, source_target_pairs={{0,12},{2,14},{4,8},{6,10},{8,4},{10,6},{12,0},{14,2},{1,13},{3,15... | collective-permute-start | bytes 110600 | tf_op jit(solution)/shard_map/ppermute | solution.py:400
  19.1 0.5 %collective-permute-start.5 = (bf16[576,128]{1,0:T(8,128)(2,1)S(1)}, bf16[576,128]{1,0:T(8,128)(2,1)S(1)}, u32[]{:S(2)}, u32[]{:S(2)}) collective-permute-start(bf16[576,128]{1,0:T(8,128)(2,1)S(1)} %collective-permute-done.3.x), channel_id=1, source_target_pairs={{0,1},{1,0},{2,3},{3,2},{4,5},{5,4},{6,7},{7,6},{8,9},{9,8},{10,11... | collective-permute-start | bytes 442376 | tf_op jit(solution)/shard_map/ppermute | solution.py:403
  19.6 0.0 collective-permute-done.7
  19.6 1.9 %collective-permute-done.8 = bf16[144,128]{1,0:T(8,128)(2,1)S(1)} collective-permute-done((bf16[144,128]{1,0:T(8,128)(2,1)S(1)}, bf16[144,128]{1,0:T(8,128)(2,1)S(1)}, u32[]{:S(2)}, u32[]{:S(2)}) %collective-permute-start.8) | collective-permute-done | bytes 36896 | tf_op jit(solution)/shard_map/ppermute | solution.py:400
  21.5 0.6 %collective-permute-start.9 = (bf16[576,128]{1,0:T(8,128)(2,1)S(1)}, bf16[576,128]{1,0:T(8,128)(2,1)S(1)}, u32[]{:S(2)}, u32[]{:S(2)}) collective-permute-start(bf16[576,128]{1,0:T(8,128)(2,1)S(1)} %pad_maximum_fusion.1.cot_0), channel_id=1, source_target_pairs={{0,2},{2,0},{4,6},{6,4},{8,10},{10,8},{12,14},{14,12},{1,3},{3,1},... | collective-permute-start | bytes 442376 | tf_op jit(solution)/shard_map/ppermute | solution.py:400
  22.1 0.6 %copy-done.4 = f32[128]{0:T(128)S(1)} copy-done((f32[128]{0:T(128)S(1)}, f32[128]{0:T(128)}, u32[]{:S(2)}) %copy-start.4) | copy-done | bytes 536
  22.7 0.0 copy-done.5
  22.7 0.6 %own_edges.2 = (bf16[576,128]{1,0:T(8,128)(2,1)S(1)}, f32[576,128]{1,0:T(8,128)S(1)}, f32[576,128]{1,0:T(8,128)S(1)}, f32[576,128]{1,0:T(8,128)S(1)}, f32[576,12...) custom-call(bf16[576,128]{1,0:T(8,128)(2,1)S(1)} %pad_maximum_fusion.x, f32[1,128]{1,0:T(1,128)S(1)} %bitcast.13, ...), custom_call_target="tpu_custom_call" | custom-call | tf_op jit(solution)/shard_map/own_edges/pallas_call | solution.py:391
  23.4 0.6 %own_edges.3 = (bf16[576,128]{1,0:T(8,128)(2,1)S(1)}, f32[576,128]{1,0:T(8,128)S(1)}, f32[576,128]{1,0:T(8,128)S(1)}, f32[576,128]{1,0:T(8,128)S(1)}, f32[576,12...) custom-call(bf16[576,128]{1,0:T(8,128)(2,1)S(1)} %collective-permute-done.3.x, ...), custom_call_target="tpu_custom_call" | custom-call | tf_op jit(solution)/shard_map/own_edges/pallas_call | solution.py:391
  24.0 0.6 %mate_edges.2 = (f32[576,128]{1,0:T(8,128)S(1)}, f32[576,128]{1,0:T(8,128)S(1)}) custom-call(bf16[576,128]{1,0:T(8,128)(2,1)S(1)} %collective-permute-done.4.x, f32[1,128]{1,0:T(1,128)S(1)} %bitcast.15, f32[1,128]{1,0:T(1,128)S(1)} %bitcast.20, bf16[128,512]{1,0:T(8,128)(2,1)S(1)} %copy-done), custom_call_target="tpu_custom_call" | custom-call | tf_op jit(solution)/shard_map/mate_edges/pallas_call | solution.py:391
  24.7 0.6 %mate_edges.3 = (f32[576,128]{1,0:T(8,128)S(1)}, f32[576,128]{1,0:T(8,128)S(1)}) custom-call(bf16[576,128]{1,0:T(8,128)(2,1)S(1)} %collective-permute-done.5.x, f32[1,128]{1,0:T(1,128)S(1)} %bitcast.16, f32[1,128]{1,0:T(1,128)S(1)} %bitcast.21, bf16[128,512]{1,0:T(8,128)(2,1)S(1)} %copy-done), custom_call_target="tpu_custom_call" | custom-call | tf_op jit(solution)/shard_map/mate_edges/pallas_call | solution.py:391
  25.3 0.0 copy-start.2
  25.3 0.0 copy-start.3
  25.4 2.4 %triangle.1.tri = f32[1152,128]{1,0:T(8,128)S(1)} custom-call(f32[576,128]{1,0:T(8,128)S(1)} %get-tuple-element.36.refs_0_.left_0, f32[576,128]{1,0:T(8,128)S(1)} %get-tuple-element.37.refs_1_.left_1, f32[576,128]{1,0:T(8,128)S(1)} %get-tuple-element.38.refs_2_, f32[576,128]{1,0:T(8,128)S(1)} %get-tuple-element.39.refs_3_, ...), custom_call_target="tpu_custom_call" | custom-call | tf_op jit(solution)/shard_map/triangle/pallas_call | solution.py:391
  27.8 0.0 copy-start.7
  27.8 0.6 %copy-done.6 = f32[128]{0:T(128)S(1)} copy-done((f32[128]{0:T(128)S(1)}, f32[128]{0:T(128)}, u32[]{:S(2)}) %copy-start.6) | copy-done | bytes 536
  28.4 0.0 copy-done.7
  28.5 2.1 %cells.1 = (bf16[144,128]{1,0:T(8,128)(2,1)}, bf16[1152,128]{1,0:T(8,128)(2,1)S(1)}, bf16[1152,128]{1,0:T(8,128)(2,1)S(1)}, bf16[1152,128]{1,0:T(8,128)(2,1)S(1)}, bf16[1152,128]{1,0:T(8,128)(2,1)S(1)}) custom-call(f32[1152,128]{1,0:T(8,128)S(1)} %triangle.1.tri, bf16[576,128]{1,0:T(8,128)(2,1)S(1)} %get-tuple-element.44.normed_0, ...), custom_call_target="tpu_custom_call" | custom-call | tf_op jit(solution)/shard_map/cells/pallas_call | solution.py:391
  30.6 2.7 %early.1 = (f32[1152,128]{1,0:T(8,128)S(1)}, f32[1152,128]{1,0:T(8,128)S(1)}, bf16[1152,128]{1,0:T(8,128)(2,1)S(1)}, f32[1152,128]{1,0:T(8,128)S(1)}, f32[576,128]{1,0:T(8,128)S(1)}, /*index=5*/f32[128,256]{1,0:T(8,128)S(1)}) custom-call(bf16[1152,128]{1,0:T(8,128)(2,1)S(1)} %get-tuple-element.47.d_tri_ref, bf16[1152,128]{1,0:T(8,128)(2,1)S(1)} %get-tuple-element.48.d_gate, ...), custom_call_target="tpu_custom_call" | custom-call | tf_op jit(solution)/shard_map/early/pallas_call | solution.py:391
  33.3 0.6 %collective-permute-start.12 = (f32[128,256]{1,0:T(8,128)S(1)}, f32[128,256]{1,0:T(8,128)S(1)}, u32[]{:S(2)}, u32[]{:S(2)}) collective-permute-start(f32[128,256]{1,0:T(8,128)S(1)} %get-tuple-element.66), channel_id=1, source_target_pairs={{0,1},{1,0},{2,3},{3,2},{4,5},{5,4},{6,7},{7,6},{8,9},{9,8},{10,11... | collective-permute-start | bytes 393224 | tf_op jit(solution)/shard_map/ppermute | solution.py:403
  33.8 3.7 %late.1 = (f32[144,128]{1,0:T(8,128)}, f32[128,512]{1,0:T(8,128)S(1)}) custom-call(bf16[144,128]{1,0:T(8,128)(2,1)S(1)} %bitcast.12, bf16[1152,128]{1,0:T(8,128)(2,1)S(1)} %collective-permute-done.10.d_tri_ref, bf16[1152,128]{1,0:T(8,128)(2,1)S(1)} %get-tuple-element.48.d_gate, f32[1152,128]{1,0:T(8,128)S(1)} %get-tuple-element.51.left, ...), custom_call_target="tpu_custom_call" | custom-call | tf_op jit(solution)/shard_map/late/pallas_call | solution.py:391
  37.6 0.0 collective-permute-start.11
  37.6 0.7 %fusion = (f32[128,128]{1,0:T(8,128)}, f32[128,128]{1,0:T(8,128)}) fusion(f32[128,256]{1,0:T(8,128)S(1)} %add.7), kind=kLoop, calls=%fused_computation.2 | loop fusion | bytes 262144 | tf_op jit(solution)/shard_map/slice | solution.py:505
  38.3 0.8 %collective-permute-done.11 = f32[128,512]{1,0:T(8,128)S(1)} collective-permute-done((f32[128,512]{1,0:T(8,128)S(1)}, f32[128,512]{1,0:T(8,128)S(1)}, u32[]{:S(2)}, u32[]{:S(2)}) %collective-permute-start.11) | collective-permute-done | bytes 262176 | tf_op jit(solution)/shard_map/ppermute | solution.py:403
  39.1 0.7 %add.6 = f32[128,512]{1,0:T(8,128)} add(f32[128,512]{1,0:T(8,128)S(1)} %get-tuple-element.65, f32[128,512]{1,0:T(8,128)S(1)} %collective-permute-done.11) | non-fusion elementwise | flops 65536 | bytes 786432 | tf_op jit(solution)/shard_map/add | solution.py:503
  (25 shorter events, 0.1 us)
Async XLA Ops:
  0.6 14.0 %copy-start.8 = (bf16[6,24,128]{2,1,0:T(8,128)(2,1)S(1)}, bf16[6,24,128]{2,1,0:T(8,128)(2,1)}, u32[]{:S(2)}) copy-start(bf16[6,24,128]{2,1,0:T(8,128)(2,1)} %param.10) | copy-start | bytes 110596
  0.6 5.7 %collective-permute-start = (bf16[144,128]{1,0:T(8,128)(2,1)}, bf16[144,128]{1,0:T(8,128)(2,1)S(1)}, u32[]{:S(2)}, u32[]{:S(2)}) collective-permute-start(bf16[144,128]{1,0:T(8,128)(2,1)} %bitcast.8), channel_id=1, source_target_pairs={{0,4},{2,6},{4,0},{6,2},{8,12},{10,14},{12,8},{14,10},{1,5},{3,7},... | collective-permute-start | bytes 110600 | tf_op jit(solution)/shard_map/ppermute | solution.py:400
  3.7 5.7 %collective-permute-start.1 = (bf16[144,128]{1,0:T(8,128)(2,1)}, bf16[144,128]{1,0:T(8,128)(2,1)S(1)}, u32[]{:S(2)}, u32[]{:S(2)}) collective-permute-start(bf16[144,128]{1,0:T(8,128)(2,1)} %bitcast.9), channel_id=1, source_target_pairs={{0,8},{2,10},{4,12},{6,14},{8,0},{10,2},{12,4},{14,6},{1,9},{3,11}... | collective-permute-start | bytes 110600 | tf_op jit(solution)/shard_map/ppermute | solution.py:400
  6.3 6.0 %collective-permute-start.2 = (bf16[144,128]{1,0:T(8,128)(2,1)}, bf16[144,128]{1,0:T(8,128)(2,1)S(1)}, u32[]{:S(2)}, u32[]{:S(2)}) collective-permute-start(bf16[144,128]{1,0:T(8,128)(2,1)} %bitcast.10), channel_id=1, source_target_pairs={{0,12},{2,14},{4,8},{6,10},{8,4},{10,6},{12,0},{14,2},{1,13},{3,15... | collective-permute-start | bytes 110600 | tf_op jit(solution)/shard_map/ppermute | solution.py:400
  13.1 6.0 %collective-permute-start.3 = (bf16[576,128]{1,0:T(8,128)(2,1)S(1)}, bf16[576,128]{1,0:T(8,128)(2,1)S(1)}, u32[]{:S(2)}, u32[]{:S(2)}) collective-permute-start(bf16[576,128]{1,0:T(8,128)(2,1)S(1)} %pad_maximum_fusion.x), channel_id=1, source_target_pairs={{0,2},{2,0},{4,6},{6,4},{8,10},{10,8},{12,14},{14,12},{1,3},{3,1},... | collective-permute-start | bytes 442376 | tf_op jit(solution)/shard_map/ppermute | solution.py:400
  14.7 7.4 %copy-start = (bf16[128,512]{1,0:T(8,128)(2,1)S(1)}, bf16[128,512]{1,0:T(8,128)(2,1)}, u32[]{:S(2)}) copy-start(bf16[128,512]{1,0:T(8,128)(2,1)} %proj_weight.1) | copy-start | bytes 393220
  14.7 4.9 %collective-permute-start.6 = (bf16[144,128]{1,0:T(8,128)(2,1)S(1)}, bf16[144,128]{1,0:T(8,128)(2,1)S(1)}, u32[]{:S(2)}, u32[]{:S(2)}) collective-permute-start(bf16[144,128]{1,0:T(8,128)(2,1)S(1)} %bitcast.25), channel_id=1, source_target_pairs={{0,4},{2,6},{4,0},{6,2},{8,12},{10,14},{12,8},{14,10},{1,5},{3,7},... | collective-permute-start | bytes 110600 | tf_op jit(solution)/shard_map/ppermute | solution.py:400
  14.7 4.9 %collective-permute-start.7 = (bf16[144,128]{1,0:T(8,128)(2,1)S(1)}, bf16[144,128]{1,0:T(8,128)(2,1)S(1)}, u32[]{:S(2)}, u32[]{:S(2)}) collective-permute-start(bf16[144,128]{1,0:T(8,128)(2,1)S(1)} %bitcast.26), channel_id=1, source_target_pairs={{0,8},{2,10},{4,12},{6,14},{8,0},{10,2},{12,4},{14,6},{1,9},{3,11}... | collective-permute-start | bytes 110600 | tf_op jit(solution)/shard_map/ppermute | solution.py:400
  15.7 5.8 %collective-permute-start.8 = (bf16[144,128]{1,0:T(8,128)(2,1)S(1)}, bf16[144,128]{1,0:T(8,128)(2,1)S(1)}, u32[]{:S(2)}, u32[]{:S(2)}) collective-permute-start(bf16[144,128]{1,0:T(8,128)(2,1)S(1)} %bitcast.27), channel_id=1, source_target_pairs={{0,12},{2,14},{4,8},{6,10},{8,4},{10,6},{12,0},{14,2},{1,13},{3,15... | collective-permute-start | bytes 110600 | tf_op jit(solution)/shard_map/ppermute | solution.py:400
  19.0 5.0 %collective-permute-start.4 = (bf16[576,128]{1,0:T(8,128)(2,1)S(1)}, bf16[576,128]{1,0:T(8,128)(2,1)S(1)}, u32[]{:S(2)}, u32[]{:S(2)}) collective-permute-start(bf16[576,128]{1,0:T(8,128)(2,1)S(1)} %pad_maximum_fusion.x), channel_id=1, source_target_pairs={{0,1},{1,0},{2,3},{3,2},{4,5},{5,4},{6,7},{7,6},{8,9},{9,8},{10,11... | collective-permute-start | bytes 442376 | tf_op jit(solution)/shard_map/ppermute | solution.py:403
  19.1 5.6 %collective-permute-start.5 = (bf16[576,128]{1,0:T(8,128)(2,1)S(1)}, bf16[576,128]{1,0:T(8,128)(2,1)S(1)}, u32[]{:S(2)}, u32[]{:S(2)}) collective-permute-start(bf16[576,128]{1,0:T(8,128)(2,1)S(1)} %collective-permute-done.3.x), channel_id=1, source_target_pairs={{0,1},{1,0},{2,3},{3,2},{4,5},{5,4},{6,7},{7,6},{8,9},{9,8},{10,11... | collective-permute-start | bytes 442376 | tf_op jit(solution)/shard_map/ppermute | solution.py:403
  21.5 6.3 %collective-permute-start.9 = (bf16[576,128]{1,0:T(8,128)(2,1)S(1)}, bf16[576,128]{1,0:T(8,128)(2,1)S(1)}, u32[]{:S(2)}, u32[]{:S(2)}) collective-permute-start(bf16[576,128]{1,0:T(8,128)(2,1)S(1)} %pad_maximum_fusion.1.cot_0), channel_id=1, source_target_pairs={{0,2},{2,0},{4,6},{6,4},{8,10},{10,8},{12,14},{14,12},{1,3},{3,1},... | collective-permute-start | bytes 442376 | tf_op jit(solution)/shard_map/ppermute | solution.py:400
  22.1 0.7 %copy-start.4 = (f32[128]{0:T(128)S(1)}, f32[128]{0:T(128)}, u32[]{:S(2)}) copy-start(f32[128]{0:T(128)} %param.11) | copy-start | bytes 1540
  22.1 0.7 %copy-start.5 = (f32[128]{0:T(128)S(1)}, f32[128]{0:T(128)}, u32[]{:S(2)}) copy-start(f32[128]{0:T(128)} %param.12) | copy-start | bytes 1540
  25.3 2.5 %copy-start.2 = (bf16[128,128]{1,0:T(8,128)(2,1)S(1)}, bf16[128,128]{1,0:T(8,128)(2,1)}, u32[]{:S(2)}) copy-start(bf16[128,128]{1,0:T(8,128)(2,1)} %gate_weight.3) | copy-start | bytes 98308
  25.3 2.5 %copy-start.3 = (bf16[128,128]{1,0:T(8,128)(2,1)S(1)}, bf16[128,128]{1,0:T(8,128)(2,1)}, u32[]{:S(2)}) copy-start(bf16[128,128]{1,0:T(8,128)(2,1)} %out_weight.1) | copy-start | bytes 98308
  27.8 0.7 %copy-start.6 = (f32[128]{0:T(128)S(1)}, f32[128]{0:T(128)}, u32[]{:S(2)}) copy-start(f32[128]{0:T(128)} %param.15) | copy-start | bytes 1540
  27.8 0.7 %copy-start.7 = (f32[128]{0:T(128)S(1)}, f32[128]{0:T(128)}, u32[]{:S(2)}) copy-start(f32[128]{0:T(128)} %param.16) | copy-start | bytes 1540
  30.6 3.3 %collective-permute-start.10 = (bf16[1152,128]{1,0:T(8,128)(2,1)S(1)}, bf16[1152,128]{1,0:T(8,128)(2,1)S(1)}, u32[]{:S(2)}, u32[]{:S(2)}) collective-permute-start(bf16[1152,128]{1,0:T(8,128)(2,1)S(1)} %get-tuple-element.47.d_tri_ref), channel_id=1, source_target_pairs={{0,1},{1,0},{2,3},{3,2},{4,5},{5,4},{6,7},{7,6},{8,9},{9,8},{10,11... | collective-permute-start | bytes 884744 | tf_op jit(solution)/shard_map/ppermute | solution.py:403
  30.6 3.3 %copy-start.1 = (bf16[6,24,128]{2,1,0:T(8,128)(2,1)S(1)}, bf16[6,24,128]{2,1,0:T(8,128)(2,1)}, u32[]{:S(2)}) copy-start(bf16[6,24,128]{2,1,0:T(8,128)(2,1)} %param.9) | copy-start | bytes 110596
  33.3 4.3 %collective-permute-start.12 = (f32[128,256]{1,0:T(8,128)S(1)}, f32[128,256]{1,0:T(8,128)S(1)}, u32[]{:S(2)}, u32[]{:S(2)}) collective-permute-start(f32[128,256]{1,0:T(8,128)S(1)} %get-tuple-element.66), channel_id=1, source_target_pairs={{0,1},{1,0},{2,3},{3,2},{4,5},{5,4},{6,7},{7,6},{8,9},{9,8},{10,11... | collective-permute-start | bytes 393224 | tf_op jit(solution)/shard_map/ppermute | solution.py:403
  37.6 1.5 %collective-permute-start.11 = (f32[128,512]{1,0:T(8,128)S(1)}, f32[128,512]{1,0:T(8,128)S(1)}, u32[]{:S(2)}, u32[]{:S(2)}) collective-permute-start(f32[128,512]{1,0:T(8,128)S(1)} %get-tuple-element.65), channel_id=1, source_target_pairs={{0,1},{1,0},{2,3},{3,2},{4,5},{5,4},{6,7},{7,6},{8,9},{9,8},{10,11... | collective-permute-start | bytes 786440 | tf_op jit(solution)/shard_map/ppermute | solution.py:403

commit v3 on v2

--- a/solution.py
+++ b/solution.py
@@ -57,10 +57,11 @@
     return 2 * b + (parity if which == 0 else 1 - parity)
 
 
-def edges(values, norm_gain, norm_bias, proj_weight):
+def edges(blocks, params, proj_weight):
     hidden = proj_weight.shape[1] // 4
-    normed = layer_norm(values.astype(F32), norm_gain, norm_bias)[0].astype(BF16)
-    projected = dot(normed, proj_weight)
+    values = jnp.concatenate([block[...] for block in blocks], axis=0).astype(F32)
+    normed = layer_norm(values, params[0:1, :], params[1:2, :])[0].astype(BF16)
+    projected = dot(normed, proj_weight[...])
     sides = []
     for start in (0, 2 * hidden):
         gate = sigmoid(projected[:, start : start + hidden])
@@ -69,10 +70,11 @@
     return normed, sides
 
 
-def own_edges_kernel(sizes, x, gain, bias, weight, normed_out, *outs):
+def own_edges_kernel(sizes, params, weight, *refs):
     rows, cols, groups = sizes
     cells = rows * cols
-    normed, sides = edges(x[...], gain[...], bias[...], weight[...])
+    blocks, normed_out, outs = refs[:-7], refs[-7], refs[-6:]
+    normed, sides = edges(blocks, params, weight)
     for t, b in enumerate(places(groups)):
         part = slice(t * cells, (t + 1) * cells)
         place = at(b, cells)
@@ -81,10 +83,11 @@
             out[place, :] = value[part]
 
 
-def mate_edges_kernel(sizes, x, gain, bias, weight, left, right):
+def mate_edges_kernel(sizes, params, weight, *refs):
     rows, cols, groups = sizes
     cells = rows * cols
-    _, sides = edges(x[...], gain[...], bias[...], weight[...])
+    blocks, left, right = refs[:-2], refs[-2], refs[-1]
+    _, sides = edges(blocks, params, weight)
     for t, b in enumerate(places(groups)):
         part = slice(t * cells, (t + 1) * cells)
         left[at(b, cells), :] = sides[0][0][part]
@@ -135,37 +138,33 @@
 
 def cells_kernel(
     sizes,
+    params,
     tri,
     normed_0,
     normed_1,
-    cot_0,
-    cot_1,
     gate_weight,
-    gain,
-    bias,
     out_weight,
-    block_out,
-    d_tri,
-    d_gate,
-    tri_norm_out,
-    d_update_out,
+    *refs,
 ):
     rows, cols, groups = sizes
     cells = rows * cols
-    for which, normed, cot in ((0, normed_0, cot_0), (1, normed_1, cot_1)):
+    cots, (block_out, d_tri, d_gate, tri_norm_out, d_update_out) = refs[:-5], refs[-5:]
+    gain, bias = params[2:3, :], params[3:4, :]
+    for which, normed in ((0, normed_0), (1, normed_1)):
         for t, b in enumerate(places(groups)):
+            cot = cots[t][which * cells : (which + 1) * cells, :]
             place = at(row_block(which, b), cells)
-            tri_f, hat, inverse = layer_norm(tri[place, :], gain[...], bias[...])
+            tri_f, hat, inverse = layer_norm(tri[place, :], gain, bias)
             tri_norm = tri_f.astype(BF16)
             update = dot(tri_norm, out_weight[...])
             out_gate = sigmoid(dot(normed[at(b, cells), :], gate_weight[...]))
             if which == 0 and t == 0:
                 block_out[...] = (out_gate * update).astype(BF16)
-            gated = cot[t * cells : (t + 1) * cells, :].astype(F32) * out_gate
+            gated = cot.astype(F32) * out_gate
             d_update = gated.astype(BF16)
             d_gate[place, :] = (gated * update * (1.0 - out_gate)).astype(BF16)
             d_norm = dot(d_update, out_weight[...], TRANSPOSED)
-            d_tri[place, :] = norm_back(d_norm, gain[...], hat, inverse).astype(BF16)
+            d_tri[place, :] = norm_back(d_norm, gain, hat, inverse).astype(BF16)
             tri_norm_out[place, :] = tri_norm
             d_update_out[place, :] = d_update
 
@@ -264,6 +263,7 @@
 
 def late_kernel(
     sizes,
+    params,
     pair,
     d_tri_ref,
     d_gate,
@@ -280,8 +280,6 @@
     right_gate_1,
     right_value_0,
     right_value_1,
-    norm_gain,
-    norm_bias,
     proj_weight,
     gate_weight,
     pair_grad,
@@ -362,8 +360,9 @@
     d_normed = dot(d_proj[own, :], proj_weight[...], TRANSPOSED) + dot(
         d_gate[own, :], gate_weight[...], TRANSPOSED
     )
-    _, hat, inverse = layer_norm(pair[...].astype(F32), norm_gain[...], norm_bias[...])
-    pair_grad[...] = norm_back(d_normed, norm_gain[...], hat, inverse)
+    gain = params[0:1, :]
+    _, hat, inverse = layer_norm(pair[...].astype(F32), gain, params[1:2, :])
+    pair_grad[...] = norm_back(d_normed, gain, hat, inverse)
 
 
 def replicated(
@@ -384,15 +383,15 @@
     every = cells * groups
     some = every // 2
     sizes = (rows, cols, groups)
-    norm_gain, norm_bias = norm_gain[None], norm_bias[None]
-    tri_gain, tri_bias = tri_gain[None], tri_bias[None]
-
-    def call(kernel, outs, *args, scratch=(), name):
+
+    def call(kernel, outs, *args, scratch=(), micros=1, name):
+        cost = pl.CostEstimate(flops=micros * 10**9, bytes_accessed=0, transcendentals=0)
         return pl.pallas_call(
             functools.partial(kernel, sizes),
             out_shape=[jax.ShapeDtypeStruct(*out) for out in outs],
             scratch_shapes=[pltpu.VMEM(*one) for one in scratch],
             compiler_params=pltpu.CompilerParams(vmem_limit_bytes=VMEM_BUDGET),
+            cost_estimate=cost,
             name=name,
         )(*args)
 
@@ -402,31 +401,42 @@
     def over(value):
         return lax.ppermute(value, "col", SWAP)
 
-    def gather(value):
-        got = [value] + [across(value, 2 * s) for s in range(1, groups // 2)]
-        near = jnp.concatenate(got, axis=0)
-        return near, across(near, 1)
+    def along(value):
+        return [across(value, 2 * s) for s in range(1, groups // 2)]
+
+    def join(*values):
+        return jnp.concatenate(values, axis=0)
+
+    def after(value, *others):
+        return lax.optimization_barrier((value, *others))[0]
+
+    full, part = (every, hidden), (some, hidden)
+
+    def own_edges(*blocks):
+        outs = [((some, channels), BF16)] + [(part, F32)] * 6
+        return call(own_edges_kernel, outs, params, proj_weight, *blocks, name="own_edges")
+
+    def mate_edges(*blocks):
+        outs = [(part, F32)] * 2
+        return call(mate_edges_kernel, outs, params, proj_weight, *blocks, name="mate_edges")
 
     pair = pair_rep.reshape(cells, channels)
-    pairs = gather(pair)
-    cots = gather(cotangent.reshape(cells, channels))
-    mates = [over(part) for part in pairs]
-    weights = (norm_gain, norm_bias, proj_weight)
-
-    full, part = (every, hidden), (some, hidden)
-    own = [
-        call(
-            own_edges_kernel,
-            [((some, channels), BF16)] + [(part, F32)] * 6,
-            x,
-            *weights,
-            name="own_edges",
-        )
-        for x in pairs
-    ]
-    mate = [
-        call(mate_edges_kernel, [(part, F32)] * 2, x, *weights, name="mate_edges") for x in mates
-    ]
+    cot = cotangent.reshape(cells, channels)
+    params = jnp.stack([norm_gain, norm_bias, tri_gain, tri_bias])
+    pair_far = across(pair, 1)
+    near = along(pair)
+    mate_pair = over(pair)
+    cot_far = across(after(cot, params), 1)
+    far = along(pair_far)
+    near_all = join(*near)
+    own_0 = own_edges(pair, near_all)
+    mate_0 = mate_edges(mate_pair, over(near_all))
+    cots = join(cot, cot_far)
+    cots = [cots] + along(after(cots, own_0[0]))
+    far_all = after(join(pair_far, *far), own_0[0], mate_0[0])
+    own_1 = own_edges(far_all)
+    mate_1 = mate_edges(over(far_all))
+    own, mate = (own_0, own_1), (mate_0, mate_1)
     normed = [o[0] for o in own]
     left, left_gate, left_value = ([o[n] for o in own] for n in (1, 2, 3))
     right, right_gate, right_value = ([o[n] for o in own] for n in (4, 5, 6))
@@ -438,18 +448,19 @@
         *right,
         *(m[1] for m in mate),
         scratch=[((cols * cols, hidden), F32)] * 2,
+        micros=2,
         name="triangle",
     )
     block_out, d_tri, d_gate, tri_norm, d_update = call(
         cells_kernel,
         [((cells, channels), BF16)] + [(full, BF16)] * 4,
+        params,
         tri,
         *normed,
+        gate_weight,
+        out_weight,
         *cots,
-        gate_weight,
-        tri_gain,
-        tri_bias,
-        out_weight,
+        micros=2,
         name="cells",
     )
     d_tri_mate = over(d_tri)
@@ -471,12 +482,14 @@
         *left,
         *right,
         scratch=[(full, F32)],
+        micros=3,
         name="early",
     )
     small_mate = over(small_grads)
     pair_grad, proj_grad = call(
         late_kernel,
         [((cells, channels), F32), ((channels, 4 * hidden), F32)],
+        params,
         pair,
         d_tri_mate,
         d_gate,
@@ -489,11 +502,10 @@
         *left_value,
         *right_gate,
         *right_value,
-        norm_gain,
-        norm_bias,
         proj_weight,
         gate_weight,
         scratch=[(full, F32), (full, F32), ((every, 4 * hidden), BF16)],
+        micros=4,
         name="late",
     )
     small = small_grads + small_mate

time: 40 us -> 42.5 us (1.062)
  starting transfers between devices: 13.4 us -> 17.4 us
  waiting for transfers between devices: 8.7 us -> 7.66 us
  local copies, waits for them, and re-layouts: 1.99 us -> 1.37 us
    ppermute x8 -> x11, starting transfers between devices: 12.2 us -> 16.7 us  [across(): return lax.ppermute(value, 'row', [(i, i ^ mask) for i in range(groups)])]
    ppermute x8 -> x11, waiting for transfers between devices: 7.88 us -> 6.83 us  [across(): return lax.ppermute(value, 'row', [(i, i ^ mask) for i in range(groups)])]
    concatenate x2, other arithmetic: 0.79 us -> 0.02 us  [join(): return jnp.concatenate(values, axis=0)]
    another operation x0 -> x1, other arithmetic: none -> 0.71 us  [replicated(): params = jnp.stack([norm_gain, norm_bias, tri_gain, tri_bias])]
    unnamed x18 -> x12, local copies, waits for them, and re-layouts: 1.33 us -> 0.7 us
    ppermute x5 -> x6, starting transfers between devices: 1.13 us -> 0.76 us  [over(): return lax.ppermute(value, 'col', SWAP)]
  transfers between devices with their start and end apart: 13 -> 17, of which waited for: 4 -> 5; matrix products, arithmetic and copies ran while one was open for 2% -> 3% of each run, Pallas kernels for 29% -> 27%
where the time goes in v3:
time: 42.5 us; the launch traced here: 42.2 us
  starting transfers between devices  17.4 us (41%)
  Pallas kernels  13.4 us (32%)
  waiting for transfers between devices  7.66 us (18%)
  other arithmetic  1.49 us (4%)
  local copies, waits for them, and re-layouts  1.37 us (3%)
  between operations  0.84 us (2%)
    ppermute x11, starting transfers between devices, across(): return lax.ppermute(value, 'row', [(i, i ^ mask) for i in range(groups)])  16.7 us
    pallas_call x8, Pallas kernels, call(): pl.pallas_call(functools.partial(kernel, sizes), out_shape=[jax.ShapeDtyp...  13.4 us
    ppermute x11, waiting for transfers between devices, across(): return lax.ppermute(value, 'row', [(i, i ^ mask) for i in range(groups)])  6.83 us
  transfers between devices with their start and end apart: 17, of which 5 were waited for; matrix products, arithmetic and copies ran while one was open for 3% of the time, Pallas kernels for 27%

profile of v3, /device:TPU:0, one launch (start us, length us, event | category | flops | bytes accessed | tf_op | source)
XLA Modules:
  0.0 42.2 jit_solution(13147458130063827597)
XLA Ops:
  0.6 3.1 %collective-permute-start = (bf16[144,128]{1,0:T(8,128)(2,1)}, bf16[144,128]{1,0:T(8,128)(2,1)S(1)}, u32[]{:S(2)}, u32[]{:S(2)}) collective-permute-start(bf16[144,128]{1,0:T(8,128)(2,1)} %bitcast.8), channel_id=1, source_target_pairs={{0,4},{2,6},{4,0},{6,2},{8,12},{10,14},{12,8},{14,10},{1,5},{3,7},... | collective-permute-start | bytes 110600 | tf_op jit(solution)/shard_map/ppermute | solution.py:399
  3.7 2.6 %collective-permute-start.1 = (bf16[144,128]{1,0:T(8,128)(2,1)}, bf16[144,128]{1,0:T(8,128)(2,1)S(1)}, u32[]{:S(2)}, u32[]{:S(2)}) collective-permute-start(bf16[144,128]{1,0:T(8,128)(2,1)} %bitcast.9), channel_id=1, source_target_pairs={{0,8},{2,10},{4,12},{6,14},{8,0},{10,2},{12,4},{14,6},{1,9},{3,11}... | collective-permute-start | bytes 110600 | tf_op jit(solution)/shard_map/ppermute | solution.py:399
  6.3 1.7 %collective-permute-start.3 = (bf16[144,128]{1,0:T(8,128)(2,1)}, bf16[144,128]{1,0:T(8,128)(2,1)S(1)}, u32[]{:S(2)}, u32[]{:S(2)}) collective-permute-start(bf16[144,128]{1,0:T(8,128)(2,1)} %bitcast.11), channel_id=1, source_target_pairs={{0,2},{2,0},{4,6},{6,4},{8,10},{10,8},{12,14},{14,12},{1,3},{3,1},... | collective-permute-start | bytes 110600 | tf_op jit(solution)/shard_map/ppermute | solution.py:399
  8.1 0.7 %pad_maximum_fusion.2.params = f32[4,128]{1,0:T(4,128)S(1)} fusion(f32[1,128]{1,0:T(1,128)} %bitcast.17, f32[1,128]{1,0:T(1,128)} %bitcast.18, f32[1,128]{1,0:T(1,128)} %bitcast.19, f32[1,128]{1,0:T(1,128)} %bitcast.20), kind=kLoop, calls=%fused_computation.5 | loop fusion | flops 1536 | bytes 4096 | tf_op jit(solution)/shard_map/stack | solution.py:425
  8.8 0.4 collective-permute-start.10
  9.1 1.4 %collective-permute-done.3 = bf16[144,128]{1,0:T(8,128)(2,1)S(1)} collective-permute-done((bf16[144,128]{1,0:T(8,128)(2,1)}, bf16[144,128]{1,0:T(8,128)(2,1)S(1)}, u32[]{:S(2)}, u32[]{:S(2)}) %collective-permute-start.3) | collective-permute-done | bytes 36896 | tf_op jit(solution)/shard_map/ppermute | solution.py:399
  10.5 0.9 %collective-permute-start.4 = (bf16[144,128]{1,0:T(8,128)(2,1)S(1)}, bf16[144,128]{1,0:T(8,128)(2,1)S(1)}, u32[]{:S(2)}, u32[]{:S(2)}) collective-permute-start(bf16[144,128]{1,0:T(8,128)(2,1)S(1)} %collective-permute-done.3), channel_id=1, source_target_pairs={{0,4},{2,6},{4,0},{6,2},{8,12},{10,14},{12,8},{14,10},{1,5},{3,7},... | collective-permute-start | bytes 110600 | tf_op jit(solution)/shard_map/ppermute | solution.py:399
  11.4 3.5 %collective-permute-start.5 = (bf16[144,128]{1,0:T(8,128)(2,1)S(1)}, bf16[144,128]{1,0:T(8,128)(2,1)S(1)}, u32[]{:S(2)}, u32[]{:S(2)}) collective-permute-start(bf16[144,128]{1,0:T(8,128)(2,1)S(1)} %collective-permute-done.3), channel_id=1, source_target_pairs={{0,8},{2,10},{4,12},{6,14},{8,0},{10,2},{12,4},{14,6},{1,9},{3,11}... | collective-permute-start | bytes 110600 | tf_op jit(solution)/shard_map/ppermute | solution.py:399
  14.9 0.1 collective-permute-start.6
  15.0 0.6 %copy-done.1 = bf16[6,24,128]{2,1,0:T(8,128)(2,1)S(1)} copy-done((bf16[6,24,128]{2,1,0:T(8,128)(2,1)S(1)}, bf16[6,24,128]{2,1,0:T(8,128)(2,1)}, u32[]{:S(2)}) %copy-start.1) | copy-done | bytes 36888
  15.7 0.6 %own_edges.2 = (bf16[576,128]{1,0:T(8,128)(2,1)S(1)}, f32[576,128]{1,0:T(8,128)S(1)}, f32[576,128]{1,0:T(8,128)S(1)}, f32[576,128]{1,0:T(8,128)S(1)}, f32[576,12...) custom-call(f32[4,128]{1,0:T(4,128)S(1)} %pad_maximum_fusion.2.params, bf16[128,512]{1,0:T(8,128)(2,1)S(1)} %copy-done, ...), custom_call_target="tpu_custom_call" | custom-call | flops 1000000000 | tf_op jit(solution)/shard_map/own_edges/pallas_call | solution.py:389
  16.3 0.1 collective-permute-start.8
  16.4 0.8 %collective-permute-done.5 = bf16[144,128]{1,0:T(8,128)(2,1)S(1)} collective-permute-done((bf16[144,128]{1,0:T(8,128)(2,1)S(1)}, bf16[144,128]{1,0:T(8,128)(2,1)S(1)}, u32[]{:S(2)}, u32[]{:S(2)}) %collective-permute-start.5) | collective-permute-done | bytes 36896 | tf_op jit(solution)/shard_map/ppermute | solution.py:399
  17.2 3.5 %collective-permute-done.6 = bf16[144,128]{1,0:T(8,128)(2,1)S(1)} collective-permute-done((bf16[144,128]{1,0:T(8,128)(2,1)S(1)}, bf16[144,128]{1,0:T(8,128)(2,1)S(1)}, u32[]{:S(2)}, u32[]{:S(2)}) %collective-permute-start.6) | collective-permute-done | bytes 36896 | tf_op jit(solution)/shard_map/ppermute | solution.py:399
  20.8 0.6 %mate_edges.2 = (f32[576,128]{1,0:T(8,128)S(1)}, f32[576,128]{1,0:T(8,128)S(1)}) custom-call(f32[4,128]{1,0:T(4,128)S(1)} %pad_maximum_fusion.2.params, bf16[128,512]{1,0:T(8,128)(2,1)S(1)} %copy-done, bf16[144,128]{1,0:T(8,128)(2,1)S(1)} %collective-permute-done.7.refs_0_, bf16[432,128]{1,0:T(8,128)(2,1)S(1)} %collective-permute-done.8.refs_1_), custom_call_target="tpu_custom_call" | custom-call | flops 1000000000 | tf_op jit(solution)/shard_map/mate_edges/pallas_call | solution.py:389
  21.4 0.1 collective-permute-start.9
  21.5 0.0 copy-done.4
  21.5 0.1 collective-permute-start.11
  21.6 0.9 %collective-permute-start.12 = (bf16[288,128]{1,0:T(8,128)(2,1)S(1)}, bf16[288,128]{1,0:T(8,128)(2,1)S(1)}, u32[]{:S(2)}, u32[]{:S(2)}) collective-permute-start(bf16[288,128]{1,0:T(8,128)(2,1)S(1)} %pad_maximum_fusion.1.refs_0_), channel_id=1, source_target_pairs={{0,8},{2,10},{4,12},{6,14},{8,0},{10,2},{12,4},{14,6},{1,9},{3,11}... | collective-permute-start | bytes 221192 | tf_op jit(solution)/shard_map/ppermute | solution.py:399
  22.5 3.5 %collective-permute-start.13 = (bf16[288,128]{1,0:T(8,128)(2,1)S(1)}, bf16[288,128]{1,0:T(8,128)(2,1)S(1)}, u32[]{:S(2)}, u32[]{:S(2)}) collective-permute-start(bf16[288,128]{1,0:T(8,128)(2,1)S(1)} %pad_maximum_fusion.1.refs_0_), channel_id=1, source_target_pairs={{0,12},{2,14},{4,8},{6,10},{8,4},{10,6},{12,0},{14,2},{1,13},{3,15... | collective-permute-start | bytes 221192 | tf_op jit(solution)/shard_map/ppermute | solution.py:399
  26.0 0.6 %own_edges.3 = (bf16[576,128]{1,0:T(8,128)(2,1)S(1)}, f32[576,128]{1,0:T(8,128)S(1)}, f32[576,128]{1,0:T(8,128)S(1)}, f32[576,128]{1,0:T(8,128)S(1)}, f32[576,12...) custom-call(f32[4,128]{1,0:T(4,128)S(1)} %pad_maximum_fusion.2.params, bf16[128,512]{1,0:T(8,128)(2,1)S(1)} %copy-done, ...), custom_call_target="tpu_custom_call" | custom-call | flops 1000000000 | tf_op jit(solution)/shard_map/own_edges/pallas_call | solution.py:389
  26.6 0.6 %mate_edges.3 = (f32[576,128]{1,0:T(8,128)S(1)}, f32[576,128]{1,0:T(8,128)S(1)}) custom-call(f32[4,128]{1,0:T(4,128)S(1)} %pad_maximum_fusion.2.params, bf16[128,512]{1,0:T(8,128)(2,1)S(1)} %copy-done, bf16[576,128]{1,0:T(8,128)(2,1)S(1)} %collective-permute-done.9.refs_0_), custom_call_target="tpu_custom_call" | custom-call | flops 1000000000 | tf_op jit(solution)/shard_map/mate_edges/pallas_call | solution.py:389
  27.3 2.4 %triangle.1.tri = f32[1152,128]{1,0:T(8,128)S(1)} custom-call(f32[576,128]{1,0:T(8,128)S(1)} %get-tuple-element.39.refs_0_.left_0, f32[576,128]{1,0:T(8,128)S(1)} %get-tuple-element.43.refs_1_.left_1, f32[576,128]{1,0:T(8,128)S(1)} %get-tuple-element.41.refs_2_, f32[576,128]{1,0:T(8,128)S(1)} %get-tuple-element.44.refs_3_, ...), custom_call_target="tpu_custom_call" | custom-call | flops 2000000000 | tf_op jit(solution)/shard_map/triangle/pallas_call | solution.py:389
  29.7 1.1 %collective-permute-done.12.refs_2_ = bf16[288,128]{1,0:T(8,128)(2,1)S(1)} collective-permute-done((bf16[288,128]{1,0:T(8,128)(2,1)S(1)}, bf16[288,128]{1,0:T(8,128)(2,1)S(1)}, u32[]{:S(2)}, u32[]{:S(2)}) %collective-permute-start.12) | collective-permute-done | bytes 73760 | tf_op jit(solution)/shard_map/ppermute | solution.py:399
  30.9 2.1 %cells.1 = (bf16[144,128]{1,0:T(8,128)(2,1)}, bf16[1152,128]{1,0:T(8,128)(2,1)S(1)}, bf16[1152,128]{1,0:T(8,128)(2,1)S(1)}, bf16[1152,128]{1,0:T(8,128)(2,1)S(1)}, bf16[1152,128]{1,0:T(8,128)(2,1)S(1)}) custom-call(f32[4,128]{1,0:T(4,128)S(1)} %pad_maximum_fusion.2.params, f32[1152,128]{1,0:T(8,128)S(1)} %triangle.1.tri, ...), custom_call_target="tpu_custom_call" | custom-call | flops 2000000000 | tf_op jit(solution)/shard_map/cells/pallas_call | solution.py:389
  33.0 2.7 %early.1 = (f32[1152,128]{1,0:T(8,128)S(1)}, f32[1152,128]{1,0:T(8,128)S(1)}, bf16[1152,128]{1,0:T(8,128)(2,1)S(1)}, f32[1152,128]{1,0:T(8,128)S(1)}, f32[576,128]{1,0:T(8,128)S(1)}, /*index=5*/f32[128,256]{1,0:T(8,128)S(1)}) custom-call(bf16[1152,128]{1,0:T(8,128)(2,1)S(1)} %get-tuple-element.53.d_tri_ref, bf16[1152,128]{1,0:T(8,128)(2,1)S(1)} %get-tuple-element.54.d_gate, ...), custom_call_target="tpu_custom_call" | custom-call | flops 3000000000 | tf_op jit(solution)/shard_map/early/pallas_call | solution.py:389
  35.7 0.6 %collective-permute-start.16 = (f32[128,256]{1,0:T(8,128)S(1)}, f32[128,256]{1,0:T(8,128)S(1)}, u32[]{:S(2)}, u32[]{:S(2)}) collective-permute-start(f32[128,256]{1,0:T(8,128)S(1)} %get-tuple-element.72), channel_id=1, source_target_pairs={{0,1},{1,0},{2,3},{3,2},{4,5},{5,4},{6,7},{7,6},{8,9},{9,8},{10,11... | collective-permute-start | bytes 393224 | tf_op jit(solution)/shard_map/ppermute | solution.py:402
  36.3 3.7 %late.1 = (f32[144,128]{1,0:T(8,128)}, f32[128,512]{1,0:T(8,128)S(1)}) custom-call(f32[4,128]{1,0:T(4,128)S(1)} %pad_maximum_fusion.2.params, bf16[144,128]{1,0:T(8,128)(2,1)S(1)} %bitcast.14, bf16[1152,128]{1,0:T(8,128)(2,1)S(1)} %collective-permute-done.14.d_tri_ref, bf16[1152,128]{1,0:T(8,128)(2,1)S(1)} %get-tuple-element.54.d_gate, ...), custom_call_target="tpu_custom_call" | custom-call | flops 4000000000 | tf_op jit(solution)/shard_map/late/pallas_call | solution.py:389
  39.9 0.0 collective-permute-start.15
  40.0 0.7 %fusion = (f32[128,128]{1,0:T(8,128)}, f32[128,128]{1,0:T(8,128)}) fusion(f32[128,256]{1,0:T(8,128)S(1)} %add.7), kind=kLoop, calls=%fused_computation.6 | loop fusion | bytes 262144 | tf_op jit(solution)/shard_map/slice | solution.py:517
  40.6 0.8 %collective-permute-done.15 = f32[128,512]{1,0:T(8,128)S(1)} collective-permute-done((f32[128,512]{1,0:T(8,128)S(1)}, f32[128,512]{1,0:T(8,128)S(1)}, u32[]{:S(2)}, u32[]{:S(2)}) %collective-permute-start.15) | collective-permute-done | bytes 262176 | tf_op jit(solution)/shard_map/ppermute | solution.py:402
  41.5 0.7 %add.6 = f32[128,512]{1,0:T(8,128)} add(f32[128,512]{1,0:T(8,128)S(1)} %get-tuple-element.71, f32[128,512]{1,0:T(8,128)S(1)} %collective-permute-done.15) | non-fusion elementwise | flops 65536 | bytes 786432 | tf_op jit(solution)/shard_map/add | solution.py:515
  (29 shorter events, 0.1 us)
Async XLA Ops:
  0.6 14.4 %copy-start = (bf16[128,512]{1,0:T(8,128)(2,1)S(1)}, bf16[128,512]{1,0:T(8,128)(2,1)}, u32[]{:S(2)}) copy-start(bf16[128,512]{1,0:T(8,128)(2,1)} %proj_weight.1) | copy-start | bytes 393220
  0.6 8.1 %collective-permute-start = (bf16[144,128]{1,0:T(8,128)(2,1)}, bf16[144,128]{1,0:T(8,128)(2,1)S(1)}, u32[]{:S(2)}, u32[]{:S(2)}) collective-permute-start(bf16[144,128]{1,0:T(8,128)(2,1)} %bitcast.8), channel_id=1, source_target_pairs={{0,4},{2,6},{4,0},{6,2},{8,12},{10,14},{12,8},{14,10},{1,5},{3,7},... | collective-permute-start | bytes 110600 | tf_op jit(solution)/shard_map/ppermute | solution.py:399
  3.7 7.7 %collective-permute-start.1 = (bf16[144,128]{1,0:T(8,128)(2,1)}, bf16[144,128]{1,0:T(8,128)(2,1)S(1)}, u32[]{:S(2)}, u32[]{:S(2)}) collective-permute-start(bf16[144,128]{1,0:T(8,128)(2,1)} %bitcast.9), channel_id=1, source_target_pairs={{0,8},{2,10},{4,12},{6,14},{8,0},{10,2},{12,4},{14,6},{1,9},{3,11}... | collective-permute-start | bytes 110600 | tf_op jit(solution)/shard_map/ppermute | solution.py:399
  6.3 8.6 %collective-permute-start.2 = (bf16[144,128]{1,0:T(8,128)(2,1)}, bf16[144,128]{1,0:T(8,128)(2,1)S(1)}, u32[]{:S(2)}, u32[]{:S(2)}) collective-permute-start(bf16[144,128]{1,0:T(8,128)(2,1)} %bitcast.10), channel_id=1, source_target_pairs={{0,12},{2,14},{4,8},{6,10},{8,4},{10,6},{12,0},{14,2},{1,13},{3,15... | collective-permute-start | bytes 110600 | tf_op jit(solution)/shard_map/ppermute | solution.py:399
  6.3 4.2 %collective-permute-start.3 = (bf16[144,128]{1,0:T(8,128)(2,1)}, bf16[144,128]{1,0:T(8,128)(2,1)S(1)}, u32[]{:S(2)}, u32[]{:S(2)}) collective-permute-start(bf16[144,128]{1,0:T(8,128)(2,1)} %bitcast.11), channel_id=1, source_target_pairs={{0,2},{2,0},{4,6},{6,4},{8,10},{10,8},{12,14},{14,12},{1,3},{3,1},... | collective-permute-start | bytes 110600 | tf_op jit(solution)/shard_map/ppermute | solution.py:399
  8.1 12.7 %collective-permute-start.7 = (bf16[144,128]{1,0:T(8,128)(2,1)}, bf16[144,128]{1,0:T(8,128)(2,1)S(1)}, u32[]{:S(2)}, u32[]{:S(2)}) collective-permute-start(bf16[144,128]{1,0:T(8,128)(2,1)} %bitcast.12), channel_id=1, source_target_pairs={{0,1},{1,0},{2,3},{3,2},{4,5},{5,4},{6,7},{7,6},{8,9},{9,8},{10,11... | collective-permute-start | bytes 110600 | tf_op jit(solution)/shard_map/ppermute | solution.py:402
  8.8 12.7 %collective-permute-start.10 = (bf16[144,128]{1,0:T(8,128)(2,1)}, bf16[144,128]{1,0:T(8,128)(2,1)S(1)}, u32[]{:S(2)}, u32[]{:S(2)}) collective-permute-start(bf16[144,128]{1,0:T(8,128)(2,1)} %bitcast.15), channel_id=1, source_target_pairs={{0,2},{2,0},{4,6},{6,4},{8,10},{10,8},{12,14},{14,12},{1,3},{3,1},... | collective-permute-start | bytes 110600 | tf_op jit(solution)/shard_map/ppermute | solution.py:399
  10.5 5.8 %collective-permute-start.4 = (bf16[144,128]{1,0:T(8,128)(2,1)S(1)}, bf16[144,128]{1,0:T(8,128)(2,1)S(1)}, u32[]{:S(2)}, u32[]{:S(2)}) collective-permute-start(bf16[144,128]{1,0:T(8,128)(2,1)S(1)} %collective-permute-done.3), channel_id=1, source_target_pairs={{0,4},{2,6},{4,0},{6,2},{8,12},{10,14},{12,8},{14,10},{1,5},{3,7},... | collective-permute-start | bytes 110600 | tf_op jit(solution)/shard_map/ppermute | solution.py:399
  11.4 5.8 %collective-permute-start.5 = (bf16[144,128]{1,0:T(8,128)(2,1)S(1)}, bf16[144,128]{1,0:T(8,128)(2,1)S(1)}, u32[]{:S(2)}, u32[]{:S(2)}) collective-permute-start(bf16[144,128]{1,0:T(8,128)(2,1)S(1)} %collective-permute-done.3), channel_id=1, source_target_pairs={{0,8},{2,10},{4,12},{6,14},{8,0},{10,2},{12,4},{14,6},{1,9},{3,11}... | collective-permute-start | bytes 110600 | tf_op jit(solution)/shard_map/ppermute | solution.py:399
  14.9 0.8 %copy-start.1 = (bf16[6,24,128]{2,1,0:T(8,128)(2,1)S(1)}, bf16[6,24,128]{2,1,0:T(8,128)(2,1)}, u32[]{:S(2)}) copy-start(bf16[6,24,128]{2,1,0:T(8,128)(2,1)} %param.9) | copy-start | bytes 110596
  14.9 5.8 %collective-permute-start.6 = (bf16[144,128]{1,0:T(8,128)(2,1)S(1)}, bf16[144,128]{1,0:T(8,128)(2,1)S(1)}, u32[]{:S(2)}, u32[]{:S(2)}) collective-permute-start(bf16[144,128]{1,0:T(8,128)(2,1)S(1)} %collective-permute-done.3), channel_id=1, source_target_pairs={{0,12},{2,14},{4,8},{6,10},{8,4},{10,6},{12,0},{14,2},{1,13},{3,15... | collective-permute-start | bytes 110600 | tf_op jit(solution)/shard_map/ppermute | solution.py:399
  16.3 4.5 %collective-permute-start.8 = (bf16[432,128]{1,0:T(8,128)(2,1)S(1)}, bf16[432,128]{1,0:T(8,128)(2,1)S(1)}, u32[]{:S(2)}, u32[]{:S(2)}) collective-permute-start(bf16[432,128]{1,0:T(8,128)(2,1)S(1)} %constant_dynamic-update-slice_fusion.refs_1_), channel_id=1, source_target_pairs={{0,1},{1,0},{2,3},{3,2},{4,5},{5,4},{6,7},{7,6},{8,9},{9,8},{10,11... | collective-permute-start | bytes 331784 | tf_op jit(solution)/shard_map/ppermute | solution.py:402
  20.7 0.8 %copy-start.4 = (bf16[6,24,128]{2,1,0:T(8,128)(2,1)S(1)}, bf16[6,24,128]{2,1,0:T(8,128)(2,1)}, u32[]{:S(2)}) copy-start(bf16[6,24,128]{2,1,0:T(8,128)(2,1)} %param.10) | copy-start | bytes 110596
  21.4 5.2 %collective-permute-start.9 = (bf16[576,128]{1,0:T(8,128)(2,1)S(1)}, bf16[576,128]{1,0:T(8,128)(2,1)S(1)}, u32[]{:S(2)}, u32[]{:S(2)}) collective-permute-start(bf16[576,128]{1,0:T(8,128)(2,1)S(1)} %pad_maximum_fusion.refs_0_), channel_id=1, source_target_pairs={{0,1},{1,0},{2,3},{3,2},{4,5},{5,4},{6,7},{7,6},{8,9},{9,8},{10,11... | collective-permute-start | bytes 442376 | tf_op jit(solution)/shard_map/ppermute | solution.py:402
  21.5 8.2 %collective-permute-start.11 = (bf16[288,128]{1,0:T(8,128)(2,1)S(1)}, bf16[288,128]{1,0:T(8,128)(2,1)S(1)}, u32[]{:S(2)}, u32[]{:S(2)}) collective-permute-start(bf16[288,128]{1,0:T(8,128)(2,1)S(1)} %pad_maximum_fusion.1.refs_0_), channel_id=1, source_target_pairs={{0,4},{2,6},{4,0},{6,2},{8,12},{10,14},{12,8},{14,10},{1,5},{3,7},... | collective-permute-start | bytes 221192 | tf_op jit(solution)/shard_map/ppermute | solution.py:399
  21.6 9.2 %collective-permute-start.12 = (bf16[288,128]{1,0:T(8,128)(2,1)S(1)}, bf16[288,128]{1,0:T(8,128)(2,1)S(1)}, u32[]{:S(2)}, u32[]{:S(2)}) collective-permute-start(bf16[288,128]{1,0:T(8,128)(2,1)S(1)} %pad_maximum_fusion.1.refs_0_), channel_id=1, source_target_pairs={{0,8},{2,10},{4,12},{6,14},{8,0},{10,2},{12,4},{14,6},{1,9},{3,11}... | collective-permute-start | bytes 221192 | tf_op jit(solution)/shard_map/ppermute | solution.py:399
  22.5 8.4 %collective-permute-start.13 = (bf16[288,128]{1,0:T(8,128)(2,1)S(1)}, bf16[288,128]{1,0:T(8,128)(2,1)S(1)}, u32[]{:S(2)}, u32[]{:S(2)}) collective-permute-start(bf16[288,128]{1,0:T(8,128)(2,1)S(1)} %pad_maximum_fusion.1.refs_0_), channel_id=1, source_target_pairs={{0,12},{2,14},{4,8},{6,10},{8,4},{10,6},{12,0},{14,2},{1,13},{3,15... | collective-permute-start | bytes 221192 | tf_op jit(solution)/shard_map/ppermute | solution.py:399
  27.3 3.6 %copy-start.2 = (bf16[128,128]{1,0:T(8,128)(2,1)S(1)}, bf16[128,128]{1,0:T(8,128)(2,1)}, u32[]{:S(2)}) copy-start(bf16[128,128]{1,0:T(8,128)(2,1)} %out_weight.1) | copy-start | bytes 98308
  27.3 3.6 %copy-start.3 = (bf16[128,128]{1,0:T(8,128)(2,1)S(1)}, bf16[128,128]{1,0:T(8,128)(2,1)}, u32[]{:S(2)}) copy-start(bf16[128,128]{1,0:T(8,128)(2,1)} %gate_weight.3) | copy-start | bytes 98308
  33.0 3.3 %collective-permute-start.14 = (bf16[1152,128]{1,0:T(8,128)(2,1)S(1)}, bf16[1152,128]{1,0:T(8,128)(2,1)S(1)}, u32[]{:S(2)}, u32[]{:S(2)}) collective-permute-start(bf16[1152,128]{1,0:T(8,128)(2,1)S(1)} %get-tuple-element.53.d_tri_ref), channel_id=1, source_target_pairs={{0,1},{1,0},{2,3},{3,2},{4,5},{5,4},{6,7},{7,6},{8,9},{9,8},{10,11... | collective-permute-start | bytes 884744 | tf_op jit(solution)/shard_map/ppermute | solution.py:402
  35.7 4.3 %collective-permute-start.16 = (f32[128,256]{1,0:T(8,128)S(1)}, f32[128,256]{1,0:T(8,128)S(1)}, u32[]{:S(2)}, u32[]{:S(2)}) collective-permute-start(f32[128,256]{1,0:T(8,128)S(1)} %get-tuple-element.72), channel_id=1, source_target_pairs={{0,1},{1,0},{2,3},{3,2},{4,5},{5,4},{6,7},{7,6},{8,9},{9,8},{10,11... | collective-permute-start | bytes 393224 | tf_op jit(solution)/shard_map/ppermute | solution.py:402
  39.9 1.5 %collective-permute-start.15 = (f32[128,512]{1,0:T(8,128)S(1)}, f32[128,512]{1,0:T(8,128)S(1)}, u32[]{:S(2)}, u32[]{:S(2)}) collective-permute-start(f32[128,512]{1,0:T(8,128)S(1)} %get-tuple-element.71), channel_id=1, source_target_pairs={{0,1},{1,0},{2,3},{3,2},{4,5},{5,4},{6,7},{7,6},{8,9},{9,8},{10,11... | collective-permute-start | bytes 786440 | tf_op jit(solution)/shard_map/ppermute | solution.py:402

commit v4 on v3

--- a/solution.py
+++ b/solution.py
@@ -152,7 +152,7 @@
     gain, bias = params[2:3, :], params[3:4, :]
     for which, normed in ((0, normed_0), (1, normed_1)):
         for t, b in enumerate(places(groups)):
-            cot = cots[t][which * cells : (which + 1) * cells, :]
+            cot = cots[which][t * cells : (t + 1) * cells, :]
             place = at(row_block(which, b), cells)
             tri_f, hat, inverse = layer_norm(tri[place, :], gain, bias)
             tri_norm = tri_f.astype(BF16)
@@ -385,7 +385,7 @@
     sizes = (rows, cols, groups)
 
     def call(kernel, outs, *args, scratch=(), micros=1, name):
-        cost = pl.CostEstimate(flops=micros * 10**9, bytes_accessed=0, transcendentals=0)
+        cost = pl.CostEstimate(flops=micros * 10**8, bytes_accessed=0, transcendentals=0)
         return pl.pallas_call(
             functools.partial(kernel, sizes),
             out_shape=[jax.ShapeDtypeStruct(*out) for out in outs],
@@ -402,7 +402,11 @@
         return lax.ppermute(value, "col", SWAP)
 
     def along(value):
-        return [across(value, 2 * s) for s in range(1, groups // 2)]
+        got = []
+        for s in reversed(range(1, groups // 2)):
+            arrived = across(value, 2 * s)
+            got.append(after(arrived, got[-1]) if got else arrived)
+        return got[::-1]
 
     def join(*values):
         return jnp.concatenate(values, axis=0)
@@ -414,26 +418,24 @@
 
     def own_edges(*blocks):
         outs = [((some, channels), BF16)] + [(part, F32)] * 6
-        return call(own_edges_kernel, outs, params, proj_weight, *blocks, name="own_edges")
+        return call(own_edges_kernel, outs, params, proj_weight, *blocks, micros=7, name="own_edges")
 
     def mate_edges(*blocks):
         outs = [(part, F32)] * 2
-        return call(mate_edges_kernel, outs, params, proj_weight, *blocks, name="mate_edges")
+        return call(mate_edges_kernel, outs, params, proj_weight, *blocks, micros=7, name="mate_edges")
 
     pair = pair_rep.reshape(cells, channels)
     cot = cotangent.reshape(cells, channels)
     params = jnp.stack([norm_gain, norm_bias, tri_gain, tri_bias])
+    near = along(pair)
     pair_far = across(pair, 1)
-    near = along(pair)
-    mate_pair = over(pair)
-    cot_far = across(after(cot, params), 1)
-    far = along(pair_far)
-    near_all = join(*near)
+    near_all = after(join(*near), params, pair_far)
+    far = across(near_all, 1)
     own_0 = own_edges(pair, near_all)
-    mate_0 = mate_edges(mate_pair, over(near_all))
-    cots = join(cot, cot_far)
-    cots = [cots] + along(after(cots, own_0[0]))
-    far_all = after(join(pair_far, *far), own_0[0], mate_0[0])
+    mate_0 = mate_edges(over(join(pair, near_all)))
+    cot_near = join(cot, *along(cot))
+    cot_far = across(cot_near, 1)
+    far_all = after(join(pair_far, far), own_0[0], mate_0[0])
     own_1 = own_edges(far_all)
     mate_1 = mate_edges(over(far_all))
     own, mate = (own_0, own_1), (mate_0, mate_1)
@@ -459,7 +461,8 @@
         *normed,
         gate_weight,
         out_weight,
-        *cots,
+        cot_near,
+        cot_far,
         micros=2,
         name="cells",
     )

time: 42.5 us -> 36.7 us (0.86)
  starting transfers between devices: 17.4 us -> 14 us
  waiting for transfers between devices: 7.66 us -> 6 us
  other arithmetic: 1.49 us -> 0.81 us
    ppermute x11 -> x9, starting transfers between devices: 16.7 us -> 13.2 us  [across(): return lax.ppermute(value, 'row', [(i, i ^ mask) for i in range(groups)])]
    ppermute x11 -> x9, waiting for transfers between devices: 6.83 us -> 5.18 us  [across(): return lax.ppermute(value, 'row', [(i, i ^ mask) for i in range(groups)])]
    another operation x1, other arithmetic: 0.71 us -> 0.01 us  [replicated(): params = jnp.stack([norm_gain, norm_bias, tri_gain, tri_bias])]
    unnamed x12 -> x18, local copies, waits for them, and re-layouts: 0.7 us -> 0.88 us
  transfers between devices with their start and end apart: 17 -> 14, of which waited for: 5 -> 4; matrix products, arithmetic and copies ran while one was open for 3% -> 2% of each run, Pallas kernels for 27% -> 29%
where the time goes in v4:
time: 36.7 us; the launch traced here: 36.5 us
  starting transfers between devices  14 us (38%)
  Pallas kernels  13.4 us (37%)
  waiting for transfers between devices  6 us (16%)
  local copies, waits for them, and re-layouts  1.53 us (4%)
  between operations  0.82 us (2%)
  other arithmetic  0.81 us (2%)
    pallas_call x8, Pallas kernels, call(): pl.pallas_call(functools.partial(kernel, sizes), out_shape=[jax.ShapeDtyp...  13.4 us
    ppermute x9, starting transfers between devices, across(): return lax.ppermute(value, 'row', [(i, i ^ mask) for i in range(groups)])  13.2 us
    ppermute x9, waiting for transfers between devices, across(): return lax.ppermute(value, 'row', [(i, i ^ mask) for i in range(groups)])  5.18 us
    unnamed x18, local copies, waits for them, and re-layouts  0.88 us
    ppermute x5, waiting for transfers between devices, over(): return lax.ppermute(value, 'col', SWAP)  0.82 us
    ppermute x5, starting transfers between devices, over(): return lax.ppermute(value, 'col', SWAP)  0.76 us
    add x1, other arithmetic, replicated(): proj_grad + over(proj_grad)  0.74 us
  transfers between devices with their start and end apart: 14, of which 4 were waited for; matrix products, arithmetic and copies ran while one was open for 2% of the time, Pallas kernels for 29%

profile of v4, /device:TPU:0, one launch (start us, length us, event | category | flops | bytes accessed | tf_op | source)
XLA Modules:
  0.0 36.5 jit_solution(2701119974185908512)
XLA Ops:
  0.6 5.1 %collective-permute-start.2 = (bf16[144,128]{1,0:T(8,128)(2,1)}, bf16[144,128]{1,0:T(8,128)(2,1)S(1)}, u32[]{:S(2)}, u32[]{:S(2)}) collective-permute-start(bf16[144,128]{1,0:T(8,128)(2,1)} %bitcast.8), channel_id=1, source_target_pairs={{0,12},{2,14},{4,8},{6,10},{8,4},{10,6},{12,0},{14,2},{1,13},{3,15... | collective-permute-start | bytes 110600 | tf_op jit(solution)/shard_map/ppermute | solution.py:399
  5.8 0.6 %collective-permute-start = (bf16[144,128]{1,0:T(8,128)(2,1)}, bf16[144,128]{1,0:T(8,128)(2,1)S(1)}, u32[]{:S(2)}, u32[]{:S(2)}) collective-permute-start(bf16[144,128]{1,0:T(8,128)(2,1)} %bitcast.10), channel_id=1, source_target_pairs={{0,4},{2,6},{4,0},{6,2},{8,12},{10,14},{12,8},{14,10},{1,5},{3,7},... | collective-permute-start | bytes 110600 | tf_op jit(solution)/shard_map/ppermute | solution.py:399
  6.4 1.7 %collective-permute-start.3 = (bf16[144,128]{1,0:T(8,128)(2,1)}, bf16[144,128]{1,0:T(8,128)(2,1)S(1)}, u32[]{:S(2)}, u32[]{:S(2)}) collective-permute-start(bf16[144,128]{1,0:T(8,128)(2,1)} %bitcast.11), channel_id=1, source_target_pairs={{0,2},{2,0},{4,6},{6,4},{8,10},{10,8},{12,14},{14,12},{1,3},{3,1},... | collective-permute-start | bytes 110600 | tf_op jit(solution)/shard_map/ppermute | solution.py:399
  8.1 3.6 %collective-permute-start.9 = (bf16[144,128]{1,0:T(8,128)(2,1)}, bf16[144,128]{1,0:T(8,128)(2,1)S(1)}, u32[]{:S(2)}, u32[]{:S(2)}) collective-permute-start(bf16[144,128]{1,0:T(8,128)(2,1)} %bitcast.15), channel_id=1, source_target_pairs={{0,12},{2,14},{4,8},{6,10},{8,4},{10,6},{12,0},{14,2},{1,13},{3,15... | collective-permute-start | bytes 110600 | tf_op jit(solution)/shard_map/ppermute | solution.py:399
  11.7 0.6 %copy-done.8 = f32[128]{0:T(128)S(1)} copy-done((f32[128]{0:T(128)S(1)}, f32[128]{0:T(128)}, u32[]{:S(2)}) %copy-start.8) | copy-done | bytes 536
  12.3 0.0 copy-done.5
  12.3 0.0 copy-done.6
  12.3 0.0 copy-done.7
  12.4 0.1 collective-permute-start.8
  12.5 0.8 %collective-permute-start.7 = (bf16[144,128]{1,0:T(8,128)(2,1)}, bf16[144,128]{1,0:T(8,128)(2,1)S(1)}, u32[]{:S(2)}, u32[]{:S(2)}) collective-permute-start(bf16[144,128]{1,0:T(8,128)(2,1)} %bitcast.17), channel_id=1, source_target_pairs={{0,4},{2,6},{4,0},{6,2},{8,12},{10,14},{12,8},{14,10},{1,5},{3,7},... | collective-permute-start | bytes 110600 | tf_op jit(solution)/shard_map/ppermute | solution.py:399
  13.3 0.7 %collective-permute-start.4 = (bf16[432,128]{1,0:T(8,128)(2,1)S(1)}, bf16[432,128]{1,0:T(8,128)(2,1)S(1)}, u32[]{:S(2)}, u32[]{:S(2)}) collective-permute-start(bf16[432,128]{1,0:T(8,128)(2,1)S(1)} %pad_maximum_fusion.3.refs_1_), channel_id=1, source_target_pairs={{0,2},{2,0},{4,6},{6,4},{8,10},{10,8},{12,14},{14,12},{1,3},{3,1},... | collective-permute-start | bytes 331784 | tf_op jit(solution)/shard_map/ppermute | solution.py:399
  14.0 0.1 collective-permute-start.5
  14.1 0.1 copy-done.2
  14.2 0.6 %own_edges.2 = (bf16[576,128]{1,0:T(8,128)(2,1)S(1)}, f32[576,128]{1,0:T(8,128)S(1)}, f32[576,128]{1,0:T(8,128)S(1)}, f32[576,128]{1,0:T(8,128)S(1)}, f32[576,12...) custom-call(f32[4,128]{1,0:T(4,128)S(1)} %pad_maximum_fusion.4.params, ...), custom_call_target="tpu_custom_call" | custom-call | flops 700000000 | tf_op jit(solution)/shard_map/own_edges/pallas_call | solution.py:389
  14.8 2.7 %collective-permute-done.8 = bf16[144,128]{1,0:T(8,128)(2,1)S(1)} collective-permute-done((bf16[144,128]{1,0:T(8,128)(2,1)}, bf16[144,128]{1,0:T(8,128)(2,1)S(1)}, u32[]{:S(2)}, u32[]{:S(2)}) %collective-permute-start.8) | collective-permute-done | bytes 36896 | tf_op jit(solution)/shard_map/ppermute | solution.py:399
  17.5 0.6 %collective-permute-done.4 = bf16[432,128]{1,0:T(8,128)(2,1)S(1)} collective-permute-done((bf16[432,128]{1,0:T(8,128)(2,1)S(1)}, bf16[432,128]{1,0:T(8,128)(2,1)S(1)}, u32[]{:S(2)}, u32[]{:S(2)}) %collective-permute-start.4) | collective-permute-done | bytes 110624 | tf_op jit(solution)/shard_map/ppermute | solution.py:399
  18.1 0.6 %mate_edges.2 = (f32[576,128]{1,0:T(8,128)S(1)}, f32[576,128]{1,0:T(8,128)S(1)}) custom-call(f32[4,128]{1,0:T(4,128)S(1)} %pad_maximum_fusion.4.params, bf16[128,512]{1,0:T(8,128)(2,1)S(1)} %copy-done.2, bf16[576,128]{1,0:T(8,128)(2,1)S(1)} %collective-permute-done.5.refs_0_), custom_call_target="tpu_custom_call" | custom-call | flops 700000000 | tf_op jit(solution)/shard_map/mate_edges/pallas_call | solution.py:389
  18.8 0.1 collective-permute-start.6
  18.9 0.0 copy-done.4
  18.9 0.7 %collective-permute-start.10 = (bf16[576,128]{1,0:T(8,128)(2,1)S(1)}, bf16[576,128]{1,0:T(8,128)(2,1)S(1)}, u32[]{:S(2)}, u32[]{:S(2)}) collective-permute-start(bf16[576,128]{1,0:T(8,128)(2,1)S(1)} %pad_maximum_fusion.2.refs_0_), channel_id=1, source_target_pairs={{0,2},{2,0},{4,6},{6,4},{8,10},{10,8},{12,14},{14,12},{1,3},{3,1},... | collective-permute-start | bytes 442376 | tf_op jit(solution)/shard_map/ppermute | solution.py:399
  19.6 0.6 %own_edges.3 = (bf16[576,128]{1,0:T(8,128)(2,1)S(1)}, f32[576,128]{1,0:T(8,128)S(1)}, f32[576,128]{1,0:T(8,128)S(1)}, f32[576,128]{1,0:T(8,128)S(1)}, f32[576,12...) custom-call(f32[4,128]{1,0:T(4,128)S(1)} %pad_maximum_fusion.4.params, ...), custom_call_target="tpu_custom_call" | custom-call | flops 700000000 | tf_op jit(solution)/shard_map/own_edges/pallas_call | solution.py:389
  20.2 0.6 %mate_edges.3 = (f32[576,128]{1,0:T(8,128)S(1)}, f32[576,128]{1,0:T(8,128)S(1)}) custom-call(f32[4,128]{1,0:T(4,128)S(1)} %pad_maximum_fusion.4.params, bf16[128,512]{1,0:T(8,128)(2,1)S(1)} %copy-done.2, bf16[576,128]{1,0:T(8,128)(2,1)S(1)} %collective-permute-done.6.refs_0_), custom_call_target="tpu_custom_call" | custom-call | flops 700000000 | tf_op jit(solution)/shard_map/mate_edges/pallas_call | solution.py:389
  20.9 2.4 %triangle.1.tri = f32[1152,128]{1,0:T(8,128)S(1)} custom-call(f32[576,128]{1,0:T(8,128)S(1)} %get-tuple-element.45.refs_0_.left_0, f32[576,128]{1,0:T(8,128)S(1)} %get-tuple-element.49.refs_1_.left_1, f32[576,128]{1,0:T(8,128)S(1)} %get-tuple-element.47.refs_2_, f32[576,128]{1,0:T(8,128)S(1)} %get-tuple-element.50.refs_3_, ...), custom_call_target="tpu_custom_call" | custom-call | flops 200000000 | tf_op jit(solution)/shard_map/triangle/pallas_call | solution.py:389
  23.3 1.9 %collective-permute-done.10.refs_1_ = bf16[576,128]{1,0:T(8,128)(2,1)S(1)} collective-permute-done((bf16[576,128]{1,0:T(8,128)(2,1)S(1)}, bf16[576,128]{1,0:T(8,128)(2,1)S(1)}, u32[]{:S(2)}, u32[]{:S(2)}) %collective-permute-start.10) | collective-permute-done | bytes 147488 | tf_op jit(solution)/shard_map/ppermute | solution.py:399
  25.2 2.1 %cells.1 = (bf16[144,128]{1,0:T(8,128)(2,1)}, bf16[1152,128]{1,0:T(8,128)(2,1)S(1)}, bf16[1152,128]{1,0:T(8,128)(2,1)S(1)}, bf16[1152,128]{1,0:T(8,128)(2,1)S(1)}, bf16[1152,128]{1,0:T(8,128)(2,1)S(1)}) custom-call(f32[4,128]{1,0:T(4,128)S(1)} %pad_maximum_fusion.4.params, f32[1152,128]{1,0:T(8,128)S(1)} %triangle.1.tri, ...), custom_call_target="tpu_custom_call" | custom-call | flops 200000000 | tf_op jit(solution)/shard_map/cells/pallas_call | solution.py:389
  27.3 2.7 %early.1 = (f32[1152,128]{1,0:T(8,128)S(1)}, f32[1152,128]{1,0:T(8,128)S(1)}, bf16[1152,128]{1,0:T(8,128)(2,1)S(1)}, f32[1152,128]{1,0:T(8,128)S(1)}, f32[576,128]{1,0:T(8,128)S(1)}, /*index=5*/f32[128,256]{1,0:T(8,128)S(1)}) custom-call(bf16[1152,128]{1,0:T(8,128)(2,1)S(1)} %get-tuple-element.59.d_tri_ref, bf16[1152,128]{1,0:T(8,128)(2,1)S(1)} %get-tuple-element.60.d_gate, ...), custom_call_target="tpu_custom_call" | custom-call | flops 300000000 | tf_op jit(solution)/shard_map/early/pallas_call | solution.py:389
  30.0 0.6 %collective-permute-start.13 = (f32[128,256]{1,0:T(8,128)S(1)}, f32[128,256]{1,0:T(8,128)S(1)}, u32[]{:S(2)}, u32[]{:S(2)}) collective-permute-start(f32[128,256]{1,0:T(8,128)S(1)} %get-tuple-element.78), channel_id=1, source_target_pairs={{0,1},{1,0},{2,3},{3,2},{4,5},{5,4},{6,7},{7,6},{8,9},{9,8},{10,11... | collective-permute-start | bytes 393224 | tf_op jit(solution)/shard_map/ppermute | solution.py:402
  30.6 3.7 %late.1 = (f32[144,128]{1,0:T(8,128)}, f32[128,512]{1,0:T(8,128)S(1)}) custom-call(f32[4,128]{1,0:T(4,128)S(1)} %pad_maximum_fusion.4.params, bf16[144,128]{1,0:T(8,128)(2,1)S(1)} %bitcast.14, bf16[1152,128]{1,0:T(8,128)(2,1)S(1)} %collective-permute-done.11.d_tri_ref, bf16[1152,128]{1,0:T(8,128)(2,1)S(1)} %get-tuple-element.60.d_gate, ...), custom_call_target="tpu_custom_call" | custom-call | flops 400000000 | tf_op jit(solution)/shard_map/late/pallas_call | solution.py:389
  34.2 0.0 collective-permute-start.12
  34.3 0.7 %fusion = (f32[128,128]{1,0:T(8,128)}, f32[128,128]{1,0:T(8,128)}) fusion(f32[128,256]{1,0:T(8,128)S(1)} %add.7), kind=kLoop, calls=%fused_computation.5 | loop fusion | bytes 262144 | tf_op jit(solution)/shard_map/slice | solution.py:520
  35.0 0.8 %collective-permute-done.12 = f32[128,512]{1,0:T(8,128)S(1)} collective-permute-done((f32[128,512]{1,0:T(8,128)S(1)}, f32[128,512]{1,0:T(8,128)S(1)}, u32[]{:S(2)}, u32[]{:S(2)}) %collective-permute-start.12) | collective-permute-done | bytes 262176 | tf_op jit(solution)/shard_map/ppermute | solution.py:402
  35.8 0.7 %add.6 = f32[128,512]{1,0:T(8,128)} add(f32[128,512]{1,0:T(8,128)S(1)} %get-tuple-element.77, f32[128,512]{1,0:T(8,128)S(1)} %collective-permute-done.12) | non-fusion elementwise | flops 65536 | bytes 786432 | tf_op jit(solution)/shard_map/add | solution.py:518
  (30 shorter events, 0.1 us)
Async XLA Ops:
  0.6 11.8 %collective-permute-start.2 = (bf16[144,128]{1,0:T(8,128)(2,1)}, bf16[144,128]{1,0:T(8,128)(2,1)S(1)}, u32[]{:S(2)}, u32[]{:S(2)}) collective-permute-start(bf16[144,128]{1,0:T(8,128)(2,1)} %bitcast.8), channel_id=1, source_target_pairs={{0,12},{2,14},{4,8},{6,10},{8,4},{10,6},{12,0},{14,2},{1,13},{3,15... | collective-permute-start | bytes 110600 | tf_op jit(solution)/shard_map/ppermute | solution.py:399
  5.7 6.7 %collective-permute-start.1 = (bf16[144,128]{1,0:T(8,128)(2,1)}, bf16[144,128]{1,0:T(8,128)(2,1)S(1)}, u32[]{:S(2)}, u32[]{:S(2)}) collective-permute-start(bf16[144,128]{1,0:T(8,128)(2,1)} %bitcast.9), channel_id=1, source_target_pairs={{0,8},{2,10},{4,12},{6,14},{8,0},{10,2},{12,4},{14,6},{1,9},{3,11}... | collective-permute-start | bytes 110600 | tf_op jit(solution)/shard_map/ppermute | solution.py:399
  5.8 7.5 %collective-permute-start = (bf16[144,128]{1,0:T(8,128)(2,1)}, bf16[144,128]{1,0:T(8,128)(2,1)S(1)}, u32[]{:S(2)}, u32[]{:S(2)}) collective-permute-start(bf16[144,128]{1,0:T(8,128)(2,1)} %bitcast.10), channel_id=1, source_target_pairs={{0,4},{2,6},{4,0},{6,2},{8,12},{10,14},{12,8},{14,10},{1,5},{3,7},... | collective-permute-start | bytes 110600 | tf_op jit(solution)/shard_map/ppermute | solution.py:399
  6.4 6.9 %collective-permute-start.3 = (bf16[144,128]{1,0:T(8,128)(2,1)}, bf16[144,128]{1,0:T(8,128)(2,1)S(1)}, u32[]{:S(2)}, u32[]{:S(2)}) collective-permute-start(bf16[144,128]{1,0:T(8,128)(2,1)} %bitcast.11), channel_id=1, source_target_pairs={{0,2},{2,0},{4,6},{6,4},{8,10},{10,8},{12,14},{14,12},{1,3},{3,1},... | collective-permute-start | bytes 110600 | tf_op jit(solution)/shard_map/ppermute | solution.py:399
  8.1 6.8 %collective-permute-start.9 = (bf16[144,128]{1,0:T(8,128)(2,1)}, bf16[144,128]{1,0:T(8,128)(2,1)S(1)}, u32[]{:S(2)}, u32[]{:S(2)}) collective-permute-start(bf16[144,128]{1,0:T(8,128)(2,1)} %bitcast.15), channel_id=1, source_target_pairs={{0,12},{2,14},{4,8},{6,10},{8,4},{10,6},{12,0},{14,2},{1,13},{3,15... | collective-permute-start | bytes 110600 | tf_op jit(solution)/shard_map/ppermute | solution.py:399
  11.7 0.7 %copy-start.8 = (f32[128]{0:T(128)S(1)}, f32[128]{0:T(128)}, u32[]{:S(2)}) copy-start(f32[128]{0:T(128)} %param.11) | copy-start | bytes 1540
  11.7 0.7 %copy-start.5 = (f32[128]{0:T(128)S(1)}, f32[128]{0:T(128)}, u32[]{:S(2)}) copy-start(f32[128]{0:T(128)} %param.16) | copy-start | bytes 1540
  11.7 0.7 %copy-start.6 = (f32[128]{0:T(128)S(1)}, f32[128]{0:T(128)}, u32[]{:S(2)}) copy-start(f32[128]{0:T(128)} %param.15) | copy-start | bytes 1540
  11.7 0.7 %copy-start.7 = (f32[128]{0:T(128)S(1)}, f32[128]{0:T(128)}, u32[]{:S(2)}) copy-start(f32[128]{0:T(128)} %param.12) | copy-start | bytes 1540
  12.4 1.6 %copy-start = (bf16[6,24,128]{2,1,0:T(8,128)(2,1)S(1)}, bf16[6,24,128]{2,1,0:T(8,128)(2,1)}, u32[]{:S(2)}) copy-start(bf16[6,24,128]{2,1,0:T(8,128)(2,1)} %param.9) | copy-start | bytes 110596
  12.4 5.1 %collective-permute-start.8 = (bf16[144,128]{1,0:T(8,128)(2,1)}, bf16[144,128]{1,0:T(8,128)(2,1)S(1)}, u32[]{:S(2)}, u32[]{:S(2)}) collective-permute-start(bf16[144,128]{1,0:T(8,128)(2,1)} %bitcast.16), channel_id=1, source_target_pairs={{0,8},{2,10},{4,12},{6,14},{8,0},{10,2},{12,4},{14,6},{1,9},{3,11}... | collective-permute-start | bytes 110600 | tf_op jit(solution)/shard_map/ppermute | solution.py:399
  12.5 5.0 %collective-permute-start.7 = (bf16[144,128]{1,0:T(8,128)(2,1)}, bf16[144,128]{1,0:T(8,128)(2,1)S(1)}, u32[]{:S(2)}, u32[]{:S(2)}) collective-permute-start(bf16[144,128]{1,0:T(8,128)(2,1)} %bitcast.17), channel_id=1, source_target_pairs={{0,4},{2,6},{4,0},{6,2},{8,12},{10,14},{12,8},{14,10},{1,5},{3,7},... | collective-permute-start | bytes 110600 | tf_op jit(solution)/shard_map/ppermute | solution.py:399
  13.3 0.9 %copy-start.2 = (bf16[128,512]{1,0:T(8,128)(2,1)S(1)}, bf16[128,512]{1,0:T(8,128)(2,1)}, u32[]{:S(2)}) copy-start(bf16[128,512]{1,0:T(8,128)(2,1)} %proj_weight.1) | copy-start | bytes 393220
  13.3 4.8 %collective-permute-start.4 = (bf16[432,128]{1,0:T(8,128)(2,1)S(1)}, bf16[432,128]{1,0:T(8,128)(2,1)S(1)}, u32[]{:S(2)}, u32[]{:S(2)}) collective-permute-start(bf16[432,128]{1,0:T(8,128)(2,1)S(1)} %pad_maximum_fusion.3.refs_1_), channel_id=1, source_target_pairs={{0,2},{2,0},{4,6},{6,4},{8,10},{10,8},{12,14},{14,12},{1,3},{3,1},... | collective-permute-start | bytes 331784 | tf_op jit(solution)/shard_map/ppermute | solution.py:399
  14.0 4.2 %collective-permute-start.5 = (bf16[576,128]{1,0:T(8,128)(2,1)S(1)}, bf16[576,128]{1,0:T(8,128)(2,1)S(1)}, u32[]{:S(2)}, u32[]{:S(2)}) collective-permute-start(bf16[576,128]{1,0:T(8,128)(2,1)S(1)} %pad_maximum_fusion.1), channel_id=1, source_target_pairs={{0,1},{1,0},{2,3},{3,2},{4,5},{5,4},{6,7},{7,6},{8,9},{9,8},{10,11... | collective-permute-start | bytes 442376 | tf_op jit(solution)/shard_map/ppermute | solution.py:402
  18.1 0.8 %copy-start.4 = (bf16[6,24,128]{2,1,0:T(8,128)(2,1)S(1)}, bf16[6,24,128]{2,1,0:T(8,128)(2,1)}, u32[]{:S(2)}) copy-start(bf16[6,24,128]{2,1,0:T(8,128)(2,1)} %param.10) | copy-start | bytes 110596
  18.8 1.4 %collective-permute-start.6 = (bf16[576,128]{1,0:T(8,128)(2,1)S(1)}, bf16[576,128]{1,0:T(8,128)(2,1)S(1)}, u32[]{:S(2)}, u32[]{:S(2)}) collective-permute-start(bf16[576,128]{1,0:T(8,128)(2,1)S(1)} %pad_maximum_fusion.refs_0_), channel_id=1, source_target_pairs={{0,1},{1,0},{2,3},{3,2},{4,5},{5,4},{6,7},{7,6},{8,9},{9,8},{10,11... | collective-permute-start | bytes 442376 | tf_op jit(solution)/shard_map/ppermute | solution.py:402
  18.9 6.3 %collective-permute-start.10 = (bf16[576,128]{1,0:T(8,128)(2,1)S(1)}, bf16[576,128]{1,0:T(8,128)(2,1)S(1)}, u32[]{:S(2)}, u32[]{:S(2)}) collective-permute-start(bf16[576,128]{1,0:T(8,128)(2,1)S(1)} %pad_maximum_fusion.2.refs_0_), channel_id=1, source_target_pairs={{0,2},{2,0},{4,6},{6,4},{8,10},{10,8},{12,14},{14,12},{1,3},{3,1},... | collective-permute-start | bytes 442376 | tf_op jit(solution)/shard_map/ppermute | solution.py:399
  20.9 4.3 %copy-start.1 = (bf16[128,128]{1,0:T(8,128)(2,1)S(1)}, bf16[128,128]{1,0:T(8,128)(2,1)}, u32[]{:S(2)}) copy-start(bf16[128,128]{1,0:T(8,128)(2,1)} %gate_weight.3) | copy-start | bytes 98308
  20.9 4.3 %copy-start.3 = (bf16[128,128]{1,0:T(8,128)(2,1)S(1)}, bf16[128,128]{1,0:T(8,128)(2,1)}, u32[]{:S(2)}) copy-start(bf16[128,128]{1,0:T(8,128)(2,1)} %out_weight.1) | copy-start | bytes 98308
  27.3 3.3 %collective-permute-start.11 = (bf16[1152,128]{1,0:T(8,128)(2,1)S(1)}, bf16[1152,128]{1,0:T(8,128)(2,1)S(1)}, u32[]{:S(2)}, u32[]{:S(2)}) collective-permute-start(bf16[1152,128]{1,0:T(8,128)(2,1)S(1)} %get-tuple-element.59.d_tri_ref), channel_id=1, source_target_pairs={{0,1},{1,0},{2,3},{3,2},{4,5},{5,4},{6,7},{7,6},{8,9},{9,8},{10,11... | collective-permute-start | bytes 884744 | tf_op jit(solution)/shard_map/ppermute | solution.py:402
  30.0 4.3 %collective-permute-start.13 = (f32[128,256]{1,0:T(8,128)S(1)}, f32[128,256]{1,0:T(8,128)S(1)}, u32[]{:S(2)}, u32[]{:S(2)}) collective-permute-start(f32[128,256]{1,0:T(8,128)S(1)} %get-tuple-element.78), channel_id=1, source_target_pairs={{0,1},{1,0},{2,3},{3,2},{4,5},{5,4},{6,7},{7,6},{8,9},{9,8},{10,11... | collective-permute-start | bytes 393224 | tf_op jit(solution)/shard_map/ppermute | solution.py:402
  34.2 1.5 %collective-permute-start.12 = (f32[128,512]{1,0:T(8,128)S(1)}, f32[128,512]{1,0:T(8,128)S(1)}, u32[]{:S(2)}, u32[]{:S(2)}) collective-permute-start(f32[128,512]{1,0:T(8,128)S(1)} %get-tuple-element.77), channel_id=1, source_target_pairs={{0,1},{1,0},{2,3},{3,2},{4,5},{5,4},{6,7},{7,6},{8,9},{9,8},{10,11... | collective-permute-start | bytes 786440 | tf_op jit(solution)/shard_map/ppermute | solution.py:402

commit v5 on v4

--- a/solution.py
+++ b/solution.py
@@ -152,7 +152,7 @@
     gain, bias = params[2:3, :], params[3:4, :]
     for which, normed in ((0, normed_0), (1, normed_1)):
         for t, b in enumerate(places(groups)):
-            cot = cots[which][t * cells : (t + 1) * cells, :]
+            cot = cots[t][which * cells : (which + 1) * cells, :]
             place = at(row_block(which, b), cells)
             tri_f, hat, inverse = layer_norm(tri[place, :], gain, bias)
             tri_norm = tri_f.astype(BF16)
@@ -385,7 +385,7 @@
     sizes = (rows, cols, groups)
 
     def call(kernel, outs, *args, scratch=(), micros=1, name):
-        cost = pl.CostEstimate(flops=micros * 10**8, bytes_accessed=0, transcendentals=0)
+        cost = pl.CostEstimate(flops=micros * 10**10, bytes_accessed=0, transcendentals=0)
         return pl.pallas_call(
             functools.partial(kernel, sizes),
             out_shape=[jax.ShapeDtypeStruct(*out) for out in outs],
@@ -401,11 +401,11 @@
     def over(value):
         return lax.ppermute(value, "col", SWAP)
 
-    def along(value):
+    def along(value, tied=False):
         got = []
         for s in reversed(range(1, groups // 2)):
             arrived = across(value, 2 * s)
-            got.append(after(arrived, got[-1]) if got else arrived)
+            got.append(after(arrived, got[-1]) if got and tied else arrived)
         return got[::-1]
 
     def join(*values):
@@ -418,24 +418,26 @@
 
     def own_edges(*blocks):
         outs = [((some, channels), BF16)] + [(part, F32)] * 6
-        return call(own_edges_kernel, outs, params, proj_weight, *blocks, micros=7, name="own_edges")
+        return call(own_edges_kernel, outs, params, proj_weight, *blocks, name="own_edges")
 
     def mate_edges(*blocks):
         outs = [(part, F32)] * 2
-        return call(mate_edges_kernel, outs, params, proj_weight, *blocks, micros=7, name="mate_edges")
+        return call(mate_edges_kernel, outs, params, proj_weight, *blocks, name="mate_edges")
 
     pair = pair_rep.reshape(cells, channels)
     cot = cotangent.reshape(cells, channels)
     params = jnp.stack([norm_gain, norm_bias, tri_gain, tri_bias])
-    near = along(pair)
+    near = along(pair, tied=True)
     pair_far = across(pair, 1)
-    near_all = after(join(*near), params, pair_far)
+    cot_far = across(cot, 1)
+    near_all = after(join(*near), params, pair_far, cot_far)
     far = across(near_all, 1)
+    mate_near = over(join(pair, near_all))
+    cots = after(join(cot, cot_far), near_all)
     own_0 = own_edges(pair, near_all)
-    mate_0 = mate_edges(over(join(pair, near_all)))
-    cot_near = join(cot, *along(cot))
-    cot_far = across(cot_near, 1)
+    mate_0 = mate_edges(mate_near)
     far_all = after(join(pair_far, far), own_0[0], mate_0[0])
+    cots = [cots] + along(cots)
     own_1 = own_edges(far_all)
     mate_1 = mate_edges(over(far_all))
     own, mate = (own_0, own_1), (mate_0, mate_1)
@@ -461,8 +463,7 @@
         *normed,
         gate_weight,
         out_weight,
-        cot_near,
-        cot_far,
+        *cots,
         micros=2,
         name="cells",
     )

time: 36.7 us -> 35.3 us (0.962)
  waiting for transfers between devices: 6 us -> 5.03 us
  starting transfers between devices: 14 us -> 13.6 us
    ppermute x9, waiting for transfers between devices: 5.18 us -> 3.05 us  [across(): return lax.ppermute(value, 'row', [(i, i ^ mask) for i in range(groups)])]
    ppermute x5, waiting for transfers between devices: 0.82 us -> 1.98 us  [over(): return lax.ppermute(value, 'col', SWAP)]
    ppermute x9, starting transfers between devices: 13.2 us -> 12.7 us  [across(): return lax.ppermute(value, 'row', [(i, i ^ mask) for i in range(groups)])]
  transfers between devices with their start and end apart: 14 -> 14, of which waited for: 4 -> 5; matrix products, arithmetic and copies ran while one was open for 2% -> 2% of each run, Pallas kernels for 29% -> 32%
where the time goes in v5:
time: 35.3 us; the launch traced here: 35.1 us
  starting transfers between devices  13.6 us (39%)
  Pallas kernels  13.4 us (38%)
  waiting for transfers between devices  5.03 us (14%)
  local copies, waits for them, and re-layouts  1.39 us (4%)
  between operations  0.82 us (2%)
  other arithmetic  0.8 us (2%)
    pallas_call x8, Pallas kernels, call(): pl.pallas_call(functools.partial(kernel, sizes), out_shape=[jax.ShapeDtyp...  13.4 us
    ppermute x9, starting transfers between devices, across(): return lax.ppermute(value, 'row', [(i, i ^ mask) for i in range(groups)])  12.7 us
    ppermute x9, waiting for transfers between devices, across(): return lax.ppermute(value, 'row', [(i, i ^ mask) for i in range(groups)])  3.05 us
    ppermute x5, waiting for transfers between devices, over(): return lax.ppermute(value, 'col', SWAP)  1.98 us
    ppermute x5, starting transfers between devices, over(): return lax.ppermute(value, 'col', SWAP)  0.94 us
    add x1, other arithmetic, replicated(): proj_grad + over(proj_grad)  0.74 us
    unnamed x18, local copies, waits for them, and re-layouts  0.73 us
  transfers between devices with their start and end apart: 14, of which 5 were waited for; matrix products, arithmetic and copies ran while one was open for 2% of the time, Pallas kernels for 32%

profile of v5, /device:TPU:0, one launch (start us, length us, event | category | flops | bytes accessed | tf_op | source)
XLA Modules:
  0.0 35.1 jit_solution(7478041851655509322)
XLA Ops:
  0.6 5.1 %collective-permute-start.2 = (bf16[144,128]{1,0:T(8,128)(2,1)}, bf16[144,128]{1,0:T(8,128)(2,1)S(1)}, u32[]{:S(2)}, u32[]{:S(2)}) collective-permute-start(bf16[144,128]{1,0:T(8,128)(2,1)} %bitcast.8), channel_id=1, source_target_pairs={{0,12},{2,14},{4,8},{6,10},{8,4},{10,6},{12,0},{14,2},{1,13},{3,15... | collective-permute-start | bytes 110600 | tf_op jit(solution)/shard_map/ppermute | solution.py:399
  5.8 0.6 %collective-permute-start = (bf16[144,128]{1,0:T(8,128)(2,1)}, bf16[144,128]{1,0:T(8,128)(2,1)S(1)}, u32[]{:S(2)}, u32[]{:S(2)}) collective-permute-start(bf16[144,128]{1,0:T(8,128)(2,1)} %bitcast.10), channel_id=1, source_target_pairs={{0,4},{2,6},{4,0},{6,2},{8,12},{10,14},{12,8},{14,10},{1,5},{3,7},... | collective-permute-start | bytes 110600 | tf_op jit(solution)/shard_map/ppermute | solution.py:399
  6.4 1.7 %collective-permute-start.3 = (bf16[144,128]{1,0:T(8,128)(2,1)}, bf16[144,128]{1,0:T(8,128)(2,1)S(1)}, u32[]{:S(2)}, u32[]{:S(2)}) collective-permute-start(bf16[144,128]{1,0:T(8,128)(2,1)} %bitcast.11), channel_id=1, source_target_pairs={{0,2},{2,0},{4,6},{6,4},{8,10},{10,8},{12,14},{14,12},{1,3},{3,1},... | collective-permute-start | bytes 110600 | tf_op jit(solution)/shard_map/ppermute | solution.py:399
  8.1 0.4 %collective-permute-start.4 = (bf16[144,128]{1,0:T(8,128)(2,1)}, bf16[144,128]{1,0:T(8,128)(2,1)S(1)}, u32[]{:S(2)}, u32[]{:S(2)}) collective-permute-start(bf16[144,128]{1,0:T(8,128)(2,1)} %bitcast.15), channel_id=1, source_target_pairs={{0,2},{2,0},{4,6},{6,4},{8,10},{10,8},{12,14},{14,12},{1,3},{3,1},... | collective-permute-start | bytes 110600 | tf_op jit(solution)/shard_map/ppermute | solution.py:399
  8.4 0.6 %copy-done.8 = f32[128]{0:T(128)S(1)} copy-done((f32[128]{0:T(128)S(1)}, f32[128]{0:T(128)}, u32[]{:S(2)}) %copy-start.8) | copy-done | bytes 536
  9.1 0.0 copy-done.5
  9.1 0.0 copy-done.6
  9.1 0.0 copy-done.7
  9.2 1.7 %collective-permute-done.1 = bf16[144,128]{1,0:T(8,128)(2,1)S(1)} collective-permute-done((bf16[144,128]{1,0:T(8,128)(2,1)}, bf16[144,128]{1,0:T(8,128)(2,1)S(1)}, u32[]{:S(2)}, u32[]{:S(2)}) %collective-permute-start.1) | collective-permute-done | bytes 36896 | tf_op jit(solution)/shard_map/ppermute | solution.py:399
  10.9 1.4 %collective-permute-done.4 = bf16[144,128]{1,0:T(8,128)(2,1)S(1)} collective-permute-done((bf16[144,128]{1,0:T(8,128)(2,1)}, bf16[144,128]{1,0:T(8,128)(2,1)S(1)}, u32[]{:S(2)}, u32[]{:S(2)}) %collective-permute-start.4) | collective-permute-done | bytes 36896 | tf_op jit(solution)/shard_map/ppermute | solution.py:399
  12.3 0.5 %collective-permute-start.5 = (bf16[432,128]{1,0:T(8,128)(2,1)S(1)}, bf16[432,128]{1,0:T(8,128)(2,1)S(1)}, u32[]{:S(2)}, u32[]{:S(2)}) collective-permute-start(bf16[432,128]{1,0:T(8,128)(2,1)S(1)} %pad_maximum_fusion.2.refs_1_), channel_id=1, source_target_pairs={{0,2},{2,0},{4,6},{6,4},{8,10},{10,8},{12,14},{14,12},{1,3},{3,1},... | collective-permute-start | bytes 331784 | tf_op jit(solution)/shard_map/ppermute | solution.py:399
  12.7 3.8 %collective-permute-start.10 = (bf16[288,128]{1,0:T(8,128)(2,1)S(1)}, bf16[288,128]{1,0:T(8,128)(2,1)S(1)}, u32[]{:S(2)}, u32[]{:S(2)}) collective-permute-start(bf16[288,128]{1,0:T(8,128)(2,1)S(1)} %pad_maximum_fusion.3.refs_0_), channel_id=1, source_target_pairs={{0,12},{2,14},{4,8},{6,10},{8,4},{10,6},{12,0},{14,2},{1,13},{3,15... | collective-permute-start | bytes 221192 | tf_op jit(solution)/shard_map/ppermute | solution.py:399
  16.5 0.7 %collective-permute-start.9 = (bf16[288,128]{1,0:T(8,128)(2,1)S(1)}, bf16[288,128]{1,0:T(8,128)(2,1)S(1)}, u32[]{:S(2)}, u32[]{:S(2)}) collective-permute-start(bf16[288,128]{1,0:T(8,128)(2,1)S(1)} %pad_maximum_fusion.3.refs_0_), channel_id=1, source_target_pairs={{0,8},{2,10},{4,12},{6,14},{8,0},{10,2},{12,4},{14,6},{1,9},{3,11}... | collective-permute-start | bytes 221192 | tf_op jit(solution)/shard_map/ppermute | solution.py:399
  17.2 0.6 %own_edges.2 = (bf16[576,128]{1,0:T(8,128)(2,1)S(1)}, f32[576,128]{1,0:T(8,128)S(1)}, f32[576,128]{1,0:T(8,128)S(1)}, f32[576,128]{1,0:T(8,128)S(1)}, f32[576,12...) custom-call(f32[4,128]{1,0:T(4,128)S(1)} %pad_maximum_fusion.4.params, ...), custom_call_target="tpu_custom_call" | custom-call | flops 10000000000 | tf_op jit(solution)/shard_map/own_edges/pallas_call | solution.py:389
  17.9 0.7 %collective-permute-done.6.refs_0_ = bf16[576,128]{1,0:T(8,128)(2,1)S(1)} collective-permute-done((bf16[576,128]{1,0:T(8,128)(2,1)S(1)}, bf16[576,128]{1,0:T(8,128)(2,1)S(1)}, u32[]{:S(2)}, u32[]{:S(2)}) %collective-permute-start.6) | collective-permute-done | bytes 147488 | tf_op jit(solution)/shard_map/ppermute | solution.py:402
  18.6 0.6 %mate_edges.2 = (f32[576,128]{1,0:T(8,128)S(1)}, f32[576,128]{1,0:T(8,128)S(1)}) custom-call(f32[4,128]{1,0:T(4,128)S(1)} %pad_maximum_fusion.4.params, bf16[128,512]{1,0:T(8,128)(2,1)S(1)} %copy-done.1, bf16[576,128]{1,0:T(8,128)(2,1)S(1)} %collective-permute-done.6.refs_0_), custom_call_target="tpu_custom_call" | custom-call | flops 10000000000 | tf_op jit(solution)/shard_map/mate_edges/pallas_call | solution.py:389
  19.2 0.2 collective-permute-start.7
  19.4 0.6 %own_edges.3 = (bf16[576,128]{1,0:T(8,128)(2,1)S(1)}, f32[576,128]{1,0:T(8,128)S(1)}, f32[576,128]{1,0:T(8,128)S(1)}, f32[576,128]{1,0:T(8,128)S(1)}, f32[576,12...) custom-call(f32[4,128]{1,0:T(4,128)S(1)} %pad_maximum_fusion.4.params, ...), custom_call_target="tpu_custom_call" | custom-call | flops 10000000000 | tf_op jit(solution)/shard_map/own_edges/pallas_call | solution.py:389
  20.0 0.6 %collective-permute-done.7.refs_0_ = bf16[576,128]{1,0:T(8,128)(2,1)S(1)} collective-permute-done((bf16[576,128]{1,0:T(8,128)(2,1)S(1)}, bf16[576,128]{1,0:T(8,128)(2,1)S(1)}, u32[]{:S(2)}, u32[]{:S(2)}) %collective-permute-start.7) | collective-permute-done | bytes 147488 | tf_op jit(solution)/shard_map/ppermute | solution.py:402
  20.6 0.6 %mate_edges.3 = (f32[576,128]{1,0:T(8,128)S(1)}, f32[576,128]{1,0:T(8,128)S(1)}) custom-call(f32[4,128]{1,0:T(4,128)S(1)} %pad_maximum_fusion.4.params, bf16[128,512]{1,0:T(8,128)(2,1)S(1)} %copy-done.1, bf16[576,128]{1,0:T(8,128)(2,1)S(1)} %collective-permute-done.7.refs_0_), custom_call_target="tpu_custom_call" | custom-call | flops 10000000000 | tf_op jit(solution)/shard_map/mate_edges/pallas_call | solution.py:389
  21.3 0.0 copy-start.2
  21.3 0.0 copy-start.3
  21.3 2.4 %triangle.1.tri = f32[1152,128]{1,0:T(8,128)S(1)} custom-call(f32[576,128]{1,0:T(8,128)S(1)} %get-tuple-element.44.refs_0_.left_0, f32[576,128]{1,0:T(8,128)S(1)} %get-tuple-element.48.refs_1_.left_1, f32[576,128]{1,0:T(8,128)S(1)} %get-tuple-element.46.refs_2_, f32[576,128]{1,0:T(8,128)S(1)} %get-tuple-element.49.refs_3_, ...), custom_call_target="tpu_custom_call" | custom-call | flops 20000000000 | tf_op jit(solution)/shard_map/triangle/pallas_call | solution.py:389
  23.7 2.1 %cells.1 = (bf16[144,128]{1,0:T(8,128)(2,1)}, bf16[1152,128]{1,0:T(8,128)(2,1)S(1)}, bf16[1152,128]{1,0:T(8,128)(2,1)S(1)}, bf16[1152,128]{1,0:T(8,128)(2,1)S(1)}, bf16[1152,128]{1,0:T(8,128)(2,1)S(1)}) custom-call(f32[4,128]{1,0:T(4,128)S(1)} %pad_maximum_fusion.4.params, f32[1152,128]{1,0:T(8,128)S(1)} %triangle.1.tri, ...), custom_call_target="tpu_custom_call" | custom-call | flops 20000000000 | tf_op jit(solution)/shard_map/cells/pallas_call | solution.py:389
  25.9 0.1 collective-permute-start.11
  26.0 2.7 %early.1 = (f32[1152,128]{1,0:T(8,128)S(1)}, f32[1152,128]{1,0:T(8,128)S(1)}, bf16[1152,128]{1,0:T(8,128)(2,1)S(1)}, f32[1152,128]{1,0:T(8,128)S(1)}, f32[576,128]{1,0:T(8,128)S(1)}, /*index=5*/f32[128,256]{1,0:T(8,128)S(1)}) custom-call(bf16[1152,128]{1,0:T(8,128)(2,1)S(1)} %get-tuple-element.57.d_tri_ref, bf16[1152,128]{1,0:T(8,128)(2,1)S(1)} %get-tuple-element.58.d_gate, ...), custom_call_target="tpu_custom_call" | custom-call | flops 30000001024 | tf_op jit(solution)/shard_map/early/pallas_call | solution.py:389
  28.7 0.4 %collective-permute-start.13 = (f32[128,256]{1,0:T(8,128)S(1)}, f32[128,256]{1,0:T(8,128)S(1)}, u32[]{:S(2)}, u32[]{:S(2)}) collective-permute-start(f32[128,256]{1,0:T(8,128)S(1)} %get-tuple-element.76), channel_id=1, source_target_pairs={{0,1},{1,0},{2,3},{3,2},{4,5},{5,4},{6,7},{7,6},{8,9},{9,8},{10,11... | collective-permute-start | bytes 393224 | tf_op jit(solution)/shard_map/ppermute | solution.py:402
  29.1 3.7 %late.1 = (f32[144,128]{1,0:T(8,128)}, f32[128,512]{1,0:T(8,128)S(1)}) custom-call(f32[4,128]{1,0:T(4,128)S(1)} %pad_maximum_fusion.4.params, bf16[144,128]{1,0:T(8,128)(2,1)S(1)} %bitcast.14, bf16[1152,128]{1,0:T(8,128)(2,1)S(1)} %collective-permute-done.11.d_tri_ref, bf16[1152,128]{1,0:T(8,128)(2,1)S(1)} %get-tuple-element.58.d_gate, ...), custom_call_target="tpu_custom_call" | custom-call | flops 40000000000 | tf_op jit(solution)/shard_map/late/pallas_call | solution.py:389
  32.8 0.1 collective-permute-start.12
  33.0 0.7 %fusion = (f32[128,128]{1,0:T(8,128)}, f32[128,128]{1,0:T(8,128)}) fusion(f32[128,256]{1,0:T(8,128)S(1)} %add.7), kind=kLoop, calls=%fused_computation.5 | loop fusion | bytes 262144 | tf_op jit(solution)/shard_map/slice | solution.py:521
  33.6 0.7 %collective-permute-done.12 = f32[128,512]{1,0:T(8,128)S(1)} collective-permute-done((f32[128,512]{1,0:T(8,128)S(1)}, f32[128,512]{1,0:T(8,128)S(1)}, u32[]{:S(2)}, u32[]{:S(2)}) %collective-permute-start.12) | collective-permute-done | bytes 262176 | tf_op jit(solution)/shard_map/ppermute | solution.py:402
  34.4 0.7 %add.6 = f32[128,512]{1,0:T(8,128)} add(f32[128,512]{1,0:T(8,128)S(1)} %get-tuple-element.75, f32[128,512]{1,0:T(8,128)S(1)} %collective-permute-done.12) | non-fusion elementwise | flops 65536 | bytes 786432 | tf_op jit(solution)/shard_map/add | solution.py:519
  (30 shorter events, 0.1 us)
Async XLA Ops:
  0.6 8.5 %collective-permute-start.2 = (bf16[144,128]{1,0:T(8,128)(2,1)}, bf16[144,128]{1,0:T(8,128)(2,1)S(1)}, u32[]{:S(2)}, u32[]{:S(2)}) collective-permute-start(bf16[144,128]{1,0:T(8,128)(2,1)} %bitcast.8), channel_id=1, source_target_pairs={{0,12},{2,14},{4,8},{6,10},{8,4},{10,6},{12,0},{14,2},{1,13},{3,15... | collective-permute-start | bytes 110600 | tf_op jit(solution)/shard_map/ppermute | solution.py:399
  5.7 5.1 %collective-permute-start.1 = (bf16[144,128]{1,0:T(8,128)(2,1)}, bf16[144,128]{1,0:T(8,128)(2,1)S(1)}, u32[]{:S(2)}, u32[]{:S(2)}) collective-permute-start(bf16[144,128]{1,0:T(8,128)(2,1)} %bitcast.9), channel_id=1, source_target_pairs={{0,8},{2,10},{4,12},{6,14},{8,0},{10,2},{12,4},{14,6},{1,9},{3,11}... | collective-permute-start | bytes 110600 | tf_op jit(solution)/shard_map/ppermute | solution.py:399
  5.8 5.1 %collective-permute-start = (bf16[144,128]{1,0:T(8,128)(2,1)}, bf16[144,128]{1,0:T(8,128)(2,1)S(1)}, u32[]{:S(2)}, u32[]{:S(2)}) collective-permute-start(bf16[144,128]{1,0:T(8,128)(2,1)} %bitcast.10), channel_id=1, source_target_pairs={{0,4},{2,6},{4,0},{6,2},{8,12},{10,14},{12,8},{14,10},{1,5},{3,7},... | collective-permute-start | bytes 110600 | tf_op jit(solution)/shard_map/ppermute | solution.py:399
  6.4 4.5 %collective-permute-start.3 = (bf16[144,128]{1,0:T(8,128)(2,1)}, bf16[144,128]{1,0:T(8,128)(2,1)S(1)}, u32[]{:S(2)}, u32[]{:S(2)}) collective-permute-start(bf16[144,128]{1,0:T(8,128)(2,1)} %bitcast.11), channel_id=1, source_target_pairs={{0,2},{2,0},{4,6},{6,4},{8,10},{10,8},{12,14},{14,12},{1,3},{3,1},... | collective-permute-start | bytes 110600 | tf_op jit(solution)/shard_map/ppermute | solution.py:399
  8.1 4.2 %collective-permute-start.4 = (bf16[144,128]{1,0:T(8,128)(2,1)}, bf16[144,128]{1,0:T(8,128)(2,1)S(1)}, u32[]{:S(2)}, u32[]{:S(2)}) collective-permute-start(bf16[144,128]{1,0:T(8,128)(2,1)} %bitcast.15), channel_id=1, source_target_pairs={{0,2},{2,0},{4,6},{6,4},{8,10},{10,8},{12,14},{14,12},{1,3},{3,1},... | collective-permute-start | bytes 110600 | tf_op jit(solution)/shard_map/ppermute | solution.py:399
  8.4 0.7 %copy-start.8 = (f32[128]{0:T(128)S(1)}, f32[128]{0:T(128)}, u32[]{:S(2)}) copy-start(f32[128]{0:T(128)} %param.11) | copy-start | bytes 1540
  8.4 0.7 %copy-start.5 = (f32[128]{0:T(128)S(1)}, f32[128]{0:T(128)}, u32[]{:S(2)}) copy-start(f32[128]{0:T(128)} %param.16) | copy-start | bytes 1540
  8.4 0.7 %copy-start.6 = (f32[128]{0:T(128)S(1)}, f32[128]{0:T(128)}, u32[]{:S(2)}) copy-start(f32[128]{0:T(128)} %param.15) | copy-start | bytes 1540
  8.4 0.7 %copy-start.7 = (f32[128]{0:T(128)S(1)}, f32[128]{0:T(128)}, u32[]{:S(2)}) copy-start(f32[128]{0:T(128)} %param.12) | copy-start | bytes 1540
  9.1 3.1 %copy-start = (bf16[6,24,128]{2,1,0:T(8,128)(2,1)S(1)}, bf16[6,24,128]{2,1,0:T(8,128)(2,1)}, u32[]{:S(2)}) copy-start(bf16[6,24,128]{2,1,0:T(8,128)(2,1)} %param.9) | copy-start | bytes 110596
  10.8 1.9 %copy-start.4 = (bf16[6,24,128]{2,1,0:T(8,128)(2,1)S(1)}, bf16[6,24,128]{2,1,0:T(8,128)(2,1)}, u32[]{:S(2)}) copy-start(bf16[6,24,128]{2,1,0:T(8,128)(2,1)} %param.10) | copy-start | bytes 110596
  12.2 4.9 %copy-start.1 = (bf16[128,512]{1,0:T(8,128)(2,1)S(1)}, bf16[128,512]{1,0:T(8,128)(2,1)}, u32[]{:S(2)}) copy-start(bf16[128,512]{1,0:T(8,128)(2,1)} %proj_weight.1) | copy-start | bytes 393220
  12.3 5.6 %collective-permute-start.5 = (bf16[432,128]{1,0:T(8,128)(2,1)S(1)}, bf16[432,128]{1,0:T(8,128)(2,1)S(1)}, u32[]{:S(2)}, u32[]{:S(2)}) collective-permute-start(bf16[432,128]{1,0:T(8,128)(2,1)S(1)} %pad_maximum_fusion.2.refs_1_), channel_id=1, source_target_pairs={{0,2},{2,0},{4,6},{6,4},{8,10},{10,8},{12,14},{14,12},{1,3},{3,1},... | collective-permute-start | bytes 331784 | tf_op jit(solution)/shard_map/ppermute | solution.py:399
  12.7 11.0 %collective-permute-start.10 = (bf16[288,128]{1,0:T(8,128)(2,1)S(1)}, bf16[288,128]{1,0:T(8,128)(2,1)S(1)}, u32[]{:S(2)}, u32[]{:S(2)}) collective-permute-start(bf16[288,128]{1,0:T(8,128)(2,1)S(1)} %pad_maximum_fusion.3.refs_0_), channel_id=1, source_target_pairs={{0,12},{2,14},{4,8},{6,10},{8,4},{10,6},{12,0},{14,2},{1,13},{3,15... | collective-permute-start | bytes 221192 | tf_op jit(solution)/shard_map/ppermute | solution.py:399
  16.5 7.2 %collective-permute-start.8 = (bf16[288,128]{1,0:T(8,128)(2,1)S(1)}, bf16[288,128]{1,0:T(8,128)(2,1)S(1)}, u32[]{:S(2)}, u32[]{:S(2)}) collective-permute-start(bf16[288,128]{1,0:T(8,128)(2,1)S(1)} %pad_maximum_fusion.3.refs_0_), channel_id=1, source_target_pairs={{0,4},{2,6},{4,0},{6,2},{8,12},{10,14},{12,8},{14,10},{1,5},{3,7},... | collective-permute-start | bytes 221192 | tf_op jit(solution)/shard_map/ppermute | solution.py:399
  16.5 7.2 %collective-permute-start.9 = (bf16[288,128]{1,0:T(8,128)(2,1)S(1)}, bf16[288,128]{1,0:T(8,128)(2,1)S(1)}, u32[]{:S(2)}, u32[]{:S(2)}) collective-permute-start(bf16[288,128]{1,0:T(8,128)(2,1)S(1)} %pad_maximum_fusion.3.refs_0_), channel_id=1, source_target_pairs={{0,8},{2,10},{4,12},{6,14},{8,0},{10,2},{12,4},{14,6},{1,9},{3,11}... | collective-permute-start | bytes 221192 | tf_op jit(solution)/shard_map/ppermute | solution.py:399
  17.2 1.4 %collective-permute-start.6 = (bf16[576,128]{1,0:T(8,128)(2,1)S(1)}, bf16[576,128]{1,0:T(8,128)(2,1)S(1)}, u32[]{:S(2)}, u32[]{:S(2)}) collective-permute-start(bf16[576,128]{1,0:T(8,128)(2,1)S(1)} %pad_maximum_fusion.1), channel_id=1, source_target_pairs={{0,1},{1,0},{2,3},{3,2},{4,5},{5,4},{6,7},{7,6},{8,9},{9,8},{10,11... | collective-permute-start | bytes 442376 | tf_op jit(solution)/shard_map/ppermute | solution.py:402
  19.2 1.4 %collective-permute-start.7 = (bf16[576,128]{1,0:T(8,128)(2,1)S(1)}, bf16[576,128]{1,0:T(8,128)(2,1)S(1)}, u32[]{:S(2)}, u32[]{:S(2)}) collective-permute-start(bf16[576,128]{1,0:T(8,128)(2,1)S(1)} %pad_maximum_fusion.refs_0_), channel_id=1, source_target_pairs={{0,1},{1,0},{2,3},{3,2},{4,5},{5,4},{6,7},{7,6},{8,9},{9,8},{10,11... | collective-permute-start | bytes 442376 | tf_op jit(solution)/shard_map/ppermute | solution.py:402
  21.3 2.5 %copy-start.2 = (bf16[128,128]{1,0:T(8,128)(2,1)S(1)}, bf16[128,128]{1,0:T(8,128)(2,1)}, u32[]{:S(2)}) copy-start(bf16[128,128]{1,0:T(8,128)(2,1)} %out_weight.1) | copy-start | bytes 98308
  21.3 2.5 %copy-start.3 = (bf16[128,128]{1,0:T(8,128)(2,1)S(1)}, bf16[128,128]{1,0:T(8,128)(2,1)}, u32[]{:S(2)}) copy-start(bf16[128,128]{1,0:T(8,128)(2,1)} %gate_weight.3) | copy-start | bytes 98308
  25.9 3.3 %collective-permute-start.11 = (bf16[1152,128]{1,0:T(8,128)(2,1)S(1)}, bf16[1152,128]{1,0:T(8,128)(2,1)S(1)}, u32[]{:S(2)}, u32[]{:S(2)}) collective-permute-start(bf16[1152,128]{1,0:T(8,128)(2,1)S(1)} %get-tuple-element.57.d_tri_ref), channel_id=1, source_target_pairs={{0,1},{1,0},{2,3},{3,2},{4,5},{5,4},{6,7},{7,6},{8,9},{9,8},{10,11... | collective-permute-start | bytes 884744 | tf_op jit(solution)/shard_map/ppermute | solution.py:402
  28.7 4.3 %collective-permute-start.13 = (f32[128,256]{1,0:T(8,128)S(1)}, f32[128,256]{1,0:T(8,128)S(1)}, u32[]{:S(2)}, u32[]{:S(2)}) collective-permute-start(f32[128,256]{1,0:T(8,128)S(1)} %get-tuple-element.76), channel_id=1, source_target_pairs={{0,1},{1,0},{2,3},{3,2},{4,5},{5,4},{6,7},{7,6},{8,9},{9,8},{10,11... | collective-permute-start | bytes 393224 | tf_op jit(solution)/shard_map/ppermute | solution.py:402
  32.8 1.5 %collective-permute-start.12 = (f32[128,512]{1,0:T(8,128)S(1)}, f32[128,512]{1,0:T(8,128)S(1)}, u32[]{:S(2)}, u32[]{:S(2)}) collective-permute-start(f32[128,512]{1,0:T(8,128)S(1)} %get-tuple-element.75), channel_id=1, source_target_pairs={{0,1},{1,0},{2,3},{3,2},{4,5},{5,4},{6,7},{7,6},{8,9},{9,8},{10,11... | collective-permute-start | bytes 786440 | tf_op jit(solution)/shard_map/ppermute | solution.py:402

commit v6 on v5

--- a/solution.py
+++ b/solution.py
@@ -152,7 +152,7 @@
     gain, bias = params[2:3, :], params[3:4, :]
     for which, normed in ((0, normed_0), (1, normed_1)):
         for t, b in enumerate(places(groups)):
-            cot = cots[t][which * cells : (which + 1) * cells, :]
+            cot = cots[which][t * cells : (t + 1) * cells, :]
             place = at(row_block(which, b), cells)
             tri_f, hat, inverse = layer_norm(tri[place, :], gain, bias)
             tri_norm = tri_f.astype(BF16)
@@ -263,10 +263,7 @@
 
 def late_kernel(
     sizes,
-    params,
-    pair,
     d_tri_ref,
-    d_gate,
     left,
     right,
     normed,
@@ -280,19 +277,15 @@
     right_gate_1,
     right_value_0,
     right_value_1,
-    proj_weight,
-    gate_weight,
-    pair_grad,
     proj_grad,
+    d_proj,
     source,
     d_right_s,
-    d_proj,
 ):
     rows, cols, groups = sizes
     cells = rows * cols
     hidden = left.shape[-1]
     half = lax.axis_index("col")
-    me = lax.axis_index("row")
     zeros = (jnp.zeros((8, hidden), F32),) * (rows * cols // 8)
     source[...] = d_tri_ref[...].astype(F32)
     d_right_s[at(half, cols * cols), :] = d_right[...]
@@ -356,13 +349,38 @@
 
     scale = 1.0 / (rows * groups)
     proj_grad[...] = dot(normed[...], d_proj[...], BY_ROWS) * scale
-    own = at(me, cells)
+
+
+def outputs_kernel(
+    sizes,
+    params,
+    pair,
+    d_proj,
+    d_gate,
+    proj_weight,
+    gate_weight,
+    block_in,
+    small_own,
+    small_mate,
+    block_out,
+    pair_grad,
+    gate_grad,
+    out_grad,
+):
+    rows, cols, _ = sizes
+    cells = rows * cols
+    own = at(lax.axis_index("row"), cells)
     d_normed = dot(d_proj[own, :], proj_weight[...], TRANSPOSED) + dot(
         d_gate[own, :], gate_weight[...], TRANSPOSED
     )
     gain = params[0:1, :]
     _, hat, inverse = layer_norm(pair[...].astype(F32), gain, params[1:2, :])
     pair_grad[...] = norm_back(d_normed, gain, hat, inverse)
+    block_out[...] = block_in[...]
+    channels = gate_grad.shape[1]
+    small = small_own[...] + small_mate[...]
+    gate_grad[...] = small[:, :channels]
+    out_grad[...] = small[:, channels:]
 
 
 def replicated(
@@ -385,7 +403,7 @@
     sizes = (rows, cols, groups)
 
     def call(kernel, outs, *args, scratch=(), micros=1, name):
-        cost = pl.CostEstimate(flops=micros * 10**10, bytes_accessed=0, transcendentals=0)
+        cost = pl.CostEstimate(flops=micros * 10**9, bytes_accessed=0, transcendentals=0)
         return pl.pallas_call(
             functools.partial(kernel, sizes),
             out_shape=[jax.ShapeDtypeStruct(*out) for out in outs],
@@ -428,16 +446,15 @@
     cot = cotangent.reshape(cells, channels)
     params = jnp.stack([norm_gain, norm_bias, tri_gain, tri_bias])
     near = along(pair, tied=True)
-    pair_far = across(pair, 1)
-    cot_far = across(cot, 1)
-    near_all = after(join(*near), params, pair_far, cot_far)
+    pair_far = across(after(pair, params), 1)
+    near_all = after(join(*near), params)
     far = across(near_all, 1)
     mate_near = over(join(pair, near_all))
-    cots = after(join(cot, cot_far), near_all)
+    cot_near = join(cot, *along(cot))
+    cot_far = across(cot_near, 1)
     own_0 = own_edges(pair, near_all)
     mate_0 = mate_edges(mate_near)
-    far_all = after(join(pair_far, far), own_0[0], mate_0[0])
-    cots = [cots] + along(cots)
+    far_all = join(pair_far, far)
     own_1 = own_edges(far_all)
     mate_1 = mate_edges(over(far_all))
     own, mate = (own_0, own_1), (mate_0, mate_1)
@@ -463,7 +480,8 @@
         *normed,
         gate_weight,
         out_weight,
-        *cots,
+        cot_near,
+        cot_far,
         micros=2,
         name="cells",
     )
@@ -486,17 +504,14 @@
         *left,
         *right,
         scratch=[(full, F32)],
-        micros=3,
+        micros=30,
         name="early",
     )
     small_mate = over(small_grads)
-    pair_grad, proj_grad = call(
+    proj_grad, d_proj = call(
         late_kernel,
-        [((cells, channels), F32), ((channels, 4 * hidden), F32)],
-        params,
-        pair,
+        [((channels, 4 * hidden), F32), ((every, 4 * hidden), BF16)],
         d_tri_mate,
-        d_gate,
         left_all,
         right_all,
         normed_all,
@@ -506,19 +521,32 @@
         *left_value,
         *right_gate,
         *right_value,
+        scratch=[(full, F32), (full, F32)],
+        micros=40,
+        name="late",
+    )
+    proj_mate = over(proj_grad)
+    square = ((channels, channels), F32)
+    block_out, pair_grad, gate_grad, out_grad = call(
+        outputs_kernel,
+        [((cells, channels), BF16), ((cells, channels), F32), square, square],
+        params,
+        pair,
+        d_proj,
+        d_gate,
         proj_weight,
         gate_weight,
-        scratch=[(full, F32), (full, F32), ((every, 4 * hidden), BF16)],
-        micros=4,
-        name="late",
-    )
-    small = small_grads + small_mate
+        block_out,
+        small_grads,
+        small_mate,
+        name="outputs",
+    )
     return (
         block_out.reshape(pair_rep.shape),
         pair_grad.reshape(pair_rep.shape),
-        proj_grad + over(proj_grad),
-        small[:, :channels],
-        small[:, channels:],
+        proj_grad + proj_mate,
+        gate_grad,
+        out_grad,
     )
 
 

time: 35.3 us -> 35.2 us (level)
  waiting for transfers between devices: 5.03 us -> 1.57 us
  starting transfers between devices: 13.6 us -> 15.4 us
  other arithmetic: 0.8 us -> 2.25 us
    ppermute x9, waiting for transfers between devices: 3.05 us -> 0.28 us  [across(): return lax.ppermute(value, 'row', [(i, i ^ mask) for i in range(groups)])]
    ppermute x9, starting transfers between devices: 12.7 us -> 14.2 us  [across(): return lax.ppermute(value, 'row', [(i, i ^ mask) for i in range(groups)])]
    unnamed x18 -> x15, local copies, waits for them, and re-layouts: 0.73 us -> 1.7 us
    concatenate x4 -> x3, other arithmetic: 0.04 us -> 0.8 us  [join(): return jnp.concatenate(values, axis=0)]
    another operation x1, other arithmetic: 0.01 us -> 0.71 us  [replicated(): params = jnp.stack([norm_gain, norm_bias, tri_gain, tri_bias])]
    ppermute x5, waiting for transfers between devices: 1.98 us -> 1.29 us  [over(): return lax.ppermute(value, 'col', SWAP)]
    slice x1 -> x0, local copies, waits for them, and re-layouts: 0.66 us -> none  [replicated(): small[:, channels:]]
    pallas_call x8 -> x9, Pallas kernels: 13.4 us -> 13.1 us  [call(): pl.pallas_call(functools.partial(kernel, sizes), out_shape=[jax.ShapeDtyp...]
  transfers between devices with their start and end apart: 14 -> 14, of which waited for: 5 -> 3; matrix products, arithmetic and copies ran while one was open for 2% -> 4% of each run, Pallas kernels for 32% -> 25%
where the time goes in v6:
time: 35.2 us; the launch traced here: 34.9 us
  starting transfers between devices  15.4 us (44%)
  Pallas kernels  13.1 us (37%)
  other arithmetic  2.25 us (6%)
  local copies, waits for them, and re-layouts  1.72 us (5%)
  waiting for transfers between devices  1.57 us (4%)
  between operations  0.84 us (2%)
    ppermute x9, starting transfers between devices, across(): return lax.ppermute(value, 'row', [(i, i ^ mask) for i in range(groups)])  14.2 us
    pallas_call x9, Pallas kernels, call(): pl.pallas_call(functools.partial(kernel, sizes), out_shape=[jax.ShapeDtyp...  13.1 us
    unnamed x15, local copies, waits for them, and re-layouts  1.7 us
    ppermute x5, waiting for transfers between devices, over(): return lax.ppermute(value, 'col', SWAP)  1.29 us
    ppermute x5, starting transfers between devices, over(): return lax.ppermute(value, 'col', SWAP)  1.22 us
    concatenate x3, other arithmetic, join(): return jnp.concatenate(values, axis=0)  0.8 us
    add x1, other arithmetic, replicated(): proj_grad + proj_mate  0.74 us
    another operation x1, other arithmetic, replicated(): params = jnp.stack([norm_gain, norm_bias, tri_gain, tri_bias])  0.71 us
  transfers between devices with their start and end apart: 14, of which 3 were waited for; matrix products, arithmetic and copies ran while one was open for 4% of the time, Pallas kernels for 25%

profile of v6, /device:TPU:0, one launch (start us, length us, event | category | flops | bytes accessed | tf_op | source)
XLA Modules:
  0.0 34.9 jit_solution(14589674914989242657)
XLA Ops:
  0.6 5.1 %collective-permute-start.2 = (bf16[144,128]{1,0:T(8,128)(2,1)}, bf16[144,128]{1,0:T(8,128)(2,1)S(1)}, u32[]{:S(2)}, u32[]{:S(2)}) collective-permute-start(bf16[144,128]{1,0:T(8,128)(2,1)} %bitcast.8), channel_id=1, source_target_pairs={{0,12},{2,14},{4,8},{6,10},{8,4},{10,6},{12,0},{14,2},{1,13},{3,15... | collective-permute-start | bytes 110600 | tf_op jit(solution)/shard_map/ppermute | solution.py:417
  5.8 0.6 %collective-permute-start = (bf16[144,128]{1,0:T(8,128)(2,1)}, bf16[144,128]{1,0:T(8,128)(2,1)S(1)}, u32[]{:S(2)}, u32[]{:S(2)}) collective-permute-start(bf16[144,128]{1,0:T(8,128)(2,1)} %bitcast.10), channel_id=1, source_target_pairs={{0,4},{2,6},{4,0},{6,2},{8,12},{10,14},{12,8},{14,10},{1,5},{3,7},... | collective-permute-start | bytes 110600 | tf_op jit(solution)/shard_map/ppermute | solution.py:417
  6.4 1.4 %collective-permute-start.7 = (bf16[144,128]{1,0:T(8,128)(2,1)}, bf16[144,128]{1,0:T(8,128)(2,1)S(1)}, u32[]{:S(2)}, u32[]{:S(2)}) collective-permute-start(bf16[144,128]{1,0:T(8,128)(2,1)} %bitcast.15), channel_id=1, source_target_pairs={{0,4},{2,6},{4,0},{6,2},{8,12},{10,14},{12,8},{14,10},{1,5},{3,7},... | collective-permute-start | bytes 110600 | tf_op jit(solution)/shard_map/ppermute | solution.py:417
  7.8 2.9 %collective-permute-start.8 = (bf16[144,128]{1,0:T(8,128)(2,1)}, bf16[144,128]{1,0:T(8,128)(2,1)S(1)}, u32[]{:S(2)}, u32[]{:S(2)}) collective-permute-start(bf16[144,128]{1,0:T(8,128)(2,1)} %bitcast.16), channel_id=1, source_target_pairs={{0,8},{2,10},{4,12},{6,14},{8,0},{10,2},{12,4},{14,6},{1,9},{3,11}... | collective-permute-start | bytes 110600 | tf_op jit(solution)/shard_map/ppermute | solution.py:417
  10.7 0.7 %pad_maximum_fusion.3.params = f32[4,128]{1,0:T(4,128)S(1)} fusion(f32[1,128]{1,0:T(1,128)} %bitcast.19, f32[1,128]{1,0:T(1,128)} %bitcast.20, f32[1,128]{1,0:T(1,128)} %bitcast.21, f32[1,128]{1,0:T(1,128)} %bitcast.22), kind=kLoop, calls=%fused_computation.5 | loop fusion | flops 1536 | bytes 4096 | tf_op jit(solution)/shard_map/stack | solution.py:447
  11.4 0.5 %collective-permute-start.9 = (bf16[144,128]{1,0:T(8,128)(2,1)}, bf16[144,128]{1,0:T(8,128)(2,1)S(1)}, u32[]{:S(2)}, u32[]{:S(2)}) collective-permute-start(bf16[144,128]{1,0:T(8,128)(2,1)} %bitcast.17), channel_id=1, source_target_pairs={{0,12},{2,14},{4,8},{6,10},{8,4},{10,6},{12,0},{14,2},{1,13},{3,15... | collective-permute-start | bytes 110600 | tf_op jit(solution)/shard_map/ppermute | solution.py:417
  11.9 1.5 %collective-permute-start.3 = (bf16[144,128]{1,0:T(8,128)(2,1)}, bf16[144,128]{1,0:T(8,128)(2,1)S(1)}, u32[]{:S(2)}, u32[]{:S(2)}) collective-permute-start(bf16[144,128]{1,0:T(8,128)(2,1)} %bitcast.11), channel_id=1, source_target_pairs={{0,2},{2,0},{4,6},{6,4},{8,10},{10,8},{12,14},{14,12},{1,3},{3,1},... | collective-permute-start | bytes 110600 | tf_op jit(solution)/shard_map/ppermute | solution.py:417
  13.4 0.6 %collective-permute-start.4 = (bf16[432,128]{1,0:T(8,128)(2,1)S(1)}, bf16[432,128]{1,0:T(8,128)(2,1)S(1)}, u32[]{:S(2)}, u32[]{:S(2)}) collective-permute-start(bf16[432,128]{1,0:T(8,128)(2,1)S(1)} %pad_maximum_fusion.2.refs_1_), channel_id=1, source_target_pairs={{0,2},{2,0},{4,6},{6,4},{8,10},{10,8},{12,14},{14,12},{1,3},{3,1},... | collective-permute-start | bytes 331784 | tf_op jit(solution)/shard_map/ppermute | solution.py:417
  14.0 0.8 %pad_maximum_fusion = bf16[576,128]{1,0:T(8,128)(2,1)S(1)} fusion(bf16[432,128]{1,0:T(8,128)(2,1)S(1)} %pad_maximum_fusion.2.refs_1_, bf16[144,128]{1,0:T(8,128)(2,1)} %bitcast.12), kind=kLoop, calls=%fused_computation | loop fusion | flops 294912 | bytes 294912 | tf_op jit(solution)/shard_map/concatenate | solution.py:430
  14.8 0.8 %copy-done = bf16[6,24,128]{2,1,0:T(8,128)(2,1)S(1)} copy-done((bf16[6,24,128]{2,1,0:T(8,128)(2,1)S(1)}, bf16[6,24,128]{2,1,0:T(8,128)(2,1)}, u32[]{:S(2)}) %copy-start) | copy-done | bytes 36888
  15.5 0.9 %copy-done.2 = bf16[128,512]{1,0:T(8,128)(2,1)S(1)} copy-done((bf16[128,512]{1,0:T(8,128)(2,1)S(1)}, bf16[128,512]{1,0:T(8,128)(2,1)}, u32[]{:S(2)}) %copy-start.2) | copy-done | bytes 131096
  16.4 0.6 %own_edges.2 = (bf16[576,128]{1,0:T(8,128)(2,1)S(1)}, f32[576,128]{1,0:T(8,128)S(1)}, f32[576,128]{1,0:T(8,128)S(1)}, f32[576,128]{1,0:T(8,128)S(1)}, f32[576,12...) custom-call(f32[4,128]{1,0:T(4,128)S(1)} %pad_maximum_fusion.3.params, ...), custom_call_target="tpu_custom_call" | custom-call | flops 1000000000 | tf_op jit(solution)/shard_map/own_edges/pallas_call | solution.py:407
  17.1 0.1 collective-permute-start.5
  17.2 0.3 collective-permute-done.9
  17.5 1.6 %collective-permute-start.10 = (bf16[576,128]{1,0:T(8,128)(2,1)S(1)}, bf16[576,128]{1,0:T(8,128)(2,1)S(1)}, u32[]{:S(2)}, u32[]{:S(2)}) collective-permute-start(bf16[576,128]{1,0:T(8,128)(2,1)S(1)} %pad_maximum_fusion.1.refs_0_), channel_id=1, source_target_pairs={{0,2},{2,0},{4,6},{6,4},{8,10},{10,8},{12,14},{14,12},{1,3},{3,1},... | collective-permute-start | bytes 442376 | tf_op jit(solution)/shard_map/ppermute | solution.py:417
  19.1 0.1 collective-permute-start.6
  19.2 0.6 %own_edges.3 = (bf16[576,128]{1,0:T(8,128)(2,1)S(1)}, f32[576,128]{1,0:T(8,128)S(1)}, f32[576,128]{1,0:T(8,128)S(1)}, f32[576,128]{1,0:T(8,128)S(1)}, f32[576,12...) custom-call(f32[4,128]{1,0:T(4,128)S(1)} %pad_maximum_fusion.3.params, ...), custom_call_target="tpu_custom_call" | custom-call | flops 1000000000 | tf_op jit(solution)/shard_map/own_edges/pallas_call | solution.py:407
  19.8 0.6 %mate_edges.2 = (f32[576,128]{1,0:T(8,128)S(1)}, f32[576,128]{1,0:T(8,128)S(1)}) custom-call(f32[4,128]{1,0:T(4,128)S(1)} %pad_maximum_fusion.3.params, bf16[128,512]{1,0:T(8,128)(2,1)S(1)} %copy-done.2, bf16[576,128]{1,0:T(8,128)(2,1)S(1)} %collective-permute-done.5.refs_0_), custom_call_target="tpu_custom_call" | custom-call | flops 1000000000 | tf_op jit(solution)/shard_map/mate_edges/pallas_call | solution.py:407
  20.5 0.1 collective-permute-done.6.refs_0_
  20.5 0.6 %mate_edges.3 = (f32[576,128]{1,0:T(8,128)S(1)}, f32[576,128]{1,0:T(8,128)S(1)}) custom-call(f32[4,128]{1,0:T(4,128)S(1)} %pad_maximum_fusion.3.params, bf16[128,512]{1,0:T(8,128)(2,1)S(1)} %copy-done.2, bf16[576,128]{1,0:T(8,128)(2,1)S(1)} %collective-permute-done.6.refs_0_), custom_call_target="tpu_custom_call" | custom-call | flops 1000000000 | tf_op jit(solution)/shard_map/mate_edges/pallas_call | solution.py:407
  21.2 0.0 copy-start.5
  21.2 2.4 %triangle.1.tri = f32[1152,128]{1,0:T(8,128)S(1)} custom-call(f32[576,128]{1,0:T(8,128)S(1)} %get-tuple-element.47.refs_0_.left_0, f32[576,128]{1,0:T(8,128)S(1)} %get-tuple-element.49.refs_1_.left_1, f32[576,128]{1,0:T(8,128)S(1)} %get-tuple-element.50.refs_2_, f32[576,128]{1,0:T(8,128)S(1)} %get-tuple-element.51.refs_3_, ...), custom_call_target="tpu_custom_call" | custom-call | flops 2000000000 | tf_op jit(solution)/shard_map/triangle/pallas_call | solution.py:407
  23.6 1.7 %cells.1 = (bf16[144,128]{1,0:T(8,128)(2,1)S(1)}, bf16[1152,128]{1,0:T(8,128)(2,1)S(1)}, bf16[1152,128]{1,0:T(8,128)(2,1)S(1)}, bf16[1152,128]{1,0:T(8,128)(2,1)S(1)}, bf16[1152,128]{1,0:T(8,128)(2,1)S(1)}) custom-call(f32[4,128]{1,0:T(4,128)S(1)} %pad_maximum_fusion.3.params, f32[1152,128]{1,0:T(8,128)S(1)} %triangle.1.tri, ...), custom_call_target="tpu_custom_call" | custom-call | flops 2000000000 | tf_op jit(solution)/shard_map/cells/pallas_call | solution.py:407
  25.3 0.5 %collective-permute-start.11 = (bf16[1152,128]{1,0:T(8,128)(2,1)S(1)}, bf16[1152,128]{1,0:T(8,128)(2,1)S(1)}, u32[]{:S(2)}, u32[]{:S(2)}) collective-permute-start(bf16[1152,128]{1,0:T(8,128)(2,1)S(1)} %get-tuple-element.58.d_tri_ref), channel_id=1, source_target_pairs={{0,1},{1,0},{2,3},{3,2},{4,5},{5,4},{6,7},{7,6},{8,9},{9,8},{10,11... | collective-permute-start | bytes 884744 | tf_op jit(solution)/shard_map/ppermute | solution.py:420
  25.8 2.7 %early.1 = (f32[1152,128]{1,0:T(8,128)S(1)}, f32[1152,128]{1,0:T(8,128)S(1)}, bf16[1152,128]{1,0:T(8,128)(2,1)S(1)}, f32[1152,128]{1,0:T(8,128)S(1)}, f32[576,128]{1,0:T(8,128)S(1)}, /*index=5*/f32[128,256]{1,0:T(8,128)S(1)}) custom-call(bf16[1152,128]{1,0:T(8,128)(2,1)S(1)} %get-tuple-element.58.d_tri_ref, bf16[1152,128]{1,0:T(8,128)(2,1)S(1)} %get-tuple-element.59.d_gate, ...), custom_call_target="tpu_custom_call" | custom-call | flops 30000001024 | tf_op jit(solution)/shard_map/early/pallas_call | solution.py:407
  28.5 0.0 copy-start.3
  28.5 2.9 %late.1 = (f32[128,512]{1,0:T(8,128)S(1)}, bf16[1152,512]{1,0:T(8,128)(2,1)S(1)}) custom-call(bf16[1152,128]{1,0:T(8,128)(2,1)S(1)} %collective-permute-done.11.d_tri_ref, f32[1152,128]{1,0:T(8,128)S(1)} %get-tuple-element.62.left, f32[1152,128]{1,0:T(8,128)S(1)} %get-tuple-element.63.right, bf16[1152,128]{1,0:T(8,128)(2,1)S(1)} %get-tuple-element.64.normed, ...), custom_call_target="tpu_custom_call" | custom-call | flops 40000000000 | tf_op jit(solution)/shard_map/late/pallas_call | solution.py:407
  31.4 0.1 collective-permute-start.13
  31.5 0.4 %collective-permute-start.12 = (f32[128,256]{1,0:T(8,128)S(1)}, f32[128,256]{1,0:T(8,128)S(1)}, u32[]{:S(2)}, u32[]{:S(2)}) collective-permute-start(f32[128,256]{1,0:T(8,128)S(1)} %get-tuple-element.77.small_own), channel_id=1, source_target_pairs={{0,1},{1,0},{2,3},{3,2},{4,5},{5,4},{6,7},{7,6},{8,9},{9,8},{10,11... | collective-permute-start | bytes 393224 | tf_op jit(solution)/shard_map/ppermute | solution.py:420
  32.0 1.2 %collective-permute-done.12.small_mate = f32[128,256]{1,0:T(8,128)S(1)} collective-permute-done((f32[128,256]{1,0:T(8,128)S(1)}, f32[128,256]{1,0:T(8,128)S(1)}, u32[]{:S(2)}, u32[]{:S(2)}) %collective-permute-start.12) | collective-permute-done | bytes 131104 | tf_op jit(solution)/shard_map/ppermute | solution.py:420
  33.2 1.0 %outputs.1 = (bf16[144,128]{1,0:T(8,128)(2,1)}, f32[144,128]{1,0:T(8,128)}, f32[128,128]{1,0:T(8,128)}, f32[128,128]{1,0:T(8,128)}) custom-call(f32[4,128]{1,0:T(4,128)S(1)} %pad_maximum_fusion.3.params, bf16[144,128]{1,0:T(8,128)(2,1)S(1)} %bitcast.14, bf16[1152,512]{1,0:T(8,128)(2,1)S(1)} %get-tuple-element.75.d_proj, ...), custom_call_target="tpu_custom_call" | custom-call | flops 1000000000 | tf_op jit(solution)/shard_map/outputs/pallas_call | solution.py:407
  34.2 0.7 %add.3 = f32[128,512]{1,0:T(8,128)} add(f32[128,512]{1,0:T(8,128)S(1)} %get-tuple-element.80, f32[128,512]{1,0:T(8,128)S(1)} %collective-permute-done.13) | non-fusion elementwise | flops 65536 | bytes 786432 | tf_op jit(solution)/shard_map/add | solution.py:547
  (26 shorter events, 0.1 us)
Async XLA Ops:
  0.6 10.8 %collective-permute-start.2 = (bf16[144,128]{1,0:T(8,128)(2,1)}, bf16[144,128]{1,0:T(8,128)(2,1)S(1)}, u32[]{:S(2)}, u32[]{:S(2)}) collective-permute-start(bf16[144,128]{1,0:T(8,128)(2,1)} %bitcast.8), channel_id=1, source_target_pairs={{0,12},{2,14},{4,8},{6,10},{8,4},{10,6},{12,0},{14,2},{1,13},{3,15... | collective-permute-start | bytes 110600 | tf_op jit(solution)/shard_map/ppermute | solution.py:417
  5.7 6.1 %collective-permute-start.1 = (bf16[144,128]{1,0:T(8,128)(2,1)}, bf16[144,128]{1,0:T(8,128)(2,1)S(1)}, u32[]{:S(2)}, u32[]{:S(2)}) collective-permute-start(bf16[144,128]{1,0:T(8,128)(2,1)} %bitcast.9), channel_id=1, source_target_pairs={{0,8},{2,10},{4,12},{6,14},{8,0},{10,2},{12,4},{14,6},{1,9},{3,11}... | collective-permute-start | bytes 110600 | tf_op jit(solution)/shard_map/ppermute | solution.py:417
  5.8 7.7 %collective-permute-start = (bf16[144,128]{1,0:T(8,128)(2,1)}, bf16[144,128]{1,0:T(8,128)(2,1)S(1)}, u32[]{:S(2)}, u32[]{:S(2)}) collective-permute-start(bf16[144,128]{1,0:T(8,128)(2,1)} %bitcast.10), channel_id=1, source_target_pairs={{0,4},{2,6},{4,0},{6,2},{8,12},{10,14},{12,8},{14,10},{1,5},{3,7},... | collective-permute-start | bytes 110600 | tf_op jit(solution)/shard_map/ppermute | solution.py:417
  6.4 10.7 %collective-permute-start.7 = (bf16[144,128]{1,0:T(8,128)(2,1)}, bf16[144,128]{1,0:T(8,128)(2,1)S(1)}, u32[]{:S(2)}, u32[]{:S(2)}) collective-permute-start(bf16[144,128]{1,0:T(8,128)(2,1)} %bitcast.15), channel_id=1, source_target_pairs={{0,4},{2,6},{4,0},{6,2},{8,12},{10,14},{12,8},{14,10},{1,5},{3,7},... | collective-permute-start | bytes 110600 | tf_op jit(solution)/shard_map/ppermute | solution.py:417
  7.8 9.4 %collective-permute-start.8 = (bf16[144,128]{1,0:T(8,128)(2,1)}, bf16[144,128]{1,0:T(8,128)(2,1)S(1)}, u32[]{:S(2)}, u32[]{:S(2)}) collective-permute-start(bf16[144,128]{1,0:T(8,128)(2,1)} %bitcast.16), channel_id=1, source_target_pairs={{0,8},{2,10},{4,12},{6,14},{8,0},{10,2},{12,4},{14,6},{1,9},{3,11}... | collective-permute-start | bytes 110600 | tf_op jit(solution)/shard_map/ppermute | solution.py:417
  11.4 6.0 %collective-permute-start.9 = (bf16[144,128]{1,0:T(8,128)(2,1)}, bf16[144,128]{1,0:T(8,128)(2,1)S(1)}, u32[]{:S(2)}, u32[]{:S(2)}) collective-permute-start(bf16[144,128]{1,0:T(8,128)(2,1)} %bitcast.17), channel_id=1, source_target_pairs={{0,12},{2,14},{4,8},{6,10},{8,4},{10,6},{12,0},{14,2},{1,13},{3,15... | collective-permute-start | bytes 110600 | tf_op jit(solution)/shard_map/ppermute | solution.py:417
  11.9 7.2 %collective-permute-start.3 = (bf16[144,128]{1,0:T(8,128)(2,1)}, bf16[144,128]{1,0:T(8,128)(2,1)S(1)}, u32[]{:S(2)}, u32[]{:S(2)}) collective-permute-start(bf16[144,128]{1,0:T(8,128)(2,1)} %bitcast.11), channel_id=1, source_target_pairs={{0,2},{2,0},{4,6},{6,4},{8,10},{10,8},{12,14},{14,12},{1,3},{3,1},... | collective-permute-start | bytes 110600 | tf_op jit(solution)/shard_map/ppermute | solution.py:417
  13.4 5.6 %collective-permute-start.4 = (bf16[432,128]{1,0:T(8,128)(2,1)S(1)}, bf16[432,128]{1,0:T(8,128)(2,1)S(1)}, u32[]{:S(2)}, u32[]{:S(2)}) collective-permute-start(bf16[432,128]{1,0:T(8,128)(2,1)S(1)} %pad_maximum_fusion.2.refs_1_), channel_id=1, source_target_pairs={{0,2},{2,0},{4,6},{6,4},{8,10},{10,8},{12,14},{14,12},{1,3},{3,1},... | collective-permute-start | bytes 331784 | tf_op jit(solution)/shard_map/ppermute | solution.py:417
  14.8 0.8 %copy-start = (bf16[6,24,128]{2,1,0:T(8,128)(2,1)S(1)}, bf16[6,24,128]{2,1,0:T(8,128)(2,1)}, u32[]{:S(2)}) copy-start(bf16[6,24,128]{2,1,0:T(8,128)(2,1)} %param.9) | copy-start | bytes 110596
  15.5 0.9 %copy-start.2 = (bf16[128,512]{1,0:T(8,128)(2,1)S(1)}, bf16[128,512]{1,0:T(8,128)(2,1)}, u32[]{:S(2)}) copy-start(bf16[128,512]{1,0:T(8,128)(2,1)} %proj_weight.1) | copy-start | bytes 393220
  16.4 1.0 %copy-start.6 = (bf16[6,24,128]{2,1,0:T(8,128)(2,1)S(1)}, bf16[6,24,128]{2,1,0:T(8,128)(2,1)}, u32[]{:S(2)}) copy-start(bf16[6,24,128]{2,1,0:T(8,128)(2,1)} %param.10) | copy-start | bytes 110596
  17.1 2.7 %collective-permute-start.5 = (bf16[576,128]{1,0:T(8,128)(2,1)S(1)}, bf16[576,128]{1,0:T(8,128)(2,1)S(1)}, u32[]{:S(2)}, u32[]{:S(2)}) collective-permute-start(bf16[576,128]{1,0:T(8,128)(2,1)S(1)} %pad_maximum_fusion), channel_id=1, source_target_pairs={{0,1},{1,0},{2,3},{3,2},{4,5},{5,4},{6,7},{7,6},{8,9},{9,8},{10,11... | collective-permute-start | bytes 442376 | tf_op jit(solution)/shard_map/ppermute | solution.py:420
  17.5 6.1 %collective-permute-start.10 = (bf16[576,128]{1,0:T(8,128)(2,1)S(1)}, bf16[576,128]{1,0:T(8,128)(2,1)S(1)}, u32[]{:S(2)}, u32[]{:S(2)}) collective-permute-start(bf16[576,128]{1,0:T(8,128)(2,1)S(1)} %pad_maximum_fusion.1.refs_0_), channel_id=1, source_target_pairs={{0,2},{2,0},{4,6},{6,4},{8,10},{10,8},{12,14},{14,12},{1,3},{3,1},... | collective-permute-start | bytes 442376 | tf_op jit(solution)/shard_map/ppermute | solution.py:417
  19.1 1.4 %collective-permute-start.6 = (bf16[576,128]{1,0:T(8,128)(2,1)S(1)}, bf16[576,128]{1,0:T(8,128)(2,1)S(1)}, u32[]{:S(2)}, u32[]{:S(2)}) collective-permute-start(bf16[576,128]{1,0:T(8,128)(2,1)S(1)} %constant_dynamic-update-slice_fusion.refs_0_), channel_id=1, source_target_pairs={{0,1},{1,0},{2,3},{3,2},{4,5},{5,4},{6,7},{7,6},{8,9},{9,8},{10,11... | collective-permute-start | bytes 442376 | tf_op jit(solution)/shard_map/ppermute | solution.py:420
  21.2 2.4 %copy-start.4 = (bf16[128,128]{1,0:T(8,128)(2,1)S(1)}, bf16[128,128]{1,0:T(8,128)(2,1)}, u32[]{:S(2)}) copy-start(bf16[128,128]{1,0:T(8,128)(2,1)} %out_weight.1) | copy-start | bytes 98308
  21.2 2.4 %copy-start.5 = (bf16[128,128]{1,0:T(8,128)(2,1)S(1)}, bf16[128,128]{1,0:T(8,128)(2,1)}, u32[]{:S(2)}) copy-start(bf16[128,128]{1,0:T(8,128)(2,1)} %gate_weight.3) | copy-start | bytes 98308
  25.3 3.2 %collective-permute-start.11 = (bf16[1152,128]{1,0:T(8,128)(2,1)S(1)}, bf16[1152,128]{1,0:T(8,128)(2,1)S(1)}, u32[]{:S(2)}, u32[]{:S(2)}) collective-permute-start(bf16[1152,128]{1,0:T(8,128)(2,1)S(1)} %get-tuple-element.58.d_tri_ref), channel_id=1, source_target_pairs={{0,1},{1,0},{2,3},{3,2},{4,5},{5,4},{6,7},{7,6},{8,9},{9,8},{10,11... | collective-permute-start | bytes 884744 | tf_op jit(solution)/shard_map/ppermute | solution.py:420
  28.5 4.7 %copy-start.1 = (bf16[6,24,128]{2,1,0:T(8,128)(2,1)S(1)}, bf16[6,24,128]{2,1,0:T(8,128)(2,1)}, u32[]{:S(2)}) copy-start(bf16[6,24,128]{2,1,0:T(8,128)(2,1)} %param.9) | copy-start | bytes 110596
  28.5 4.7 %copy-start.3 = (bf16[128,512]{1,0:T(8,128)(2,1)S(1)}, bf16[128,512]{1,0:T(8,128)(2,1)}, u32[]{:S(2)}) copy-start(bf16[128,512]{1,0:T(8,128)(2,1)} %proj_weight.1) | copy-start | bytes 393220
  31.4 2.8 %collective-permute-start.13 = (f32[128,512]{1,0:T(8,128)S(1)}, f32[128,512]{1,0:T(8,128)S(1)}, u32[]{:S(2)}, u32[]{:S(2)}) collective-permute-start(f32[128,512]{1,0:T(8,128)S(1)} %get-tuple-element.80), channel_id=1, source_target_pairs={{0,1},{1,0},{2,3},{3,2},{4,5},{5,4},{6,7},{7,6},{8,9},{9,8},{10,11... | collective-permute-start | bytes 786440 | tf_op jit(solution)/shard_map/ppermute | solution.py:420
  31.5 1.7 %collective-permute-start.12 = (f32[128,256]{1,0:T(8,128)S(1)}, f32[128,256]{1,0:T(8,128)S(1)}, u32[]{:S(2)}, u32[]{:S(2)}) collective-permute-start(f32[128,256]{1,0:T(8,128)S(1)} %get-tuple-element.77.small_own), channel_id=1, source_target_pairs={{0,1},{1,0},{2,3},{3,2},{4,5},{5,4},{6,7},{7,6},{8,9},{9,8},{10,11... | collective-permute-start | bytes 393224 | tf_op jit(solution)/shard_map/ppermute | solution.py:420

commit v7 on v6

--- a/solution.py
+++ b/solution.py
@@ -68,6 +68,15 @@
         edge = gate * projected[:, start + hidden : start + 2 * hidden]
         sides.append((edge.astype(BF16).astype(F32), gate, edge * (1.0 - gate)))
     return normed, sides
+
+
+def fetch_kernel(sizes, *refs):
+    half = (len(refs) + 3) // 2
+    vectors, ins, params, outs = refs[:4], refs[4:half], refs[half], refs[half + 1 :]
+    for n, vector in enumerate(vectors):
+        params[n : n + 1, :] = vector[...]
+    for given, out in zip(ins, outs, strict=True):
+        out[...] = given[...]
 
 
 def own_edges_kernel(sizes, params, weight, *refs):
@@ -442,11 +451,18 @@
         outs = [(part, F32)] * 2
         return call(mate_edges_kernel, outs, params, proj_weight, *blocks, name="mate_edges")
 
-    pair = pair_rep.reshape(cells, channels)
-    cot = cotangent.reshape(cells, channels)
-    params = jnp.stack([norm_gain, norm_bias, tri_gain, tri_bias])
-    near = along(pair, tied=True)
-    pair_far = across(after(pair, params), 1)
+    pair_in = pair_rep.reshape(cells, channels)
+    near = along(pair_in, tied=True)
+    vectors = [v[None] for v in (norm_gain, norm_bias, tri_gain, tri_bias)]
+    arrays = (pair_in, cotangent.reshape(cells, channels), proj_weight, gate_weight, out_weight)
+    params, pair, cot, proj_weight, gate_weight, out_weight = call(
+        fetch_kernel,
+        [((4, channels), F32)] + [(a.shape, a.dtype) for a in arrays],
+        *vectors,
+        *arrays,
+        name="fetch",
+    )
+    pair_far = across(pair, 1)
     near_all = after(join(*near), params)
     far = across(near_all, 1)
     mate_near = over(join(pair, near_all))
@@ -539,6 +555,7 @@
         block_out,
         small_grads,
         small_mate,
+        micros=10,
         name="outputs",
     )
     return (

time: 35.2 us -> 40 us (1.14)
  local copies, waits for them, and re-layouts: 1.72 us -> 6.63 us
  other arithmetic: 2.25 us -> 0.76 us
  waiting for transfers between devices: 1.57 us -> 3.04 us
    unnamed x15 -> x22, local copies, waits for them, and re-layouts: 1.7 us -> 6.6 us
    ppermute x9, waiting for transfers between devices: 0.28 us -> 2.79 us  [across(): return lax.ppermute(value, 'row', [(i, i ^ mask) for i in range(groups)])]
    ppermute x5, waiting for transfers between devices: 1.29 us -> 0.24 us  [over(): return lax.ppermute(value, 'col', SWAP)]
    concatenate x3 -> x2, other arithmetic: 0.8 us -> 0.02 us  [join(): return jnp.concatenate(values, axis=0)]
    another operation x1 -> x0, other arithmetic: 0.71 us -> none  [replicated(): params = jnp.stack([norm_gain, norm_bias, tri_gain, tri_bias])]
    pallas_call x9 -> x10, Pallas kernels: 13.1 us -> 13.2 us  [call(): pl.pallas_call(functools.partial(kernel, sizes), out_shape=[jax.ShapeDtyp...]
  transfers between devices with their start and end apart: 14 -> 14, of which waited for: 3 -> 3; matrix products, arithmetic and copies ran while one was open for 4% -> 0% of each run, Pallas kernels for 25% -> 29%
where the time goes in v7:
time: 40 us; the launch traced here: 39.6 us
  starting transfers between devices  15.2 us (38%)
  Pallas kernels  13.2 us (33%)
  local copies, waits for them, and re-layouts  6.63 us (17%)
  waiting for transfers between devices  3.04 us (8%)
  between operations  0.79 us (2%)
  other arithmetic  0.76 us (2%)
    ppermute x9, starting transfers between devices, across(): return lax.ppermute(value, 'row', [(i, i ^ mask) for i in range(groups)])  13.9 us
    pallas_call x10, Pallas kernels, call(): pl.pallas_call(functools.partial(kernel, sizes), out_shape=[jax.ShapeDtyp...  13.2 us
    unnamed x22, local copies, waits for them, and re-layouts  6.6 us
    ppermute x9, waiting for transfers between devices, across(): return lax.ppermute(value, 'row', [(i, i ^ mask) for i in range(groups)])  2.79 us
    ppermute x5, starting transfers between devices, over(): return lax.ppermute(value, 'col', SWAP)  1.29 us
  transfers between devices with their start and end apart: 14, of which 3 were waited for; matrix products, arithmetic and copies ran while one was open for 0% of the time, Pallas kernels for 29%

profile of v7, /device:TPU:0, one launch (start us, length us, event | category | flops | bytes accessed | tf_op | source)
XLA Modules:
  0.0 39.6 jit_solution(12018137460172661830)
XLA Ops:
  0.6 5.1 %collective-permute-start.2 = (bf16[144,128]{1,0:T(8,128)(2,1)}, bf16[144,128]{1,0:T(8,128)(2,1)S(1)}, u32[]{:S(2)}, u32[]{:S(2)}) collective-permute-start(bf16[144,128]{1,0:T(8,128)(2,1)} %bitcast.9), channel_id=1, source_target_pairs={{0,12},{2,14},{4,8},{6,10},{8,4},{10,6},{12,0},{14,2},{1,13},{3,15... | collective-permute-start | bytes 110600 | tf_op jit(solution)/shard_map/ppermute | solution.py:426
  5.8 0.6 %collective-permute-start = (bf16[144,128]{1,0:T(8,128)(2,1)}, bf16[144,128]{1,0:T(8,128)(2,1)S(1)}, u32[]{:S(2)}, u32[]{:S(2)}) collective-permute-start(bf16[144,128]{1,0:T(8,128)(2,1)} %bitcast.11), channel_id=1, source_target_pairs={{0,4},{2,6},{4,0},{6,2},{8,12},{10,14},{12,8},{14,10},{1,5},{3,7},... | collective-permute-start | bytes 110600 | tf_op jit(solution)/shard_map/ppermute | solution.py:426
  6.4 0.9 %copy-done = bf16[128,512]{1,0:T(8,128)(2,1)S(1)} copy-done((bf16[128,512]{1,0:T(8,128)(2,1)S(1)}, bf16[128,512]{1,0:T(8,128)(2,1)}, u32[]{:S(2)}) %copy-start) | copy-done | bytes 131096
  7.3 0.8 %copy-done.1 = bf16[6,24,128]{2,1,0:T(8,128)(2,1)S(1)} copy-done((bf16[6,24,128]{2,1,0:T(8,128)(2,1)S(1)}, bf16[6,24,128]{2,1,0:T(8,128)(2,1)}, u32[]{:S(2)}) %copy-start.1) | copy-done | bytes 36888
  8.1 0.8 %copy-done.2 = bf16[6,24,128]{2,1,0:T(8,128)(2,1)S(1)} copy-done((bf16[6,24,128]{2,1,0:T(8,128)(2,1)S(1)}, bf16[6,24,128]{2,1,0:T(8,128)(2,1)}, u32[]{:S(2)}) %copy-start.2) | copy-done | bytes 36888
  8.8 0.8 %copy-done.3 = bf16[128,128]{1,0:T(8,128)(2,1)S(1)} copy-done((bf16[128,128]{1,0:T(8,128)(2,1)S(1)}, bf16[128,128]{1,0:T(8,128)(2,1)}, u32[]{:S(2)}) %copy-start.3) | copy-done | bytes 32792
  9.6 0.8 %copy-done.4 = bf16[128,128]{1,0:T(8,128)(2,1)S(1)} copy-done((bf16[128,128]{1,0:T(8,128)(2,1)S(1)}, bf16[128,128]{1,0:T(8,128)(2,1)}, u32[]{:S(2)}) %copy-start.4) | copy-done | bytes 32792
  10.4 0.7 %copy-done.5 = f32[128]{0:T(128)S(1)} copy-done((f32[128]{0:T(128)S(1)}, f32[128]{0:T(128)}, u32[]{:S(2)}) %copy-start.5) | copy-done | bytes 536
  11.0 0.7 %copy-done.6 = f32[128]{0:T(128)S(1)} copy-done((f32[128]{0:T(128)S(1)}, f32[128]{0:T(128)}, u32[]{:S(2)}) %copy-start.6) | copy-done | bytes 536
  11.7 0.7 %copy-done.7 = f32[128]{0:T(128)S(1)} copy-done((f32[128]{0:T(128)S(1)}, f32[128]{0:T(128)}, u32[]{:S(2)}) %copy-start.7) | copy-done | bytes 536
  12.3 0.7 %copy-done.8 = f32[128]{0:T(128)S(1)} copy-done((f32[128]{0:T(128)S(1)}, f32[128]{0:T(128)}, u32[]{:S(2)}) %copy-start.8) | copy-done | bytes 536
  13.0 1.5 %collective-permute-start.7 = (bf16[144,128]{1,0:T(8,128)(2,1)S(1)}, bf16[144,128]{1,0:T(8,128)(2,1)S(1)}, u32[]{:S(2)}, u32[]{:S(2)}) collective-permute-start(bf16[144,128]{1,0:T(8,128)(2,1)S(1)} %get-tuple-element.67), channel_id=1, source_target_pairs={{0,4},{2,6},{4,0},{6,2},{8,12},{10,14},{12,8},{14,10},{1,5},{3,7},... | collective-permute-start | bytes 110600 | tf_op jit(solution)/shard_map/ppermute | solution.py:426
  14.4 2.9 %collective-permute-start.8 = (bf16[144,128]{1,0:T(8,128)(2,1)S(1)}, bf16[144,128]{1,0:T(8,128)(2,1)S(1)}, u32[]{:S(2)}, u32[]{:S(2)}) collective-permute-start(bf16[144,128]{1,0:T(8,128)(2,1)S(1)} %get-tuple-element.67), channel_id=1, source_target_pairs={{0,8},{2,10},{4,12},{6,14},{8,0},{10,2},{12,4},{14,6},{1,9},{3,11}... | collective-permute-start | bytes 110600 | tf_op jit(solution)/shard_map/ppermute | solution.py:426
  17.4 0.1 collective-permute-start.9
  17.5 1.7 %collective-permute-start.3 = (bf16[144,128]{1,0:T(8,128)(2,1)S(1)}, bf16[144,128]{1,0:T(8,128)(2,1)S(1)}, u32[]{:S(2)}, u32[]{:S(2)}) collective-permute-start(bf16[144,128]{1,0:T(8,128)(2,1)S(1)} %get-tuple-element.50.refs_0_.pair), channel_id=1, source_target_pairs={{0,2},{2,0},{4,6},{6,4},{8,10},{10,8},{12,14},{14,12},{1,3},{3,1},... | collective-permute-start | bytes 110600 | tf_op jit(solution)/shard_map/ppermute | solution.py:426
  19.1 0.4 %collective-permute-start.4 = (bf16[432,128]{1,0:T(8,128)(2,1)S(1)}, bf16[432,128]{1,0:T(8,128)(2,1)S(1)}, u32[]{:S(2)}, u32[]{:S(2)}) collective-permute-start(bf16[432,128]{1,0:T(8,128)(2,1)S(1)} %pad_maximum_fusion.1.refs_1_), channel_id=1, source_target_pairs={{0,2},{2,0},{4,6},{6,4},{8,10},{10,8},{12,14},{14,12},{1,3},{3,1},... | collective-permute-start | bytes 331784 | tf_op jit(solution)/shard_map/ppermute | solution.py:426
  19.6 0.6 %own_edges.2 = (bf16[576,128]{1,0:T(8,128)(2,1)S(1)}, f32[576,128]{1,0:T(8,128)S(1)}, f32[576,128]{1,0:T(8,128)S(1)}, f32[576,128]{1,0:T(8,128)S(1)}, f32[576,12...) custom-call(f32[4,128]{1,0:T(4,128)S(1)} %get-tuple-element.49.params, ...), custom_call_target="tpu_custom_call" | custom-call | flops 1000000000 | tf_op jit(solution)/shard_map/own_edges/pallas_call | solution.py:416
  20.4 2.8 %collective-permute-done.9 = bf16[144,128]{1,0:T(8,128)(2,1)S(1)} collective-permute-done((bf16[144,128]{1,0:T(8,128)(2,1)S(1)}, bf16[144,128]{1,0:T(8,128)(2,1)S(1)}, u32[]{:S(2)}, u32[]{:S(2)}) %collective-permute-start.9) | collective-permute-done | bytes 36896 | tf_op jit(solution)/shard_map/ppermute | solution.py:426
  23.1 1.6 %collective-permute-start.10 = (bf16[576,128]{1,0:T(8,128)(2,1)S(1)}, bf16[576,128]{1,0:T(8,128)(2,1)S(1)}, u32[]{:S(2)}, u32[]{:S(2)}) collective-permute-start(bf16[576,128]{1,0:T(8,128)(2,1)S(1)} %constant_dynamic-update-slice_fusion.2.refs_0_), channel_id=1, source_target_pairs={{0,2},{2,0},{4,6},{6,4},{8,10},{10,8},{12,14},{14,12},{1,3},{3,1},... | collective-permute-start | bytes 442376 | tf_op jit(solution)/shard_map/ppermute | solution.py:426
  24.8 0.6 %own_edges.3 = (bf16[576,128]{1,0:T(8,128)(2,1)S(1)}, f32[576,128]{1,0:T(8,128)S(1)}, f32[576,128]{1,0:T(8,128)S(1)}, f32[576,128]{1,0:T(8,128)S(1)}, f32[576,12...) custom-call(f32[4,128]{1,0:T(4,128)S(1)} %get-tuple-element.49.params, ...), custom_call_target="tpu_custom_call" | custom-call | flops 1000000000 | tf_op jit(solution)/shard_map/own_edges/pallas_call | solution.py:416
  25.5 0.6 %mate_edges.2 = (f32[576,128]{1,0:T(8,128)S(1)}, f32[576,128]{1,0:T(8,128)S(1)}) custom-call(f32[4,128]{1,0:T(4,128)S(1)} %get-tuple-element.49.params, bf16[128,512]{1,0:T(8,128)(2,1)S(1)} %get-tuple-element.51.weight.proj_weight, bf16[576,128]{1,0:T(8,128)(2,1)S(1)} %collective-permute-done.5.refs_0_), custom_call_target="tpu_custom_call" | custom-call | flops 1000000000 | tf_op jit(solution)/shard_map/mate_edges/pallas_call | solution.py:416
  26.2 0.6 %mate_edges.3 = (f32[576,128]{1,0:T(8,128)S(1)}, f32[576,128]{1,0:T(8,128)S(1)}) custom-call(f32[4,128]{1,0:T(4,128)S(1)} %get-tuple-element.49.params, bf16[128,512]{1,0:T(8,128)(2,1)S(1)} %get-tuple-element.51.weight.proj_weight, bf16[576,128]{1,0:T(8,128)(2,1)S(1)} %collective-permute-done.6.refs_0_), custom_call_target="tpu_custom_call" | custom-call | flops 1000000000 | tf_op jit(solution)/shard_map/mate_edges/pallas_call | solution.py:416
  26.8 2.4 %triangle.1.tri = f32[1152,128]{1,0:T(8,128)S(1)} custom-call(f32[576,128]{1,0:T(8,128)S(1)} %get-tuple-element.55.refs_0_.left_0, f32[576,128]{1,0:T(8,128)S(1)} %get-tuple-element.56.refs_1_.left_1, f32[576,128]{1,0:T(8,128)S(1)} %get-tuple-element.57.refs_2_, f32[576,128]{1,0:T(8,128)S(1)} %get-tuple-element.58.refs_3_, ...), custom_call_target="tpu_custom_call" | custom-call | flops 2000000000 | tf_op jit(solution)/shard_map/triangle/pallas_call | solution.py:416
  29.3 1.7 %cells.1 = (bf16[144,128]{1,0:T(8,128)(2,1)S(1)}, bf16[1152,128]{1,0:T(8,128)(2,1)S(1)}, bf16[1152,128]{1,0:T(8,128)(2,1)S(1)}, bf16[1152,128]{1,0:T(8,128)(2,1)S(1)}, bf16[1152,128]{1,0:T(8,128)(2,1)S(1)}) custom-call(f32[4,128]{1,0:T(4,128)S(1)} %get-tuple-element.49.params, f32[1152,128]{1,0:T(8,128)S(1)} %triangle.1.tri, ...), custom_call_target="tpu_custom_call" | custom-call | flops 2000000000 | tf_op jit(solution)/shard_map/cells/pallas_call | solution.py:416
  30.9 0.5 %collective-permute-start.11 = (bf16[1152,128]{1,0:T(8,128)(2,1)S(1)}, bf16[1152,128]{1,0:T(8,128)(2,1)S(1)}, u32[]{:S(2)}, u32[]{:S(2)}) collective-permute-start(bf16[1152,128]{1,0:T(8,128)(2,1)S(1)} %get-tuple-element.68.d_tri_ref), channel_id=1, source_target_pairs={{0,1},{1,0},{2,3},{3,2},{4,5},{5,4},{6,7},{7,6},{8,9},{9,8},{10,11... | collective-permute-start | bytes 884744 | tf_op jit(solution)/shard_map/ppermute | solution.py:429
  31.4 2.7 %early.1 = (f32[1152,128]{1,0:T(8,128)S(1)}, f32[1152,128]{1,0:T(8,128)S(1)}, bf16[1152,128]{1,0:T(8,128)(2,1)S(1)}, f32[1152,128]{1,0:T(8,128)S(1)}, f32[576,128]{1,0:T(8,128)S(1)}, /*index=5*/f32[128,256]{1,0:T(8,128)S(1)}) custom-call(bf16[1152,128]{1,0:T(8,128)(2,1)S(1)} %get-tuple-element.68.d_tri_ref, bf16[1152,128]{1,0:T(8,128)(2,1)S(1)} %get-tuple-element.69.d_gate, ...), custom_call_target="tpu_custom_call" | custom-call | flops 30000001024 | tf_op jit(solution)/shard_map/early/pallas_call | solution.py:416
  34.1 0.1 collective-permute-start.12
  34.3 2.9 %late.1 = (f32[128,512]{1,0:T(8,128)S(1)}, bf16[1152,512]{1,0:T(8,128)(2,1)S(1)}) custom-call(bf16[1152,128]{1,0:T(8,128)(2,1)S(1)} %collective-permute-done.11.d_tri_ref, f32[1152,128]{1,0:T(8,128)S(1)} %get-tuple-element.72.left, f32[1152,128]{1,0:T(8,128)S(1)} %get-tuple-element.73.right, bf16[1152,128]{1,0:T(8,128)(2,1)S(1)} %get-tuple-element.74.normed, ...), custom_call_target="tpu_custom_call" | custom-call | flops 40000000000 | tf_op jit(solution)/shard_map/late/pallas_call | solution.py:416
  37.2 0.5 %collective-permute-start.13 = (f32[128,512]{1,0:T(8,128)S(1)}, f32[128,512]{1,0:T(8,128)S(1)}, u32[]{:S(2)}, u32[]{:S(2)}) collective-permute-start(f32[128,512]{1,0:T(8,128)S(1)} %get-tuple-element.90), channel_id=1, source_target_pairs={{0,1},{1,0},{2,3},{3,2},{4,5},{5,4},{6,7},{7,6},{8,9},{9,8},{10,11... | collective-permute-start | bytes 786440 | tf_op jit(solution)/shard_map/ppermute | solution.py:429
  37.7 1.0 %outputs.1 = (bf16[144,128]{1,0:T(8,128)(2,1)}, f32[144,128]{1,0:T(8,128)}, f32[128,128]{1,0:T(8,128)}, f32[128,128]{1,0:T(8,128)}) custom-call(f32[4,128]{1,0:T(4,128)S(1)} %get-tuple-element.49.params, bf16[144,128]{1,0:T(8,128)(2,1)S(1)} %get-tuple-element.50.refs_0_.pair, bf16[1152,512]{1,0:T(8,128)(2,1)S(1)} %get-tuple-element.85.d_proj, ...), custom_call_target="tpu_custom_call" | custom-call | flops 10000000000 | tf_op jit(solution)/shard_map/outputs/pallas_call | solution.py:416
  38.6 0.2 collective-permute-done.13
  38.8 0.7 %add.3 = f32[128,512]{1,0:T(8,128)} add(f32[128,512]{1,0:T(8,128)S(1)} %get-tuple-element.90, f32[128,512]{1,0:T(8,128)S(1)} %collective-permute-done.13) | non-fusion elementwise | flops 65536 | bytes 786432 | tf_op jit(solution)/shard_map/add | solution.py:564
  (33 shorter events, 0.3 us)
Async XLA Ops:
  0.6 16.7 %collective-permute-start.2 = (bf16[144,128]{1,0:T(8,128)(2,1)}, bf16[144,128]{1,0:T(8,128)(2,1)S(1)}, u32[]{:S(2)}, u32[]{:S(2)}) collective-permute-start(bf16[144,128]{1,0:T(8,128)(2,1)} %bitcast.9), channel_id=1, source_target_pairs={{0,12},{2,14},{4,8},{6,10},{8,4},{10,6},{12,0},{14,2},{1,13},{3,15... | collective-permute-start | bytes 110600 | tf_op jit(solution)/shard_map/ppermute | solution.py:426
  5.7 11.7 %collective-permute-start.1 = (bf16[144,128]{1,0:T(8,128)(2,1)}, bf16[144,128]{1,0:T(8,128)(2,1)S(1)}, u32[]{:S(2)}, u32[]{:S(2)}) collective-permute-start(bf16[144,128]{1,0:T(8,128)(2,1)} %bitcast.10), channel_id=1, source_target_pairs={{0,8},{2,10},{4,12},{6,14},{8,0},{10,2},{12,4},{14,6},{1,9},{3,11}... | collective-permute-start | bytes 110600 | tf_op jit(solution)/shard_map/ppermute | solution.py:426
  5.8 13.4 %collective-permute-start = (bf16[144,128]{1,0:T(8,128)(2,1)}, bf16[144,128]{1,0:T(8,128)(2,1)S(1)}, u32[]{:S(2)}, u32[]{:S(2)}) collective-permute-start(bf16[144,128]{1,0:T(8,128)(2,1)} %bitcast.11), channel_id=1, source_target_pairs={{0,4},{2,6},{4,0},{6,2},{8,12},{10,14},{12,8},{14,10},{1,5},{3,7},... | collective-permute-start | bytes 110600 | tf_op jit(solution)/shard_map/ppermute | solution.py:426
  6.4 0.9 %copy-start = (bf16[128,512]{1,0:T(8,128)(2,1)S(1)}, bf16[128,512]{1,0:T(8,128)(2,1)}, u32[]{:S(2)}) copy-start(bf16[128,512]{1,0:T(8,128)(2,1)} %refs_6_.1) | copy-start | bytes 393220
  7.3 0.8 %copy-start.1 = (bf16[6,24,128]{2,1,0:T(8,128)(2,1)S(1)}, bf16[6,24,128]{2,1,0:T(8,128)(2,1)}, u32[]{:S(2)}) copy-start(bf16[6,24,128]{2,1,0:T(8,128)(2,1)} %param.10) | copy-start | bytes 110596
  8.1 0.8 %copy-start.2 = (bf16[6,24,128]{2,1,0:T(8,128)(2,1)S(1)}, bf16[6,24,128]{2,1,0:T(8,128)(2,1)}, u32[]{:S(2)}) copy-start(bf16[6,24,128]{2,1,0:T(8,128)(2,1)} %param.9) | copy-start | bytes 110596
  8.8 0.8 %copy-start.3 = (bf16[128,128]{1,0:T(8,128)(2,1)S(1)}, bf16[128,128]{1,0:T(8,128)(2,1)}, u32[]{:S(2)}) copy-start(bf16[128,128]{1,0:T(8,128)(2,1)} %refs_7_.1) | copy-start | bytes 98308
  9.6 0.8 %copy-start.4 = (bf16[128,128]{1,0:T(8,128)(2,1)S(1)}, bf16[128,128]{1,0:T(8,128)(2,1)}, u32[]{:S(2)}) copy-start(bf16[128,128]{1,0:T(8,128)(2,1)} %refs_8_.1) | copy-start | bytes 98308
  10.3 0.7 %copy-start.5 = (f32[128]{0:T(128)S(1)}, f32[128]{0:T(128)}, u32[]{:S(2)}) copy-start(f32[128]{0:T(128)} %param.11) | copy-start | bytes 1540
  11.0 0.7 %copy-start.6 = (f32[128]{0:T(128)S(1)}, f32[128]{0:T(128)}, u32[]{:S(2)}) copy-start(f32[128]{0:T(128)} %param.12) | copy-start | bytes 1540
  11.7 0.7 %copy-start.7 = (f32[128]{0:T(128)S(1)}, f32[128]{0:T(128)}, u32[]{:S(2)}) copy-start(f32[128]{0:T(128)} %param.15) | copy-start | bytes 1540
  12.3 0.7 %copy-start.8 = (f32[128]{0:T(128)S(1)}, f32[128]{0:T(128)}, u32[]{:S(2)}) copy-start(f32[128]{0:T(128)} %param.16) | copy-start | bytes 1540
  13.0 7.2 %collective-permute-start.7 = (bf16[144,128]{1,0:T(8,128)(2,1)S(1)}, bf16[144,128]{1,0:T(8,128)(2,1)S(1)}, u32[]{:S(2)}, u32[]{:S(2)}) collective-permute-start(bf16[144,128]{1,0:T(8,128)(2,1)S(1)} %get-tuple-element.67), channel_id=1, source_target_pairs={{0,4},{2,6},{4,0},{6,2},{8,12},{10,14},{12,8},{14,10},{1,5},{3,7},... | collective-permute-start | bytes 110600 | tf_op jit(solution)/shard_map/ppermute | solution.py:426
  14.4 5.9 %collective-permute-start.8 = (bf16[144,128]{1,0:T(8,128)(2,1)S(1)}, bf16[144,128]{1,0:T(8,128)(2,1)S(1)}, u32[]{:S(2)}, u32[]{:S(2)}) collective-permute-start(bf16[144,128]{1,0:T(8,128)(2,1)S(1)} %get-tuple-element.67), channel_id=1, source_target_pairs={{0,8},{2,10},{4,12},{6,14},{8,0},{10,2},{12,4},{14,6},{1,9},{3,11}... | collective-permute-start | bytes 110600 | tf_op jit(solution)/shard_map/ppermute | solution.py:426
  17.4 5.8 %collective-permute-start.9 = (bf16[144,128]{1,0:T(8,128)(2,1)S(1)}, bf16[144,128]{1,0:T(8,128)(2,1)S(1)}, u32[]{:S(2)}, u32[]{:S(2)}) collective-permute-start(bf16[144,128]{1,0:T(8,128)(2,1)S(1)} %get-tuple-element.67), channel_id=1, source_target_pairs={{0,12},{2,14},{4,8},{6,10},{8,4},{10,6},{12,0},{14,2},{1,13},{3,15... | collective-permute-start | bytes 110600 | tf_op jit(solution)/shard_map/ppermute | solution.py:426
  17.5 7.3 %collective-permute-start.3 = (bf16[144,128]{1,0:T(8,128)(2,1)S(1)}, bf16[144,128]{1,0:T(8,128)(2,1)S(1)}, u32[]{:S(2)}, u32[]{:S(2)}) collective-permute-start(bf16[144,128]{1,0:T(8,128)(2,1)S(1)} %get-tuple-element.50.refs_0_.pair), channel_id=1, source_target_pairs={{0,2},{2,0},{4,6},{6,4},{8,10},{10,8},{12,14},{14,12},{1,3},{3,1},... | collective-permute-start | bytes 110600 | tf_op jit(solution)/shard_map/ppermute | solution.py:426
  19.1 5.6 %collective-permute-start.4 = (bf16[432,128]{1,0:T(8,128)(2,1)S(1)}, bf16[432,128]{1,0:T(8,128)(2,1)S(1)}, u32[]{:S(2)}, u32[]{:S(2)}) collective-permute-start(bf16[432,128]{1,0:T(8,128)(2,1)S(1)} %pad_maximum_fusion.1.refs_1_), channel_id=1, source_target_pairs={{0,2},{2,0},{4,6},{6,4},{8,10},{10,8},{12,14},{14,12},{1,3},{3,1},... | collective-permute-start | bytes 331784 | tf_op jit(solution)/shard_map/ppermute | solution.py:426
  20.2 5.2 %collective-permute-start.5 = (bf16[576,128]{1,0:T(8,128)(2,1)S(1)}, bf16[576,128]{1,0:T(8,128)(2,1)S(1)}, u32[]{:S(2)}, u32[]{:S(2)}) collective-permute-start(bf16[576,128]{1,0:T(8,128)(2,1)S(1)} %pad_maximum_fusion), channel_id=1, source_target_pairs={{0,1},{1,0},{2,3},{3,2},{4,5},{5,4},{6,7},{7,6},{8,9},{9,8},{10,11... | collective-permute-start | bytes 442376 | tf_op jit(solution)/shard_map/ppermute | solution.py:429
  23.1 6.1 %collective-permute-start.10 = (bf16[576,128]{1,0:T(8,128)(2,1)S(1)}, bf16[576,128]{1,0:T(8,128)(2,1)S(1)}, u32[]{:S(2)}, u32[]{:S(2)}) collective-permute-start(bf16[576,128]{1,0:T(8,128)(2,1)S(1)} %constant_dynamic-update-slice_fusion.2.refs_0_), channel_id=1, source_target_pairs={{0,2},{2,0},{4,6},{6,4},{8,10},{10,8},{12,14},{14,12},{1,3},{3,1},... | collective-permute-start | bytes 442376 | tf_op jit(solution)/shard_map/ppermute | solution.py:426
  24.8 1.4 %collective-permute-start.6 = (bf16[576,128]{1,0:T(8,128)(2,1)S(1)}, bf16[576,128]{1,0:T(8,128)(2,1)S(1)}, u32[]{:S(2)}, u32[]{:S(2)}) collective-permute-start(bf16[576,128]{1,0:T(8,128)(2,1)S(1)} %constant_dynamic-update-slice_fusion.refs_0_), channel_id=1, source_target_pairs={{0,1},{1,0},{2,3},{3,2},{4,5},{5,4},{6,7},{7,6},{8,9},{9,8},{10,11... | collective-permute-start | bytes 442376 | tf_op jit(solution)/shard_map/ppermute | solution.py:429
  30.9 3.4 %collective-permute-start.11 = (bf16[1152,128]{1,0:T(8,128)(2,1)S(1)}, bf16[1152,128]{1,0:T(8,128)(2,1)S(1)}, u32[]{:S(2)}, u32[]{:S(2)}) collective-permute-start(bf16[1152,128]{1,0:T(8,128)(2,1)S(1)} %get-tuple-element.68.d_tri_ref), channel_id=1, source_target_pairs={{0,1},{1,0},{2,3},{3,2},{4,5},{5,4},{6,7},{7,6},{8,9},{9,8},{10,11... | collective-permute-start | bytes 884744 | tf_op jit(solution)/shard_map/ppermute | solution.py:429
  34.1 3.5 %collective-permute-start.12 = (f32[128,256]{1,0:T(8,128)S(1)}, f32[128,256]{1,0:T(8,128)S(1)}, u32[]{:S(2)}, u32[]{:S(2)}) collective-permute-start(f32[128,256]{1,0:T(8,128)S(1)} %get-tuple-element.87.small_own), channel_id=1, source_target_pairs={{0,1},{1,0},{2,3},{3,2},{4,5},{5,4},{6,7},{7,6},{8,9},{9,8},{10,11... | collective-permute-start | bytes 393224 | tf_op jit(solution)/shard_map/ppermute | solution.py:429
  37.2 1.7 %collective-permute-start.13 = (f32[128,512]{1,0:T(8,128)S(1)}, f32[128,512]{1,0:T(8,128)S(1)}, u32[]{:S(2)}, u32[]{:S(2)}) collective-permute-start(f32[128,512]{1,0:T(8,128)S(1)} %get-tuple-element.90), channel_id=1, source_target_pairs={{0,1},{1,0},{2,3},{3,2},{4,5},{5,4},{6,7},{7,6},{8,9},{9,8},{10,11... | collective-permute-start | bytes 786440 | tf_op jit(solution)/shard_map/ppermute | solution.py:429

commit v8 on v6

--- a/solution.py
+++ b/solution.py
@@ -68,6 +68,21 @@
         edge = gate * projected[:, start + hidden : start + 2 * hidden]
         sides.append((edge.astype(BF16).astype(F32), gate, edge * (1.0 - gate)))
     return normed, sides
+
+
+def fetch_kernel(sizes, *refs):
+    cells = sizes[0] * sizes[1]
+    pair, cot, gain_0, bias_0, gain_1, bias_1, *weights = refs[:9]
+    both, params, *held = refs[9:14]
+    sems = refs[14]
+    moves = [(pair, both.at[:cells]), (cot, both.at[cells:])]
+    moves += [(v, params.at[n : n + 1]) for n, v in enumerate((gain_0, bias_0, gain_1, bias_1))]
+    moves += list(zip(weights, held, strict=True))
+    copies = [pltpu.make_async_copy(a, b, sems.at[n]) for n, (a, b) in enumerate(moves)]
+    for copy in copies:
+        copy.start()
+    for copy in copies:
+        copy.wait()
 
 
 def own_edges_kernel(sizes, params, weight, *refs):
@@ -152,7 +167,8 @@
     gain, bias = params[2:3, :], params[3:4, :]
     for which, normed in ((0, normed_0), (1, normed_1)):
         for t, b in enumerate(places(groups)):
-            cot = cots[which][t * cells : (t + 1) * cells, :]
+            block = cots[2 * which + min(t, 1)]
+            cot = block[max(t - 1, 0) * cells : max(t, 1) * cells, :]
             place = at(row_block(which, b), cells)
             tri_f, hat, inverse = layer_norm(tri[place, :], gain, bias)
             tri_norm = tri_f.astype(BF16)
@@ -402,12 +418,13 @@
     some = every // 2
     sizes = (rows, cols, groups)
 
-    def call(kernel, outs, *args, scratch=(), micros=1, name):
+    def call(kernel, outs, *args, scratch=(), micros=1, name, **more):
         cost = pl.CostEstimate(flops=micros * 10**9, bytes_accessed=0, transcendentals=0)
         return pl.pallas_call(
             functools.partial(kernel, sizes),
             out_shape=[jax.ShapeDtypeStruct(*out) for out in outs],
-            scratch_shapes=[pltpu.VMEM(*one) for one in scratch],
+            scratch_shapes=[pltpu.VMEM(*one) if isinstance(one, tuple) else one for one in scratch],
+            **more,
             compiler_params=pltpu.CompilerParams(vmem_limit_bytes=VMEM_BUDGET),
             cost_estimate=cost,
             name=name,
@@ -442,16 +459,27 @@
         outs = [(part, F32)] * 2
         return call(mate_edges_kernel, outs, params, proj_weight, *blocks, name="mate_edges")
 
-    pair = pair_rep.reshape(cells, channels)
-    cot = cotangent.reshape(cells, channels)
-    params = jnp.stack([norm_gain, norm_bias, tri_gain, tri_bias])
-    near = along(pair, tied=True)
-    pair_far = across(after(pair, params), 1)
-    near_all = after(join(*near), params)
+    given = [pair_rep.reshape(cells, channels), cotangent.reshape(cells, channels)]
+    given += [v[None] for v in (norm_gain, norm_bias, tri_gain, tri_bias)]
+    given += [proj_weight, gate_weight, out_weight]
+    given = [pltpu.with_memory_space_constraint(v, pltpu.HBM) for v in given]
+    both, params, proj_weight, gate_weight, out_weight = call(
+        fetch_kernel,
+        [((2 * cells, channels), BF16), ((4, channels), F32)] + [(a.shape, BF16) for a in given[6:]],
+        *given,
+        scratch=[pltpu.SemaphoreType.DMA((len(given),))],
+        in_specs=[pl.BlockSpec(memory_space=pltpu.HBM)] * len(given),
+        name="fetch",
+    )
+    got = along(both, tied=True)
+    both_far = across(both, 1)
+    pair, pair_far = both[:cells], both_far[:cells]
+    cot_0, cot_1 = both[cells:], both_far[cells:]
+    near_all = join(*(block[:cells] for block in got))
     far = across(near_all, 1)
+    cot_near = join(*(block[cells:] for block in got))
+    cot_far = across(cot_near, 1)
     mate_near = over(join(pair, near_all))
-    cot_near = join(cot, *along(cot))
-    cot_far = across(cot_near, 1)
     own_0 = own_edges(pair, near_all)
     mate_0 = mate_edges(mate_near)
     far_all = join(pair_far, far)
@@ -480,7 +508,9 @@
         *normed,
         gate_weight,
         out_weight,
+        cot_0,
         cot_near,
+        cot_1,
         cot_far,
         micros=2,
         name="cells",
@@ -539,6 +569,7 @@
         block_out,
         small_grads,
         small_mate,
+        micros=10,
         name="outputs",
     )
     return (

time: 35.2 us -> 33 us (0.937)
  starting transfers between devices: 15.4 us -> 10.9 us
  waiting for transfers between devices: 1.57 us -> 6.06 us
  local copies, waits for them, and re-layouts: 1.72 us -> 0.03 us
  other arithmetic: 2.25 us -> 0.78 us
  Pallas kernels: 13.1 us -> 14.2 us
    ppermute x9 -> x6, waiting for transfers between devices: 0.28 us -> 5.81 us  [across(): return lax.ppermute(value, 'row', [(i, i ^ mask) for i in range(groups)])]
    ppermute x9 -> x6, starting transfers between devices: 14.2 us -> 9.58 us  [across(): return lax.ppermute(value, 'row', [(i, i ^ mask) for i in range(groups)])]
    unnamed x15 -> x0, local copies, waits for them, and re-layouts: 1.7 us -> none
    pallas_call x9 -> x10, Pallas kernels: 13.1 us -> 14.2 us  [call(): pl.pallas_call(functools.partial(kernel, sizes), out_shape=[jax.ShapeDtyp...]
    ppermute x5, waiting for transfers between devices: 1.29 us -> 0.25 us  [over(): return lax.ppermute(value, 'col', SWAP)]
    concatenate x3 -> x4, other arithmetic: 0.8 us -> 0.04 us  [join(): return jnp.concatenate(values, axis=0)]
    another operation x1 -> x0, other arithmetic: 0.71 us -> none  [replicated(): params = jnp.stack([norm_gain, norm_bias, tri_gain, tri_bias])]
  transfers between devices with their start and end apart: 14 -> 11, of which waited for: 3 -> 5; matrix products, arithmetic and copies ran while one was open for 4% -> 0% of each run, Pallas kernels for 25% -> 35%
where the time goes in v8:
time: 33 us; the launch traced here: 32.8 us
  Pallas kernels  14.2 us (43%)
  starting transfers between devices  10.9 us (33%)
  waiting for transfers between devices  6.06 us (18%)
  other arithmetic  0.78 us (2%)
  between operations  0.77 us (2%)
    pallas_call x10, Pallas kernels, call(): pl.pallas_call(functools.partial(kernel, sizes), out_shape=[jax.ShapeDtyp...  14.2 us
    ppermute x6, starting transfers between devices, across(): return lax.ppermute(value, 'row', [(i, i ^ mask) for i in range(groups)])  9.58 us
    ppermute x6, waiting for transfers between devices, across(): return lax.ppermute(value, 'row', [(i, i ^ mask) for i in range(groups)])  5.81 us
    ppermute x5, starting transfers between devices, over(): return lax.ppermute(value, 'col', SWAP)  1.29 us
    add x1, other arithmetic, replicated(): proj_grad + proj_mate  0.74 us
  transfers between devices with their start and end apart: 11, of which 5 were waited for; matrix products, arithmetic and copies ran while one was open for 0% of the time, Pallas kernels for 35%

profile of v8, /device:TPU:0, one launch (start us, length us, event | category | flops | bytes accessed | tf_op | source)
XLA Modules:
  0.0 32.8 jit_solution(11673015518036596455)
XLA Ops:
  0.6 1.1 %fetch.1 = (bf16[288,128]{1,0:T(8,128)(2,1)S(1)}, f32[4,128]{1,0:T(4,128)S(1)}, bf16[128,512]{1,0:T(8,128)(2,1)S(1)}, bf16[128,128]{1,0:T(8,128)(2,1)S(1)}, bf16[128,128]{1,0:T(8,128)(2,1)S(1)}) custom-call(bf16[144,128]{1,0:T(8,128)(2,1)} %bitcast.8, bf16[144,128]{1,0:T(8,128)(2,1)} %bitcast.9, f32[1,128]{1,0:T(1,128)} %bitcast.10, f32[1,128]{1,0:T(1,128)} %bitcast.11, ...), custom_call_target="tpu_custom_call" | custom-call | flops 1000000000 | tf_op jit(solution)/shard_map/fetch/pallas_call | solution.py:423
  1.7 5.1 %collective-permute-start.2 = (bf16[288,128]{1,0:T(8,128)(2,1)S(1)}, bf16[288,128]{1,0:T(8,128)(2,1)S(1)}, u32[]{:S(2)}, u32[]{:S(2)}) collective-permute-start(bf16[288,128]{1,0:T(8,128)(2,1)S(1)} %get-tuple-element.48), channel_id=1, source_target_pairs={{0,12},{2,14},{4,8},{6,10},{8,4},{10,6},{12,0},{14,2},{1,13},{3,15... | collective-permute-start | bytes 221192 | tf_op jit(solution)/shard_map/ppermute | solution.py:434
  6.9 0.0 collective-permute-start.1
  6.9 0.6 %collective-permute-start = (bf16[288,128]{1,0:T(8,128)(2,1)S(1)}, bf16[288,128]{1,0:T(8,128)(2,1)S(1)}, u32[]{:S(2)}, u32[]{:S(2)}) collective-permute-start(bf16[288,128]{1,0:T(8,128)(2,1)S(1)} %get-tuple-element.48), channel_id=1, source_target_pairs={{0,4},{2,6},{4,0},{6,2},{8,12},{10,14},{12,8},{14,10},{1,5},{3,7},... | collective-permute-start | bytes 221192 | tf_op jit(solution)/shard_map/ppermute | solution.py:434
  7.5 1.7 %collective-permute-start.3 = (bf16[288,128]{1,0:T(8,128)(2,1)S(1)}, bf16[288,128]{1,0:T(8,128)(2,1)S(1)}, u32[]{:S(2)}, u32[]{:S(2)}) collective-permute-start(bf16[288,128]{1,0:T(8,128)(2,1)S(1)} %get-tuple-element.48), channel_id=1, source_target_pairs={{0,2},{2,0},{4,6},{6,4},{8,10},{10,8},{12,14},{14,12},{1,3},{3,1},... | collective-permute-start | bytes 221192 | tf_op jit(solution)/shard_map/ppermute | solution.py:434
  9.2 0.4 %collective-permute-done.2 = bf16[288,128]{1,0:T(8,128)(2,1)S(1)} collective-permute-done((bf16[288,128]{1,0:T(8,128)(2,1)S(1)}, bf16[288,128]{1,0:T(8,128)(2,1)S(1)}, u32[]{:S(2)}, u32[]{:S(2)}) %collective-permute-start.2) | collective-permute-done | bytes 73760 | tf_op jit(solution)/shard_map/ppermute | solution.py:434
  9.6 3.5 %collective-permute-done.1 = bf16[288,128]{1,0:T(8,128)(2,1)S(1)} collective-permute-done((bf16[288,128]{1,0:T(8,128)(2,1)S(1)}, bf16[288,128]{1,0:T(8,128)(2,1)S(1)}, u32[]{:S(2)}, u32[]{:S(2)}) %collective-permute-start.1) | collective-permute-done | bytes 73760 | tf_op jit(solution)/shard_map/ppermute | solution.py:434
  13.1 0.0 collective-permute-done
  13.1 1.6 %collective-permute-start.4 = (bf16[432,128]{1,0:T(8,128)(2,1)S(1)}, bf16[432,128]{1,0:T(8,128)(2,1)S(1)}, u32[]{:S(2)}, u32[]{:S(2)}) collective-permute-start(bf16[432,128]{1,0:T(8,128)(2,1)S(1)} %pad_maximum_fusion.2.refs_1_), channel_id=1, source_target_pairs={{0,2},{2,0},{4,6},{6,4},{8,10},{10,8},{12,14},{14,12},{1,3},{3,1},... | collective-permute-start | bytes 331784 | tf_op jit(solution)/shard_map/ppermute | solution.py:434
  14.7 0.1 collective-permute-start.5
  14.8 0.6 %collective-permute-start.7 = (bf16[432,128]{1,0:T(8,128)(2,1)S(1)}, bf16[432,128]{1,0:T(8,128)(2,1)S(1)}, u32[]{:S(2)}, u32[]{:S(2)}) collective-permute-start(bf16[432,128]{1,0:T(8,128)(2,1)S(1)} %pad_maximum_fusion.3.refs_1_), channel_id=1, source_target_pairs={{0,2},{2,0},{4,6},{6,4},{8,10},{10,8},{12,14},{14,12},{1,3},{3,1},... | collective-permute-start | bytes 331784 | tf_op jit(solution)/shard_map/ppermute | solution.py:434
  15.4 0.0 collective-permute-done.3
  15.4 0.6 %own_edges.2 = (bf16[576,128]{1,0:T(8,128)(2,1)S(1)}, f32[576,128]{1,0:T(8,128)S(1)}, f32[576,128]{1,0:T(8,128)S(1)}, f32[576,128]{1,0:T(8,128)S(1)}, f32[576,12...) custom-call(f32[4,128]{1,0:T(4,128)S(1)} %get-tuple-element.47.params, ...), custom_call_target="tpu_custom_call" | custom-call | flops 1000000000 | tf_op jit(solution)/shard_map/own_edges/pallas_call | solution.py:423
  16.1 1.9 %collective-permute-done.4 = bf16[432,128]{1,0:T(8,128)(2,1)S(1)} collective-permute-done((bf16[432,128]{1,0:T(8,128)(2,1)S(1)}, bf16[432,128]{1,0:T(8,128)(2,1)S(1)}, u32[]{:S(2)}, u32[]{:S(2)}) %collective-permute-start.4) | collective-permute-done | bytes 110624 | tf_op jit(solution)/shard_map/ppermute | solution.py:434
  18.0 0.1 collective-permute-start.6
  18.0 0.6 %own_edges.3 = (bf16[576,128]{1,0:T(8,128)(2,1)S(1)}, f32[576,128]{1,0:T(8,128)S(1)}, f32[576,128]{1,0:T(8,128)S(1)}, f32[576,128]{1,0:T(8,128)S(1)}, f32[576,12...) custom-call(f32[4,128]{1,0:T(4,128)S(1)} %get-tuple-element.47.params, ...), custom_call_target="tpu_custom_call" | custom-call | flops 1000000000 | tf_op jit(solution)/shard_map/own_edges/pallas_call | solution.py:423
  18.7 0.0 collective-permute-done.5.refs_0_
  18.7 0.6 %mate_edges.2 = (f32[576,128]{1,0:T(8,128)S(1)}, f32[576,128]{1,0:T(8,128)S(1)}) custom-call(f32[4,128]{1,0:T(4,128)S(1)} %get-tuple-element.47.params, bf16[128,512]{1,0:T(8,128)(2,1)S(1)} %get-tuple-element.49.weight.proj_weight, bf16[576,128]{1,0:T(8,128)(2,1)S(1)} %collective-permute-done.5.refs_0_), custom_call_target="tpu_custom_call" | custom-call | flops 1000000000 | tf_op jit(solution)/shard_map/mate_edges/pallas_call | solution.py:423
  19.3 0.1 collective-permute-done.6.refs_0_
  19.4 0.6 %mate_edges.3 = (f32[576,128]{1,0:T(8,128)S(1)}, f32[576,128]{1,0:T(8,128)S(1)}) custom-call(f32[4,128]{1,0:T(4,128)S(1)} %get-tuple-element.47.params, bf16[128,512]{1,0:T(8,128)(2,1)S(1)} %get-tuple-element.49.weight.proj_weight, bf16[576,128]{1,0:T(8,128)(2,1)S(1)} %collective-permute-done.6.refs_0_), custom_call_target="tpu_custom_call" | custom-call | flops 1000000000 | tf_op jit(solution)/shard_map/mate_edges/pallas_call | solution.py:423
  20.0 2.4 %triangle.1.tri = f32[1152,128]{1,0:T(8,128)S(1)} custom-call(f32[576,128]{1,0:T(8,128)S(1)} %get-tuple-element.52.refs_0_.left_0, f32[576,128]{1,0:T(8,128)S(1)} %get-tuple-element.53.refs_1_.left_1, f32[576,128]{1,0:T(8,128)S(1)} %get-tuple-element.54.refs_2_, f32[576,128]{1,0:T(8,128)S(1)} %get-tuple-element.55.refs_3_, ...), custom_call_target="tpu_custom_call" | custom-call | flops 2000000000 | tf_op jit(solution)/shard_map/triangle/pallas_call | solution.py:423
  22.4 0.0 collective-permute-done.7.refs_3_
  22.5 1.7 %cells.1 = (bf16[144,128]{1,0:T(8,128)(2,1)S(1)}, bf16[1152,128]{1,0:T(8,128)(2,1)S(1)}, bf16[1152,128]{1,0:T(8,128)(2,1)S(1)}, bf16[1152,128]{1,0:T(8,128)(2,1)S(1)}, bf16[1152,128]{1,0:T(8,128)(2,1)S(1)}) custom-call(f32[4,128]{1,0:T(4,128)S(1)} %get-tuple-element.47.params, f32[1152,128]{1,0:T(8,128)S(1)} %triangle.1.tri, ...), custom_call_target="tpu_custom_call" | custom-call | flops 2000000000 | tf_op jit(solution)/shard_map/cells/pallas_call | solution.py:423
  24.1 0.5 %collective-permute-start.8 = (bf16[1152,128]{1,0:T(8,128)(2,1)S(1)}, bf16[1152,128]{1,0:T(8,128)(2,1)S(1)}, u32[]{:S(2)}, u32[]{:S(2)}) collective-permute-start(bf16[1152,128]{1,0:T(8,128)(2,1)S(1)} %get-tuple-element.64.d_tri_ref), channel_id=1, source_target_pairs={{0,1},{1,0},{2,3},{3,2},{4,5},{5,4},{6,7},{7,6},{8,9},{9,8},{10,11... | collective-permute-start | bytes 884744 | tf_op jit(solution)/shard_map/ppermute | solution.py:437
  24.6 2.7 %early.1 = (f32[1152,128]{1,0:T(8,128)S(1)}, f32[1152,128]{1,0:T(8,128)S(1)}, bf16[1152,128]{1,0:T(8,128)(2,1)S(1)}, f32[1152,128]{1,0:T(8,128)S(1)}, f32[576,128]{1,0:T(8,128)S(1)}, /*index=5*/f32[128,256]{1,0:T(8,128)S(1)}) custom-call(bf16[1152,128]{1,0:T(8,128)(2,1)S(1)} %get-tuple-element.64.d_tri_ref, bf16[1152,128]{1,0:T(8,128)(2,1)S(1)} %get-tuple-element.65.d_gate, ...), custom_call_target="tpu_custom_call" | custom-call | flops 30000001024 | tf_op jit(solution)/shard_map/early/pallas_call | solution.py:423
  27.3 0.1 collective-permute-start.9
  27.5 2.9 %late.1 = (f32[128,512]{1,0:T(8,128)S(1)}, bf16[1152,512]{1,0:T(8,128)(2,1)S(1)}) custom-call(bf16[1152,128]{1,0:T(8,128)(2,1)S(1)} %collective-permute-done.8.d_tri_ref, f32[1152,128]{1,0:T(8,128)S(1)} %get-tuple-element.68.left, f32[1152,128]{1,0:T(8,128)S(1)} %get-tuple-element.69.right, bf16[1152,128]{1,0:T(8,128)(2,1)S(1)} %get-tuple-element.70.normed, ...), custom_call_target="tpu_custom_call" | custom-call | flops 40000000000 | tf_op jit(solution)/shard_map/late/pallas_call | solution.py:423
  30.3 0.5 %collective-permute-start.10 = (f32[128,512]{1,0:T(8,128)S(1)}, f32[128,512]{1,0:T(8,128)S(1)}, u32[]{:S(2)}, u32[]{:S(2)}) collective-permute-start(f32[128,512]{1,0:T(8,128)S(1)} %get-tuple-element.86), channel_id=1, source_target_pairs={{0,1},{1,0},{2,3},{3,2},{4,5},{5,4},{6,7},{7,6},{8,9},{9,8},{10,11... | collective-permute-start | bytes 786440 | tf_op jit(solution)/shard_map/ppermute | solution.py:437
  30.8 0.0 collective-permute-done.9.small_mate
  30.9 1.0 %outputs.1 = (bf16[144,128]{1,0:T(8,128)(2,1)}, f32[144,128]{1,0:T(8,128)}, f32[128,128]{1,0:T(8,128)}, f32[128,128]{1,0:T(8,128)}) custom-call(f32[4,128]{1,0:T(4,128)S(1)} %get-tuple-element.47.params, bf16[144,128]{1,0:T(8,128)(2,1)S(1)} %get-tuple-element.98.refs_0_.pair, bf16[1152,512]{1,0:T(8,128)(2,1)S(1)} %get-tuple-element.81.d_proj, ...), custom_call_target="tpu_custom_call" | custom-call | flops 10000000000 | tf_op jit(solution)/shard_map/outputs/pallas_call | solution.py:423
  31.8 0.2 collective-permute-done.10
  32.0 0.7 %add.3 = f32[128,512]{1,0:T(8,128)} add(f32[128,512]{1,0:T(8,128)S(1)} %get-tuple-element.86, f32[128,512]{1,0:T(8,128)S(1)} %collective-permute-done.10) | non-fusion elementwise | flops 65536 | bytes 786432 | tf_op jit(solution)/shard_map/add | solution.py:578
  (9 shorter events, 0.1 us)
Async XLA Ops:
  1.7 7.9 %collective-permute-start.2 = (bf16[288,128]{1,0:T(8,128)(2,1)S(1)}, bf16[288,128]{1,0:T(8,128)(2,1)S(1)}, u32[]{:S(2)}, u32[]{:S(2)}) collective-permute-start(bf16[288,128]{1,0:T(8,128)(2,1)S(1)} %get-tuple-element.48), channel_id=1, source_target_pairs={{0,12},{2,14},{4,8},{6,10},{8,4},{10,6},{12,0},{14,2},{1,13},{3,15... | collective-permute-start | bytes 221192 | tf_op jit(solution)/shard_map/ppermute | solution.py:434
  6.9 6.2 %collective-permute-start.1 = (bf16[288,128]{1,0:T(8,128)(2,1)S(1)}, bf16[288,128]{1,0:T(8,128)(2,1)S(1)}, u32[]{:S(2)}, u32[]{:S(2)}) collective-permute-start(bf16[288,128]{1,0:T(8,128)(2,1)S(1)} %get-tuple-element.48), channel_id=1, source_target_pairs={{0,8},{2,10},{4,12},{6,14},{8,0},{10,2},{12,4},{14,6},{1,9},{3,11}... | collective-permute-start | bytes 221192 | tf_op jit(solution)/shard_map/ppermute | solution.py:434
  6.9 6.2 %collective-permute-start = (bf16[288,128]{1,0:T(8,128)(2,1)S(1)}, bf16[288,128]{1,0:T(8,128)(2,1)S(1)}, u32[]{:S(2)}, u32[]{:S(2)}) collective-permute-start(bf16[288,128]{1,0:T(8,128)(2,1)S(1)} %get-tuple-element.48), channel_id=1, source_target_pairs={{0,4},{2,6},{4,0},{6,2},{8,12},{10,14},{12,8},{14,10},{1,5},{3,7},... | collective-permute-start | bytes 221192 | tf_op jit(solution)/shard_map/ppermute | solution.py:434
  7.5 7.9 %collective-permute-start.3 = (bf16[288,128]{1,0:T(8,128)(2,1)S(1)}, bf16[288,128]{1,0:T(8,128)(2,1)S(1)}, u32[]{:S(2)}, u32[]{:S(2)}) collective-permute-start(bf16[288,128]{1,0:T(8,128)(2,1)S(1)} %get-tuple-element.48), channel_id=1, source_target_pairs={{0,2},{2,0},{4,6},{6,4},{8,10},{10,8},{12,14},{14,12},{1,3},{3,1},... | collective-permute-start | bytes 221192 | tf_op jit(solution)/shard_map/ppermute | solution.py:434
  13.1 4.8 %collective-permute-start.4 = (bf16[432,128]{1,0:T(8,128)(2,1)S(1)}, bf16[432,128]{1,0:T(8,128)(2,1)S(1)}, u32[]{:S(2)}, u32[]{:S(2)}) collective-permute-start(bf16[432,128]{1,0:T(8,128)(2,1)S(1)} %pad_maximum_fusion.2.refs_1_), channel_id=1, source_target_pairs={{0,2},{2,0},{4,6},{6,4},{8,10},{10,8},{12,14},{14,12},{1,3},{3,1},... | collective-permute-start | bytes 331784 | tf_op jit(solution)/shard_map/ppermute | solution.py:434
  14.7 4.0 %collective-permute-start.5 = (bf16[576,128]{1,0:T(8,128)(2,1)S(1)}, bf16[576,128]{1,0:T(8,128)(2,1)S(1)}, u32[]{:S(2)}, u32[]{:S(2)}) collective-permute-start(bf16[576,128]{1,0:T(8,128)(2,1)S(1)} %pad_maximum_fusion.1), channel_id=1, source_target_pairs={{0,1},{1,0},{2,3},{3,2},{4,5},{5,4},{6,7},{7,6},{8,9},{9,8},{10,11... | collective-permute-start | bytes 442376 | tf_op jit(solution)/shard_map/ppermute | solution.py:437
  14.8 7.6 %collective-permute-start.7 = (bf16[432,128]{1,0:T(8,128)(2,1)S(1)}, bf16[432,128]{1,0:T(8,128)(2,1)S(1)}, u32[]{:S(2)}, u32[]{:S(2)}) collective-permute-start(bf16[432,128]{1,0:T(8,128)(2,1)S(1)} %pad_maximum_fusion.3.refs_1_), channel_id=1, source_target_pairs={{0,2},{2,0},{4,6},{6,4},{8,10},{10,8},{12,14},{14,12},{1,3},{3,1},... | collective-permute-start | bytes 331784 | tf_op jit(solution)/shard_map/ppermute | solution.py:434
  18.0 1.4 %collective-permute-start.6 = (bf16[576,128]{1,0:T(8,128)(2,1)S(1)}, bf16[576,128]{1,0:T(8,128)(2,1)S(1)}, u32[]{:S(2)}, u32[]{:S(2)}) collective-permute-start(bf16[576,128]{1,0:T(8,128)(2,1)S(1)} %pad_maximum_fusion.refs_0_), channel_id=1, source_target_pairs={{0,1},{1,0},{2,3},{3,2},{4,5},{5,4},{6,7},{7,6},{8,9},{9,8},{10,11... | collective-permute-start | bytes 442376 | tf_op jit(solution)/shard_map/ppermute | solution.py:437
  24.1 3.4 %collective-permute-start.8 = (bf16[1152,128]{1,0:T(8,128)(2,1)S(1)}, bf16[1152,128]{1,0:T(8,128)(2,1)S(1)}, u32[]{:S(2)}, u32[]{:S(2)}) collective-permute-start(bf16[1152,128]{1,0:T(8,128)(2,1)S(1)} %get-tuple-element.64.d_tri_ref), channel_id=1, source_target_pairs={{0,1},{1,0},{2,3},{3,2},{4,5},{5,4},{6,7},{7,6},{8,9},{9,8},{10,11... | collective-permute-start | bytes 884744 | tf_op jit(solution)/shard_map/ppermute | solution.py:437
  27.3 3.5 %collective-permute-start.9 = (f32[128,256]{1,0:T(8,128)S(1)}, f32[128,256]{1,0:T(8,128)S(1)}, u32[]{:S(2)}, u32[]{:S(2)}) collective-permute-start(f32[128,256]{1,0:T(8,128)S(1)} %get-tuple-element.83.small_own), channel_id=1, source_target_pairs={{0,1},{1,0},{2,3},{3,2},{4,5},{5,4},{6,7},{7,6},{8,9},{9,8},{10,11... | collective-permute-start | bytes 393224 | tf_op jit(solution)/shard_map/ppermute | solution.py:437
  30.3 1.7 %collective-permute-start.10 = (f32[128,512]{1,0:T(8,128)S(1)}, f32[128,512]{1,0:T(8,128)S(1)}, u32[]{:S(2)}, u32[]{:S(2)}) collective-permute-start(f32[128,512]{1,0:T(8,128)S(1)} %get-tuple-element.86), channel_id=1, source_target_pairs={{0,1},{1,0},{2,3},{3,2},{4,5},{5,4},{6,7},{7,6},{8,9},{9,8},{10,11... | collective-permute-start | bytes 786440 | tf_op jit(solution)/shard_map/ppermute | solution.py:437

commit v9 on v8

--- a/solution.py
+++ b/solution.py
@@ -436,12 +436,11 @@
     def over(value):
         return lax.ppermute(value, "col", SWAP)
 
-    def along(value, tied=False):
-        got = []
-        for s in reversed(range(1, groups // 2)):
-            arrived = across(value, 2 * s)
-            got.append(after(arrived, got[-1]) if got and tied else arrived)
-        return got[::-1]
+    def along(value, last):
+        got = [last]
+        for s in reversed(range(1, groups // 2 - 1)):
+            got.append(after(across(value, 2 * s), got[-1]))
+        return got[:0:-1]
 
     def join(*values):
         return jnp.concatenate(values, axis=0)
@@ -459,7 +458,10 @@
         outs = [(part, F32)] * 2
         return call(mate_edges_kernel, outs, params, proj_weight, *blocks, name="mate_edges")
 
-    given = [pair_rep.reshape(cells, channels), cotangent.reshape(cells, channels)]
+    pair_in = pair_rep.reshape(cells, channels)
+    span = groups - 2
+    pair_last = across(pair_in, span)
+    given = [pair_in, cotangent.reshape(cells, channels)]
     given += [v[None] for v in (norm_gain, norm_bias, tri_gain, tri_bias)]
     given += [proj_weight, gate_weight, out_weight]
     given = [pltpu.with_memory_space_constraint(v, pltpu.HBM) for v in given]
@@ -471,13 +473,14 @@
         in_specs=[pl.BlockSpec(memory_space=pltpu.HBM)] * len(given),
         name="fetch",
     )
-    got = along(both, tied=True)
+    got = along(both, pair_last)
     both_far = across(both, 1)
     pair, pair_far = both[:cells], both_far[:cells]
     cot_0, cot_1 = both[cells:], both_far[cells:]
-    near_all = join(*(block[:cells] for block in got))
+    near_all = join(*(block[:cells] for block in got), pair_last)
     far = across(near_all, 1)
-    cot_near = join(*(block[cells:] for block in got))
+    cot_last = across(cot_0, span)
+    cot_near = join(*(block[cells:] for block in got), cot_last)
     cot_far = across(cot_near, 1)
     mate_near = over(join(pair, near_all))
     own_0 = own_edges(pair, near_all)
@@ -678,7 +681,7 @@
     groups = lax.axis_size("row")
     every = rows * groups * cols
     fits = 24 * every * channels * 4 <= VMEM_BUDGET and hidden == channels
-    paired = lax.axis_size("col") == 2 and groups & (groups - 1) == 0 and groups >= 2
+    paired = lax.axis_size("col") == 2 and groups & (groups - 1) == 0 and groups >= 4
     whole_tiles = cols % 8 == 0 and cols % (2 * rows) == 0 and rows * cols % 16 == 0
     plan = replicated if fits and paired and whole_tiles else sharded
     return plan(pair_rep, *others)

time: 33 us -> 33 us (level)
  starting transfers between devices: 10.9 us -> 14.6 us
  waiting for transfers between devices: 6.06 us -> 2.4 us
    ppermute x6 -> x7, starting transfers between devices: 9.58 us -> 13.3 us  [across(): return lax.ppermute(value, 'row', [(i, i ^ mask) for i in range(groups)])]
    ppermute x6 -> x7, waiting for transfers between devices: 5.81 us -> 2.15 us  [across(): return lax.ppermute(value, 'row', [(i, i ^ mask) for i in range(groups)])]
  transfers between devices with their start and end apart: 11 -> 12, of which waited for: 5 -> 5; matrix products, arithmetic and copies ran while one was open for 0% -> 0% of each run, Pallas kernels for 35% -> 38%
where the time goes in v9:
time: 33 us; the launch traced here: 32.8 us
  starting transfers between devices  14.6 us (44%)
  Pallas kernels  14.2 us (43%)
  waiting for transfers between devices  2.4 us (7%)
  other arithmetic  0.78 us (2%)
  between operations  0.77 us (2%)
    pallas_call x10, Pallas kernels, call(): pl.pallas_call(functools.partial(kernel, sizes), out_shape=[jax.ShapeDtyp...  14.2 us
    ppermute x7, starting transfers between devices, across(): return lax.ppermute(value, 'row', [(i, i ^ mask) for i in range(groups)])  13.3 us
    ppermute x7, waiting for transfers between devices, across(): return lax.ppermute(value, 'row', [(i, i ^ mask) for i in range(groups)])  2.15 us
    ppermute x5, starting transfers between devices, over(): return lax.ppermute(value, 'col', SWAP)  1.29 us
    add x1, other arithmetic, replicated(): proj_grad + proj_mate  0.74 us
  transfers between devices with their start and end apart: 12, of which 5 were waited for; matrix products, arithmetic and copies ran while one was open for 0% of the time, Pallas kernels for 38%

profile of v9, /device:TPU:0, one launch (start us, length us, event | category | flops | bytes accessed | tf_op | source)
XLA Modules:
  0.0 32.8 jit_solution(928800393558913013)
XLA Ops:
  0.6 5.1 %collective-permute-start.2 = (bf16[144,128]{1,0:T(8,128)(2,1)}, bf16[144,128]{1,0:T(8,128)(2,1)S(1)}, u32[]{:S(2)}, u32[]{:S(2)}) collective-permute-start(bf16[144,128]{1,0:T(8,128)(2,1)} %bitcast.9), channel_id=1, source_target_pairs={{0,12},{2,14},{4,8},{6,10},{8,4},{10,6},{12,0},{14,2},{1,13},{3,15... | collective-permute-start | bytes 110600 | tf_op jit(solution)/shard_map/ppermute | solution.py:434
  5.7 1.1 %fetch.1 = (bf16[288,128]{1,0:T(8,128)(2,1)S(1)}, f32[4,128]{1,0:T(4,128)S(1)}, bf16[128,512]{1,0:T(8,128)(2,1)S(1)}, bf16[128,128]{1,0:T(8,128)(2,1)S(1)}, bf16[128,128]{1,0:T(8,128)(2,1)S(1)}) custom-call(bf16[144,128]{1,0:T(8,128)(2,1)} %bitcast.10, bf16[144,128]{1,0:T(8,128)(2,1)} %bitcast.8, f32[1,128]{1,0:T(1,128)} %bitcast.11, f32[1,128]{1,0:T(1,128)} %bitcast.12, ...), custom_call_target="tpu_custom_call" | custom-call | flops 1000000000 | tf_op jit(solution)/shard_map/fetch/pallas_call | solution.py:423
  6.8 0.1 collective-permute-start.1
  6.9 0.6 %collective-permute-start = (bf16[288,128]{1,0:T(8,128)(2,1)S(1)}, bf16[288,128]{1,0:T(8,128)(2,1)S(1)}, u32[]{:S(2)}, u32[]{:S(2)}) collective-permute-start(bf16[288,128]{1,0:T(8,128)(2,1)S(1)} %get-tuple-element.48), channel_id=1, source_target_pairs={{0,4},{2,6},{4,0},{6,2},{8,12},{10,14},{12,8},{14,10},{1,5},{3,7},... | collective-permute-start | bytes 221192 | tf_op jit(solution)/shard_map/ppermute | solution.py:434
  7.5 1.7 %collective-permute-start.3 = (bf16[288,128]{1,0:T(8,128)(2,1)S(1)}, bf16[288,128]{1,0:T(8,128)(2,1)S(1)}, u32[]{:S(2)}, u32[]{:S(2)}) collective-permute-start(bf16[288,128]{1,0:T(8,128)(2,1)S(1)} %get-tuple-element.48), channel_id=1, source_target_pairs={{0,2},{2,0},{4,6},{6,4},{8,10},{10,8},{12,14},{14,12},{1,3},{3,1},... | collective-permute-start | bytes 221192 | tf_op jit(solution)/shard_map/ppermute | solution.py:434
  9.2 3.6 %collective-permute-start.7 = (bf16[144,128]{1,0:T(8,128)(2,1)S(1)}, bf16[144,128]{1,0:T(8,128)(2,1)S(1)}, u32[]{:S(2)}, u32[]{:S(2)}) collective-permute-start(bf16[144,128]{1,0:T(8,128)(2,1)S(1)} %get-tuple-element.95.refs_0_), channel_id=1, source_target_pairs={{0,12},{2,14},{4,8},{6,10},{8,4},{10,6},{12,0},{14,2},{1,13},{3,15... | collective-permute-start | bytes 110600 | tf_op jit(solution)/shard_map/ppermute | solution.py:434
  12.8 0.3 collective-permute-done.1
  13.1 0.0 collective-permute-done
  13.2 1.6 %collective-permute-start.4 = (bf16[432,128]{1,0:T(8,128)(2,1)S(1)}, bf16[432,128]{1,0:T(8,128)(2,1)S(1)}, u32[]{:S(2)}, u32[]{:S(2)}) collective-permute-start(bf16[432,128]{1,0:T(8,128)(2,1)S(1)} %pad_maximum_fusion.2.refs_1_), channel_id=1, source_target_pairs={{0,2},{2,0},{4,6},{6,4},{8,10},{10,8},{12,14},{14,12},{1,3},{3,1},... | collective-permute-start | bytes 331784 | tf_op jit(solution)/shard_map/ppermute | solution.py:434
  14.8 0.1 collective-permute-start.5
  14.8 0.1 collective-permute-done.7
  15.0 0.6 %collective-permute-start.8 = (bf16[432,128]{1,0:T(8,128)(2,1)S(1)}, bf16[432,128]{1,0:T(8,128)(2,1)S(1)}, u32[]{:S(2)}, u32[]{:S(2)}) collective-permute-start(bf16[432,128]{1,0:T(8,128)(2,1)S(1)} %pad_maximum_fusion.3.refs_1_), channel_id=1, source_target_pairs={{0,2},{2,0},{4,6},{6,4},{8,10},{10,8},{12,14},{14,12},{1,3},{3,1},... | collective-permute-start | bytes 331784 | tf_op jit(solution)/shard_map/ppermute | solution.py:434
  15.6 0.0 collective-permute-done.3
  15.6 0.6 %own_edges.2 = (bf16[576,128]{1,0:T(8,128)(2,1)S(1)}, f32[576,128]{1,0:T(8,128)S(1)}, f32[576,128]{1,0:T(8,128)S(1)}, f32[576,128]{1,0:T(8,128)S(1)}, f32[576,12...) custom-call(f32[4,128]{1,0:T(4,128)S(1)} %get-tuple-element.47.params, ...), custom_call_target="tpu_custom_call" | custom-call | flops 1000000000 | tf_op jit(solution)/shard_map/own_edges/pallas_call | solution.py:423
  16.3 1.7 %collective-permute-done.4 = bf16[432,128]{1,0:T(8,128)(2,1)S(1)} collective-permute-done((bf16[432,128]{1,0:T(8,128)(2,1)S(1)}, bf16[432,128]{1,0:T(8,128)(2,1)S(1)}, u32[]{:S(2)}, u32[]{:S(2)}) %collective-permute-start.4) | collective-permute-done | bytes 110624 | tf_op jit(solution)/shard_map/ppermute | solution.py:434
  18.0 0.1 collective-permute-start.6
  18.1 0.6 %own_edges.3 = (bf16[576,128]{1,0:T(8,128)(2,1)S(1)}, f32[576,128]{1,0:T(8,128)S(1)}, f32[576,128]{1,0:T(8,128)S(1)}, f32[576,128]{1,0:T(8,128)S(1)}, f32[576,12...) custom-call(f32[4,128]{1,0:T(4,128)S(1)} %get-tuple-element.47.params, ...), custom_call_target="tpu_custom_call" | custom-call | flops 1000000000 | tf_op jit(solution)/shard_map/own_edges/pallas_call | solution.py:423
  18.7 0.6 %mate_edges.2 = (f32[576,128]{1,0:T(8,128)S(1)}, f32[576,128]{1,0:T(8,128)S(1)}) custom-call(f32[4,128]{1,0:T(4,128)S(1)} %get-tuple-element.47.params, bf16[128,512]{1,0:T(8,128)(2,1)S(1)} %get-tuple-element.49.weight.proj_weight, bf16[576,128]{1,0:T(8,128)(2,1)S(1)} %collective-permute-done.5.refs_0_), custom_call_target="tpu_custom_call" | custom-call | flops 1000000000 | tf_op jit(solution)/shard_map/mate_edges/pallas_call | solution.py:423
  19.4 0.1 collective-permute-done.6.refs_0_
  19.4 0.6 %mate_edges.3 = (f32[576,128]{1,0:T(8,128)S(1)}, f32[576,128]{1,0:T(8,128)S(1)}) custom-call(f32[4,128]{1,0:T(4,128)S(1)} %get-tuple-element.47.params, bf16[128,512]{1,0:T(8,128)(2,1)S(1)} %get-tuple-element.49.weight.proj_weight, bf16[576,128]{1,0:T(8,128)(2,1)S(1)} %collective-permute-done.6.refs_0_), custom_call_target="tpu_custom_call" | custom-call | flops 1000000000 | tf_op jit(solution)/shard_map/mate_edges/pallas_call | solution.py:423
  20.1 2.4 %triangle.1.tri = f32[1152,128]{1,0:T(8,128)S(1)} custom-call(f32[576,128]{1,0:T(8,128)S(1)} %get-tuple-element.52.refs_0_.left_0, f32[576,128]{1,0:T(8,128)S(1)} %get-tuple-element.53.refs_1_.left_1, f32[576,128]{1,0:T(8,128)S(1)} %get-tuple-element.54.refs_2_, f32[576,128]{1,0:T(8,128)S(1)} %get-tuple-element.55.refs_3_, ...), custom_call_target="tpu_custom_call" | custom-call | flops 2000000000 | tf_op jit(solution)/shard_map/triangle/pallas_call | solution.py:423
  22.5 0.0 collective-permute-done.8.refs_3_
  22.5 1.7 %cells.1 = (bf16[144,128]{1,0:T(8,128)(2,1)S(1)}, bf16[1152,128]{1,0:T(8,128)(2,1)S(1)}, bf16[1152,128]{1,0:T(8,128)(2,1)S(1)}, bf16[1152,128]{1,0:T(8,128)(2,1)S(1)}, bf16[1152,128]{1,0:T(8,128)(2,1)S(1)}) custom-call(f32[4,128]{1,0:T(4,128)S(1)} %get-tuple-element.47.params, f32[1152,128]{1,0:T(8,128)S(1)} %triangle.1.tri, ...), custom_call_target="tpu_custom_call" | custom-call | flops 2000000000 | tf_op jit(solution)/shard_map/cells/pallas_call | solution.py:423
  24.2 0.5 %collective-permute-start.9 = (bf16[1152,128]{1,0:T(8,128)(2,1)S(1)}, bf16[1152,128]{1,0:T(8,128)(2,1)S(1)}, u32[]{:S(2)}, u32[]{:S(2)}) collective-permute-start(bf16[1152,128]{1,0:T(8,128)(2,1)S(1)} %get-tuple-element.64.d_tri_ref), channel_id=1, source_target_pairs={{0,1},{1,0},{2,3},{3,2},{4,5},{5,4},{6,7},{7,6},{8,9},{9,8},{10,11... | collective-permute-start | bytes 884744 | tf_op jit(solution)/shard_map/ppermute | solution.py:437
  24.7 2.7 %early.1 = (f32[1152,128]{1,0:T(8,128)S(1)}, f32[1152,128]{1,0:T(8,128)S(1)}, bf16[1152,128]{1,0:T(8,128)(2,1)S(1)}, f32[1152,128]{1,0:T(8,128)S(1)}, f32[576,128]{1,0:T(8,128)S(1)}, /*index=5*/f32[128,256]{1,0:T(8,128)S(1)}) custom-call(bf16[1152,128]{1,0:T(8,128)(2,1)S(1)} %get-tuple-element.64.d_tri_ref, bf16[1152,128]{1,0:T(8,128)(2,1)S(1)} %get-tuple-element.65.d_gate, ...), custom_call_target="tpu_custom_call" | custom-call | flops 30000001024 | tf_op jit(solution)/shard_map/early/pallas_call | solution.py:423
  27.4 0.1 collective-permute-start.10
  27.5 0.0 collective-permute-done.9.d_tri_ref
  27.5 2.9 %late.1 = (f32[128,512]{1,0:T(8,128)S(1)}, bf16[1152,512]{1,0:T(8,128)(2,1)S(1)}) custom-call(bf16[1152,128]{1,0:T(8,128)(2,1)S(1)} %collective-permute-done.9.d_tri_ref, f32[1152,128]{1,0:T(8,128)S(1)} %get-tuple-element.68.left, f32[1152,128]{1,0:T(8,128)S(1)} %get-tuple-element.69.right, bf16[1152,128]{1,0:T(8,128)(2,1)S(1)} %get-tuple-element.70.normed, ...), custom_call_target="tpu_custom_call" | custom-call | flops 40000000000 | tf_op jit(solution)/shard_map/late/pallas_call | solution.py:423
  30.4 0.5 %collective-permute-start.11 = (f32[128,512]{1,0:T(8,128)S(1)}, f32[128,512]{1,0:T(8,128)S(1)}, u32[]{:S(2)}, u32[]{:S(2)}) collective-permute-start(f32[128,512]{1,0:T(8,128)S(1)} %get-tuple-element.86), channel_id=1, source_target_pairs={{0,1},{1,0},{2,3},{3,2},{4,5},{5,4},{6,7},{7,6},{8,9},{9,8},{10,11... | collective-permute-start | bytes 786440 | tf_op jit(solution)/shard_map/ppermute | solution.py:437
  30.9 1.0 %outputs.1 = (bf16[144,128]{1,0:T(8,128)(2,1)}, f32[144,128]{1,0:T(8,128)}, f32[128,128]{1,0:T(8,128)}, f32[128,128]{1,0:T(8,128)}) custom-call(f32[4,128]{1,0:T(4,128)S(1)} %get-tuple-element.47.params, bf16[144,128]{1,0:T(8,128)(2,1)S(1)} %get-tuple-element.96.refs_0_.pair, bf16[1152,512]{1,0:T(8,128)(2,1)S(1)} %get-tuple-element.81.d_proj, ...), custom_call_target="tpu_custom_call" | custom-call | flops 10000000000 | tf_op jit(solution)/shard_map/outputs/pallas_call | solution.py:423
  31.9 0.2 collective-permute-done.11
  32.1 0.7 %add.3 = f32[128,512]{1,0:T(8,128)} add(f32[128,512]{1,0:T(8,128)S(1)} %get-tuple-element.86, f32[128,512]{1,0:T(8,128)S(1)} %collective-permute-done.11) | non-fusion elementwise | flops 65536 | bytes 786432 | tf_op jit(solution)/shard_map/add | solution.py:581
  (10 shorter events, 0.1 us)
Async XLA Ops:
  0.6 12.2 %collective-permute-start.2 = (bf16[144,128]{1,0:T(8,128)(2,1)}, bf16[144,128]{1,0:T(8,128)(2,1)S(1)}, u32[]{:S(2)}, u32[]{:S(2)}) collective-permute-start(bf16[144,128]{1,0:T(8,128)(2,1)} %bitcast.9), channel_id=1, source_target_pairs={{0,12},{2,14},{4,8},{6,10},{8,4},{10,6},{12,0},{14,2},{1,13},{3,15... | collective-permute-start | bytes 110600 | tf_op jit(solution)/shard_map/ppermute | solution.py:434
  6.8 6.3 %collective-permute-start.1 = (bf16[288,128]{1,0:T(8,128)(2,1)S(1)}, bf16[288,128]{1,0:T(8,128)(2,1)S(1)}, u32[]{:S(2)}, u32[]{:S(2)}) collective-permute-start(bf16[288,128]{1,0:T(8,128)(2,1)S(1)} %get-tuple-element.48), channel_id=1, source_target_pairs={{0,8},{2,10},{4,12},{6,14},{8,0},{10,2},{12,4},{14,6},{1,9},{3,11}... | collective-permute-start | bytes 221192 | tf_op jit(solution)/shard_map/ppermute | solution.py:434
  6.9 6.2 %collective-permute-start = (bf16[288,128]{1,0:T(8,128)(2,1)S(1)}, bf16[288,128]{1,0:T(8,128)(2,1)S(1)}, u32[]{:S(2)}, u32[]{:S(2)}) collective-permute-start(bf16[288,128]{1,0:T(8,128)(2,1)S(1)} %get-tuple-element.48), channel_id=1, source_target_pairs={{0,4},{2,6},{4,0},{6,2},{8,12},{10,14},{12,8},{14,10},{1,5},{3,7},... | collective-permute-start | bytes 221192 | tf_op jit(solution)/shard_map/ppermute | solution.py:434
  7.5 8.1 %collective-permute-start.3 = (bf16[288,128]{1,0:T(8,128)(2,1)S(1)}, bf16[288,128]{1,0:T(8,128)(2,1)S(1)}, u32[]{:S(2)}, u32[]{:S(2)}) collective-permute-start(bf16[288,128]{1,0:T(8,128)(2,1)S(1)} %get-tuple-element.48), channel_id=1, source_target_pairs={{0,2},{2,0},{4,6},{6,4},{8,10},{10,8},{12,14},{14,12},{1,3},{3,1},... | collective-permute-start | bytes 221192 | tf_op jit(solution)/shard_map/ppermute | solution.py:434
  9.2 5.8 %collective-permute-start.7 = (bf16[144,128]{1,0:T(8,128)(2,1)S(1)}, bf16[144,128]{1,0:T(8,128)(2,1)S(1)}, u32[]{:S(2)}, u32[]{:S(2)}) collective-permute-start(bf16[144,128]{1,0:T(8,128)(2,1)S(1)} %get-tuple-element.95.refs_0_), channel_id=1, source_target_pairs={{0,12},{2,14},{4,8},{6,10},{8,4},{10,6},{12,0},{14,2},{1,13},{3,15... | collective-permute-start | bytes 110600 | tf_op jit(solution)/shard_map/ppermute | solution.py:434
  13.2 4.8 %collective-permute-start.4 = (bf16[432,128]{1,0:T(8,128)(2,1)S(1)}, bf16[432,128]{1,0:T(8,128)(2,1)S(1)}, u32[]{:S(2)}, u32[]{:S(2)}) collective-permute-start(bf16[432,128]{1,0:T(8,128)(2,1)S(1)} %pad_maximum_fusion.2.refs_1_), channel_id=1, source_target_pairs={{0,2},{2,0},{4,6},{6,4},{8,10},{10,8},{12,14},{14,12},{1,3},{3,1},... | collective-permute-start | bytes 331784 | tf_op jit(solution)/shard_map/ppermute | solution.py:434
  14.8 4.0 %collective-permute-start.5 = (bf16[576,128]{1,0:T(8,128)(2,1)S(1)}, bf16[576,128]{1,0:T(8,128)(2,1)S(1)}, u32[]{:S(2)}, u32[]{:S(2)}) collective-permute-start(bf16[576,128]{1,0:T(8,128)(2,1)S(1)} %pad_maximum_fusion.1), channel_id=1, source_target_pairs={{0,1},{1,0},{2,3},{3,2},{4,5},{5,4},{6,7},{7,6},{8,9},{9,8},{10,11... | collective-permute-start | bytes 442376 | tf_op jit(solution)/shard_map/ppermute | solution.py:437
  15.0 7.5 %collective-permute-start.8 = (bf16[432,128]{1,0:T(8,128)(2,1)S(1)}, bf16[432,128]{1,0:T(8,128)(2,1)S(1)}, u32[]{:S(2)}, u32[]{:S(2)}) collective-permute-start(bf16[432,128]{1,0:T(8,128)(2,1)S(1)} %pad_maximum_fusion.3.refs_1_), channel_id=1, source_target_pairs={{0,2},{2,0},{4,6},{6,4},{8,10},{10,8},{12,14},{14,12},{1,3},{3,1},... | collective-permute-start | bytes 331784 | tf_op jit(solution)/shard_map/ppermute | solution.py:434
  18.0 1.4 %collective-permute-start.6 = (bf16[576,128]{1,0:T(8,128)(2,1)S(1)}, bf16[576,128]{1,0:T(8,128)(2,1)S(1)}, u32[]{:S(2)}, u32[]{:S(2)}) collective-permute-start(bf16[576,128]{1,0:T(8,128)(2,1)S(1)} %pad_maximum_fusion.refs_0_), channel_id=1, source_target_pairs={{0,1},{1,0},{2,3},{3,2},{4,5},{5,4},{6,7},{7,6},{8,9},{9,8},{10,11... | collective-permute-start | bytes 442376 | tf_op jit(solution)/shard_map/ppermute | solution.py:437
  24.2 3.4 %collective-permute-start.9 = (bf16[1152,128]{1,0:T(8,128)(2,1)S(1)}, bf16[1152,128]{1,0:T(8,128)(2,1)S(1)}, u32[]{:S(2)}, u32[]{:S(2)}) collective-permute-start(bf16[1152,128]{1,0:T(8,128)(2,1)S(1)} %get-tuple-element.64.d_tri_ref), channel_id=1, source_target_pairs={{0,1},{1,0},{2,3},{3,2},{4,5},{5,4},{6,7},{7,6},{8,9},{9,8},{10,11... | collective-permute-start | bytes 884744 | tf_op jit(solution)/shard_map/ppermute | solution.py:437
  27.4 3.5 %collective-permute-start.10 = (f32[128,256]{1,0:T(8,128)S(1)}, f32[128,256]{1,0:T(8,128)S(1)}, u32[]{:S(2)}, u32[]{:S(2)}) collective-permute-start(f32[128,256]{1,0:T(8,128)S(1)} %get-tuple-element.83.small_own), channel_id=1, source_target_pairs={{0,1},{1,0},{2,3},{3,2},{4,5},{5,4},{6,7},{7,6},{8,9},{9,8},{10,11... | collective-permute-start | bytes 393224 | tf_op jit(solution)/shard_map/ppermute | solution.py:437
  30.4 1.7 %collective-permute-start.11 = (f32[128,512]{1,0:T(8,128)S(1)}, f32[128,512]{1,0:T(8,128)S(1)}, u32[]{:S(2)}, u32[]{:S(2)}) collective-permute-start(f32[128,512]{1,0:T(8,128)S(1)} %get-tuple-element.86), channel_id=1, source_target_pairs={{0,1},{1,0},{2,3},{3,2},{4,5},{5,4},{6,7},{7,6},{8,9},{9,8},{10,11... | collective-permute-start | bytes 786440 | tf_op jit(solution)/shard_map/ppermute | solution.py:437

commit v10 on v9

--- a/solution.py
+++ b/solution.py
@@ -167,8 +167,12 @@
     gain, bias = params[2:3, :], params[3:4, :]
     for which, normed in ((0, normed_0), (1, normed_1)):
         for t, b in enumerate(places(groups)):
-            block = cots[2 * which + min(t, 1)]
-            cot = block[max(t - 1, 0) * cells : max(t, 1) * cells, :]
+            if t == 0:
+                cot = cots[2 * which][...]
+            elif t < groups // 2 - 1:
+                cot = cots[2 * which + 1][(t - 1) * cells : t * cells, :]
+            else:
+                cot = cots[4][which * cells : (which + 1) * cells, :]
             place = at(row_block(which, b), cells)
             tri_f, hat, inverse = layer_norm(tri[place, :], gain, bias)
             tri_norm = tri_f.astype(BF16)
@@ -479,9 +483,9 @@
     cot_0, cot_1 = both[cells:], both_far[cells:]
     near_all = join(*(block[:cells] for block in got), pair_last)
     far = across(near_all, 1)
-    cot_last = across(cot_0, span)
-    cot_near = join(*(block[cells:] for block in got), cot_last)
+    cot_near = join(*(block[cells:] for block in got))
     cot_far = across(cot_near, 1)
+    cot_last = across(after(join(cot_0, cot_1), near_all), span)
     mate_near = over(join(pair, near_all))
     own_0 = own_edges(pair, near_all)
     mate_0 = mate_edges(mate_near)
@@ -515,6 +519,7 @@
         cot_near,
         cot_1,
         cot_far,
+        cot_last,
         micros=2,
         name="cells",
     )

time: 33 us -> 32.9 us (level)
  starting transfers between devices: 14.6 us -> 13.4 us
  waiting for transfers between devices: 2.4 us -> 3.45 us
    ppermute x7, starting transfers between devices: 13.3 us -> 12.1 us  [across(): return lax.ppermute(value, 'row', [(i, i ^ mask) for i in range(groups)])]
    ppermute x7, waiting for transfers between devices: 2.15 us -> 3.2 us  [across(): return lax.ppermute(value, 'row', [(i, i ^ mask) for i in range(groups)])]
  transfers between devices with their start and end apart: 12 -> 12, of which waited for: 5 -> 3; matrix products, arithmetic and copies ran while one was open for 0% -> 0% of each run, Pallas kernels for 38% -> 38%
where the time goes in v10:
time: 32.9 us; the launch traced here: 32.7 us
  Pallas kernels  14.2 us (43%)
  starting transfers between devices  13.4 us (41%)
  waiting for transfers between devices  3.45 us (10%)
  between operations  0.81 us (2%)
  other arithmetic  0.79 us (2%)
    pallas_call x10, Pallas kernels, call(): pl.pallas_call(functools.partial(kernel, sizes), out_shape=[jax.ShapeDtyp...  14.2 us
    ppermute x7, starting transfers between devices, across(): return lax.ppermute(value, 'row', [(i, i ^ mask) for i in range(groups)])  12.1 us
    ppermute x7, waiting for transfers between devices, across(): return lax.ppermute(value, 'row', [(i, i ^ mask) for i in range(groups)])  3.2 us
    ppermute x5, starting transfers between devices, over(): return lax.ppermute(value, 'col', SWAP)  1.29 us
    add x1, other arithmetic, replicated(): proj_grad + proj_mate  0.74 us
  transfers between devices with their start and end apart: 12, of which 3 were waited for; matrix products, arithmetic and copies ran while one was open for 0% of the time, Pallas kernels for 38%

profile of v10, /device:TPU:0, one launch (start us, length us, event | category | flops | bytes accessed | tf_op | source)
XLA Modules:
  0.0 32.7 jit_solution(543199151920032025)
XLA Ops:
  0.6 5.1 %collective-permute-start.2 = (bf16[144,128]{1,0:T(8,128)(2,1)}, bf16[144,128]{1,0:T(8,128)(2,1)S(1)}, u32[]{:S(2)}, u32[]{:S(2)}) collective-permute-start(bf16[144,128]{1,0:T(8,128)(2,1)} %bitcast.9), channel_id=1, source_target_pairs={{0,12},{2,14},{4,8},{6,10},{8,4},{10,6},{12,0},{14,2},{1,13},{3,15... | collective-permute-start | bytes 110600 | tf_op jit(solution)/shard_map/ppermute | solution.py:438
  5.7 1.1 %fetch.1 = (bf16[288,128]{1,0:T(8,128)(2,1)S(1)}, f32[4,128]{1,0:T(4,128)S(1)}, bf16[128,512]{1,0:T(8,128)(2,1)S(1)}, bf16[128,128]{1,0:T(8,128)(2,1)S(1)}, bf16[128,128]{1,0:T(8,128)(2,1)S(1)}) custom-call(bf16[144,128]{1,0:T(8,128)(2,1)} %bitcast.10, bf16[144,128]{1,0:T(8,128)(2,1)} %bitcast.8, f32[1,128]{1,0:T(1,128)} %bitcast.11, f32[1,128]{1,0:T(1,128)} %bitcast.12, ...), custom_call_target="tpu_custom_call" | custom-call | flops 1000000000 | tf_op jit(solution)/shard_map/fetch/pallas_call | solution.py:427
  6.8 0.1 collective-permute-start.1
  6.9 0.6 %collective-permute-start = (bf16[288,128]{1,0:T(8,128)(2,1)S(1)}, bf16[288,128]{1,0:T(8,128)(2,1)S(1)}, u32[]{:S(2)}, u32[]{:S(2)}) collective-permute-start(bf16[288,128]{1,0:T(8,128)(2,1)S(1)} %get-tuple-element.49), channel_id=1, source_target_pairs={{0,4},{2,6},{4,0},{6,2},{8,12},{10,14},{12,8},{14,10},{1,5},{3,7},... | collective-permute-start | bytes 221192 | tf_op jit(solution)/shard_map/ppermute | solution.py:438
  7.5 1.7 %collective-permute-start.3 = (bf16[288,128]{1,0:T(8,128)(2,1)S(1)}, bf16[288,128]{1,0:T(8,128)(2,1)S(1)}, u32[]{:S(2)}, u32[]{:S(2)}) collective-permute-start(bf16[288,128]{1,0:T(8,128)(2,1)S(1)} %get-tuple-element.49), channel_id=1, source_target_pairs={{0,2},{2,0},{4,6},{6,4},{8,10},{10,8},{12,14},{14,12},{1,3},{3,1},... | collective-permute-start | bytes 221192 | tf_op jit(solution)/shard_map/ppermute | solution.py:438
  9.2 0.0 collective-permute-done.2
  9.2 3.2 %collective-permute-done.1 = bf16[288,128]{1,0:T(8,128)(2,1)S(1)} collective-permute-done((bf16[288,128]{1,0:T(8,128)(2,1)S(1)}, bf16[288,128]{1,0:T(8,128)(2,1)S(1)}, u32[]{:S(2)}, u32[]{:S(2)}) %collective-permute-start.1) | collective-permute-done | bytes 73760 | tf_op jit(solution)/shard_map/ppermute | solution.py:438
  12.4 0.0 collective-permute-done
  12.5 1.6 %collective-permute-start.4 = (bf16[432,128]{1,0:T(8,128)(2,1)S(1)}, bf16[432,128]{1,0:T(8,128)(2,1)S(1)}, u32[]{:S(2)}, u32[]{:S(2)}) collective-permute-start(bf16[432,128]{1,0:T(8,128)(2,1)S(1)} %pad_maximum_fusion.2.refs_1_), channel_id=1, source_target_pairs={{0,2},{2,0},{4,6},{6,4},{8,10},{10,8},{12,14},{14,12},{1,3},{3,1},... | collective-permute-start | bytes 331784 | tf_op jit(solution)/shard_map/ppermute | solution.py:438
  14.1 0.1 collective-permute-start.5
  14.1 0.0 collective-permute-done.3
  14.2 2.0 %collective-permute-start.8 = (bf16[288,128]{1,0:T(8,128)(2,1)S(1)}, bf16[288,128]{1,0:T(8,128)(2,1)S(1)}, u32[]{:S(2)}, u32[]{:S(2)}) collective-permute-start(bf16[288,128]{1,0:T(8,128)(2,1)S(1)} %pad_maximum_fusion.4), channel_id=1, source_target_pairs={{0,12},{2,14},{4,8},{6,10},{8,4},{10,6},{12,0},{14,2},{1,13},{3,15... | collective-permute-start | bytes 221192 | tf_op jit(solution)/shard_map/ppermute | solution.py:438
  16.2 1.0 %collective-permute-start.7 = (bf16[288,128]{1,0:T(8,128)(2,1)S(1)}, bf16[288,128]{1,0:T(8,128)(2,1)S(1)}, u32[]{:S(2)}, u32[]{:S(2)}) collective-permute-start(bf16[288,128]{1,0:T(8,128)(2,1)S(1)} %pad_maximum_fusion.3.refs_1_), channel_id=1, source_target_pairs={{0,2},{2,0},{4,6},{6,4},{8,10},{10,8},{12,14},{14,12},{1,3},{3,1},... | collective-permute-start | bytes 221192 | tf_op jit(solution)/shard_map/ppermute | solution.py:438
  17.3 0.6 %own_edges.2 = (bf16[576,128]{1,0:T(8,128)(2,1)S(1)}, f32[576,128]{1,0:T(8,128)S(1)}, f32[576,128]{1,0:T(8,128)S(1)}, f32[576,128]{1,0:T(8,128)S(1)}, f32[576,12...) custom-call(f32[4,128]{1,0:T(4,128)S(1)} %get-tuple-element.48.params, ...), custom_call_target="tpu_custom_call" | custom-call | flops 1000000000 | tf_op jit(solution)/shard_map/own_edges/pallas_call | solution.py:427
  17.9 0.0 collective-permute-done.4
  17.9 0.1 collective-permute-start.6
  18.0 0.6 %own_edges.3 = (bf16[576,128]{1,0:T(8,128)(2,1)S(1)}, f32[576,128]{1,0:T(8,128)S(1)}, f32[576,128]{1,0:T(8,128)S(1)}, f32[576,128]{1,0:T(8,128)S(1)}, f32[576,12...) custom-call(f32[4,128]{1,0:T(4,128)S(1)} %get-tuple-element.48.params, ...), custom_call_target="tpu_custom_call" | custom-call | flops 1000000000 | tf_op jit(solution)/shard_map/own_edges/pallas_call | solution.py:427
  18.7 0.6 %mate_edges.2 = (f32[576,128]{1,0:T(8,128)S(1)}, f32[576,128]{1,0:T(8,128)S(1)}) custom-call(f32[4,128]{1,0:T(4,128)S(1)} %get-tuple-element.48.params, bf16[128,512]{1,0:T(8,128)(2,1)S(1)} %get-tuple-element.50.weight.proj_weight, bf16[576,128]{1,0:T(8,128)(2,1)S(1)} %collective-permute-done.5.refs_0_), custom_call_target="tpu_custom_call" | custom-call | flops 1000000000 | tf_op jit(solution)/shard_map/mate_edges/pallas_call | solution.py:427
  19.3 0.1 collective-permute-done.6.refs_0_
  19.4 0.6 %mate_edges.3 = (f32[576,128]{1,0:T(8,128)S(1)}, f32[576,128]{1,0:T(8,128)S(1)}) custom-call(f32[4,128]{1,0:T(4,128)S(1)} %get-tuple-element.48.params, bf16[128,512]{1,0:T(8,128)(2,1)S(1)} %get-tuple-element.50.weight.proj_weight, bf16[576,128]{1,0:T(8,128)(2,1)S(1)} %collective-permute-done.6.refs_0_), custom_call_target="tpu_custom_call" | custom-call | flops 1000000000 | tf_op jit(solution)/shard_map/mate_edges/pallas_call | solution.py:427
  20.0 2.4 %triangle.1.tri = f32[1152,128]{1,0:T(8,128)S(1)} custom-call(f32[576,128]{1,0:T(8,128)S(1)} %get-tuple-element.53.refs_0_.left_0, f32[576,128]{1,0:T(8,128)S(1)} %get-tuple-element.54.refs_1_.left_1, f32[576,128]{1,0:T(8,128)S(1)} %get-tuple-element.55.refs_2_, f32[576,128]{1,0:T(8,128)S(1)} %get-tuple-element.56.refs_3_, ...), custom_call_target="tpu_custom_call" | custom-call | flops 2000000000 | tf_op jit(solution)/shard_map/triangle/pallas_call | solution.py:427
  22.4 0.0 collective-permute-done.8.refs_4_
  22.4 1.7 %cells.1 = (bf16[144,128]{1,0:T(8,128)(2,1)S(1)}, bf16[1152,128]{1,0:T(8,128)(2,1)S(1)}, bf16[1152,128]{1,0:T(8,128)(2,1)S(1)}, bf16[1152,128]{1,0:T(8,128)(2,1)S(1)}, bf16[1152,128]{1,0:T(8,128)(2,1)S(1)}) custom-call(f32[4,128]{1,0:T(4,128)S(1)} %get-tuple-element.48.params, f32[1152,128]{1,0:T(8,128)S(1)} %triangle.1.tri, ...), custom_call_target="tpu_custom_call" | custom-call | flops 2000000000 | tf_op jit(solution)/shard_map/cells/pallas_call | solution.py:427
  24.1 0.5 %collective-permute-start.9 = (bf16[1152,128]{1,0:T(8,128)(2,1)S(1)}, bf16[1152,128]{1,0:T(8,128)(2,1)S(1)}, u32[]{:S(2)}, u32[]{:S(2)}) collective-permute-start(bf16[1152,128]{1,0:T(8,128)(2,1)S(1)} %get-tuple-element.66.d_tri_ref), channel_id=1, source_target_pairs={{0,1},{1,0},{2,3},{3,2},{4,5},{5,4},{6,7},{7,6},{8,9},{9,8},{10,11... | collective-permute-start | bytes 884744 | tf_op jit(solution)/shard_map/ppermute | solution.py:441
  24.6 2.7 %early.1 = (f32[1152,128]{1,0:T(8,128)S(1)}, f32[1152,128]{1,0:T(8,128)S(1)}, bf16[1152,128]{1,0:T(8,128)(2,1)S(1)}, f32[1152,128]{1,0:T(8,128)S(1)}, f32[576,128]{1,0:T(8,128)S(1)}, /*index=5*/f32[128,256]{1,0:T(8,128)S(1)}) custom-call(bf16[1152,128]{1,0:T(8,128)(2,1)S(1)} %get-tuple-element.66.d_tri_ref, bf16[1152,128]{1,0:T(8,128)(2,1)S(1)} %get-tuple-element.67.d_gate, ...), custom_call_target="tpu_custom_call" | custom-call | flops 30000001024 | tf_op jit(solution)/shard_map/early/pallas_call | solution.py:427
  27.3 0.1 collective-permute-start.10
  27.4 0.0 collective-permute-done.9.d_tri_ref
  27.4 2.9 %late.1 = (f32[128,512]{1,0:T(8,128)S(1)}, bf16[1152,512]{1,0:T(8,128)(2,1)S(1)}) custom-call(bf16[1152,128]{1,0:T(8,128)(2,1)S(1)} %collective-permute-done.9.d_tri_ref, f32[1152,128]{1,0:T(8,128)S(1)} %get-tuple-element.70.left, f32[1152,128]{1,0:T(8,128)S(1)} %get-tuple-element.71.right, bf16[1152,128]{1,0:T(8,128)(2,1)S(1)} %get-tuple-element.72.normed, ...), custom_call_target="tpu_custom_call" | custom-call | flops 40000000000 | tf_op jit(solution)/shard_map/late/pallas_call | solution.py:427
  30.3 0.5 %collective-permute-start.11 = (f32[128,512]{1,0:T(8,128)S(1)}, f32[128,512]{1,0:T(8,128)S(1)}, u32[]{:S(2)}, u32[]{:S(2)}) collective-permute-start(f32[128,512]{1,0:T(8,128)S(1)} %get-tuple-element.88), channel_id=1, source_target_pairs={{0,1},{1,0},{2,3},{3,2},{4,5},{5,4},{6,7},{7,6},{8,9},{9,8},{10,11... | collective-permute-start | bytes 786440 | tf_op jit(solution)/shard_map/ppermute | solution.py:441
  30.8 1.0 %outputs.1 = (bf16[144,128]{1,0:T(8,128)(2,1)}, f32[144,128]{1,0:T(8,128)}, f32[128,128]{1,0:T(8,128)}, f32[128,128]{1,0:T(8,128)}) custom-call(f32[4,128]{1,0:T(4,128)S(1)} %get-tuple-element.48.params, bf16[144,128]{1,0:T(8,128)(2,1)S(1)} %get-tuple-element.98.refs_0_.pair, bf16[1152,512]{1,0:T(8,128)(2,1)S(1)} %get-tuple-element.83.d_proj, ...), custom_call_target="tpu_custom_call" | custom-call | flops 10000000000 | tf_op jit(solution)/shard_map/outputs/pallas_call | solution.py:427
  31.8 0.2 collective-permute-done.11
  32.0 0.7 %add.3 = f32[128,512]{1,0:T(8,128)} add(f32[128,512]{1,0:T(8,128)S(1)} %get-tuple-element.88, f32[128,512]{1,0:T(8,128)S(1)} %collective-permute-done.11) | non-fusion elementwise | flops 65536 | bytes 786432 | tf_op jit(solution)/shard_map/add | solution.py:586
  (11 shorter events, 0.1 us)
Async XLA Ops:
  0.6 8.6 %collective-permute-start.2 = (bf16[144,128]{1,0:T(8,128)(2,1)}, bf16[144,128]{1,0:T(8,128)(2,1)S(1)}, u32[]{:S(2)}, u32[]{:S(2)}) collective-permute-start(bf16[144,128]{1,0:T(8,128)(2,1)} %bitcast.9), channel_id=1, source_target_pairs={{0,12},{2,14},{4,8},{6,10},{8,4},{10,6},{12,0},{14,2},{1,13},{3,15... | collective-permute-start | bytes 110600 | tf_op jit(solution)/shard_map/ppermute | solution.py:438
  6.8 5.6 %collective-permute-start.1 = (bf16[288,128]{1,0:T(8,128)(2,1)S(1)}, bf16[288,128]{1,0:T(8,128)(2,1)S(1)}, u32[]{:S(2)}, u32[]{:S(2)}) collective-permute-start(bf16[288,128]{1,0:T(8,128)(2,1)S(1)} %get-tuple-element.49), channel_id=1, source_target_pairs={{0,8},{2,10},{4,12},{6,14},{8,0},{10,2},{12,4},{14,6},{1,9},{3,11}... | collective-permute-start | bytes 221192 | tf_op jit(solution)/shard_map/ppermute | solution.py:438
  6.9 5.5 %collective-permute-start = (bf16[288,128]{1,0:T(8,128)(2,1)S(1)}, bf16[288,128]{1,0:T(8,128)(2,1)S(1)}, u32[]{:S(2)}, u32[]{:S(2)}) collective-permute-start(bf16[288,128]{1,0:T(8,128)(2,1)S(1)} %get-tuple-element.49), channel_id=1, source_target_pairs={{0,4},{2,6},{4,0},{6,2},{8,12},{10,14},{12,8},{14,10},{1,5},{3,7},... | collective-permute-start | bytes 221192 | tf_op jit(solution)/shard_map/ppermute | solution.py:438
  7.5 6.6 %collective-permute-start.3 = (bf16[288,128]{1,0:T(8,128)(2,1)S(1)}, bf16[288,128]{1,0:T(8,128)(2,1)S(1)}, u32[]{:S(2)}, u32[]{:S(2)}) collective-permute-start(bf16[288,128]{1,0:T(8,128)(2,1)S(1)} %get-tuple-element.49), channel_id=1, source_target_pairs={{0,2},{2,0},{4,6},{6,4},{8,10},{10,8},{12,14},{14,12},{1,3},{3,1},... | collective-permute-start | bytes 221192 | tf_op jit(solution)/shard_map/ppermute | solution.py:438
  12.5 5.5 %collective-permute-start.4 = (bf16[432,128]{1,0:T(8,128)(2,1)S(1)}, bf16[432,128]{1,0:T(8,128)(2,1)S(1)}, u32[]{:S(2)}, u32[]{:S(2)}) collective-permute-start(bf16[432,128]{1,0:T(8,128)(2,1)S(1)} %pad_maximum_fusion.2.refs_1_), channel_id=1, source_target_pairs={{0,2},{2,0},{4,6},{6,4},{8,10},{10,8},{12,14},{14,12},{1,3},{3,1},... | collective-permute-start | bytes 331784 | tf_op jit(solution)/shard_map/ppermute | solution.py:438
  14.1 4.6 %collective-permute-start.5 = (bf16[576,128]{1,0:T(8,128)(2,1)S(1)}, bf16[576,128]{1,0:T(8,128)(2,1)S(1)}, u32[]{:S(2)}, u32[]{:S(2)}) collective-permute-start(bf16[576,128]{1,0:T(8,128)(2,1)S(1)} %pad_maximum_fusion.1), channel_id=1, source_target_pairs={{0,1},{1,0},{2,3},{3,2},{4,5},{5,4},{6,7},{7,6},{8,9},{9,8},{10,11... | collective-permute-start | bytes 442376 | tf_op jit(solution)/shard_map/ppermute | solution.py:441
  14.2 8.2 %collective-permute-start.8 = (bf16[288,128]{1,0:T(8,128)(2,1)S(1)}, bf16[288,128]{1,0:T(8,128)(2,1)S(1)}, u32[]{:S(2)}, u32[]{:S(2)}) collective-permute-start(bf16[288,128]{1,0:T(8,128)(2,1)S(1)} %pad_maximum_fusion.4), channel_id=1, source_target_pairs={{0,12},{2,14},{4,8},{6,10},{8,4},{10,6},{12,0},{14,2},{1,13},{3,15... | collective-permute-start | bytes 221192 | tf_op jit(solution)/shard_map/ppermute | solution.py:438
  16.2 6.2 %collective-permute-start.7 = (bf16[288,128]{1,0:T(8,128)(2,1)S(1)}, bf16[288,128]{1,0:T(8,128)(2,1)S(1)}, u32[]{:S(2)}, u32[]{:S(2)}) collective-permute-start(bf16[288,128]{1,0:T(8,128)(2,1)S(1)} %pad_maximum_fusion.3.refs_1_), channel_id=1, source_target_pairs={{0,2},{2,0},{4,6},{6,4},{8,10},{10,8},{12,14},{14,12},{1,3},{3,1},... | collective-permute-start | bytes 221192 | tf_op jit(solution)/shard_map/ppermute | solution.py:438
  17.9 1.4 %collective-permute-start.6 = (bf16[576,128]{1,0:T(8,128)(2,1)S(1)}, bf16[576,128]{1,0:T(8,128)(2,1)S(1)}, u32[]{:S(2)}, u32[]{:S(2)}) collective-permute-start(bf16[576,128]{1,0:T(8,128)(2,1)S(1)} %pad_maximum_fusion.refs_0_), channel_id=1, source_target_pairs={{0,1},{1,0},{2,3},{3,2},{4,5},{5,4},{6,7},{7,6},{8,9},{9,8},{10,11... | collective-permute-start | bytes 442376 | tf_op jit(solution)/shard_map/ppermute | solution.py:441
  24.1 3.3 %collective-permute-start.9 = (bf16[1152,128]{1,0:T(8,128)(2,1)S(1)}, bf16[1152,128]{1,0:T(8,128)(2,1)S(1)}, u32[]{:S(2)}, u32[]{:S(2)}) collective-permute-start(bf16[1152,128]{1,0:T(8,128)(2,1)S(1)} %get-tuple-element.66.d_tri_ref), channel_id=1, source_target_pairs={{0,1},{1,0},{2,3},{3,2},{4,5},{5,4},{6,7},{7,6},{8,9},{9,8},{10,11... | collective-permute-start | bytes 884744 | tf_op jit(solution)/shard_map/ppermute | solution.py:441
  27.3 3.5 %collective-permute-start.10 = (f32[128,256]{1,0:T(8,128)S(1)}, f32[128,256]{1,0:T(8,128)S(1)}, u32[]{:S(2)}, u32[]{:S(2)}) collective-permute-start(f32[128,256]{1,0:T(8,128)S(1)} %get-tuple-element.85.small_own), channel_id=1, source_target_pairs={{0,1},{1,0},{2,3},{3,2},{4,5},{5,4},{6,7},{7,6},{8,9},{9,8},{10,11... | collective-permute-start | bytes 393224 | tf_op jit(solution)/shard_map/ppermute | solution.py:441
  30.3 1.7 %collective-permute-start.11 = (f32[128,512]{1,0:T(8,128)S(1)}, f32[128,512]{1,0:T(8,128)S(1)}, u32[]{:S(2)}, u32[]{:S(2)}) collective-permute-start(f32[128,512]{1,0:T(8,128)S(1)} %get-tuple-element.88), channel_id=1, source_target_pairs={{0,1},{1,0},{2,3},{3,2},{4,5},{5,4},{6,7},{7,6},{8,9},{9,8},{10,11... | collective-permute-start | bytes 786440 | tf_op jit(solution)/shard_map/ppermute | solution.py:441

commit v11 on v8

--- a/solution.py
+++ b/solution.py
@@ -167,8 +167,7 @@
     gain, bias = params[2:3, :], params[3:4, :]
     for which, normed in ((0, normed_0), (1, normed_1)):
         for t, b in enumerate(places(groups)):
-            block = cots[2 * which + min(t, 1)]
-            cot = block[max(t - 1, 0) * cells : max(t, 1) * cells, :]
+            cot = cots[t][which * cells : (which + 1) * cells, :]
             place = at(row_block(which, b), cells)
             tri_f, hat, inverse = layer_norm(tri[place, :], gain, bias)
             tri_norm = tri_f.astype(BF16)
@@ -459,7 +458,9 @@
         outs = [(part, F32)] * 2
         return call(mate_edges_kernel, outs, params, proj_weight, *blocks, name="mate_edges")
 
-    given = [pair_rep.reshape(cells, channels), cotangent.reshape(cells, channels)]
+    pair_in = pair_rep.reshape(cells, channels)
+    near = along(pair_in, tied=True)
+    given = [pair_in, cotangent.reshape(cells, channels)]
     given += [v[None] for v in (norm_gain, norm_bias, tri_gain, tri_bias)]
     given += [proj_weight, gate_weight, out_weight]
     given = [pltpu.with_memory_space_constraint(v, pltpu.HBM) for v in given]
@@ -471,14 +472,12 @@
         in_specs=[pl.BlockSpec(memory_space=pltpu.HBM)] * len(given),
         name="fetch",
     )
-    got = along(both, tied=True)
     both_far = across(both, 1)
     pair, pair_far = both[:cells], both_far[:cells]
-    cot_0, cot_1 = both[cells:], both_far[cells:]
-    near_all = join(*(block[:cells] for block in got))
+    near_all = join(*near)
     far = across(near_all, 1)
-    cot_near = join(*(block[cells:] for block in got))
-    cot_far = across(cot_near, 1)
+    cots = after(join(both[cells:], both_far[cells:]), near_all)
+    cots = [cots] + along(cots)
     mate_near = over(join(pair, near_all))
     own_0 = own_edges(pair, near_all)
     mate_0 = mate_edges(mate_near)
@@ -508,10 +507,7 @@
         *normed,
         gate_weight,
         out_weight,
-        cot_0,
-        cot_near,
-        cot_1,
-        cot_far,
+        *cots,
         micros=2,
         name="cells",
     )
@@ -678,7 +674,7 @@
     groups = lax.axis_size("row")
     every = rows * groups * cols
     fits = 24 * every * channels * 4 <= VMEM_BUDGET and hidden == channels
-    paired = lax.axis_size("col") == 2 and groups & (groups - 1) == 0 and groups >= 2
+    paired = lax.axis_size("col") == 2 and groups & (groups - 1) == 0 and groups >= 4
     whole_tiles = cols % 8 == 0 and cols % (2 * rows) == 0 and rows * cols % 16 == 0
     plan = replicated if fits and paired and whole_tiles else sharded
     return plan(pair_rep, *others)

time: 33 us -> 33.5 us (1.015)
  starting transfers between devices: 10.9 us -> 14.4 us
  waiting for transfers between devices: 6.06 us -> 3.1 us
    ppermute x6 -> x8, starting transfers between devices: 9.58 us -> 13.5 us  [across(): return lax.ppermute(value, 'row', [(i, i ^ mask) for i in range(groups)])]
    ppermute x6 -> x8, waiting for transfers between devices: 5.81 us -> 2.51 us  [across(): return lax.ppermute(value, 'row', [(i, i ^ mask) for i in range(groups)])]
    ppermute x5, starting transfers between devices: 1.29 us -> 0.86 us  [over(): return lax.ppermute(value, 'col', SWAP)]
    ppermute x5, waiting for transfers between devices: 0.25 us -> 0.59 us  [over(): return lax.ppermute(value, 'col', SWAP)]
  transfers between devices with their start and end apart: 11 -> 13, of which waited for: 5 -> 4; matrix products, arithmetic and copies ran while one was open for 0% -> 0% of each run, Pallas kernels for 35% -> 38%
where the time goes in v11:
time: 33.5 us; the launch traced here: 33.3 us
  starting transfers between devices  14.4 us (43%)
  Pallas kernels  14.2 us (42%)
  waiting for transfers between devices  3.1 us (9%)
  between operations  0.8 us (2%)
  other arithmetic  0.77 us (2%)
    pallas_call x10, Pallas kernels, call(): pl.pallas_call(functools.partial(kernel, sizes), out_shape=[jax.ShapeDtyp...  14.2 us
    ppermute x8, starting transfers between devices, across(): return lax.ppermute(value, 'row', [(i, i ^ mask) for i in range(groups)])  13.5 us
    ppermute x8, waiting for transfers between devices, across(): return lax.ppermute(value, 'row', [(i, i ^ mask) for i in range(groups)])  2.51 us
    ppermute x5, starting transfers between devices, over(): return lax.ppermute(value, 'col', SWAP)  0.86 us
    add x1, other arithmetic, replicated(): proj_grad + proj_mate  0.74 us
  transfers between devices with their start and end apart: 13, of which 4 were waited for; matrix products, arithmetic and copies ran while one was open for 0% of the time, Pallas kernels for 38%

profile of v11, /device:TPU:0, one launch (start us, length us, event | category | flops | bytes accessed | tf_op | source)
XLA Modules:
  0.0 33.3 jit_solution(15502133365537508808)
XLA Ops:
  0.6 5.1 %collective-permute-start.2 = (bf16[144,128]{1,0:T(8,128)(2,1)}, bf16[144,128]{1,0:T(8,128)(2,1)S(1)}, u32[]{:S(2)}, u32[]{:S(2)}) collective-permute-start(bf16[144,128]{1,0:T(8,128)(2,1)} %bitcast.9), channel_id=1, source_target_pairs={{0,12},{2,14},{4,8},{6,10},{8,4},{10,6},{12,0},{14,2},{1,13},{3,15... | collective-permute-start | bytes 110600 | tf_op jit(solution)/shard_map/ppermute | solution.py:433
  5.8 0.6 %collective-permute-start = (bf16[144,128]{1,0:T(8,128)(2,1)}, bf16[144,128]{1,0:T(8,128)(2,1)S(1)}, u32[]{:S(2)}, u32[]{:S(2)}) collective-permute-start(bf16[144,128]{1,0:T(8,128)(2,1)} %bitcast.11), channel_id=1, source_target_pairs={{0,4},{2,6},{4,0},{6,2},{8,12},{10,14},{12,8},{14,10},{1,5},{3,7},... | collective-permute-start | bytes 110600 | tf_op jit(solution)/shard_map/ppermute | solution.py:433
  6.4 1.1 %fetch.1 = (bf16[288,128]{1,0:T(8,128)(2,1)S(1)}, f32[4,128]{1,0:T(4,128)S(1)}, bf16[128,512]{1,0:T(8,128)(2,1)S(1)}, bf16[128,128]{1,0:T(8,128)(2,1)S(1)}, bf16[128,128]{1,0:T(8,128)(2,1)S(1)}) custom-call(bf16[144,128]{1,0:T(8,128)(2,1)} %bitcast.12, bf16[144,128]{1,0:T(8,128)(2,1)} %bitcast.8, f32[1,128]{1,0:T(1,128)} %bitcast.13, f32[1,128]{1,0:T(1,128)} %bitcast.14, ...), custom_call_target="tpu_custom_call" | custom-call | flops 1000000000 | tf_op jit(solution)/shard_map/fetch/pallas_call | solution.py:422
  7.5 1.7 %collective-permute-start.3 = (bf16[288,128]{1,0:T(8,128)(2,1)S(1)}, bf16[288,128]{1,0:T(8,128)(2,1)S(1)}, u32[]{:S(2)}, u32[]{:S(2)}) collective-permute-start(bf16[288,128]{1,0:T(8,128)(2,1)S(1)} %get-tuple-element.49), channel_id=1, source_target_pairs={{0,2},{2,0},{4,6},{6,4},{8,10},{10,8},{12,14},{14,12},{1,3},{3,1},... | collective-permute-start | bytes 221192 | tf_op jit(solution)/shard_map/ppermute | solution.py:433
  9.2 0.0 collective-permute-done.2
  9.2 1.6 %collective-permute-done.1 = bf16[144,128]{1,0:T(8,128)(2,1)S(1)} collective-permute-done((bf16[144,128]{1,0:T(8,128)(2,1)}, bf16[144,128]{1,0:T(8,128)(2,1)S(1)}, u32[]{:S(2)}, u32[]{:S(2)}) %collective-permute-start.1) | collective-permute-done | bytes 36896 | tf_op jit(solution)/shard_map/ppermute | solution.py:433
  10.9 1.6 %collective-permute-start.4 = (bf16[432,128]{1,0:T(8,128)(2,1)S(1)}, bf16[432,128]{1,0:T(8,128)(2,1)S(1)}, u32[]{:S(2)}, u32[]{:S(2)}) collective-permute-start(bf16[432,128]{1,0:T(8,128)(2,1)S(1)} %constant_dynamic-update-slice_fusion.refs_1_), channel_id=1, source_target_pairs={{0,2},{2,0},{4,6},{6,4},{8,10},{10,8},{12,14},{14,12},{1,3},{3,1},... | collective-permute-start | bytes 331784 | tf_op jit(solution)/shard_map/ppermute | solution.py:433
  12.5 0.1 collective-permute-start.5
  12.5 0.6 %own_edges.2 = (bf16[576,128]{1,0:T(8,128)(2,1)S(1)}, f32[576,128]{1,0:T(8,128)S(1)}, f32[576,128]{1,0:T(8,128)S(1)}, f32[576,128]{1,0:T(8,128)S(1)}, f32[576,12...) custom-call(f32[4,128]{1,0:T(4,128)S(1)} %get-tuple-element.48.params, ...), custom_call_target="tpu_custom_call" | custom-call | flops 1000000000 | tf_op jit(solution)/shard_map/own_edges/pallas_call | solution.py:422
  13.2 0.9 %collective-permute-start.7 = (bf16[288,128]{1,0:T(8,128)(2,1)S(1)}, bf16[288,128]{1,0:T(8,128)(2,1)S(1)}, u32[]{:S(2)}, u32[]{:S(2)}) collective-permute-start(bf16[288,128]{1,0:T(8,128)(2,1)S(1)} %pad_maximum_fusion.2.refs_0_), channel_id=1, source_target_pairs={{0,4},{2,6},{4,0},{6,2},{8,12},{10,14},{12,8},{14,10},{1,5},{3,7},... | collective-permute-start | bytes 221192 | tf_op jit(solution)/shard_map/ppermute | solution.py:433
  14.2 2.7 %collective-permute-start.8 = (bf16[288,128]{1,0:T(8,128)(2,1)S(1)}, bf16[288,128]{1,0:T(8,128)(2,1)S(1)}, u32[]{:S(2)}, u32[]{:S(2)}) collective-permute-start(bf16[288,128]{1,0:T(8,128)(2,1)S(1)} %pad_maximum_fusion.2.refs_0_), channel_id=1, source_target_pairs={{0,8},{2,10},{4,12},{6,14},{8,0},{10,2},{12,4},{14,6},{1,9},{3,11}... | collective-permute-start | bytes 221192 | tf_op jit(solution)/shard_map/ppermute | solution.py:433
  16.9 0.8 %collective-permute-start.9 = (bf16[288,128]{1,0:T(8,128)(2,1)S(1)}, bf16[288,128]{1,0:T(8,128)(2,1)S(1)}, u32[]{:S(2)}, u32[]{:S(2)}) collective-permute-start(bf16[288,128]{1,0:T(8,128)(2,1)S(1)} %pad_maximum_fusion.2.refs_0_), channel_id=1, source_target_pairs={{0,12},{2,14},{4,8},{6,10},{8,4},{10,6},{12,0},{14,2},{1,13},{3,15... | collective-permute-start | bytes 221192 | tf_op jit(solution)/shard_map/ppermute | solution.py:433
  17.7 0.0 collective-permute-done.4
  17.7 0.1 collective-permute-start.6
  17.8 0.6 %own_edges.3 = (bf16[576,128]{1,0:T(8,128)(2,1)S(1)}, f32[576,128]{1,0:T(8,128)S(1)}, f32[576,128]{1,0:T(8,128)S(1)}, f32[576,128]{1,0:T(8,128)S(1)}, f32[576,12...) custom-call(f32[4,128]{1,0:T(4,128)S(1)} %get-tuple-element.48.params, ...), custom_call_target="tpu_custom_call" | custom-call | flops 1000000000 | tf_op jit(solution)/shard_map/own_edges/pallas_call | solution.py:422
  18.4 0.0 collective-permute-done.5.refs_0_
  18.4 0.6 %mate_edges.2 = (f32[576,128]{1,0:T(8,128)S(1)}, f32[576,128]{1,0:T(8,128)S(1)}) custom-call(f32[4,128]{1,0:T(4,128)S(1)} %get-tuple-element.48.params, bf16[128,512]{1,0:T(8,128)(2,1)S(1)} %get-tuple-element.50.weight.proj_weight, bf16[576,128]{1,0:T(8,128)(2,1)S(1)} %collective-permute-done.5.refs_0_), custom_call_target="tpu_custom_call" | custom-call | flops 1000000000 | tf_op jit(solution)/shard_map/mate_edges/pallas_call | solution.py:422
  19.1 0.1 collective-permute-done.6.refs_0_
  19.1 0.6 %mate_edges.3 = (f32[576,128]{1,0:T(8,128)S(1)}, f32[576,128]{1,0:T(8,128)S(1)}) custom-call(f32[4,128]{1,0:T(4,128)S(1)} %get-tuple-element.48.params, bf16[128,512]{1,0:T(8,128)(2,1)S(1)} %get-tuple-element.50.weight.proj_weight, bf16[576,128]{1,0:T(8,128)(2,1)S(1)} %collective-permute-done.6.refs_0_), custom_call_target="tpu_custom_call" | custom-call | flops 1000000000 | tf_op jit(solution)/shard_map/mate_edges/pallas_call | solution.py:422
  19.8 2.4 %triangle.1.tri = f32[1152,128]{1,0:T(8,128)S(1)} custom-call(f32[576,128]{1,0:T(8,128)S(1)} %get-tuple-element.53.refs_0_.left_0, f32[576,128]{1,0:T(8,128)S(1)} %get-tuple-element.54.refs_1_.left_1, f32[576,128]{1,0:T(8,128)S(1)} %get-tuple-element.55.refs_2_, f32[576,128]{1,0:T(8,128)S(1)} %get-tuple-element.56.refs_3_, ...), custom_call_target="tpu_custom_call" | custom-call | flops 2000000000 | tf_op jit(solution)/shard_map/triangle/pallas_call | solution.py:422
  22.2 0.0 collective-permute-done.8.refs_2_
  22.2 0.9 %collective-permute-done.9.refs_3_ = bf16[288,128]{1,0:T(8,128)(2,1)S(1)} collective-permute-done((bf16[288,128]{1,0:T(8,128)(2,1)S(1)}, bf16[288,128]{1,0:T(8,128)(2,1)S(1)}, u32[]{:S(2)}, u32[]{:S(2)}) %collective-permute-start.9) | collective-permute-done | bytes 73760 | tf_op jit(solution)/shard_map/ppermute | solution.py:433
  23.1 1.7 %cells.1 = (bf16[144,128]{1,0:T(8,128)(2,1)S(1)}, bf16[1152,128]{1,0:T(8,128)(2,1)S(1)}, bf16[1152,128]{1,0:T(8,128)(2,1)S(1)}, bf16[1152,128]{1,0:T(8,128)(2,1)S(1)}, bf16[1152,128]{1,0:T(8,128)(2,1)S(1)}) custom-call(f32[4,128]{1,0:T(4,128)S(1)} %get-tuple-element.48.params, f32[1152,128]{1,0:T(8,128)S(1)} %triangle.1.tri, ...), custom_call_target="tpu_custom_call" | custom-call | flops 2000000000 | tf_op jit(solution)/shard_map/cells/pallas_call | solution.py:422
  24.8 0.1 collective-permute-start.10
  24.8 2.7 %early.1 = (f32[1152,128]{1,0:T(8,128)S(1)}, f32[1152,128]{1,0:T(8,128)S(1)}, bf16[1152,128]{1,0:T(8,128)(2,1)S(1)}, f32[1152,128]{1,0:T(8,128)S(1)}, f32[576,128]{1,0:T(8,128)S(1)}, /*index=5*/f32[128,256]{1,0:T(8,128)S(1)}) custom-call(bf16[1152,128]{1,0:T(8,128)(2,1)S(1)} %get-tuple-element.66.d_tri_ref, bf16[1152,128]{1,0:T(8,128)(2,1)S(1)} %get-tuple-element.67.d_gate, ...), custom_call_target="tpu_custom_call" | custom-call | flops 30000001024 | tf_op jit(solution)/shard_map/early/pallas_call | solution.py:422
  27.6 0.6 %collective-permute-start.11 = (f32[128,256]{1,0:T(8,128)S(1)}, f32[128,256]{1,0:T(8,128)S(1)}, u32[]{:S(2)}, u32[]{:S(2)}) collective-permute-start(f32[128,256]{1,0:T(8,128)S(1)} %get-tuple-element.85.small_own), channel_id=1, source_target_pairs={{0,1},{1,0},{2,3},{3,2},{4,5},{5,4},{6,7},{7,6},{8,9},{9,8},{10,11... | collective-permute-start | bytes 393224 | tf_op jit(solution)/shard_map/ppermute | solution.py:436
  28.1 2.9 %late.1 = (f32[128,512]{1,0:T(8,128)S(1)}, bf16[1152,512]{1,0:T(8,128)(2,1)S(1)}) custom-call(bf16[1152,128]{1,0:T(8,128)(2,1)S(1)} %collective-permute-done.10.d_tri_ref, f32[1152,128]{1,0:T(8,128)S(1)} %get-tuple-element.70.left, f32[1152,128]{1,0:T(8,128)S(1)} %get-tuple-element.71.right, bf16[1152,128]{1,0:T(8,128)(2,1)S(1)} %get-tuple-element.72.normed, ...), custom_call_target="tpu_custom_call" | custom-call | flops 40000000000 | tf_op jit(solution)/shard_map/late/pallas_call | solution.py:422
  31.0 0.1 collective-permute-start.12
  31.1 0.0 collective-permute-done.11.small_mate
  31.1 1.0 %outputs.1 = (bf16[144,128]{1,0:T(8,128)(2,1)}, f32[144,128]{1,0:T(8,128)}, f32[128,128]{1,0:T(8,128)}, f32[128,128]{1,0:T(8,128)}) custom-call(f32[4,128]{1,0:T(4,128)S(1)} %get-tuple-element.48.params, bf16[144,128]{1,0:T(8,128)(2,1)S(1)} %get-tuple-element.92.refs_0_.pair, bf16[1152,512]{1,0:T(8,128)(2,1)S(1)} %get-tuple-element.83.d_proj, ...), custom_call_target="tpu_custom_call" | custom-call | flops 10000000000 | tf_op jit(solution)/shard_map/outputs/pallas_call | solution.py:422
  32.1 0.5 %collective-permute-done.12 = f32[128,512]{1,0:T(8,128)S(1)} collective-permute-done((f32[128,512]{1,0:T(8,128)S(1)}, f32[128,512]{1,0:T(8,128)S(1)}, u32[]{:S(2)}, u32[]{:S(2)}) %collective-permute-start.12) | collective-permute-done | bytes 262176 | tf_op jit(solution)/shard_map/ppermute | solution.py:436
  32.6 0.7 %add.3 = f32[128,512]{1,0:T(8,128)} add(f32[128,512]{1,0:T(8,128)S(1)} %get-tuple-element.88, f32[128,512]{1,0:T(8,128)S(1)} %collective-permute-done.12) | non-fusion elementwise | flops 65536 | bytes 786432 | tf_op jit(solution)/shard_map/add | solution.py:574
  (13 shorter events, 0.1 us)
Async XLA Ops:
  0.6 8.6 %collective-permute-start.2 = (bf16[144,128]{1,0:T(8,128)(2,1)}, bf16[144,128]{1,0:T(8,128)(2,1)S(1)}, u32[]{:S(2)}, u32[]{:S(2)}) collective-permute-start(bf16[144,128]{1,0:T(8,128)(2,1)} %bitcast.9), channel_id=1, source_target_pairs={{0,12},{2,14},{4,8},{6,10},{8,4},{10,6},{12,0},{14,2},{1,13},{3,15... | collective-permute-start | bytes 110600 | tf_op jit(solution)/shard_map/ppermute | solution.py:433
  5.7 5.1 %collective-permute-start.1 = (bf16[144,128]{1,0:T(8,128)(2,1)}, bf16[144,128]{1,0:T(8,128)(2,1)S(1)}, u32[]{:S(2)}, u32[]{:S(2)}) collective-permute-start(bf16[144,128]{1,0:T(8,128)(2,1)} %bitcast.10), channel_id=1, source_target_pairs={{0,8},{2,10},{4,12},{6,14},{8,0},{10,2},{12,4},{14,6},{1,9},{3,11}... | collective-permute-start | bytes 110600 | tf_op jit(solution)/shard_map/ppermute | solution.py:433
  5.8 5.1 %collective-permute-start = (bf16[144,128]{1,0:T(8,128)(2,1)}, bf16[144,128]{1,0:T(8,128)(2,1)S(1)}, u32[]{:S(2)}, u32[]{:S(2)}) collective-permute-start(bf16[144,128]{1,0:T(8,128)(2,1)} %bitcast.11), channel_id=1, source_target_pairs={{0,4},{2,6},{4,0},{6,2},{8,12},{10,14},{12,8},{14,10},{1,5},{3,7},... | collective-permute-start | bytes 110600 | tf_op jit(solution)/shard_map/ppermute | solution.py:433
  7.5 5.7 %collective-permute-start.3 = (bf16[288,128]{1,0:T(8,128)(2,1)S(1)}, bf16[288,128]{1,0:T(8,128)(2,1)S(1)}, u32[]{:S(2)}, u32[]{:S(2)}) collective-permute-start(bf16[288,128]{1,0:T(8,128)(2,1)S(1)} %get-tuple-element.49), channel_id=1, source_target_pairs={{0,2},{2,0},{4,6},{6,4},{8,10},{10,8},{12,14},{14,12},{1,3},{3,1},... | collective-permute-start | bytes 221192 | tf_op jit(solution)/shard_map/ppermute | solution.py:433
  10.9 6.8 %collective-permute-start.4 = (bf16[432,128]{1,0:T(8,128)(2,1)S(1)}, bf16[432,128]{1,0:T(8,128)(2,1)S(1)}, u32[]{:S(2)}, u32[]{:S(2)}) collective-permute-start(bf16[432,128]{1,0:T(8,128)(2,1)S(1)} %constant_dynamic-update-slice_fusion.refs_1_), channel_id=1, source_target_pairs={{0,2},{2,0},{4,6},{6,4},{8,10},{10,8},{12,14},{14,12},{1,3},{3,1},... | collective-permute-start | bytes 331784 | tf_op jit(solution)/shard_map/ppermute | solution.py:433
  12.5 6.0 %collective-permute-start.5 = (bf16[576,128]{1,0:T(8,128)(2,1)S(1)}, bf16[576,128]{1,0:T(8,128)(2,1)S(1)}, u32[]{:S(2)}, u32[]{:S(2)}) collective-permute-start(bf16[576,128]{1,0:T(8,128)(2,1)S(1)} %pad_maximum_fusion.1), channel_id=1, source_target_pairs={{0,1},{1,0},{2,3},{3,2},{4,5},{5,4},{6,7},{7,6},{8,9},{9,8},{10,11... | collective-permute-start | bytes 442376 | tf_op jit(solution)/shard_map/ppermute | solution.py:436
  13.2 9.0 %collective-permute-start.7 = (bf16[288,128]{1,0:T(8,128)(2,1)S(1)}, bf16[288,128]{1,0:T(8,128)(2,1)S(1)}, u32[]{:S(2)}, u32[]{:S(2)}) collective-permute-start(bf16[288,128]{1,0:T(8,128)(2,1)S(1)} %pad_maximum_fusion.2.refs_0_), channel_id=1, source_target_pairs={{0,4},{2,6},{4,0},{6,2},{8,12},{10,14},{12,8},{14,10},{1,5},{3,7},... | collective-permute-start | bytes 221192 | tf_op jit(solution)/shard_map/ppermute | solution.py:433
  14.2 8.0 %collective-permute-start.8 = (bf16[288,128]{1,0:T(8,128)(2,1)S(1)}, bf16[288,128]{1,0:T(8,128)(2,1)S(1)}, u32[]{:S(2)}, u32[]{:S(2)}) collective-permute-start(bf16[288,128]{1,0:T(8,128)(2,1)S(1)} %pad_maximum_fusion.2.refs_0_), channel_id=1, source_target_pairs={{0,8},{2,10},{4,12},{6,14},{8,0},{10,2},{12,4},{14,6},{1,9},{3,11}... | collective-permute-start | bytes 221192 | tf_op jit(solution)/shard_map/ppermute | solution.py:433
  16.9 6.2 %collective-permute-start.9 = (bf16[288,128]{1,0:T(8,128)(2,1)S(1)}, bf16[288,128]{1,0:T(8,128)(2,1)S(1)}, u32[]{:S(2)}, u32[]{:S(2)}) collective-permute-start(bf16[288,128]{1,0:T(8,128)(2,1)S(1)} %pad_maximum_fusion.2.refs_0_), channel_id=1, source_target_pairs={{0,12},{2,14},{4,8},{6,10},{8,4},{10,6},{12,0},{14,2},{1,13},{3,15... | collective-permute-start | bytes 221192 | tf_op jit(solution)/shard_map/ppermute | solution.py:433
  17.7 1.4 %collective-permute-start.6 = (bf16[576,128]{1,0:T(8,128)(2,1)S(1)}, bf16[576,128]{1,0:T(8,128)(2,1)S(1)}, u32[]{:S(2)}, u32[]{:S(2)}) collective-permute-start(bf16[576,128]{1,0:T(8,128)(2,1)S(1)} %pad_maximum_fusion.refs_0_), channel_id=1, source_target_pairs={{0,1},{1,0},{2,3},{3,2},{4,5},{5,4},{6,7},{7,6},{8,9},{9,8},{10,11... | collective-permute-start | bytes 442376 | tf_op jit(solution)/shard_map/ppermute | solution.py:436
  24.8 3.3 %collective-permute-start.10 = (bf16[1152,128]{1,0:T(8,128)(2,1)S(1)}, bf16[1152,128]{1,0:T(8,128)(2,1)S(1)}, u32[]{:S(2)}, u32[]{:S(2)}) collective-permute-start(bf16[1152,128]{1,0:T(8,128)(2,1)S(1)} %get-tuple-element.66.d_tri_ref), channel_id=1, source_target_pairs={{0,1},{1,0},{2,3},{3,2},{4,5},{5,4},{6,7},{7,6},{8,9},{9,8},{10,11... | collective-permute-start | bytes 884744 | tf_op jit(solution)/shard_map/ppermute | solution.py:436
  27.6 3.5 %collective-permute-start.11 = (f32[128,256]{1,0:T(8,128)S(1)}, f32[128,256]{1,0:T(8,128)S(1)}, u32[]{:S(2)}, u32[]{:S(2)}) collective-permute-start(f32[128,256]{1,0:T(8,128)S(1)} %get-tuple-element.85.small_own), channel_id=1, source_target_pairs={{0,1},{1,0},{2,3},{3,2},{4,5},{5,4},{6,7},{7,6},{8,9},{9,8},{10,11... | collective-permute-start | bytes 393224 | tf_op jit(solution)/shard_map/ppermute | solution.py:436
  31.0 1.6 %collective-permute-start.12 = (f32[128,512]{1,0:T(8,128)S(1)}, f32[128,512]{1,0:T(8,128)S(1)}, u32[]{:S(2)}, u32[]{:S(2)}) collective-permute-start(f32[128,512]{1,0:T(8,128)S(1)} %get-tuple-element.88), channel_id=1, source_target_pairs={{0,1},{1,0},{2,3},{3,2},{4,5},{5,4},{6,7},{7,6},{8,9},{9,8},{10,11... | collective-permute-start | bytes 786440 | tf_op jit(solution)/shard_map/ppermute | solution.py:436

commit v12 on v11

--- a/solution.py
+++ b/solution.py
@@ -46,15 +46,21 @@
     return pl.ds(pl.multiple_of(start, 8), 8)
 
 
-def places(groups):
+def parts(groups):
+    distances = tuple(range(groups // 2))
+    return ((0, distances), (1, distances))
+
+
+def row_block(side, distance):
     me = lax.axis_index("row")
-    return [lax.bitwise_xor(me // 2, t) for t in range(groups // 2)]
-
-
-def row_block(which, b):
-    me = lax.axis_index("row")
-    parity = lax.rem(me, 2)
-    return 2 * b + (parity if which == 0 else 1 - parity)
+    return lax.bitwise_xor(me, 2 * distance + side)
+
+
+def slots(groups):
+    found = []
+    for n, (side, distances) in enumerate(parts(groups)):
+        found += [(n, s, row_block(side, d)) for s, d in enumerate(distances)]
+    return found
 
 
 def edges(blocks, params, proj_weight):
@@ -70,14 +76,22 @@
     return normed, sides
 
 
-def fetch_kernel(sizes, *refs):
+def fetch_inputs_kernel(sizes, pair, cot, both, sems):
     cells = sizes[0] * sizes[1]
-    pair, cot, gain_0, bias_0, gain_1, bias_1, *weights = refs[:9]
-    both, params, *held = refs[9:14]
-    sems = refs[14]
-    moves = [(pair, both.at[:cells]), (cot, both.at[cells:])]
-    moves += [(v, params.at[n : n + 1]) for n, v in enumerate((gain_0, bias_0, gain_1, bias_1))]
-    moves += list(zip(weights, held, strict=True))
+    copies = [
+        pltpu.make_async_copy(pair, both.at[:cells], sems.at[0]),
+        pltpu.make_async_copy(cot, both.at[cells:], sems.at[1]),
+    ]
+    for copy in copies:
+        copy.start()
+    for copy in copies:
+        copy.wait()
+
+
+def fetch_weights_kernel(sizes, *refs):
+    given, (params, *held), sems = refs[:7], refs[7:11], refs[11]
+    moves = [(v, params.at[n : n + 1]) for n, v in enumerate(given[:4])]
+    moves += list(zip(given[4:], held, strict=True))
     copies = [pltpu.make_async_copy(a, b, sems.at[n]) for n, (a, b) in enumerate(moves)]
     for copy in copies:
         copy.start()
@@ -86,102 +100,94 @@
 
 
 def own_edges_kernel(sizes, params, weight, *refs):
-    rows, cols, groups = sizes
-    cells = rows * cols
     blocks, normed_out, outs = refs[:-7], refs[-7], refs[-6:]
     normed, sides = edges(blocks, params, weight)
-    for t, b in enumerate(places(groups)):
-        part = slice(t * cells, (t + 1) * cells)
-        place = at(b, cells)
-        normed_out[place, :] = normed[part]
-        for out, value in zip(outs, sides[0] + sides[1], strict=True):
-            out[place, :] = value[part]
+    normed_out[...] = normed
+    for out, value in zip(outs, sides[0] + sides[1], strict=True):
+        out[...] = value
 
 
 def mate_edges_kernel(sizes, params, weight, *refs):
-    rows, cols, groups = sizes
-    cells = rows * cols
     blocks, left, right = refs[:-2], refs[-2], refs[-1]
     _, sides = edges(blocks, params, weight)
-    for t, b in enumerate(places(groups)):
-        part = slice(t * cells, (t + 1) * cells)
-        left[at(b, cells), :] = sides[0][0][part]
-        right[at(b, cells), :] = sides[1][0][part]
+    left[...] = sides[0][0]
+    right[...] = sides[1][0]
 
 
 def triangle_kernel(sizes, *refs):
     rows, cols, groups = sizes
     cells = rows * cols
-    lefts, rights, (tri,), picked = refs[:4], refs[4:8], refs[8:9], refs[9:]
+    lefts, rights, more, tri, picked = refs[:2], refs[2:4], refs[4:-2], refs[-2], refs[-1]
     hidden = tri.shape[-1]
     half = lax.axis_index("col")
-    zero = jnp.zeros((8, hidden), F32)
     count = cols // 8
     blocks = cols // rows
-    for side in range(2):
-        for which in range(2):
-            for s in range(blocks // 2):
-                b = half * (blocks // 2) + s
-                p = row_block(which, b) - half * blocks
-                picked[side][at(p, cells), :] = rights[2 * side + which][at(b, cells), :]
-
-    for which in range(2):
-
-        def tri_block(b, carry, which=which):
-            def step(k, sums):
-                new = list(sums)
-                for side in range(2):
-                    left = lefts[2 * side + which]
-                    tiles = [
-                        picked[side][pl.ds(t * 8 * cols + k, 8, stride=cols), :]
-                        for t in range(count)
-                    ]
-                    for a in range(rows):
-                        row = left[pl.ds((b * rows + a) * cols + k, 1), :]
-                        for t in range(count):
-                            new[a * count + t] += row * tiles[t]
-                return tuple(new)
-
-            sums = lax.fori_loop(0, cols, step, (zero,) * (rows * count), unroll=4)
-            start = row_block(which, b) * cells
-            for t, value in enumerate(sums):
-                tri[tile(start + t * 8), :] = value
-            return carry
-
-        lax.fori_loop(0, groups // 2, tri_block, 0)
+    for n, s, p in slots(groups):
+
+        @pl.when(p // blocks == half)
+        def _(n=n, s=s, p=p):
+            picked[at(p - half * blocks, cells), :] = rights[n][s * cells : (s + 1) * cells, :]
+
+    for n, s, p in slots(groups):
+
+        def step(k, sums, n=n, s=s):
+            new = list(sums)
+            tiles = [picked[pl.ds(t * 8 * cols + k, 8, stride=cols), :] for t in range(count)]
+            for a in range(rows):
+                row = lefts[n][pl.ds((s * rows + a) * cols + k, 1), :]
+                for t in range(count):
+                    new[a * count + t] += row * tiles[t]
+            return tuple(new)
+
+        if more:
+            first = tuple(more[0][tile(p * cells + t * 8), :] for t in range(rows * count))
+        else:
+            first = (jnp.zeros((8, hidden), F32),) * (rows * count)
+        sums = lax.fori_loop(0, cols, step, first, unroll=8)
+        for t, value in enumerate(sums):
+            tri[tile(p * cells + t * 8), :] = value
 
 
 def cells_kernel(
     sizes,
     params,
     tri,
-    normed_0,
-    normed_1,
     gate_weight,
     out_weight,
     *refs,
 ):
     rows, cols, groups = sizes
     cells = rows * cols
-    cots, (block_out, d_tri, d_gate, tri_norm_out, d_update_out) = refs[:-5], refs[-5:]
+    normed, cots, (block_out, d_tri, d_gate, tri_norm_out, d_update_out) = (
+        refs[:2],
+        refs[2:6],
+        refs[6:],
+    )
     gain, bias = params[2:3, :], params[3:4, :]
-    for which, normed in ((0, normed_0), (1, normed_1)):
-        for t, b in enumerate(places(groups)):
-            cot = cots[t][which * cells : (which + 1) * cells, :]
-            place = at(row_block(which, b), cells)
-            tri_f, hat, inverse = layer_norm(tri[place, :], gain, bias)
-            tri_norm = tri_f.astype(BF16)
-            update = dot(tri_norm, out_weight[...])
-            out_gate = sigmoid(dot(normed[at(b, cells), :], gate_weight[...]))
-            if which == 0 and t == 0:
-                block_out[...] = (out_gate * update).astype(BF16)
-            gated = cot.astype(F32) * out_gate
-            d_update = gated.astype(BF16)
-            d_gate[place, :] = (gated * update * (1.0 - out_gate)).astype(BF16)
-            d_norm = dot(d_update, out_weight[...], TRANSPOSED)
-            d_tri[place, :] = norm_back(d_norm, gain, hat, inverse).astype(BF16)
-            tri_norm_out[place, :] = tri_norm
-            d_update_out[place, :] = d_update
+    every = slots(groups)
+    for first in range(0, groups, 4):
+        chunk = every[first : first + 4]
+        places = [at(p, cells) for _, _, p in chunk]
+        here = jnp.concatenate([tri[place, :] for place in places], axis=0)
+        tri_f, hat, inverse = layer_norm(here, gain, bias)
+        tri_norm = tri_f.astype(BF16)
+        update = dot(tri_norm, out_weight[...])
+        n, s, _ = chunk[0]
+        out_gate = sigmoid(dot(normed[n][s * cells : (s + 4) * cells, :], gate_weight[...]))
+        if first == 0:
+            block_out[...] = (out_gate[:cells] * update[:cells]).astype(BF16)
+        cot = jnp.concatenate([cots[2 * n + min(s, 1)][max(s - 1, 0) * cells : max(s, 1) * cells, :] for n, s, _ in chunk], axis=0)
+        gated = cot.astype(F32) * out_gate
+        d_update = gated.astype(BF16)
+        d_gates = (gated * update * (1.0 - out_gate)).astype(BF16)
+        d_norm = dot(d_update, out_weight[...], TRANSPOSED)
+        d_tris = norm_back(d_norm, gain, hat, inverse).astype(BF16)
+        for t, place in enumerate(places):
+            part = slice(t * cells, (t + 1) * cells)
+            d_gate[place, :] = d_gates[part]
+            d_tri[place, :] = d_tris[part]
+            tri_norm_out[place, :] = tri_norm[part]
+            d_update_out[place, :] = d_update[part]
 
 
 def contract(rows, cols, count, unroll, start, source, row_at, operand, operand_at):
@@ -205,36 +211,21 @@
     d_gate,
     tri_norm,
     d_update,
-    normed_0,
-    normed_1,
-    left_0,
-    left_1,
-    right_0,
-    right_1,
-    left,
-    right,
-    normed,
-    d_left,
-    d_right,
-    small_grads,
-    source,
+    *refs,
 ):
     rows, cols, groups = sizes
+    left, right, normed, d_left, d_right, small_grads, source = refs[6:]
     cells = rows * cols
     hidden = left.shape[-1]
     channels = normed.shape[-1]
     half = lax.axis_index("col")
     zeros = (jnp.zeros((8, hidden), F32),) * (rows * cols // 8)
     source[...] = d_tri_ref[...].astype(F32)
-    for which, part_n, part_l, part_r in (
-        (0, normed_0, left_0, right_0),
-        (1, normed_1, left_1, right_1),
-    ):
-        for b in range(groups // 2):
-            place, part = at(row_block(which, b), cells), slice(b * cells, (b + 1) * cells)
-            normed[place, :] = part_n[part, :]
-            left[place, :] = part_l[part, :]
-            right[place, :] = part_r[part, :]
+    for n, s, p in slots(groups):
+        place, part = at(p, cells), slice(s * cells, (s + 1) * cells)
+        normed[place, :] = refs[n][part, :]
+        left[place, :] = refs[2 + n][part, :]
+        right[place, :] = refs[4 + n][part, :]
 
     def left_block(p, carry):
         sums = contract(
@@ -284,20 +275,11 @@
     normed,
     d_left,
     d_right,
-    left_gate_0,
-    left_gate_1,
-    left_value_0,
-    left_value_1,
-    right_gate_0,
-    right_gate_1,
-    right_value_0,
-    right_value_1,
-    proj_grad,
-    d_proj,
-    source,
-    d_right_s,
+    *refs,
 ):
     rows, cols, groups = sizes
+    left_gate, left_value, right_gate, right_value = refs[:2], refs[2:4], refs[4:6], refs[6:8]
+    proj_grad, d_proj, source, d_right_s = refs[8:]
     cells = rows * cols
     hidden = left.shape[-1]
     half = lax.axis_index("col")
@@ -324,43 +306,26 @@
 
     lax.fori_loop(0, cols // rows, right_block, 0)
 
-    for which, left_gate, left_value, right_gate, right_value in (
-        (0, left_gate_0, left_value_0, right_gate_0, right_value_0),
-        (1, left_gate_1, left_value_1, right_gate_1, right_value_1),
-    ):
-
-        def left_block(
-            b,
-            carry,
-            which=which,
-            left_gate=left_gate,
-            left_value=left_value,
-            right_gate=right_gate,
-            right_value=right_value,
-        ):
-            p = row_block(which, b)
-            start = p * cells
-            sums = contract(
-                rows,
-                cols,
-                cols,
-                8,
-                tuple(d_left[tile(start + t * 8), :] for t in range(cells // 8)),
-                source,
-                lambda a, j: (p * rows + a) * cols + j,
-                right,
-                lambda j: ((1 - half) * cols + j) * cols,
-            )
-            part, place = at(b, cells), at(p, cells)
-            grads = jnp.concatenate(sums, axis=0)
-            d_proj[place, :hidden] = (grads * left_value[part, :]).astype(BF16)
-            d_proj[place, hidden : 2 * hidden] = (grads * left_gate[part, :]).astype(BF16)
-            grads = d_right_s[place, :]
-            d_proj[place, 2 * hidden : 3 * hidden] = (grads * right_value[part, :]).astype(BF16)
-            d_proj[place, 3 * hidden :] = (grads * right_gate[part, :]).astype(BF16)
-            return carry
-
-        lax.fori_loop(0, groups // 2, left_block, 0)
+    for n, s, p in slots(groups):
+        start = p * cells
+        sums = contract(
+            rows,
+            cols,
+            cols,
+            8,
+            tuple(d_left[tile(start + t * 8), :] for t in range(cells // 8)),
+            source,
+            lambda a, j, p=p: (p * rows + a) * cols + j,
+            right,
+            lambda j: ((1 - half) * cols + j) * cols,
+        )
+        part, place = slice(s * cells, (s + 1) * cells), at(p, cells)
+        grads = jnp.concatenate(sums, axis=0)
+        d_proj[place, :hidden] = (grads * left_value[n][part, :]).astype(BF16)
+        d_proj[place, hidden : 2 * hidden] = (grads * left_gate[n][part, :]).astype(BF16)
+        grads = d_right_s[place, :]
+        d_proj[place, 2 * hidden : 3 * hidden] = (grads * right_value[n][part, :]).astype(BF16)
+        d_proj[place, 3 * hidden :] = (grads * right_gate[n][part, :]).astype(BF16)
 
     scale = 1.0 / (rows * groups)
     proj_grad[...] = dot(normed[...], d_proj[...], BY_ROWS) * scale
@@ -414,7 +379,6 @@
     groups = lax.axis_size("row")
     cells = rows * cols
     every = cells * groups
-    some = every // 2
     sizes = (rows, cols, groups)
 
     def call(kernel, outs, *args, scratch=(), micros=1, name, **more):
@@ -435,11 +399,11 @@
     def over(value):
         return lax.ppermute(value, "col", SWAP)
 
-    def along(value, tied=False):
+    def along(value):
         got = []
-        for s in reversed(range(1, groups // 2)):
-            arrived = across(value, 2 * s)
-            got.append(after(arrived, got[-1]) if got and tied else arrived)
+        for distance in reversed(range(1, groups // 2)):
+            arrived = across(value, 2 * distance)
+            got.append(after(arrived, got[-1]) if got else arrived)
         return got[::-1]
 
     def join(*values):
@@ -448,65 +412,68 @@
     def after(value, *others):
         return lax.optimization_barrier((value, *others))[0]
 
-    full, part = (every, hidden), (some, hidden)
+    full = (every, hidden)
 
     def own_edges(*blocks):
-        outs = [((some, channels), BF16)] + [(part, F32)] * 6
+        count = sum(block.shape[0] for block in blocks)
+        outs = [((count, channels), BF16)] + [((count, hidden), F32)] * 6
         return call(own_edges_kernel, outs, params, proj_weight, *blocks, name="own_edges")
 
     def mate_edges(*blocks):
-        outs = [(part, F32)] * 2
+        outs = [((sum(block.shape[0] for block in blocks), hidden), F32)] * 2
         return call(mate_edges_kernel, outs, params, proj_weight, *blocks, name="mate_edges")
 
-    pair_in = pair_rep.reshape(cells, channels)
-    near = along(pair_in, tied=True)
-    given = [pair_in, cotangent.reshape(cells, channels)]
-    given += [v[None] for v in (norm_gain, norm_bias, tri_gain, tri_bias)]
+    def fetch(kernel, outs, given, name):
+        given = [pltpu.with_memory_space_constraint(v, pltpu.HBM) for v in given]
+        return call(
+            kernel,
+            outs,
+            *given,
+            scratch=[pltpu.SemaphoreType.DMA((len(given),))],
+            in_specs=[pl.BlockSpec(memory_space=pltpu.HBM)] * len(given),
+            name=name,
+        )
+
+    given = [pair_rep.reshape(cells, channels), cotangent.reshape(cells, channels)]
+    (both,) = fetch(fetch_inputs_kernel, [((2 * cells, channels), BF16)], given, "fetch_inputs")
+    got = along(both)
+    given = [v[None] for v in (norm_gain, norm_bias, tri_gain, tri_bias)]
     given += [proj_weight, gate_weight, out_weight]
-    given = [pltpu.with_memory_space_constraint(v, pltpu.HBM) for v in given]
-    both, params, proj_weight, gate_weight, out_weight = call(
-        fetch_kernel,
-        [((2 * cells, channels), BF16), ((4, channels), F32)] + [(a.shape, BF16) for a in given[6:]],
-        *given,
-        scratch=[pltpu.SemaphoreType.DMA((len(given),))],
-        in_specs=[pl.BlockSpec(memory_space=pltpu.HBM)] * len(given),
-        name="fetch",
-    )
+    outs = [((4, channels), F32)] + [(a.shape, BF16) for a in given[4:]]
+    held = fetch(fetch_weights_kernel, outs, given, "fetch_weights")
+    params, proj_weight, gate_weight, out_weight = held
     both_far = across(both, 1)
+    near_b = after(join(*(block[:cells] for block in got)), params)
+    far_b = across(near_b, 1)
+    cot_b = join(*(block[cells:] for block in got))
+    cot_far_b = across(cot_b, 1)
     pair, pair_far = both[:cells], both_far[:cells]
-    near_all = join(*near)
-    far = across(near_all, 1)
-    cots = after(join(both[cells:], both_far[cells:]), near_all)
-    cots = [cots] + along(cots)
-    mate_near = over(join(pair, near_all))
-    own_0 = own_edges(pair, near_all)
+    mate_near = over(join(pair, near_b))
+    cots = (both[cells:], cot_b, both_far[cells:], cot_far_b)
+    own_0 = own_edges(pair, near_b)
     mate_0 = mate_edges(mate_near)
-    far_all = join(pair_far, far)
+    far_all = join(pair_far, after(far_b, mate_0[0]))
     own_1 = own_edges(far_all)
     mate_1 = mate_edges(over(far_all))
     own, mate = (own_0, own_1), (mate_0, mate_1)
     normed = [o[0] for o in own]
     left, left_gate, left_value = ([o[n] for o in own] for n in (1, 2, 3))
     right, right_gate, right_value = ([o[n] for o in own] for n in (4, 5, 6))
-    (tri,) = call(
-        triangle_kernel,
-        [(full, F32)],
-        *left,
-        *(m[0] for m in mate),
-        *right,
-        *(m[1] for m in mate),
-        scratch=[((cols * cols, hidden), F32)] * 2,
-        micros=2,
-        name="triangle",
-    )
+    def triangle(lefts, rights, *more):
+        outs, scratch = [(full, F32)], [((cols * cols, hidden), F32)]
+        args = (*lefts, *rights, *more)
+        return call(triangle_kernel, outs, *args, scratch=scratch, name="triangle")
+
+    tri = triangle(left, right)
+    (tri,) = triangle([m[0] for m in mate], [m[1] for m in mate], *tri)
     block_out, d_tri, d_gate, tri_norm, d_update = call(
         cells_kernel,
         [((cells, channels), BF16)] + [(full, BF16)] * 4,
         params,
         tri,
-        *normed,
         gate_weight,
         out_weight,
+        *normed,
         *cots,
         micros=2,
         name="cells",
@@ -519,7 +486,7 @@
             (full, F32),
             ((every, channels), BF16),
             (full, F32),
-            (part, F32),
+            ((cols * cols, hidden), F32),
             ((channels, 2 * channels), F32),
         ],
         d_tri,
@@ -674,7 +641,7 @@
     groups = lax.axis_size("row")
     every = rows * groups * cols
     fits = 24 * every * channels * 4 <= VMEM_BUDGET and hidden == channels
-    paired = lax.axis_size("col") == 2 and groups & (groups - 1) == 0 and groups >= 4
+    paired = lax.axis_size("col") == 2 and groups & (groups - 1) == 0 and groups >= 8
     whole_tiles = cols % 8 == 0 and cols % (2 * rows) == 0 and rows * cols % 16 == 0
     plan = replicated if fits and paired and whole_tiles else sharded
     return plan(pair_rep, *others)

time: 33.5 us -> 31.5 us (0.940)
  starting transfers between devices: 14.4 us -> 10.9 us
  waiting for transfers between devices: 3.1 us -> 4.3 us
    ppermute x8 -> x6, starting transfers between devices: 13.5 us -> 9.58 us  [across(): return lax.ppermute(value, 'row', [(i, i ^ mask) for i in range(groups)])]
    ppermute x8 -> x6, waiting for transfers between devices: 2.51 us -> 4.02 us  [across(): return lax.ppermute(value, 'row', [(i, i ^ mask) for i in range(groups)])]
    ppermute x5, starting transfers between devices: 0.86 us -> 1.33 us  [over(): return lax.ppermute(value, 'col', SWAP)]
    pallas_call x10 -> x12, Pallas kernels: 14.2 us -> 14.4 us  [call(): pl.pallas_call(functools.partial(kernel, sizes), out_shape=[jax.ShapeDtyp...]
  transfers between devices with their start and end apart: 13 -> 11, of which waited for: 4 -> 4; matrix products, arithmetic and copies ran while one was open for 0% -> 0% of each run, Pallas kernels for 38% -> 41%
where the time goes in v12:
time: 31.5 us; the launch traced here: 31.3 us
  Pallas kernels  14.4 us (46%)
  starting transfers between devices  10.9 us (35%)
  waiting for transfers between devices  4.3 us (14%)
  between operations  0.81 us (3%)
  other arithmetic  0.78 us (2%)
    pallas_call x12, Pallas kernels, call(): pl.pallas_call(functools.partial(kernel, sizes), out_shape=[jax.ShapeDtyp...  14.4 us
    ppermute x6, starting transfers between devices, across(): return lax.ppermute(value, 'row', [(i, i ^ mask) for i in range(groups)])  9.58 us
    ppermute x6, waiting for transfers between devices, across(): return lax.ppermute(value, 'row', [(i, i ^ mask) for i in range(groups)])  4.02 us
    ppermute x5, starting transfers between devices, over(): return lax.ppermute(value, 'col', SWAP)  1.33 us
    add x1, other arithmetic, replicated(): proj_grad + proj_mate  0.74 us
  transfers between devices with their start and end apart: 11, of which 4 were waited for; matrix products, arithmetic and copies ran while one was open for 0% of the time, Pallas kernels for 41%

profile of v12, /device:TPU:0, one launch (start us, length us, event | category | flops | bytes accessed | tf_op | source)
XLA Modules:
  0.0 31.3 jit_solution(580274190507890315)
XLA Ops:
  0.6 0.8 %fetch_inputs.1 = bf16[288,128]{1,0:T(8,128)(2,1)S(1)} custom-call(bf16[144,128]{1,0:T(8,128)(2,1)} %bitcast.8, bf16[144,128]{1,0:T(8,128)(2,1)} %bitcast.9), custom_call_target="tpu_custom_call" | custom-call | flops 1000000000 | tf_op jit(solution)/shard_map/fetch_inputs/pallas_call | solution.py:386
  1.4 5.1 %collective-permute-start.2 = (bf16[288,128]{1,0:T(8,128)(2,1)S(1)}, bf16[288,128]{1,0:T(8,128)(2,1)S(1)}, u32[]{:S(2)}, u32[]{:S(2)}) collective-permute-start(bf16[288,128]{1,0:T(8,128)(2,1)S(1)} %fetch_inputs.1), channel_id=1, source_target_pairs={{0,12},{2,14},{4,8},{6,10},{8,4},{10,6},{12,0},{14,2},{1,13},{3,15... | collective-permute-start | bytes 221192 | tf_op jit(solution)/shard_map/ppermute | solution.py:397
  6.6 0.0 collective-permute-start.1
  6.6 0.6 %collective-permute-start = (bf16[288,128]{1,0:T(8,128)(2,1)S(1)}, bf16[288,128]{1,0:T(8,128)(2,1)S(1)}, u32[]{:S(2)}, u32[]{:S(2)}) collective-permute-start(bf16[288,128]{1,0:T(8,128)(2,1)S(1)} %fetch_inputs.1), channel_id=1, source_target_pairs={{0,4},{2,6},{4,0},{6,2},{8,12},{10,14},{12,8},{14,10},{1,5},{3,7},... | collective-permute-start | bytes 221192 | tf_op jit(solution)/shard_map/ppermute | solution.py:397
  7.2 1.7 %collective-permute-start.4 = (bf16[288,128]{1,0:T(8,128)(2,1)S(1)}, bf16[288,128]{1,0:T(8,128)(2,1)S(1)}, u32[]{:S(2)}, u32[]{:S(2)}) collective-permute-start(bf16[288,128]{1,0:T(8,128)(2,1)S(1)} %fetch_inputs.1), channel_id=1, source_target_pairs={{0,2},{2,0},{4,6},{6,4},{8,10},{10,8},{12,14},{14,12},{1,3},{3,1},... | collective-permute-start | bytes 221192 | tf_op jit(solution)/shard_map/ppermute | solution.py:397
  8.9 1.0 %fetch_weights.1 = (f32[4,128]{1,0:T(4,128)S(1)}, bf16[128,512]{1,0:T(8,128)(2,1)S(1)}, bf16[128,128]{1,0:T(8,128)(2,1)S(1)}, bf16[128,128]{1,0:T(8,128)(2,1)S(1)}) custom-call(f32[1,128]{1,0:T(1,128)} %bitcast.10, f32[1,128]{1,0:T(1,128)} %bitcast.11, f32[1,128]{1,0:T(1,128)} %bitcast.12, f32[1,128]{1,0:T(1,128)} %bitcast.13, bf16[128,512]{1,0:T(8,128)(2,1)} %refs_4_.1, ...), custom_call_target="tpu_custom_call" | custom-call | flops 1000000000 | tf_op jit(solution)/shard_map/fetch_weights/pallas_call | solution.py:386
  9.9 0.0 collective-permute-done.2
  9.9 2.9 %collective-permute-done.1 = bf16[288,128]{1,0:T(8,128)(2,1)S(1)} collective-permute-done((bf16[288,128]{1,0:T(8,128)(2,1)S(1)}, bf16[288,128]{1,0:T(8,128)(2,1)S(1)}, u32[]{:S(2)}, u32[]{:S(2)}) %collective-permute-start.1) | collective-permute-done | bytes 73760 | tf_op jit(solution)/shard_map/ppermute | solution.py:397
  12.8 0.0 collective-permute-done
  12.8 1.6 %collective-permute-start.5 = (bf16[432,128]{1,0:T(8,128)(2,1)S(1)}, bf16[432,128]{1,0:T(8,128)(2,1)S(1)}, u32[]{:S(2)}, u32[]{:S(2)}) collective-permute-start(bf16[432,128]{1,0:T(8,128)(2,1)S(1)} %pad_maximum_fusion.2.refs_1_), channel_id=1, source_target_pairs={{0,2},{2,0},{4,6},{6,4},{8,10},{10,8},{12,14},{14,12},{1,3},{3,1},... | collective-permute-start | bytes 331784 | tf_op jit(solution)/shard_map/ppermute | solution.py:397
  14.4 0.1 collective-permute-start.3
  14.5 0.6 %collective-permute-start.7 = (bf16[432,128]{1,0:T(8,128)(2,1)S(1)}, bf16[432,128]{1,0:T(8,128)(2,1)S(1)}, u32[]{:S(2)}, u32[]{:S(2)}) collective-permute-start(bf16[432,128]{1,0:T(8,128)(2,1)S(1)} %pad_maximum_fusion.3.refs_3_), channel_id=1, source_target_pairs={{0,2},{2,0},{4,6},{6,4},{8,10},{10,8},{12,14},{14,12},{1,3},{3,1},... | collective-permute-start | bytes 331784 | tf_op jit(solution)/shard_map/ppermute | solution.py:397
  15.1 0.6 %own_edges.2 = (bf16[576,128]{1,0:T(8,128)(2,1)S(1)}, f32[576,128]{1,0:T(8,128)S(1)}, f32[576,128]{1,0:T(8,128)S(1)}, f32[576,128]{1,0:T(8,128)S(1)}, f32[576,12...) custom-call(f32[4,128]{1,0:T(4,128)S(1)} %get-tuple-element.48.params, ...), custom_call_target="tpu_custom_call" | custom-call | flops 1000000000 | tf_op jit(solution)/shard_map/own_edges/pallas_call | solution.py:386
  15.7 0.0 collective-permute-done.4
  15.8 0.1 collective-permute-done.3.refs_0_
  15.9 0.6 %mate_edges.2 = (f32[576,128]{1,0:T(8,128)S(1)}, f32[576,128]{1,0:T(8,128)S(1)}) custom-call(f32[4,128]{1,0:T(4,128)S(1)} %get-tuple-element.48.params, bf16[128,512]{1,0:T(8,128)(2,1)S(1)} %get-tuple-element.49.weight.proj_weight, bf16[576,128]{1,0:T(8,128)(2,1)S(1)} %collective-permute-done.3.refs_0_), custom_call_target="tpu_custom_call" | custom-call | flops 1000000000 | tf_op jit(solution)/shard_map/mate_edges/pallas_call | solution.py:386
  16.5 1.2 %collective-permute-done.5 = bf16[432,128]{1,0:T(8,128)(2,1)S(1)} collective-permute-done((bf16[432,128]{1,0:T(8,128)(2,1)S(1)}, bf16[432,128]{1,0:T(8,128)(2,1)S(1)}, u32[]{:S(2)}, u32[]{:S(2)}) %collective-permute-start.5) | collective-permute-done | bytes 110624 | tf_op jit(solution)/shard_map/ppermute | solution.py:397
  17.7 0.1 collective-permute-start.6
  17.7 0.6 %own_edges.3 = (bf16[576,128]{1,0:T(8,128)(2,1)S(1)}, f32[576,128]{1,0:T(8,128)S(1)}, f32[576,128]{1,0:T(8,128)S(1)}, f32[576,128]{1,0:T(8,128)S(1)}, f32[576,12...) custom-call(f32[4,128]{1,0:T(4,128)S(1)} %get-tuple-element.48.params, ...), custom_call_target="tpu_custom_call" | custom-call | flops 1000000000 | tf_op jit(solution)/shard_map/own_edges/pallas_call | solution.py:386
  18.4 1.3 %triangle.2.refs_4_ = f32[1152,128]{1,0:T(8,128)S(1)} custom-call(f32[576,128]{1,0:T(8,128)S(1)} %get-tuple-element.58.refs_0_.refs_2_, f32[576,128]{1,0:T(8,128)S(1)} %get-tuple-element.59.refs_1_.refs_3_, f32[576,128]{1,0:T(8,128)S(1)} %get-tuple-element.60.refs_2_.refs_4_, f32[576,128]{1,0:T(8,128)S(1)} %get-tuple-element.61.refs_3_.refs_5_), custom_call_target="tpu_custom_call" | custom-call | flops 1000000000 | tf_op jit(solution)/shard_map/triangle/pallas_call | solution.py:386
  19.7 0.0 collective-permute-done.6.refs_0_
  19.7 0.6 %mate_edges.3 = (f32[576,128]{1,0:T(8,128)S(1)}, f32[576,128]{1,0:T(8,128)S(1)}) custom-call(f32[4,128]{1,0:T(4,128)S(1)} %get-tuple-element.48.params, bf16[128,512]{1,0:T(8,128)(2,1)S(1)} %get-tuple-element.49.weight.proj_weight, bf16[576,128]{1,0:T(8,128)(2,1)S(1)} %collective-permute-done.6.refs_0_), custom_call_target="tpu_custom_call" | custom-call | flops 1000000000 | tf_op jit(solution)/shard_map/mate_edges/pallas_call | solution.py:386
  20.3 1.3 %triangle.3.tri = f32[1152,128]{1,0:T(8,128)S(1)} custom-call(f32[576,128]{1,0:T(8,128)S(1)} %get-tuple-element.53.refs_0_, f32[576,128]{1,0:T(8,128)S(1)} %get-tuple-element.55.refs_1_, f32[576,128]{1,0:T(8,128)S(1)} %get-tuple-element.56.refs_2_, f32[576,128]{1,0:T(8,128)S(1)} %get-tuple-element.57.refs_3_, f32[1152,128]{1,0:T(8,128)S(1)} %triangle.2.refs_4_), custom_call_target="tpu_custom_call" | custom-call | flops 1000000000 | tf_op jit(solution)/shard_map/triangle/pallas_call | solution.py:386
  21.6 0.9 %cells.1 = (bf16[144,128]{1,0:T(8,128)(2,1)S(1)}, bf16[1152,128]{1,0:T(8,128)(2,1)S(1)}, bf16[1152,128]{1,0:T(8,128)(2,1)S(1)}, bf16[1152,128]{1,0:T(8,128)(2,1)S(1)}, bf16[1152,128]{1,0:T(8,128)(2,1)S(1)}) custom-call(f32[4,128]{1,0:T(4,128)S(1)} %get-tuple-element.48.params, f32[1152,128]{1,0:T(8,128)S(1)} %triangle.3.tri, ...), custom_call_target="tpu_custom_call" | custom-call | flops 2000000000 | tf_op jit(solution)/shard_map/cells/pallas_call | solution.py:386
  22.6 0.6 %collective-permute-start.8 = (bf16[1152,128]{1,0:T(8,128)(2,1)S(1)}, bf16[1152,128]{1,0:T(8,128)(2,1)S(1)}, u32[]{:S(2)}, u32[]{:S(2)}) collective-permute-start(bf16[1152,128]{1,0:T(8,128)(2,1)S(1)} %get-tuple-element.66.d_tri_ref), channel_id=1, source_target_pairs={{0,1},{1,0},{2,3},{3,2},{4,5},{5,4},{6,7},{7,6},{8,9},{9,8},{10,11... | collective-permute-start | bytes 884744 | tf_op jit(solution)/shard_map/ppermute | solution.py:400
  23.1 2.8 %early.1 = (f32[1152,128]{1,0:T(8,128)S(1)}, f32[1152,128]{1,0:T(8,128)S(1)}, bf16[1152,128]{1,0:T(8,128)(2,1)S(1)}, f32[1152,128]{1,0:T(8,128)S(1)}, f32[576,128]{1,0:T(8,128)S(1)}, /*index=5*/f32[128,256]{1,0:T(8,128)S(1)}) custom-call(bf16[1152,128]{1,0:T(8,128)(2,1)S(1)} %get-tuple-element.66.d_tri_ref, bf16[1152,128]{1,0:T(8,128)(2,1)S(1)} %get-tuple-element.67.d_gate, ...), custom_call_target="tpu_custom_call" | custom-call | flops 30000001024 | tf_op jit(solution)/shard_map/early/pallas_call | solution.py:386
  25.9 0.1 collective-permute-start.9
  26.0 2.8 %late.1 = (f32[128,512]{1,0:T(8,128)S(1)}, bf16[1152,512]{1,0:T(8,128)(2,1)S(1)}) custom-call(bf16[1152,128]{1,0:T(8,128)(2,1)S(1)} %collective-permute-done.8.d_tri_ref, f32[1152,128]{1,0:T(8,128)S(1)} %get-tuple-element.70.left, f32[1152,128]{1,0:T(8,128)S(1)} %get-tuple-element.71.right, bf16[1152,128]{1,0:T(8,128)(2,1)S(1)} %get-tuple-element.72.normed, ...), custom_call_target="tpu_custom_call" | custom-call | flops 40000000000 | tf_op jit(solution)/shard_map/late/pallas_call | solution.py:386
  28.8 0.5 %collective-permute-start.10 = (f32[128,512]{1,0:T(8,128)S(1)}, f32[128,512]{1,0:T(8,128)S(1)}, u32[]{:S(2)}, u32[]{:S(2)}) collective-permute-start(f32[128,512]{1,0:T(8,128)S(1)} %get-tuple-element.88), channel_id=1, source_target_pairs={{0,1},{1,0},{2,3},{3,2},{4,5},{5,4},{6,7},{7,6},{8,9},{9,8},{10,11... | collective-permute-start | bytes 786440 | tf_op jit(solution)/shard_map/ppermute | solution.py:400
  29.4 1.0 %outputs.1 = (bf16[144,128]{1,0:T(8,128)(2,1)}, f32[144,128]{1,0:T(8,128)}, f32[128,128]{1,0:T(8,128)}, f32[128,128]{1,0:T(8,128)}) custom-call(f32[4,128]{1,0:T(4,128)S(1)} %get-tuple-element.48.params, bf16[144,128]{1,0:T(8,128)(2,1)S(1)} %get-tuple-element.100.refs_0_.pair, bf16[1152,512]{1,0:T(8,128)(2,1)S(1)} %get-tuple-element.83.d_proj, ...), custom_call_target="tpu_custom_call" | custom-call | flops 10000000000 | tf_op jit(solution)/shard_map/outputs/pallas_call | solution.py:386
  30.4 0.2 collective-permute-done.10
  30.5 0.7 %add.3 = f32[128,512]{1,0:T(8,128)} add(f32[128,512]{1,0:T(8,128)S(1)} %get-tuple-element.88, f32[128,512]{1,0:T(8,128)S(1)} %collective-permute-done.10) | non-fusion elementwise | flops 65536 | bytes 786432 | tf_op jit(solution)/shard_map/add | solution.py:541
  (11 shorter events, 0.1 us)
Async XLA Ops:
  1.4 8.5 %collective-permute-start.2 = (bf16[288,128]{1,0:T(8,128)(2,1)S(1)}, bf16[288,128]{1,0:T(8,128)(2,1)S(1)}, u32[]{:S(2)}, u32[]{:S(2)}) collective-permute-start(bf16[288,128]{1,0:T(8,128)(2,1)S(1)} %fetch_inputs.1), channel_id=1, source_target_pairs={{0,12},{2,14},{4,8},{6,10},{8,4},{10,6},{12,0},{14,2},{1,13},{3,15... | collective-permute-start | bytes 221192 | tf_op jit(solution)/shard_map/ppermute | solution.py:397
  6.6 6.2 %collective-permute-start.1 = (bf16[288,128]{1,0:T(8,128)(2,1)S(1)}, bf16[288,128]{1,0:T(8,128)(2,1)S(1)}, u32[]{:S(2)}, u32[]{:S(2)}) collective-permute-start(bf16[288,128]{1,0:T(8,128)(2,1)S(1)} %fetch_inputs.1), channel_id=1, source_target_pairs={{0,8},{2,10},{4,12},{6,14},{8,0},{10,2},{12,4},{14,6},{1,9},{3,11}... | collective-permute-start | bytes 221192 | tf_op jit(solution)/shard_map/ppermute | solution.py:397
  6.6 6.2 %collective-permute-start = (bf16[288,128]{1,0:T(8,128)(2,1)S(1)}, bf16[288,128]{1,0:T(8,128)(2,1)S(1)}, u32[]{:S(2)}, u32[]{:S(2)}) collective-permute-start(bf16[288,128]{1,0:T(8,128)(2,1)S(1)} %fetch_inputs.1), channel_id=1, source_target_pairs={{0,4},{2,6},{4,0},{6,2},{8,12},{10,14},{12,8},{14,10},{1,5},{3,7},... | collective-permute-start | bytes 221192 | tf_op jit(solution)/shard_map/ppermute | solution.py:397
  7.2 8.5 %collective-permute-start.4 = (bf16[288,128]{1,0:T(8,128)(2,1)S(1)}, bf16[288,128]{1,0:T(8,128)(2,1)S(1)}, u32[]{:S(2)}, u32[]{:S(2)}) collective-permute-start(bf16[288,128]{1,0:T(8,128)(2,1)S(1)} %fetch_inputs.1), channel_id=1, source_target_pairs={{0,2},{2,0},{4,6},{6,4},{8,10},{10,8},{12,14},{14,12},{1,3},{3,1},... | collective-permute-start | bytes 221192 | tf_op jit(solution)/shard_map/ppermute | solution.py:397
  12.8 4.8 %collective-permute-start.5 = (bf16[432,128]{1,0:T(8,128)(2,1)S(1)}, bf16[432,128]{1,0:T(8,128)(2,1)S(1)}, u32[]{:S(2)}, u32[]{:S(2)}) collective-permute-start(bf16[432,128]{1,0:T(8,128)(2,1)S(1)} %pad_maximum_fusion.2.refs_1_), channel_id=1, source_target_pairs={{0,2},{2,0},{4,6},{6,4},{8,10},{10,8},{12,14},{14,12},{1,3},{3,1},... | collective-permute-start | bytes 331784 | tf_op jit(solution)/shard_map/ppermute | solution.py:397
  14.4 1.4 %collective-permute-start.3 = (bf16[576,128]{1,0:T(8,128)(2,1)S(1)}, bf16[576,128]{1,0:T(8,128)(2,1)S(1)}, u32[]{:S(2)}, u32[]{:S(2)}) collective-permute-start(bf16[576,128]{1,0:T(8,128)(2,1)S(1)} %pad_maximum_fusion), channel_id=1, source_target_pairs={{0,1},{1,0},{2,3},{3,2},{4,5},{5,4},{6,7},{7,6},{8,9},{9,8},{10,11... | collective-permute-start | bytes 442376 | tf_op jit(solution)/shard_map/ppermute | solution.py:400
  14.5 7.1 %collective-permute-start.7 = (bf16[432,128]{1,0:T(8,128)(2,1)S(1)}, bf16[432,128]{1,0:T(8,128)(2,1)S(1)}, u32[]{:S(2)}, u32[]{:S(2)}) collective-permute-start(bf16[432,128]{1,0:T(8,128)(2,1)S(1)} %pad_maximum_fusion.3.refs_3_), channel_id=1, source_target_pairs={{0,2},{2,0},{4,6},{6,4},{8,10},{10,8},{12,14},{14,12},{1,3},{3,1},... | collective-permute-start | bytes 331784 | tf_op jit(solution)/shard_map/ppermute | solution.py:397
  17.7 2.0 %collective-permute-start.6 = (bf16[576,128]{1,0:T(8,128)(2,1)S(1)}, bf16[576,128]{1,0:T(8,128)(2,1)S(1)}, u32[]{:S(2)}, u32[]{:S(2)}) collective-permute-start(bf16[576,128]{1,0:T(8,128)(2,1)S(1)} %pad_maximum_fusion.1.refs_0_), channel_id=1, source_target_pairs={{0,1},{1,0},{2,3},{3,2},{4,5},{5,4},{6,7},{7,6},{8,9},{9,8},{10,11... | collective-permute-start | bytes 442376 | tf_op jit(solution)/shard_map/ppermute | solution.py:400
  22.6 3.4 %collective-permute-start.8 = (bf16[1152,128]{1,0:T(8,128)(2,1)S(1)}, bf16[1152,128]{1,0:T(8,128)(2,1)S(1)}, u32[]{:S(2)}, u32[]{:S(2)}) collective-permute-start(bf16[1152,128]{1,0:T(8,128)(2,1)S(1)} %get-tuple-element.66.d_tri_ref), channel_id=1, source_target_pairs={{0,1},{1,0},{2,3},{3,2},{4,5},{5,4},{6,7},{7,6},{8,9},{9,8},{10,11... | collective-permute-start | bytes 884744 | tf_op jit(solution)/shard_map/ppermute | solution.py:400
  25.9 3.5 %collective-permute-start.9 = (f32[128,256]{1,0:T(8,128)S(1)}, f32[128,256]{1,0:T(8,128)S(1)}, u32[]{:S(2)}, u32[]{:S(2)}) collective-permute-start(f32[128,256]{1,0:T(8,128)S(1)} %get-tuple-element.85.small_own), channel_id=1, source_target_pairs={{0,1},{1,0},{2,3},{3,2},{4,5},{5,4},{6,7},{7,6},{8,9},{9,8},{10,11... | collective-permute-start | bytes 393224 | tf_op jit(solution)/shard_map/ppermute | solution.py:400
  28.8 1.7 %collective-permute-start.10 = (f32[128,512]{1,0:T(8,128)S(1)}, f32[128,512]{1,0:T(8,128)S(1)}, u32[]{:S(2)}, u32[]{:S(2)}) collective-permute-start(f32[128,512]{1,0:T(8,128)S(1)} %get-tuple-element.88), channel_id=1, source_target_pairs={{0,1},{1,0},{2,3},{3,2},{4,5},{5,4},{6,7},{7,6},{8,9},{9,8},{10,11... | collective-permute-start | bytes 786440 | tf_op jit(solution)/shard_map/ppermute | solution.py:400

commit v13 on v12

--- a/solution.py
+++ b/solution.py
@@ -100,24 +100,19 @@
 
 
 def own_edges_kernel(sizes, params, weight, *refs):
-    blocks, normed_out, outs = refs[:-7], refs[-7], refs[-6:]
+    blocks, sent, normed_out, outs = refs[:-8], refs[-8], refs[-7], refs[-6:]
     normed, sides = edges(blocks, params, weight)
     normed_out[...] = normed
+    count = normed.shape[0]
+    sent[:count, :] = sides[0][0].astype(BF16)
+    sent[count:, :] = sides[1][0].astype(BF16)
     for out, value in zip(outs, sides[0] + sides[1], strict=True):
         out[...] = value
 
 
-def mate_edges_kernel(sizes, params, weight, *refs):
-    blocks, left, right = refs[:-2], refs[-2], refs[-1]
-    _, sides = edges(blocks, params, weight)
-    left[...] = sides[0][0]
-    right[...] = sides[1][0]
-
-
-def triangle_kernel(sizes, *refs):
+def triangle_half(sizes, lefts, right_of, more, tri, picked):
     rows, cols, groups = sizes
     cells = rows * cols
-    lefts, rights, more, tri, picked = refs[:2], refs[2:4], refs[4:-2], refs[-2], refs[-1]
     hidden = tri.shape[-1]
     half = lax.axis_index("col")
     count = cols // 8
@@ -126,26 +121,43 @@
 
         @pl.when(p // blocks == half)
         def _(n=n, s=s, p=p):
-            picked[at(p - half * blocks, cells), :] = rights[n][s * cells : (s + 1) * cells, :]
+            picked[at(p - half * blocks, cells), :] = right_of(n, slice(s * cells, (s + 1) * cells))
 
     for n, s, p in slots(groups):
 
-        def step(k, sums, n=n, s=s):
-            new = list(sums)
+        if more is None:
+            first = (jnp.zeros((8, hidden), F32),) * (rows * count)
+        else:
+            first = tuple(more[tile(p * cells + t * 8), :] for t in range(rows * count))
+        sums = list(first)
+        for k in range(cols):
             tiles = [picked[pl.ds(t * 8 * cols + k, 8, stride=cols), :] for t in range(count)]
             for a in range(rows):
                 row = lefts[n][pl.ds((s * rows + a) * cols + k, 1), :]
                 for t in range(count):
-                    new[a * count + t] += row * tiles[t]
-            return tuple(new)
-
-        if more:
-            first = tuple(more[0][tile(p * cells + t * 8), :] for t in range(rows * count))
-        else:
-            first = (jnp.zeros((8, hidden), F32),) * (rows * count)
-        sums = lax.fori_loop(0, cols, step, first, unroll=8)
+                    sums[a * count + t] += row * tiles[t]
         for t, value in enumerate(sums):
             tri[tile(p * cells + t * 8), :] = value
+
+
+def own_triangle_kernel(sizes, left_0, left_1, right_0, right_1, tri, picked):
+    rights = (right_0, right_1)
+    triangle_half(
+        sizes, (left_0, left_1), lambda n, part: rights[n][part, :], None, tri, picked
+    )
+
+
+def mate_triangle_kernel(sizes, edges_0, edges_1, more, tri, picked, left_0, left_1):
+    got = (edges_0, edges_1)
+    lefts = (left_0, left_1)
+    count = left_0.shape[0]
+    for edge, left in zip(got, lefts, strict=True):
+        left[...] = edge[:count, :].astype(F32)
+
+    def right_of(n, part):
+        return got[n][count + part.start : count + part.stop, :].astype(F32)
+
+    triangle_half(sizes, lefts, right_of, more, tri, picked)
 
 
 def cells_kernel(
@@ -205,6 +217,18 @@
     return lax.fori_loop(0, count, step, start, unroll=unroll)
 
 
+def contract_all(rows, cols, count, start, source, row_at, operand, operand_at):
+    tiles = cols // 8
+    sums = list(start)
+    for term in range(count):
+        loaded = [operand[tile(operand_at(term) + t * 8), :] for t in range(tiles)]
+        for a in range(rows):
+            row = source[pl.ds(row_at(a, term), 1), :]
+            for t in range(tiles):
+                sums[a * tiles + t] += row * loaded[t]
+    return sums
+
+
 def early_kernel(
     sizes,
     d_tri_ref,
@@ -227,44 +251,36 @@
         left[place, :] = refs[2 + n][part, :]
         right[place, :] = refs[4 + n][part, :]
 
-    def left_block(p, carry):
-        sums = contract(
+    scale = 1.0 / (rows * groups)
+    small_grads[:, :channels] = dot(normed[...], d_gate[...], BY_ROWS) * scale
+    small_grads[:, channels:] = dot(tri_norm[...], d_update[...], BY_ROWS) * scale
+    for p in range(groups):
+        sums = contract_all(
             rows,
             cols,
             cols,
-            8,
             zeros,
             source,
-            lambda a, j: (p * rows + a) * cols + j,
+            lambda a, j, p=p: (p * rows + a) * cols + j,
             right,
             lambda j: (half * cols + j) * cols,
         )
         for t, value in enumerate(sums):
             d_left[tile(p * cells + t * 8), :] = value
-        return carry
-
-    lax.fori_loop(0, groups, left_block, 0)
-
-    def right_block(p, carry):
-        sums = contract(
+
+    for p in range(cols // rows):
+        sums = contract_all(
             rows,
             cols,
             rows * groups,
-            8,
             zeros,
             source,
-            lambda a, i: i * cols + p * rows + a,
+            lambda a, i, p=p: i * cols + p * rows + a,
             left,
             lambda i: i * cols,
         )
         for t, value in enumerate(sums):
             d_right[tile(p * cells + t * 8), :] = value
-        return carry
-
-    lax.fori_loop(0, cols // rows, right_block, 0)
-    scale = 1.0 / (rows * groups)
-    small_grads[:, :channels] = dot(normed[...], d_gate[...], BY_ROWS) * scale
-    small_grads[:, channels:] = dot(tri_norm[...], d_update[...], BY_ROWS) * scale
 
 
 def late_kernel(
@@ -306,14 +322,20 @@
 
     lax.fori_loop(0, cols // rows, right_block, 0)
 
+    scale = 1.0 / (rows * groups)
+    for n, s, p in slots(groups):
+        part, place = slice(s * cells, (s + 1) * cells), at(p, cells)
+        grads = d_right_s[place, :]
+        d_proj[place, 2 * hidden : 3 * hidden] = (grads * right_value[n][part, :]).astype(BF16)
+        d_proj[place, 3 * hidden :] = (grads * right_gate[n][part, :]).astype(BF16)
+    proj_grad[:, 2 * hidden :] = dot(normed[...], d_proj[:, 2 * hidden :], BY_ROWS) * scale
     for n, s, p in slots(groups):
         start = p * cells
-        sums = contract(
+        sums = contract_all(
             rows,
             cols,
             cols,
-            8,
-            tuple(d_left[tile(start + t * 8), :] for t in range(cells // 8)),
+            [d_left[tile(start + t * 8), :] for t in range(cells // 8)],
             source,
             lambda a, j, p=p: (p * rows + a) * cols + j,
             right,
@@ -323,12 +345,7 @@
         grads = jnp.concatenate(sums, axis=0)
         d_proj[place, :hidden] = (grads * left_value[n][part, :]).astype(BF16)
         d_proj[place, hidden : 2 * hidden] = (grads * left_gate[n][part, :]).astype(BF16)
-        grads = d_right_s[place, :]
-        d_proj[place, 2 * hidden : 3 * hidden] = (grads * right_value[n][part, :]).astype(BF16)
-        d_proj[place, 3 * hidden :] = (grads * right_gate[n][part, :]).astype(BF16)
-
-    scale = 1.0 / (rows * groups)
-    proj_grad[...] = dot(normed[...], d_proj[...], BY_ROWS) * scale
+    proj_grad[:, : 2 * hidden] = dot(normed[...], d_proj[:, : 2 * hidden], BY_ROWS) * scale
 
 
 def outputs_kernel(
@@ -416,12 +433,9 @@
 
     def own_edges(*blocks):
         count = sum(block.shape[0] for block in blocks)
-        outs = [((count, channels), BF16)] + [((count, hidden), F32)] * 6
-        return call(own_edges_kernel, outs, params, proj_weight, *blocks, name="own_edges")
-
-    def mate_edges(*blocks):
-        outs = [((sum(block.shape[0] for block in blocks), hidden), F32)] * 2
-        return call(mate_edges_kernel, outs, params, proj_weight, *blocks, name="mate_edges")
+        outs = [((2 * count, hidden), BF16), ((count, channels), BF16)]
+        outs += [((count, hidden), F32)] * 6
+        return call(own_edges_kernel, outs, params, proj_weight, *blocks, micros=10, name="own_edges")
 
     def fetch(kernel, outs, given, name):
         given = [pltpu.with_memory_space_constraint(v, pltpu.HBM) for v in given]
@@ -446,26 +460,23 @@
     near_b = after(join(*(block[:cells] for block in got)), params)
     far_b = across(near_b, 1)
     cot_b = join(*(block[cells:] for block in got))
-    cot_far_b = across(cot_b, 1)
     pair, pair_far = both[:cells], both_far[:cells]
-    mate_near = over(join(pair, near_b))
+    own_0 = own_edges(pair, near_b)
+    mate_0 = over(own_0[0])
+    cot_far_b = across(after(cot_b, own_0[0]), 1)
     cots = (both[cells:], cot_b, both_far[cells:], cot_far_b)
-    own_0 = own_edges(pair, near_b)
-    mate_0 = mate_edges(mate_near)
-    far_all = join(pair_far, after(far_b, mate_0[0]))
-    own_1 = own_edges(far_all)
-    mate_1 = mate_edges(over(far_all))
-    own, mate = (own_0, own_1), (mate_0, mate_1)
+    own_1 = own_edges(pair_far, far_b)
+    mate_1 = over(own_1[0])
+    own = [o[1:] for o in (own_0, own_1)]
     normed = [o[0] for o in own]
     left, left_gate, left_value = ([o[n] for o in own] for n in (1, 2, 3))
     right, right_gate, right_value = ([o[n] for o in own] for n in (4, 5, 6))
-    def triangle(lefts, rights, *more):
-        outs, scratch = [(full, F32)], [((cols * cols, hidden), F32)]
-        args = (*lefts, *rights, *more)
-        return call(triangle_kernel, outs, *args, scratch=scratch, name="triangle")
-
-    tri = triangle(left, right)
-    (tri,) = triangle([m[0] for m in mate], [m[1] for m in mate], *tri)
+    outs, picked, half_left = [(full, F32)], ((cols * cols, hidden), F32), ((every // 2, hidden), F32)
+    tri = call(own_triangle_kernel, outs, *left, *right, scratch=[picked], micros=10, name="own_triangle")
+    scratch = [picked, half_left, half_left]
+
+    args = (mate_0, mate_1, *tri)
+    (tri,) = call(mate_triangle_kernel, outs, *args, scratch=scratch, name="mate_triangle")
     block_out, d_tri, d_gate, tri_norm, d_update = call(
         cells_kernel,
         [((cells, channels), BF16)] + [(full, BF16)] * 4,

time: 31.5 us -> 30 us (0.952)
  Pallas kernels: 14.4 us -> 12.4 us
  waiting for transfers between devices: 4.3 us -> 5.1 us
    pallas_call x12 -> x10, Pallas kernels: 14.4 us -> 12.4 us  [call(): pl.pallas_call(functools.partial(kernel, sizes), out_shape=[jax.ShapeDtyp...]
    ppermute x6, waiting for transfers between devices: 4.02 us -> 4.77 us  [across(): return lax.ppermute(value, 'row', [(i, i ^ mask) for i in range(groups)])]
  transfers between devices with their start and end apart: 11 -> 11, of which waited for: 4 -> 4; matrix products, arithmetic and copies ran while one was open for 0% -> 0% of each run, Pallas kernels for 41% -> 36%
where the time goes in v13:
time: 30 us; the launch traced here: 29.8 us
  Pallas kernels  12.4 us (41%)
  starting transfers between devices  10.8 us (36%)
  waiting for transfers between devices  5.1 us (17%)
  other arithmetic  0.76 us (3%)
  between operations  0.76 us (3%)
    pallas_call x10, Pallas kernels, call(): pl.pallas_call(functools.partial(kernel, sizes), out_shape=[jax.ShapeDtyp...  12.4 us
    ppermute x6, starting transfers between devices, across(): return lax.ppermute(value, 'row', [(i, i ^ mask) for i in range(groups)])  9.58 us
    ppermute x6, waiting for transfers between devices, across(): return lax.ppermute(value, 'row', [(i, i ^ mask) for i in range(groups)])  4.77 us
    ppermute x5, starting transfers between devices, over(): return lax.ppermute(value, 'col', SWAP)  1.19 us
    add x1, other arithmetic, replicated(): proj_grad + proj_mate  0.74 us
  transfers between devices with their start and end apart: 11, of which 4 were waited for; matrix products, arithmetic and copies ran while one was open for 0% of the time, Pallas kernels for 36%

profile of v13, /device:TPU:0, one launch (start us, length us, event | category | flops | bytes accessed | tf_op | source)
XLA Modules:
  0.0 29.8 jit_solution(11803408819893329855)
XLA Ops:
  0.6 0.8 %fetch_inputs.1 = bf16[288,128]{1,0:T(8,128)(2,1)S(1)} custom-call(bf16[144,128]{1,0:T(8,128)(2,1)} %bitcast.8, bf16[144,128]{1,0:T(8,128)(2,1)} %bitcast.9), custom_call_target="tpu_custom_call" | custom-call | flops 1000000000 | tf_op jit(solution)/shard_map/fetch_inputs/pallas_call | solution.py:403
  1.4 5.1 %collective-permute-start.2 = (bf16[288,128]{1,0:T(8,128)(2,1)S(1)}, bf16[288,128]{1,0:T(8,128)(2,1)S(1)}, u32[]{:S(2)}, u32[]{:S(2)}) collective-permute-start(bf16[288,128]{1,0:T(8,128)(2,1)S(1)} %fetch_inputs.1), channel_id=1, source_target_pairs={{0,12},{2,14},{4,8},{6,10},{8,4},{10,6},{12,0},{14,2},{1,13},{3,15... | collective-permute-start | bytes 221192 | tf_op jit(solution)/shard_map/ppermute | solution.py:414
  6.6 0.0 collective-permute-start.1
  6.6 0.6 %collective-permute-start = (bf16[288,128]{1,0:T(8,128)(2,1)S(1)}, bf16[288,128]{1,0:T(8,128)(2,1)S(1)}, u32[]{:S(2)}, u32[]{:S(2)}) collective-permute-start(bf16[288,128]{1,0:T(8,128)(2,1)S(1)} %fetch_inputs.1), channel_id=1, source_target_pairs={{0,4},{2,6},{4,0},{6,2},{8,12},{10,14},{12,8},{14,10},{1,5},{3,7},... | collective-permute-start | bytes 221192 | tf_op jit(solution)/shard_map/ppermute | solution.py:414
  7.2 1.7 %collective-permute-start.4 = (bf16[288,128]{1,0:T(8,128)(2,1)S(1)}, bf16[288,128]{1,0:T(8,128)(2,1)S(1)}, u32[]{:S(2)}, u32[]{:S(2)}) collective-permute-start(bf16[288,128]{1,0:T(8,128)(2,1)S(1)} %fetch_inputs.1), channel_id=1, source_target_pairs={{0,2},{2,0},{4,6},{6,4},{8,10},{10,8},{12,14},{14,12},{1,3},{3,1},... | collective-permute-start | bytes 221192 | tf_op jit(solution)/shard_map/ppermute | solution.py:414
  8.9 1.0 %fetch_weights.1 = (f32[4,128]{1,0:T(4,128)S(1)}, bf16[128,512]{1,0:T(8,128)(2,1)S(1)}, bf16[128,128]{1,0:T(8,128)(2,1)S(1)}, bf16[128,128]{1,0:T(8,128)(2,1)S(1)}) custom-call(f32[1,128]{1,0:T(1,128)} %bitcast.10, f32[1,128]{1,0:T(1,128)} %bitcast.11, f32[1,128]{1,0:T(1,128)} %bitcast.12, f32[1,128]{1,0:T(1,128)} %bitcast.13, bf16[128,512]{1,0:T(8,128)(2,1)} %refs_4_.1, ...), custom_call_target="tpu_custom_call" | custom-call | flops 1000000000 | tf_op jit(solution)/shard_map/fetch_weights/pallas_call | solution.py:403
  9.9 0.0 collective-permute-done.2
  9.9 2.9 %collective-permute-done.1 = bf16[288,128]{1,0:T(8,128)(2,1)S(1)} collective-permute-done((bf16[288,128]{1,0:T(8,128)(2,1)S(1)}, bf16[288,128]{1,0:T(8,128)(2,1)S(1)}, u32[]{:S(2)}, u32[]{:S(2)}) %collective-permute-start.1) | collective-permute-done | bytes 73760 | tf_op jit(solution)/shard_map/ppermute | solution.py:414
  12.8 0.0 collective-permute-done
  12.8 1.6 %collective-permute-start.5 = (bf16[432,128]{1,0:T(8,128)(2,1)S(1)}, bf16[432,128]{1,0:T(8,128)(2,1)S(1)}, u32[]{:S(2)}, u32[]{:S(2)}) collective-permute-start(bf16[432,128]{1,0:T(8,128)(2,1)S(1)} %pad_maximum_fusion.refs_1_), channel_id=1, source_target_pairs={{0,2},{2,0},{4,6},{6,4},{8,10},{10,8},{12,14},{14,12},{1,3},{3,1},... | collective-permute-start | bytes 331784 | tf_op jit(solution)/shard_map/ppermute | solution.py:414
  14.4 0.6 %own_edges.2 = (bf16[1152,128]{1,0:T(8,128)(2,1)S(1)}, bf16[576,128]{1,0:T(8,128)(2,1)S(1)}, f32[576,128]{1,0:T(8,128)S(1)}, f32[576,128]{1,0:T(8,128)S(1)}, f32...) custom-call(f32[4,128]{1,0:T(4,128)S(1)} %get-tuple-element.46.params, ...), custom_call_target="tpu_custom_call" | custom-call | flops 10000000000 | tf_op jit(solution)/shard_map/own_edges/pallas_call | solution.py:403
  15.1 0.1 collective-permute-start.3
  15.2 0.6 %collective-permute-start.7 = (bf16[432,128]{1,0:T(8,128)(2,1)S(1)}, bf16[432,128]{1,0:T(8,128)(2,1)S(1)}, u32[]{:S(2)}, u32[]{:S(2)}) collective-permute-start(bf16[432,128]{1,0:T(8,128)(2,1)S(1)} %pad_maximum_fusion.1.refs_3_), channel_id=1, source_target_pairs={{0,2},{2,0},{4,6},{6,4},{8,10},{10,8},{12,14},{14,12},{1,3},{3,1},... | collective-permute-start | bytes 331784 | tf_op jit(solution)/shard_map/ppermute | solution.py:414
  15.7 0.0 collective-permute-done.4
  15.7 1.9 %collective-permute-done.5.refs_1_ = bf16[432,128]{1,0:T(8,128)(2,1)S(1)} collective-permute-done((bf16[432,128]{1,0:T(8,128)(2,1)S(1)}, bf16[432,128]{1,0:T(8,128)(2,1)S(1)}, u32[]{:S(2)}, u32[]{:S(2)}) %collective-permute-start.5) | collective-permute-done | bytes 110624 | tf_op jit(solution)/shard_map/ppermute | solution.py:414
  17.6 0.6 %own_edges.3 = (bf16[1152,128]{1,0:T(8,128)(2,1)S(1)}, bf16[576,128]{1,0:T(8,128)(2,1)S(1)}, f32[576,128]{1,0:T(8,128)S(1)}, f32[576,128]{1,0:T(8,128)S(1)}, f32...) custom-call(f32[4,128]{1,0:T(4,128)S(1)} %get-tuple-element.46.params, ...), custom_call_target="tpu_custom_call" | custom-call | flops 10000000000 | tf_op jit(solution)/shard_map/own_edges/pallas_call | solution.py:403
  18.3 0.1 collective-permute-start.6
  18.4 1.4 %own_triangle.1.more = f32[1152,128]{1,0:T(8,128)S(1)} custom-call(f32[576,128]{1,0:T(8,128)S(1)} %get-tuple-element.53.left_0.refs_2_, f32[576,128]{1,0:T(8,128)S(1)} %get-tuple-element.54.left_1.refs_3_, f32[576,128]{1,0:T(8,128)S(1)} %get-tuple-element.55.right_0.refs_4_, f32[576,128]{1,0:T(8,128)S(1)} %get-tuple-element.56.right_1.refs_5_), custom_call_target="tpu_custom_call" | custom-call | flops 10000000000 | tf_op jit(solution)/shard_map/own_triangle/pallas_call | solution.py:403
  19.8 0.0 collective-permute-done.3.edges_0
  19.8 0.1 collective-permute-done.6.edges_1
  19.9 1.2 %mate_triangle.1.tri = f32[1152,128]{1,0:T(8,128)S(1)} custom-call(bf16[1152,128]{1,0:T(8,128)(2,1)S(1)} %collective-permute-done.3.edges_0, bf16[1152,128]{1,0:T(8,128)(2,1)S(1)} %collective-permute-done.6.edges_1, f32[1152,128]{1,0:T(8,128)S(1)} %own_triangle.1.more), custom_call_target="tpu_custom_call" | custom-call | flops 1000000000 | tf_op jit(solution)/shard_map/mate_triangle/pallas_call | solution.py:403
  21.1 0.0 collective-permute-done.7.refs_5_
  21.1 0.9 %cells.1 = (bf16[144,128]{1,0:T(8,128)(2,1)S(1)}, bf16[1152,128]{1,0:T(8,128)(2,1)S(1)}, bf16[1152,128]{1,0:T(8,128)(2,1)S(1)}, bf16[1152,128]{1,0:T(8,128)(2,1)S(1)}, bf16[1152,128]{1,0:T(8,128)(2,1)S(1)}) custom-call(f32[4,128]{1,0:T(4,128)S(1)} %get-tuple-element.46.params, f32[1152,128]{1,0:T(8,128)S(1)} %mate_triangle.1.tri, ...), custom_call_target="tpu_custom_call" | custom-call | flops 2000000000 | tf_op jit(solution)/shard_map/cells/pallas_call | solution.py:403
  22.1 0.4 %collective-permute-start.8 = (bf16[1152,128]{1,0:T(8,128)(2,1)S(1)}, bf16[1152,128]{1,0:T(8,128)(2,1)S(1)}, u32[]{:S(2)}, u32[]{:S(2)}) collective-permute-start(bf16[1152,128]{1,0:T(8,128)(2,1)S(1)} %get-tuple-element.62.d_tri_ref), channel_id=1, source_target_pairs={{0,1},{1,0},{2,3},{3,2},{4,5},{5,4},{6,7},{7,6},{8,9},{9,8},{10,11... | collective-permute-start | bytes 884744 | tf_op jit(solution)/shard_map/ppermute | solution.py:417
  22.5 2.1 %early.1 = (f32[1152,128]{1,0:T(8,128)S(1)}, f32[1152,128]{1,0:T(8,128)S(1)}, bf16[1152,128]{1,0:T(8,128)(2,1)S(1)}, f32[1152,128]{1,0:T(8,128)S(1)}, f32[576,128]{1,0:T(8,128)S(1)}, /*index=5*/f32[128,256]{1,0:T(8,128)S(1)}) custom-call(bf16[1152,128]{1,0:T(8,128)(2,1)S(1)} %get-tuple-element.62.d_tri_ref, bf16[1152,128]{1,0:T(8,128)(2,1)S(1)} %get-tuple-element.63.d_gate, ...), custom_call_target="tpu_custom_call" | custom-call | flops 30000001024 | tf_op jit(solution)/shard_map/early/pallas_call | solution.py:403
  24.5 0.2 collective-permute-start.9
  24.8 0.0 collective-permute-done.8.d_tri_ref
  24.8 2.6 %late.1 = (f32[128,512]{1,0:T(8,128)S(1)}, bf16[1152,512]{1,0:T(8,128)(2,1)S(1)}) custom-call(bf16[1152,128]{1,0:T(8,128)(2,1)S(1)} %collective-permute-done.8.d_tri_ref, f32[1152,128]{1,0:T(8,128)S(1)} %get-tuple-element.66.left, f32[1152,128]{1,0:T(8,128)S(1)} %get-tuple-element.67.right, bf16[1152,128]{1,0:T(8,128)(2,1)S(1)} %get-tuple-element.68.normed, ...), custom_call_target="tpu_custom_call" | custom-call | flops 40000000000 | tf_op jit(solution)/shard_map/late/pallas_call | solution.py:403
  27.4 0.4 %collective-permute-start.10 = (f32[128,512]{1,0:T(8,128)S(1)}, f32[128,512]{1,0:T(8,128)S(1)}, u32[]{:S(2)}, u32[]{:S(2)}) collective-permute-start(f32[128,512]{1,0:T(8,128)S(1)} %get-tuple-element.84), channel_id=1, source_target_pairs={{0,1},{1,0},{2,3},{3,2},{4,5},{5,4},{6,7},{7,6},{8,9},{9,8},{10,11... | collective-permute-start | bytes 786440 | tf_op jit(solution)/shard_map/ppermute | solution.py:417
  27.8 1.0 %outputs.1 = (bf16[144,128]{1,0:T(8,128)(2,1)}, f32[144,128]{1,0:T(8,128)}, f32[128,128]{1,0:T(8,128)}, f32[128,128]{1,0:T(8,128)}) custom-call(f32[4,128]{1,0:T(4,128)S(1)} %get-tuple-element.46.params, bf16[144,128]{1,0:T(8,128)(2,1)S(1)} %get-tuple-element.96.refs_0_.pair, bf16[1152,512]{1,0:T(8,128)(2,1)S(1)} %get-tuple-element.79.d_proj, ...), custom_call_target="tpu_custom_call" | custom-call | flops 10000000000 | tf_op jit(solution)/shard_map/outputs/pallas_call | solution.py:403
  28.8 0.2 collective-permute-done.10
  29.0 0.7 %add.3 = f32[128,512]{1,0:T(8,128)} add(f32[128,512]{1,0:T(8,128)S(1)} %get-tuple-element.84, f32[128,512]{1,0:T(8,128)S(1)} %collective-permute-done.10) | non-fusion elementwise | flops 65536 | bytes 786432 | tf_op jit(solution)/shard_map/add | solution.py:552
  (7 shorter events, 0.1 us)
Async XLA Ops:
  1.4 8.5 %collective-permute-start.2 = (bf16[288,128]{1,0:T(8,128)(2,1)S(1)}, bf16[288,128]{1,0:T(8,128)(2,1)S(1)}, u32[]{:S(2)}, u32[]{:S(2)}) collective-permute-start(bf16[288,128]{1,0:T(8,128)(2,1)S(1)} %fetch_inputs.1), channel_id=1, source_target_pairs={{0,12},{2,14},{4,8},{6,10},{8,4},{10,6},{12,0},{14,2},{1,13},{3,15... | collective-permute-start | bytes 221192 | tf_op jit(solution)/shard_map/ppermute | solution.py:414
  6.6 6.2 %collective-permute-start.1 = (bf16[288,128]{1,0:T(8,128)(2,1)S(1)}, bf16[288,128]{1,0:T(8,128)(2,1)S(1)}, u32[]{:S(2)}, u32[]{:S(2)}) collective-permute-start(bf16[288,128]{1,0:T(8,128)(2,1)S(1)} %fetch_inputs.1), channel_id=1, source_target_pairs={{0,8},{2,10},{4,12},{6,14},{8,0},{10,2},{12,4},{14,6},{1,9},{3,11}... | collective-permute-start | bytes 221192 | tf_op jit(solution)/shard_map/ppermute | solution.py:414
  6.6 6.2 %collective-permute-start = (bf16[288,128]{1,0:T(8,128)(2,1)S(1)}, bf16[288,128]{1,0:T(8,128)(2,1)S(1)}, u32[]{:S(2)}, u32[]{:S(2)}) collective-permute-start(bf16[288,128]{1,0:T(8,128)(2,1)S(1)} %fetch_inputs.1), channel_id=1, source_target_pairs={{0,4},{2,6},{4,0},{6,2},{8,12},{10,14},{12,8},{14,10},{1,5},{3,7},... | collective-permute-start | bytes 221192 | tf_op jit(solution)/shard_map/ppermute | solution.py:414
  7.2 8.5 %collective-permute-start.4 = (bf16[288,128]{1,0:T(8,128)(2,1)S(1)}, bf16[288,128]{1,0:T(8,128)(2,1)S(1)}, u32[]{:S(2)}, u32[]{:S(2)}) collective-permute-start(bf16[288,128]{1,0:T(8,128)(2,1)S(1)} %fetch_inputs.1), channel_id=1, source_target_pairs={{0,2},{2,0},{4,6},{6,4},{8,10},{10,8},{12,14},{14,12},{1,3},{3,1},... | collective-permute-start | bytes 221192 | tf_op jit(solution)/shard_map/ppermute | solution.py:414
  12.8 4.8 %collective-permute-start.5 = (bf16[432,128]{1,0:T(8,128)(2,1)S(1)}, bf16[432,128]{1,0:T(8,128)(2,1)S(1)}, u32[]{:S(2)}, u32[]{:S(2)}) collective-permute-start(bf16[432,128]{1,0:T(8,128)(2,1)S(1)} %pad_maximum_fusion.refs_1_), channel_id=1, source_target_pairs={{0,2},{2,0},{4,6},{6,4},{8,10},{10,8},{12,14},{14,12},{1,3},{3,1},... | collective-permute-start | bytes 331784 | tf_op jit(solution)/shard_map/ppermute | solution.py:414
  15.1 4.8 %collective-permute-start.3 = (bf16[1152,128]{1,0:T(8,128)(2,1)S(1)}, bf16[1152,128]{1,0:T(8,128)(2,1)S(1)}, u32[]{:S(2)}, u32[]{:S(2)}) collective-permute-start(bf16[1152,128]{1,0:T(8,128)(2,1)S(1)} %get-tuple-element.51), channel_id=1, source_target_pairs={{0,1},{1,0},{2,3},{3,2},{4,5},{5,4},{6,7},{7,6},{8,9},{9,8},{10,11... | collective-permute-start | bytes 884744 | tf_op jit(solution)/shard_map/ppermute | solution.py:417
  15.2 6.0 %collective-permute-start.7 = (bf16[432,128]{1,0:T(8,128)(2,1)S(1)}, bf16[432,128]{1,0:T(8,128)(2,1)S(1)}, u32[]{:S(2)}, u32[]{:S(2)}) collective-permute-start(bf16[432,128]{1,0:T(8,128)(2,1)S(1)} %pad_maximum_fusion.1.refs_3_), channel_id=1, source_target_pairs={{0,2},{2,0},{4,6},{6,4},{8,10},{10,8},{12,14},{14,12},{1,3},{3,1},... | collective-permute-start | bytes 331784 | tf_op jit(solution)/shard_map/ppermute | solution.py:414
  18.3 1.6 %collective-permute-start.6 = (bf16[1152,128]{1,0:T(8,128)(2,1)S(1)}, bf16[1152,128]{1,0:T(8,128)(2,1)S(1)}, u32[]{:S(2)}, u32[]{:S(2)}) collective-permute-start(bf16[1152,128]{1,0:T(8,128)(2,1)S(1)} %get-tuple-element.52), channel_id=1, source_target_pairs={{0,1},{1,0},{2,3},{3,2},{4,5},{5,4},{6,7},{7,6},{8,9},{9,8},{10,11... | collective-permute-start | bytes 884744 | tf_op jit(solution)/shard_map/ppermute | solution.py:417
  22.1 2.7 %collective-permute-start.8 = (bf16[1152,128]{1,0:T(8,128)(2,1)S(1)}, bf16[1152,128]{1,0:T(8,128)(2,1)S(1)}, u32[]{:S(2)}, u32[]{:S(2)}) collective-permute-start(bf16[1152,128]{1,0:T(8,128)(2,1)S(1)} %get-tuple-element.62.d_tri_ref), channel_id=1, source_target_pairs={{0,1},{1,0},{2,3},{3,2},{4,5},{5,4},{6,7},{7,6},{8,9},{9,8},{10,11... | collective-permute-start | bytes 884744 | tf_op jit(solution)/shard_map/ppermute | solution.py:417
  24.5 3.3 %collective-permute-start.9 = (f32[128,256]{1,0:T(8,128)S(1)}, f32[128,256]{1,0:T(8,128)S(1)}, u32[]{:S(2)}, u32[]{:S(2)}) collective-permute-start(f32[128,256]{1,0:T(8,128)S(1)} %get-tuple-element.81.small_own), channel_id=1, source_target_pairs={{0,1},{1,0},{2,3},{3,2},{4,5},{5,4},{6,7},{7,6},{8,9},{9,8},{10,11... | collective-permute-start | bytes 393224 | tf_op jit(solution)/shard_map/ppermute | solution.py:417
  27.4 1.6 %collective-permute-start.10 = (f32[128,512]{1,0:T(8,128)S(1)}, f32[128,512]{1,0:T(8,128)S(1)}, u32[]{:S(2)}, u32[]{:S(2)}) collective-permute-start(f32[128,512]{1,0:T(8,128)S(1)} %get-tuple-element.84), channel_id=1, source_target_pairs={{0,1},{1,0},{2,3},{3,2},{4,5},{5,4},{6,7},{7,6},{8,9},{9,8},{10,11... | collective-permute-start | bytes 786440 | tf_op jit(solution)/shard_map/ppermute | solution.py:417

commit v14 on v13

--- a/solution.py
+++ b/solution.py
@@ -417,11 +417,14 @@
         return lax.ppermute(value, "col", SWAP)
 
     def along(value):
-        got = []
-        for distance in reversed(range(1, groups // 2)):
+        got, before = {}, None
+        middle = groups // 4
+        rest = [d for d in reversed(range(1, groups // 2)) if d != middle]
+        for distance in (middle, *rest):
             arrived = across(value, 2 * distance)
-            got.append(after(arrived, got[-1]) if got else arrived)
-        return got[::-1]
+            before = arrived if before is None else after(arrived, before)
+            got[distance] = before
+        return [got[d] for d in range(1, groups // 2)]
 
     def join(*values):
         return jnp.concatenate(values, axis=0)

time: 30 us -> 29.4 us (0.980)
  waiting for transfers between devices: 5.1 us -> 4.73 us
  starting transfers between devices: 10.8 us -> 10.5 us
    ppermute x6, waiting for transfers between devices: 4.77 us -> 4.4 us  [across(): return lax.ppermute(value, 'row', [(i, i ^ mask) for i in range(groups)])]
  transfers between devices with their start and end apart: 11 -> 11, of which waited for: 4 -> 6; matrix products, arithmetic and copies ran while one was open for 0% -> 0% of each run, Pallas kernels for 36% -> 36%
where the time goes in v14:
time: 29.4 us; the launch traced here: 29.2 us
  Pallas kernels  12.4 us (42%)
  starting transfers between devices  10.5 us (36%)
  waiting for transfers between devices  4.73 us (16%)
  other arithmetic  0.76 us (3%)
  between operations  0.75 us (3%)
    pallas_call x10, Pallas kernels, call(): pl.pallas_call(functools.partial(kernel, sizes), out_shape=[jax.ShapeDtyp...  12.4 us
    ppermute x6, starting transfers between devices, across(): return lax.ppermute(value, 'row', [(i, i ^ mask) for i in range(groups)])  9.36 us
    ppermute x6, waiting for transfers between devices, across(): return lax.ppermute(value, 'row', [(i, i ^ mask) for i in range(groups)])  4.4 us
    ppermute x5, starting transfers between devices, over(): return lax.ppermute(value, 'col', SWAP)  1.19 us
    add x1, other arithmetic, replicated(): proj_grad + proj_mate  0.74 us
  transfers between devices with their start and end apart: 11, of which 6 were waited for; matrix products, arithmetic and copies ran while one was open for 0% of the time, Pallas kernels for 36%

profile of v14, /device:TPU:0, one launch (start us, length us, event | category | flops | bytes accessed | tf_op | source)
XLA Modules:
  0.0 29.2 jit_solution(10379445553992729139)
XLA Ops:
  0.6 0.8 %fetch_inputs.1 = bf16[288,128]{1,0:T(8,128)(2,1)S(1)} custom-call(bf16[144,128]{1,0:T(8,128)(2,1)} %bitcast.8, bf16[144,128]{1,0:T(8,128)(2,1)} %bitcast.9), custom_call_target="tpu_custom_call" | custom-call | flops 1000000000 | tf_op jit(solution)/shard_map/fetch_inputs/pallas_call | solution.py:403
  1.4 4.1 %collective-permute-start.2 = (bf16[288,128]{1,0:T(8,128)(2,1)S(1)}, bf16[288,128]{1,0:T(8,128)(2,1)S(1)}, u32[]{:S(2)}, u32[]{:S(2)}) collective-permute-start(bf16[288,128]{1,0:T(8,128)(2,1)S(1)} %fetch_inputs.1), channel_id=1, source_target_pairs={{0,8},{2,10},{4,12},{6,14},{8,0},{10,2},{12,4},{14,6},{1,9},{3,11}... | collective-permute-start | bytes 221192 | tf_op jit(solution)/shard_map/ppermute | solution.py:414
  5.5 1.3 %collective-permute-start.1 = (bf16[288,128]{1,0:T(8,128)(2,1)S(1)}, bf16[288,128]{1,0:T(8,128)(2,1)S(1)}, u32[]{:S(2)}, u32[]{:S(2)}) collective-permute-start(bf16[288,128]{1,0:T(8,128)(2,1)S(1)} %fetch_inputs.1), channel_id=1, source_target_pairs={{0,12},{2,14},{4,8},{6,10},{8,4},{10,6},{12,0},{14,2},{1,13},{3,15... | collective-permute-start | bytes 221192 | tf_op jit(solution)/shard_map/ppermute | solution.py:414
  6.9 0.2 collective-permute-start
  7.1 1.5 %collective-permute-start.4 = (bf16[288,128]{1,0:T(8,128)(2,1)S(1)}, bf16[288,128]{1,0:T(8,128)(2,1)S(1)}, u32[]{:S(2)}, u32[]{:S(2)}) collective-permute-start(bf16[288,128]{1,0:T(8,128)(2,1)S(1)} %fetch_inputs.1), channel_id=1, source_target_pairs={{0,2},{2,0},{4,6},{6,4},{8,10},{10,8},{12,14},{14,12},{1,3},{3,1},... | collective-permute-start | bytes 221192 | tf_op jit(solution)/shard_map/ppermute | solution.py:414
  8.7 1.0 %fetch_weights.1 = (f32[4,128]{1,0:T(4,128)S(1)}, bf16[128,512]{1,0:T(8,128)(2,1)S(1)}, bf16[128,128]{1,0:T(8,128)(2,1)S(1)}, bf16[128,128]{1,0:T(8,128)(2,1)S(1)}) custom-call(f32[1,128]{1,0:T(1,128)} %bitcast.10, f32[1,128]{1,0:T(1,128)} %bitcast.11, f32[1,128]{1,0:T(1,128)} %bitcast.12, f32[1,128]{1,0:T(1,128)} %bitcast.13, bf16[128,512]{1,0:T(8,128)(2,1)} %refs_4_.1, ...), custom_call_target="tpu_custom_call" | custom-call | flops 1000000000 | tf_op jit(solution)/shard_map/fetch_weights/pallas_call | solution.py:403
  9.7 0.7 %collective-permute-done.2 = bf16[288,128]{1,0:T(8,128)(2,1)S(1)} collective-permute-done((bf16[288,128]{1,0:T(8,128)(2,1)S(1)}, bf16[288,128]{1,0:T(8,128)(2,1)S(1)}, u32[]{:S(2)}, u32[]{:S(2)}) %collective-permute-start.2) | collective-permute-done | bytes 73760 | tf_op jit(solution)/shard_map/ppermute | solution.py:414
  10.4 1.6 %collective-permute-done.1 = bf16[288,128]{1,0:T(8,128)(2,1)S(1)} collective-permute-done((bf16[288,128]{1,0:T(8,128)(2,1)S(1)}, bf16[288,128]{1,0:T(8,128)(2,1)S(1)}, u32[]{:S(2)}, u32[]{:S(2)}) %collective-permute-start.1) | collective-permute-done | bytes 73760 | tf_op jit(solution)/shard_map/ppermute | solution.py:414
  12.0 0.2 collective-permute-done
  12.2 1.8 %collective-permute-start.5 = (bf16[432,128]{1,0:T(8,128)(2,1)S(1)}, bf16[432,128]{1,0:T(8,128)(2,1)S(1)}, u32[]{:S(2)}, u32[]{:S(2)}) collective-permute-start(bf16[432,128]{1,0:T(8,128)(2,1)S(1)} %pad_maximum_fusion.refs_1_), channel_id=1, source_target_pairs={{0,2},{2,0},{4,6},{6,4},{8,10},{10,8},{12,14},{14,12},{1,3},{3,1},... | collective-permute-start | bytes 331784 | tf_op jit(solution)/shard_map/ppermute | solution.py:414
  14.0 0.6 %own_edges.2 = (bf16[1152,128]{1,0:T(8,128)(2,1)S(1)}, bf16[576,128]{1,0:T(8,128)(2,1)S(1)}, f32[576,128]{1,0:T(8,128)S(1)}, f32[576,128]{1,0:T(8,128)S(1)}, f32...) custom-call(f32[4,128]{1,0:T(4,128)S(1)} %get-tuple-element.46.params, ...), custom_call_target="tpu_custom_call" | custom-call | flops 10000000000 | tf_op jit(solution)/shard_map/own_edges/pallas_call | solution.py:403
  14.7 0.1 collective-permute-start.3
  14.8 0.4 %collective-permute-start.7 = (bf16[432,128]{1,0:T(8,128)(2,1)S(1)}, bf16[432,128]{1,0:T(8,128)(2,1)S(1)}, u32[]{:S(2)}, u32[]{:S(2)}) collective-permute-start(bf16[432,128]{1,0:T(8,128)(2,1)S(1)} %pad_maximum_fusion.1.refs_3_), channel_id=1, source_target_pairs={{0,2},{2,0},{4,6},{6,4},{8,10},{10,8},{12,14},{14,12},{1,3},{3,1},... | collective-permute-start | bytes 331784 | tf_op jit(solution)/shard_map/ppermute | solution.py:414
  15.1 0.0 collective-permute-done.4
  15.1 1.9 %collective-permute-done.5.refs_1_ = bf16[432,128]{1,0:T(8,128)(2,1)S(1)} collective-permute-done((bf16[432,128]{1,0:T(8,128)(2,1)S(1)}, bf16[432,128]{1,0:T(8,128)(2,1)S(1)}, u32[]{:S(2)}, u32[]{:S(2)}) %collective-permute-start.5) | collective-permute-done | bytes 110624 | tf_op jit(solution)/shard_map/ppermute | solution.py:414
  17.0 0.6 %own_edges.3 = (bf16[1152,128]{1,0:T(8,128)(2,1)S(1)}, bf16[576,128]{1,0:T(8,128)(2,1)S(1)}, f32[576,128]{1,0:T(8,128)S(1)}, f32[576,128]{1,0:T(8,128)S(1)}, f32...) custom-call(f32[4,128]{1,0:T(4,128)S(1)} %get-tuple-element.46.params, ...), custom_call_target="tpu_custom_call" | custom-call | flops 10000000000 | tf_op jit(solution)/shard_map/own_edges/pallas_call | solution.py:403
  17.7 0.1 collective-permute-start.6
  17.8 1.4 %own_triangle.1.more = f32[1152,128]{1,0:T(8,128)S(1)} custom-call(f32[576,128]{1,0:T(8,128)S(1)} %get-tuple-element.53.left_0.refs_2_, f32[576,128]{1,0:T(8,128)S(1)} %get-tuple-element.54.left_1.refs_3_, f32[576,128]{1,0:T(8,128)S(1)} %get-tuple-element.55.right_0.refs_4_, f32[576,128]{1,0:T(8,128)S(1)} %get-tuple-element.56.right_1.refs_5_), custom_call_target="tpu_custom_call" | custom-call | flops 10000000000 | tf_op jit(solution)/shard_map/own_triangle/pallas_call | solution.py:403
  19.2 0.0 collective-permute-done.3.edges_0
  19.2 0.1 collective-permute-done.6.edges_1
  19.3 1.2 %mate_triangle.1.tri = f32[1152,128]{1,0:T(8,128)S(1)} custom-call(bf16[1152,128]{1,0:T(8,128)(2,1)S(1)} %collective-permute-done.3.edges_0, bf16[1152,128]{1,0:T(8,128)(2,1)S(1)} %collective-permute-done.6.edges_1, f32[1152,128]{1,0:T(8,128)S(1)} %own_triangle.1.more), custom_call_target="tpu_custom_call" | custom-call | flops 1000000000 | tf_op jit(solution)/shard_map/mate_triangle/pallas_call | solution.py:403
  20.5 0.9 %cells.1 = (bf16[144,128]{1,0:T(8,128)(2,1)S(1)}, bf16[1152,128]{1,0:T(8,128)(2,1)S(1)}, bf16[1152,128]{1,0:T(8,128)(2,1)S(1)}, bf16[1152,128]{1,0:T(8,128)(2,1)S(1)}, bf16[1152,128]{1,0:T(8,128)(2,1)S(1)}) custom-call(f32[4,128]{1,0:T(4,128)S(1)} %get-tuple-element.46.params, f32[1152,128]{1,0:T(8,128)S(1)} %mate_triangle.1.tri, ...), custom_call_target="tpu_custom_call" | custom-call | flops 2000000000 | tf_op jit(solution)/shard_map/cells/pallas_call | solution.py:403
  21.5 0.4 %collective-permute-start.8 = (bf16[1152,128]{1,0:T(8,128)(2,1)S(1)}, bf16[1152,128]{1,0:T(8,128)(2,1)S(1)}, u32[]{:S(2)}, u32[]{:S(2)}) collective-permute-start(bf16[1152,128]{1,0:T(8,128)(2,1)S(1)} %get-tuple-element.62.d_tri_ref), channel_id=1, source_target_pairs={{0,1},{1,0},{2,3},{3,2},{4,5},{5,4},{6,7},{7,6},{8,9},{9,8},{10,11... | collective-permute-start | bytes 884744 | tf_op jit(solution)/shard_map/ppermute | solution.py:417
  21.9 2.1 %early.1 = (f32[1152,128]{1,0:T(8,128)S(1)}, f32[1152,128]{1,0:T(8,128)S(1)}, bf16[1152,128]{1,0:T(8,128)(2,1)S(1)}, f32[1152,128]{1,0:T(8,128)S(1)}, f32[576,128]{1,0:T(8,128)S(1)}, /*index=5*/f32[128,256]{1,0:T(8,128)S(1)}) custom-call(bf16[1152,128]{1,0:T(8,128)(2,1)S(1)} %get-tuple-element.62.d_tri_ref, bf16[1152,128]{1,0:T(8,128)(2,1)S(1)} %get-tuple-element.63.d_gate, ...), custom_call_target="tpu_custom_call" | custom-call | flops 30000001024 | tf_op jit(solution)/shard_map/early/pallas_call | solution.py:403
  23.9 0.2 collective-permute-start.9
  24.2 0.0 collective-permute-done.8.d_tri_ref
  24.2 2.6 %late.1 = (f32[128,512]{1,0:T(8,128)S(1)}, bf16[1152,512]{1,0:T(8,128)(2,1)S(1)}) custom-call(bf16[1152,128]{1,0:T(8,128)(2,1)S(1)} %collective-permute-done.8.d_tri_ref, f32[1152,128]{1,0:T(8,128)S(1)} %get-tuple-element.66.left, f32[1152,128]{1,0:T(8,128)S(1)} %get-tuple-element.67.right, bf16[1152,128]{1,0:T(8,128)(2,1)S(1)} %get-tuple-element.68.normed, ...), custom_call_target="tpu_custom_call" | custom-call | flops 40000000000 | tf_op jit(solution)/shard_map/late/pallas_call | solution.py:403
  26.8 0.4 %collective-permute-start.10 = (f32[128,512]{1,0:T(8,128)S(1)}, f32[128,512]{1,0:T(8,128)S(1)}, u32[]{:S(2)}, u32[]{:S(2)}) collective-permute-start(f32[128,512]{1,0:T(8,128)S(1)} %get-tuple-element.84), channel_id=1, source_target_pairs={{0,1},{1,0},{2,3},{3,2},{4,5},{5,4},{6,7},{7,6},{8,9},{9,8},{10,11... | collective-permute-start | bytes 786440 | tf_op jit(solution)/shard_map/ppermute | solution.py:417
  27.2 0.0 collective-permute-done.9.small_mate
  27.2 1.0 %outputs.1 = (bf16[144,128]{1,0:T(8,128)(2,1)}, f32[144,128]{1,0:T(8,128)}, f32[128,128]{1,0:T(8,128)}, f32[128,128]{1,0:T(8,128)}) custom-call(f32[4,128]{1,0:T(4,128)S(1)} %get-tuple-element.46.params, bf16[144,128]{1,0:T(8,128)(2,1)S(1)} %get-tuple-element.96.refs_0_.pair, bf16[1152,512]{1,0:T(8,128)(2,1)S(1)} %get-tuple-element.79.d_proj, ...), custom_call_target="tpu_custom_call" | custom-call | flops 10000000000 | tf_op jit(solution)/shard_map/outputs/pallas_call | solution.py:403
  28.2 0.2 collective-permute-done.10
  28.4 0.7 %add.3 = f32[128,512]{1,0:T(8,128)} add(f32[128,512]{1,0:T(8,128)S(1)} %get-tuple-element.84, f32[128,512]{1,0:T(8,128)S(1)} %collective-permute-done.10) | non-fusion elementwise | flops 65536 | bytes 786432 | tf_op jit(solution)/shard_map/add | solution.py:555
  (7 shorter events, 0.1 us)
Async XLA Ops:
  1.4 9.0 %collective-permute-start.2 = (bf16[288,128]{1,0:T(8,128)(2,1)S(1)}, bf16[288,128]{1,0:T(8,128)(2,1)S(1)}, u32[]{:S(2)}, u32[]{:S(2)}) collective-permute-start(bf16[288,128]{1,0:T(8,128)(2,1)S(1)} %fetch_inputs.1), channel_id=1, source_target_pairs={{0,8},{2,10},{4,12},{6,14},{8,0},{10,2},{12,4},{14,6},{1,9},{3,11}... | collective-permute-start | bytes 221192 | tf_op jit(solution)/shard_map/ppermute | solution.py:414
  5.5 6.5 %collective-permute-start.1 = (bf16[288,128]{1,0:T(8,128)(2,1)S(1)}, bf16[288,128]{1,0:T(8,128)(2,1)S(1)}, u32[]{:S(2)}, u32[]{:S(2)}) collective-permute-start(bf16[288,128]{1,0:T(8,128)(2,1)S(1)} %fetch_inputs.1), channel_id=1, source_target_pairs={{0,12},{2,14},{4,8},{6,10},{8,4},{10,6},{12,0},{14,2},{1,13},{3,15... | collective-permute-start | bytes 221192 | tf_op jit(solution)/shard_map/ppermute | solution.py:414
  6.9 5.3 %collective-permute-start = (bf16[288,128]{1,0:T(8,128)(2,1)S(1)}, bf16[288,128]{1,0:T(8,128)(2,1)S(1)}, u32[]{:S(2)}, u32[]{:S(2)}) collective-permute-start(bf16[288,128]{1,0:T(8,128)(2,1)S(1)} %fetch_inputs.1), channel_id=1, source_target_pairs={{0,4},{2,6},{4,0},{6,2},{8,12},{10,14},{12,8},{14,10},{1,5},{3,7},... | collective-permute-start | bytes 221192 | tf_op jit(solution)/shard_map/ppermute | solution.py:414
  7.1 8.0 %collective-permute-start.4 = (bf16[288,128]{1,0:T(8,128)(2,1)S(1)}, bf16[288,128]{1,0:T(8,128)(2,1)S(1)}, u32[]{:S(2)}, u32[]{:S(2)}) collective-permute-start(bf16[288,128]{1,0:T(8,128)(2,1)S(1)} %fetch_inputs.1), channel_id=1, source_target_pairs={{0,2},{2,0},{4,6},{6,4},{8,10},{10,8},{12,14},{14,12},{1,3},{3,1},... | collective-permute-start | bytes 221192 | tf_op jit(solution)/shard_map/ppermute | solution.py:414
  12.2 4.8 %collective-permute-start.5 = (bf16[432,128]{1,0:T(8,128)(2,1)S(1)}, bf16[432,128]{1,0:T(8,128)(2,1)S(1)}, u32[]{:S(2)}, u32[]{:S(2)}) collective-permute-start(bf16[432,128]{1,0:T(8,128)(2,1)S(1)} %pad_maximum_fusion.refs_1_), channel_id=1, source_target_pairs={{0,2},{2,0},{4,6},{6,4},{8,10},{10,8},{12,14},{14,12},{1,3},{3,1},... | collective-permute-start | bytes 331784 | tf_op jit(solution)/shard_map/ppermute | solution.py:414
  14.7 4.5 %collective-permute-start.3 = (bf16[1152,128]{1,0:T(8,128)(2,1)S(1)}, bf16[1152,128]{1,0:T(8,128)(2,1)S(1)}, u32[]{:S(2)}, u32[]{:S(2)}) collective-permute-start(bf16[1152,128]{1,0:T(8,128)(2,1)S(1)} %get-tuple-element.51), channel_id=1, source_target_pairs={{0,1},{1,0},{2,3},{3,2},{4,5},{5,4},{6,7},{7,6},{8,9},{9,8},{10,11... | collective-permute-start | bytes 884744 | tf_op jit(solution)/shard_map/ppermute | solution.py:417
  14.8 5.8 %collective-permute-start.7 = (bf16[432,128]{1,0:T(8,128)(2,1)S(1)}, bf16[432,128]{1,0:T(8,128)(2,1)S(1)}, u32[]{:S(2)}, u32[]{:S(2)}) collective-permute-start(bf16[432,128]{1,0:T(8,128)(2,1)S(1)} %pad_maximum_fusion.1.refs_3_), channel_id=1, source_target_pairs={{0,2},{2,0},{4,6},{6,4},{8,10},{10,8},{12,14},{14,12},{1,3},{3,1},... | collective-permute-start | bytes 331784 | tf_op jit(solution)/shard_map/ppermute | solution.py:414
  17.7 1.6 %collective-permute-start.6 = (bf16[1152,128]{1,0:T(8,128)(2,1)S(1)}, bf16[1152,128]{1,0:T(8,128)(2,1)S(1)}, u32[]{:S(2)}, u32[]{:S(2)}) collective-permute-start(bf16[1152,128]{1,0:T(8,128)(2,1)S(1)} %get-tuple-element.52), channel_id=1, source_target_pairs={{0,1},{1,0},{2,3},{3,2},{4,5},{5,4},{6,7},{7,6},{8,9},{9,8},{10,11... | collective-permute-start | bytes 884744 | tf_op jit(solution)/shard_map/ppermute | solution.py:417
  21.5 2.7 %collective-permute-start.8 = (bf16[1152,128]{1,0:T(8,128)(2,1)S(1)}, bf16[1152,128]{1,0:T(8,128)(2,1)S(1)}, u32[]{:S(2)}, u32[]{:S(2)}) collective-permute-start(bf16[1152,128]{1,0:T(8,128)(2,1)S(1)} %get-tuple-element.62.d_tri_ref), channel_id=1, source_target_pairs={{0,1},{1,0},{2,3},{3,2},{4,5},{5,4},{6,7},{7,6},{8,9},{9,8},{10,11... | collective-permute-start | bytes 884744 | tf_op jit(solution)/shard_map/ppermute | solution.py:417
  23.9 3.3 %collective-permute-start.9 = (f32[128,256]{1,0:T(8,128)S(1)}, f32[128,256]{1,0:T(8,128)S(1)}, u32[]{:S(2)}, u32[]{:S(2)}) collective-permute-start(f32[128,256]{1,0:T(8,128)S(1)} %get-tuple-element.81.small_own), channel_id=1, source_target_pairs={{0,1},{1,0},{2,3},{3,2},{4,5},{5,4},{6,7},{7,6},{8,9},{9,8},{10,11... | collective-permute-start | bytes 393224 | tf_op jit(solution)/shard_map/ppermute | solution.py:417
  26.8 1.6 %collective-permute-start.10 = (f32[128,512]{1,0:T(8,128)S(1)}, f32[128,512]{1,0:T(8,128)S(1)}, u32[]{:S(2)}, u32[]{:S(2)}) collective-permute-start(f32[128,512]{1,0:T(8,128)S(1)} %get-tuple-element.84), channel_id=1, source_target_pairs={{0,1},{1,0},{2,3},{3,2},{4,5},{5,4},{6,7},{7,6},{8,9},{9,8},{10,11... | collective-permute-start | bytes 786440 | tf_op jit(solution)/shard_map/ppermute | solution.py:417

commit v15 on v14

--- a/solution.py
+++ b/solution.py
@@ -60,6 +60,17 @@
     found = []
     for n, (side, distances) in enumerate(parts(groups)):
         found += [(n, s, row_block(side, d)) for s, d in enumerate(distances)]
+    return found
+
+
+def named_slots(sizes, side, half):
+    rows, cols, _ = sizes
+    me = lax.axis_index("row")
+    blocks = cols // rows
+    found = []
+    for n in range(blocks // 2):
+        place = 2 * n + lax.rem(me + side, 2)
+        found.append((place, lax.bitwise_xor((half * blocks + place) // 2, me // 2)))
     return found
 
 
@@ -99,15 +110,20 @@
         copy.wait()
 
 
-def own_edges_kernel(sizes, params, weight, *refs):
+def own_edges_kernel(side, sizes, params, weight, *refs):
     blocks, sent, normed_out, outs = refs[:-8], refs[-8], refs[-7], refs[-6:]
     normed, sides = edges(blocks, params, weight)
     normed_out[...] = normed
+    for out, value in zip(outs, sides[0] + sides[1], strict=True):
+        out[...] = value
+    rows, cols, groups = sizes
+    cells = rows * cols
     count = normed.shape[0]
     sent[:count, :] = sides[0][0].astype(BF16)
-    sent[count:, :] = sides[1][0].astype(BF16)
-    for out, value in zip(outs, sides[0] + sides[1], strict=True):
-        out[...] = value
+    other = 1 - lax.axis_index("col")
+    for n, (_, slot) in enumerate(named_slots(sizes, side, other)):
+        place = slice(count + n * cells, count + (n + 1) * cells)
+        sent[place, :] = outs[3][at(slot, cells), :].astype(BF16)
 
 
 def triangle_half(sizes, lefts, right_of, more, tri, picked):
@@ -116,12 +132,9 @@
     hidden = tri.shape[-1]
     half = lax.axis_index("col")
     count = cols // 8
-    blocks = cols // rows
-    for n, s, p in slots(groups):
-
-        @pl.when(p // blocks == half)
-        def _(n=n, s=s, p=p):
-            picked[at(p - half * blocks, cells), :] = right_of(n, slice(s * cells, (s + 1) * cells))
+    for n in range(2):
+        for m, (place, slot) in enumerate(named_slots(sizes, n, half)):
+            picked[at(place, cells), :] = right_of(n, m, slot)
 
     for n, s, p in slots(groups):
 
@@ -143,7 +156,12 @@
 def own_triangle_kernel(sizes, left_0, left_1, right_0, right_1, tri, picked):
     rights = (right_0, right_1)
     triangle_half(
-        sizes, (left_0, left_1), lambda n, part: rights[n][part, :], None, tri, picked
+        sizes,
+        (left_0, left_1),
+        lambda n, m, slot: rights[n][at(slot, sizes[0] * sizes[1]), :],
+        None,
+        tri,
+        picked,
     )
 
 
@@ -154,8 +172,10 @@
     for edge, left in zip(got, lefts, strict=True):
         left[...] = edge[:count, :].astype(F32)
 
-    def right_of(n, part):
-        return got[n][count + part.start : count + part.stop, :].astype(F32)
+    cells = sizes[0] * sizes[1]
+
+    def right_of(n, m, slot):
+        return got[n][count + m * cells : count + (m + 1) * cells, :].astype(F32)
 
     triangle_half(sizes, lefts, right_of, more, tri, picked)
 
@@ -308,7 +328,7 @@
             rows,
             cols,
             rows * groups,
-            8,
+            24,
             zeros,
             source,
             lambda a, i: i * cols + p * rows + a,
@@ -434,11 +454,12 @@
 
     full = (every, hidden)
 
-    def own_edges(*blocks):
+    def own_edges(side, *blocks):
         count = sum(block.shape[0] for block in blocks)
-        outs = [((2 * count, hidden), BF16), ((count, channels), BF16)]
+        outs = [((count + count // 2, hidden), BF16), ((count, channels), BF16)]
         outs += [((count, hidden), F32)] * 6
-        return call(own_edges_kernel, outs, params, proj_weight, *blocks, micros=10, name="own_edges")
+        kernel = functools.partial(own_edges_kernel, side)
+        return call(kernel, outs, params, proj_weight, *blocks, micros=10, name="own_edges")
 
     def fetch(kernel, outs, given, name):
         given = [pltpu.with_memory_space_constraint(v, pltpu.HBM) for v in given]
@@ -464,11 +485,11 @@
     far_b = across(near_b, 1)
     cot_b = join(*(block[cells:] for block in got))
     pair, pair_far = both[:cells], both_far[:cells]
-    own_0 = own_edges(pair, near_b)
+    own_0 = own_edges(0, pair, near_b)
     mate_0 = over(own_0[0])
     cot_far_b = across(after(cot_b, own_0[0]), 1)
     cots = (both[cells:], cot_b, both_far[cells:], cot_far_b)
-    own_1 = own_edges(pair_far, far_b)
+    own_1 = own_edges(1, pair_far, far_b)
     mate_1 = over(own_1[0])
     own = [o[1:] for o in (own_0, own_1)]
     normed = [o[0] for o in own]

time: 29.4 us -> 29.1 us (0.990)
  Pallas kernels: 12.4 us -> 11.8 us
  waiting for transfers between devices: 4.73 us -> 5.23 us
    pallas_call x10, Pallas kernels: 12.4 us -> 11.8 us  [call(): pl.pallas_call(functools.partial(kernel, sizes), out_shape=[jax.ShapeDtyp...]
    ppermute x5, waiting for transfers between devices: 0.33 us -> 0.84 us  [over(): return lax.ppermute(value, 'col', SWAP)]
  transfers between devices with their start and end apart: 11 -> 11, of which waited for: 6 -> 6; matrix products, arithmetic and copies ran while one was open for 0% -> 0% of each run, Pallas kernels for 36% -> 35%
where the time goes in v15:
time: 29.1 us; the launch traced here: 28.9 us
  Pallas kernels  11.8 us (41%)
  starting transfers between devices  10.3 us (35%)
  waiting for transfers between devices  5.23 us (18%)
  other arithmetic  0.76 us (3%)
  between operations  0.76 us (3%)
    pallas_call x10, Pallas kernels, call(): pl.pallas_call(functools.partial(kernel, sizes), out_shape=[jax.ShapeDtyp...  11.8 us
    ppermute x6, starting transfers between devices, across(): return lax.ppermute(value, 'row', [(i, i ^ mask) for i in range(groups)])  9.36 us
    ppermute x6, waiting for transfers between devices, across(): return lax.ppermute(value, 'row', [(i, i ^ mask) for i in range(groups)])  4.39 us
    ppermute x5, starting transfers between devices, over(): return lax.ppermute(value, 'col', SWAP)  0.98 us
    ppermute x5, waiting for transfers between devices, over(): return lax.ppermute(value, 'col', SWAP)  0.84 us
    add x1, other arithmetic, replicated(): proj_grad + proj_mate  0.74 us
  transfers between devices with their start and end apart: 11, of which 6 were waited for; matrix products, arithmetic and copies ran while one was open for 0% of the time, Pallas kernels for 35%

profile of v15, /device:TPU:0, one launch (start us, length us, event | category | flops | bytes accessed | tf_op | source)
XLA Modules:
  0.0 28.9 jit_solution(17821628187965247251)
XLA Ops:
  0.6 0.8 %fetch_inputs.1 = bf16[288,128]{1,0:T(8,128)(2,1)S(1)} custom-call(bf16[144,128]{1,0:T(8,128)(2,1)} %bitcast.8, bf16[144,128]{1,0:T(8,128)(2,1)} %bitcast.9), custom_call_target="tpu_custom_call" | custom-call | flops 1000000000 | tf_op jit(solution)/shard_map/fetch_inputs/pallas_call | solution.py:423
  1.4 4.1 %collective-permute-start.2 = (bf16[288,128]{1,0:T(8,128)(2,1)S(1)}, bf16[288,128]{1,0:T(8,128)(2,1)S(1)}, u32[]{:S(2)}, u32[]{:S(2)}) collective-permute-start(bf16[288,128]{1,0:T(8,128)(2,1)S(1)} %fetch_inputs.1), channel_id=1, source_target_pairs={{0,8},{2,10},{4,12},{6,14},{8,0},{10,2},{12,4},{14,6},{1,9},{3,11}... | collective-permute-start | bytes 221192 | tf_op jit(solution)/shard_map/ppermute | solution.py:434
  5.5 1.3 %collective-permute-start.1 = (bf16[288,128]{1,0:T(8,128)(2,1)S(1)}, bf16[288,128]{1,0:T(8,128)(2,1)S(1)}, u32[]{:S(2)}, u32[]{:S(2)}) collective-permute-start(bf16[288,128]{1,0:T(8,128)(2,1)S(1)} %fetch_inputs.1), channel_id=1, source_target_pairs={{0,12},{2,14},{4,8},{6,10},{8,4},{10,6},{12,0},{14,2},{1,13},{3,15... | collective-permute-start | bytes 221192 | tf_op jit(solution)/shard_map/ppermute | solution.py:434
  6.9 0.2 collective-permute-start
  7.1 1.5 %collective-permute-start.4 = (bf16[288,128]{1,0:T(8,128)(2,1)S(1)}, bf16[288,128]{1,0:T(8,128)(2,1)S(1)}, u32[]{:S(2)}, u32[]{:S(2)}) collective-permute-start(bf16[288,128]{1,0:T(8,128)(2,1)S(1)} %fetch_inputs.1), channel_id=1, source_target_pairs={{0,2},{2,0},{4,6},{6,4},{8,10},{10,8},{12,14},{14,12},{1,3},{3,1},... | collective-permute-start | bytes 221192 | tf_op jit(solution)/shard_map/ppermute | solution.py:434
  8.7 1.0 %fetch_weights.1 = (f32[4,128]{1,0:T(4,128)S(1)}, bf16[128,512]{1,0:T(8,128)(2,1)S(1)}, bf16[128,128]{1,0:T(8,128)(2,1)S(1)}, bf16[128,128]{1,0:T(8,128)(2,1)S(1)}) custom-call(f32[1,128]{1,0:T(1,128)} %bitcast.10, f32[1,128]{1,0:T(1,128)} %bitcast.11, f32[1,128]{1,0:T(1,128)} %bitcast.12, f32[1,128]{1,0:T(1,128)} %bitcast.13, bf16[128,512]{1,0:T(8,128)(2,1)} %refs_4_.1, ...), custom_call_target="tpu_custom_call" | custom-call | flops 1000000000 | tf_op jit(solution)/shard_map/fetch_weights/pallas_call | solution.py:423
  9.7 0.7 %collective-permute-done.2 = bf16[288,128]{1,0:T(8,128)(2,1)S(1)} collective-permute-done((bf16[288,128]{1,0:T(8,128)(2,1)S(1)}, bf16[288,128]{1,0:T(8,128)(2,1)S(1)}, u32[]{:S(2)}, u32[]{:S(2)}) %collective-permute-start.2) | collective-permute-done | bytes 73760 | tf_op jit(solution)/shard_map/ppermute | solution.py:434
  10.4 1.6 %collective-permute-done.1 = bf16[288,128]{1,0:T(8,128)(2,1)S(1)} collective-permute-done((bf16[288,128]{1,0:T(8,128)(2,1)S(1)}, bf16[288,128]{1,0:T(8,128)(2,1)S(1)}, u32[]{:S(2)}, u32[]{:S(2)}) %collective-permute-start.1) | collective-permute-done | bytes 73760 | tf_op jit(solution)/shard_map/ppermute | solution.py:434
  12.0 0.2 collective-permute-done
  12.2 1.8 %collective-permute-start.5 = (bf16[432,128]{1,0:T(8,128)(2,1)S(1)}, bf16[432,128]{1,0:T(8,128)(2,1)S(1)}, u32[]{:S(2)}, u32[]{:S(2)}) collective-permute-start(bf16[432,128]{1,0:T(8,128)(2,1)S(1)} %pad_maximum_fusion.refs_1_), channel_id=1, source_target_pairs={{0,2},{2,0},{4,6},{6,4},{8,10},{10,8},{12,14},{14,12},{1,3},{3,1},... | collective-permute-start | bytes 331784 | tf_op jit(solution)/shard_map/ppermute | solution.py:434
  14.0 0.6 %own_edges.2 = (bf16[864,128]{1,0:T(8,128)(2,1)S(1)}, bf16[576,128]{1,0:T(8,128)(2,1)S(1)}, f32[576,128]{1,0:T(8,128)S(1)}, f32[576,128]{1,0:T(8,128)S(1)}, f32[...) custom-call(f32[4,128]{1,0:T(4,128)S(1)} %get-tuple-element.46.params, ...), custom_call_target="tpu_custom_call" | custom-call | flops 10000000000 | tf_op jit(solution)/shard_map/own_edges/pallas_call | solution.py:423
  14.7 0.1 collective-permute-start.3
  14.8 0.4 %collective-permute-start.7 = (bf16[432,128]{1,0:T(8,128)(2,1)S(1)}, bf16[432,128]{1,0:T(8,128)(2,1)S(1)}, u32[]{:S(2)}, u32[]{:S(2)}) collective-permute-start(bf16[432,128]{1,0:T(8,128)(2,1)S(1)} %pad_maximum_fusion.1.refs_3_), channel_id=1, source_target_pairs={{0,2},{2,0},{4,6},{6,4},{8,10},{10,8},{12,14},{14,12},{1,3},{3,1},... | collective-permute-start | bytes 331784 | tf_op jit(solution)/shard_map/ppermute | solution.py:434
  15.1 0.0 collective-permute-done.4
  15.1 1.9 %collective-permute-done.5.refs_1_ = bf16[432,128]{1,0:T(8,128)(2,1)S(1)} collective-permute-done((bf16[432,128]{1,0:T(8,128)(2,1)S(1)}, bf16[432,128]{1,0:T(8,128)(2,1)S(1)}, u32[]{:S(2)}, u32[]{:S(2)}) %collective-permute-start.5) | collective-permute-done | bytes 110624 | tf_op jit(solution)/shard_map/ppermute | solution.py:434
  17.0 0.6 %own_edges.3 = (bf16[864,128]{1,0:T(8,128)(2,1)S(1)}, bf16[576,128]{1,0:T(8,128)(2,1)S(1)}, f32[576,128]{1,0:T(8,128)S(1)}, f32[576,128]{1,0:T(8,128)S(1)}, f32[...) custom-call(f32[4,128]{1,0:T(4,128)S(1)} %get-tuple-element.46.params, ...), custom_call_target="tpu_custom_call" | custom-call | flops 10000000000 | tf_op jit(solution)/shard_map/own_edges/pallas_call | solution.py:423
  17.7 0.1 collective-permute-start.6
  17.8 1.0 %own_triangle.1.more = f32[1152,128]{1,0:T(8,128)S(1)} custom-call(f32[576,128]{1,0:T(8,128)S(1)} %get-tuple-element.53.left_0.refs_2_, f32[576,128]{1,0:T(8,128)S(1)} %get-tuple-element.54.left_1.refs_3_, f32[576,128]{1,0:T(8,128)S(1)} %get-tuple-element.55.right_0.refs_4_, f32[576,128]{1,0:T(8,128)S(1)} %get-tuple-element.56.right_1.refs_5_), custom_call_target="tpu_custom_call" | custom-call | flops 10000000000 | tf_op jit(solution)/shard_map/own_triangle/pallas_call | solution.py:423
  18.8 0.0 collective-permute-done.3.edges_0
  18.8 0.4 %collective-permute-done.6.edges_1 = bf16[864,128]{1,0:T(8,128)(2,1)S(1)} collective-permute-done((bf16[864,128]{1,0:T(8,128)(2,1)S(1)}, bf16[864,128]{1,0:T(8,128)(2,1)S(1)}, u32[]{:S(2)}, u32[]{:S(2)}) %collective-permute-start.6) | collective-permute-done | bytes 221216 | tf_op jit(solution)/shard_map/ppermute | solution.py:437
  19.2 1.1 %mate_triangle.1.tri = f32[1152,128]{1,0:T(8,128)S(1)} custom-call(bf16[864,128]{1,0:T(8,128)(2,1)S(1)} %collective-permute-done.3.edges_0, bf16[864,128]{1,0:T(8,128)(2,1)S(1)} %collective-permute-done.6.edges_1, f32[1152,128]{1,0:T(8,128)S(1)} %own_triangle.1.more), custom_call_target="tpu_custom_call" | custom-call | flops 1000000000 | tf_op jit(solution)/shard_map/mate_triangle/pallas_call | solution.py:423
  20.3 0.0 collective-permute-done.7.refs_5_
  20.3 0.9 %cells.1 = (bf16[144,128]{1,0:T(8,128)(2,1)S(1)}, bf16[1152,128]{1,0:T(8,128)(2,1)S(1)}, bf16[1152,128]{1,0:T(8,128)(2,1)S(1)}, bf16[1152,128]{1,0:T(8,128)(2,1)S(1)}, bf16[1152,128]{1,0:T(8,128)(2,1)S(1)}) custom-call(f32[4,128]{1,0:T(4,128)S(1)} %get-tuple-element.46.params, f32[1152,128]{1,0:T(8,128)S(1)} %mate_triangle.1.tri, ...), custom_call_target="tpu_custom_call" | custom-call | flops 2000000000 | tf_op jit(solution)/shard_map/cells/pallas_call | solution.py:423
  21.2 0.2 collective-permute-start.8
  21.4 2.1 %early.1 = (f32[1152,128]{1,0:T(8,128)S(1)}, f32[1152,128]{1,0:T(8,128)S(1)}, bf16[1152,128]{1,0:T(8,128)(2,1)S(1)}, f32[1152,128]{1,0:T(8,128)S(1)}, f32[576,128]{1,0:T(8,128)S(1)}, /*index=5*/f32[128,256]{1,0:T(8,128)S(1)}) custom-call(bf16[1152,128]{1,0:T(8,128)(2,1)S(1)} %get-tuple-element.62.d_tri_ref, bf16[1152,128]{1,0:T(8,128)(2,1)S(1)} %get-tuple-element.63.d_gate, ...), custom_call_target="tpu_custom_call" | custom-call | flops 30000001024 | tf_op jit(solution)/shard_map/early/pallas_call | solution.py:423
  23.5 0.4 %collective-permute-start.9 = (f32[128,256]{1,0:T(8,128)S(1)}, f32[128,256]{1,0:T(8,128)S(1)}, u32[]{:S(2)}, u32[]{:S(2)}) collective-permute-start(f32[128,256]{1,0:T(8,128)S(1)} %get-tuple-element.81.small_own), channel_id=1, source_target_pairs={{0,1},{1,0},{2,3},{3,2},{4,5},{5,4},{6,7},{7,6},{8,9},{9,8},{10,11... | collective-permute-start | bytes 393224 | tf_op jit(solution)/shard_map/ppermute | solution.py:437
  24.0 0.0 collective-permute-done.8.d_tri_ref
  24.0 2.6 %late.1 = (f32[128,512]{1,0:T(8,128)S(1)}, bf16[1152,512]{1,0:T(8,128)(2,1)S(1)}) custom-call(bf16[1152,128]{1,0:T(8,128)(2,1)S(1)} %collective-permute-done.8.d_tri_ref, f32[1152,128]{1,0:T(8,128)S(1)} %get-tuple-element.66.left, f32[1152,128]{1,0:T(8,128)S(1)} %get-tuple-element.67.right, bf16[1152,128]{1,0:T(8,128)(2,1)S(1)} %get-tuple-element.68.normed, ...), custom_call_target="tpu_custom_call" | custom-call | flops 40000000000 | tf_op jit(solution)/shard_map/late/pallas_call | solution.py:423
  26.5 0.2 collective-permute-start.10
  26.7 1.0 %outputs.1 = (bf16[144,128]{1,0:T(8,128)(2,1)}, f32[144,128]{1,0:T(8,128)}, f32[128,128]{1,0:T(8,128)}, f32[128,128]{1,0:T(8,128)}) custom-call(f32[4,128]{1,0:T(4,128)S(1)} %get-tuple-element.46.params, bf16[144,128]{1,0:T(8,128)(2,1)S(1)} %get-tuple-element.96.refs_0_.pair, bf16[1152,512]{1,0:T(8,128)(2,1)S(1)} %get-tuple-element.79.d_proj, ...), custom_call_target="tpu_custom_call" | custom-call | flops 10000000000 | tf_op jit(solution)/shard_map/outputs/pallas_call | solution.py:423
  27.7 0.4 %collective-permute-done.10 = f32[128,512]{1,0:T(8,128)S(1)} collective-permute-done((f32[128,512]{1,0:T(8,128)S(1)}, f32[128,512]{1,0:T(8,128)S(1)}, u32[]{:S(2)}, u32[]{:S(2)}) %collective-permute-start.10) | collective-permute-done | bytes 262176 | tf_op jit(solution)/shard_map/ppermute | solution.py:437
  28.1 0.7 %add.3 = f32[128,512]{1,0:T(8,128)} add(f32[128,512]{1,0:T(8,128)S(1)} %get-tuple-element.84, f32[128,512]{1,0:T(8,128)S(1)} %collective-permute-done.10) | non-fusion elementwise | flops 65536 | bytes 786432 | tf_op jit(solution)/shard_map/add | solution.py:576
  (7 shorter events, 0.1 us)
Async XLA Ops:
  1.4 9.0 %collective-permute-start.2 = (bf16[288,128]{1,0:T(8,128)(2,1)S(1)}, bf16[288,128]{1,0:T(8,128)(2,1)S(1)}, u32[]{:S(2)}, u32[]{:S(2)}) collective-permute-start(bf16[288,128]{1,0:T(8,128)(2,1)S(1)} %fetch_inputs.1), channel_id=1, source_target_pairs={{0,8},{2,10},{4,12},{6,14},{8,0},{10,2},{12,4},{14,6},{1,9},{3,11}... | collective-permute-start | bytes 221192 | tf_op jit(solution)/shard_map/ppermute | solution.py:434
  5.5 6.5 %collective-permute-start.1 = (bf16[288,128]{1,0:T(8,128)(2,1)S(1)}, bf16[288,128]{1,0:T(8,128)(2,1)S(1)}, u32[]{:S(2)}, u32[]{:S(2)}) collective-permute-start(bf16[288,128]{1,0:T(8,128)(2,1)S(1)} %fetch_inputs.1), channel_id=1, source_target_pairs={{0,12},{2,14},{4,8},{6,10},{8,4},{10,6},{12,0},{14,2},{1,13},{3,15... | collective-permute-start | bytes 221192 | tf_op jit(solution)/shard_map/ppermute | solution.py:434
  6.9 5.3 %collective-permute-start = (bf16[288,128]{1,0:T(8,128)(2,1)S(1)}, bf16[288,128]{1,0:T(8,128)(2,1)S(1)}, u32[]{:S(2)}, u32[]{:S(2)}) collective-permute-start(bf16[288,128]{1,0:T(8,128)(2,1)S(1)} %fetch_inputs.1), channel_id=1, source_target_pairs={{0,4},{2,6},{4,0},{6,2},{8,12},{10,14},{12,8},{14,10},{1,5},{3,7},... | collective-permute-start | bytes 221192 | tf_op jit(solution)/shard_map/ppermute | solution.py:434
  7.1 8.0 %collective-permute-start.4 = (bf16[288,128]{1,0:T(8,128)(2,1)S(1)}, bf16[288,128]{1,0:T(8,128)(2,1)S(1)}, u32[]{:S(2)}, u32[]{:S(2)}) collective-permute-start(bf16[288,128]{1,0:T(8,128)(2,1)S(1)} %fetch_inputs.1), channel_id=1, source_target_pairs={{0,2},{2,0},{4,6},{6,4},{8,10},{10,8},{12,14},{14,12},{1,3},{3,1},... | collective-permute-start | bytes 221192 | tf_op jit(solution)/shard_map/ppermute | solution.py:434
  12.2 4.8 %collective-permute-start.5 = (bf16[432,128]{1,0:T(8,128)(2,1)S(1)}, bf16[432,128]{1,0:T(8,128)(2,1)S(1)}, u32[]{:S(2)}, u32[]{:S(2)}) collective-permute-start(bf16[432,128]{1,0:T(8,128)(2,1)S(1)} %pad_maximum_fusion.refs_1_), channel_id=1, source_target_pairs={{0,2},{2,0},{4,6},{6,4},{8,10},{10,8},{12,14},{14,12},{1,3},{3,1},... | collective-permute-start | bytes 331784 | tf_op jit(solution)/shard_map/ppermute | solution.py:434
  14.7 4.1 %collective-permute-start.3 = (bf16[864,128]{1,0:T(8,128)(2,1)S(1)}, bf16[864,128]{1,0:T(8,128)(2,1)S(1)}, u32[]{:S(2)}, u32[]{:S(2)}) collective-permute-start(bf16[864,128]{1,0:T(8,128)(2,1)S(1)} %get-tuple-element.51), channel_id=1, source_target_pairs={{0,1},{1,0},{2,3},{3,2},{4,5},{5,4},{6,7},{7,6},{8,9},{9,8},{10,11... | collective-permute-start | bytes 663560 | tf_op jit(solution)/shard_map/ppermute | solution.py:437
  14.8 5.5 %collective-permute-start.7 = (bf16[432,128]{1,0:T(8,128)(2,1)S(1)}, bf16[432,128]{1,0:T(8,128)(2,1)S(1)}, u32[]{:S(2)}, u32[]{:S(2)}) collective-permute-start(bf16[432,128]{1,0:T(8,128)(2,1)S(1)} %pad_maximum_fusion.1.refs_3_), channel_id=1, source_target_pairs={{0,2},{2,0},{4,6},{6,4},{8,10},{10,8},{12,14},{14,12},{1,3},{3,1},... | collective-permute-start | bytes 331784 | tf_op jit(solution)/shard_map/ppermute | solution.py:434
  17.7 1.5 %collective-permute-start.6 = (bf16[864,128]{1,0:T(8,128)(2,1)S(1)}, bf16[864,128]{1,0:T(8,128)(2,1)S(1)}, u32[]{:S(2)}, u32[]{:S(2)}) collective-permute-start(bf16[864,128]{1,0:T(8,128)(2,1)S(1)} %get-tuple-element.52), channel_id=1, source_target_pairs={{0,1},{1,0},{2,3},{3,2},{4,5},{5,4},{6,7},{7,6},{8,9},{9,8},{10,11... | collective-permute-start | bytes 663560 | tf_op jit(solution)/shard_map/ppermute | solution.py:437
  21.2 2.7 %collective-permute-start.8 = (bf16[1152,128]{1,0:T(8,128)(2,1)S(1)}, bf16[1152,128]{1,0:T(8,128)(2,1)S(1)}, u32[]{:S(2)}, u32[]{:S(2)}) collective-permute-start(bf16[1152,128]{1,0:T(8,128)(2,1)S(1)} %get-tuple-element.62.d_tri_ref), channel_id=1, source_target_pairs={{0,1},{1,0},{2,3},{3,2},{4,5},{5,4},{6,7},{7,6},{8,9},{9,8},{10,11... | collective-permute-start | bytes 884744 | tf_op jit(solution)/shard_map/ppermute | solution.py:437
  23.5 3.2 %collective-permute-start.9 = (f32[128,256]{1,0:T(8,128)S(1)}, f32[128,256]{1,0:T(8,128)S(1)}, u32[]{:S(2)}, u32[]{:S(2)}) collective-permute-start(f32[128,256]{1,0:T(8,128)S(1)} %get-tuple-element.81.small_own), channel_id=1, source_target_pairs={{0,1},{1,0},{2,3},{3,2},{4,5},{5,4},{6,7},{7,6},{8,9},{9,8},{10,11... | collective-permute-start | bytes 393224 | tf_op jit(solution)/shard_map/ppermute | solution.py:437
  26.5 1.6 %collective-permute-start.10 = (f32[128,512]{1,0:T(8,128)S(1)}, f32[128,512]{1,0:T(8,128)S(1)}, u32[]{:S(2)}, u32[]{:S(2)}) collective-permute-start(f32[128,512]{1,0:T(8,128)S(1)} %get-tuple-element.84), channel_id=1, source_target_pairs={{0,1},{1,0},{2,3},{3,2},{4,5},{5,4},{6,7},{7,6},{8,9},{9,8},{10,11... | collective-permute-start | bytes 786440 | tf_op jit(solution)/shard_map/ppermute | solution.py:437

commit v16 on v15

--- a/solution.py
+++ b/solution.py
@@ -377,12 +377,8 @@
     proj_weight,
     gate_weight,
     block_in,
-    small_own,
-    small_mate,
     block_out,
     pair_grad,
-    gate_grad,
-    out_grad,
 ):
     rows, cols, _ = sizes
     cells = rows * cols
@@ -394,10 +390,15 @@
     _, hat, inverse = layer_norm(pair[...].astype(F32), gain, params[1:2, :])
     pair_grad[...] = norm_back(d_normed, gain, hat, inverse)
     block_out[...] = block_in[...]
+
+
+def sums_kernel(
+    sizes, proj_own, proj_mate, small_own, small_mate, proj_grad, gate_grad, out_grad
+):
     channels = gate_grad.shape[1]
-    small = small_own[...] + small_mate[...]
-    gate_grad[...] = small[:, :channels]
-    out_grad[...] = small[:, channels:]
+    proj_grad[...] = proj_own[...] + proj_mate[...]
+    gate_grad[...] = small_own[:, :channels] + small_mate[:, :channels]
+    out_grad[...] = small_own[:, channels:] + small_mate[:, channels:]
 
 
 def replicated(
@@ -535,7 +536,6 @@
         micros=30,
         name="early",
     )
-    small_mate = over(small_grads)
     proj_grad, d_proj = call(
         late_kernel,
         [((channels, 4 * hidden), F32), ((every, 4 * hidden), BF16)],
@@ -554,10 +554,10 @@
         name="late",
     )
     proj_mate = over(proj_grad)
-    square = ((channels, channels), F32)
-    block_out, pair_grad, gate_grad, out_grad = call(
+    small_mate = over(after(small_grads, proj_grad))
+    block_out, pair_grad = call(
         outputs_kernel,
-        [((cells, channels), BF16), ((cells, channels), F32), square, square],
+        [((cells, channels), BF16), ((cells, channels), F32)],
         params,
         pair,
         d_proj,
@@ -565,15 +565,23 @@
         proj_weight,
         gate_weight,
         block_out,
+        micros=10,
+        name="outputs",
+    )
+    square = ((channels, channels), F32)
+    proj_grad, gate_grad, out_grad = call(
+        sums_kernel,
+        [((channels, 4 * hidden), F32), square, square],
+        proj_grad,
+        proj_mate,
         small_grads,
         small_mate,
-        micros=10,
-        name="outputs",
+        name="sums",
     )
     return (
         block_out.reshape(pair_rep.shape),
         pair_grad.reshape(pair_rep.shape),
-        proj_grad + proj_mate,
+        proj_grad,
         gate_grad,
         out_grad,
     )

time: 29.1 us -> 28.9 us (level)
  other arithmetic: 0.76 us -> 0.02 us
  Pallas kernels: 11.8 us -> 12.5 us
    pallas_call x10 -> x11, Pallas kernels: 11.8 us -> 12.5 us  [call(): pl.pallas_call(functools.partial(kernel, sizes), out_shape=[jax.ShapeDtyp...]
    add x1 -> x0, other arithmetic: 0.74 us -> none  [replicated(): proj_grad + proj_mate]
  transfers between devices with their start and end apart: 11 -> 11, of which waited for: 6 -> 6; matrix products, arithmetic and copies ran while one was open for 0% -> 0% of each run, Pallas kernels for 35% -> 26%
where the time goes in v16:
time: 28.9 us; the launch traced here: 28.7 us
  Pallas kernels  12.5 us (43%)
  starting transfers between devices  10.3 us (36%)
  waiting for transfers between devices  5.07 us (18%)
  between operations  0.77 us (3%)
    pallas_call x11, Pallas kernels, call(): pl.pallas_call(functools.partial(kernel, sizes), out_shape=[jax.ShapeDtyp...  12.5 us
    ppermute x6, starting transfers between devices, across(): return lax.ppermute(value, 'row', [(i, i ^ mask) for i in range(groups)])  9.36 us
    ppermute x6, waiting for transfers between devices, across(): return lax.ppermute(value, 'row', [(i, i ^ mask) for i in range(groups)])  4.39 us
    ppermute x5, starting transfers between devices, over(): return lax.ppermute(value, 'col', SWAP)  0.92 us
    ppermute x5, waiting for transfers between devices, over(): return lax.ppermute(value, 'col', SWAP)  0.68 us
  transfers between devices with their start and end apart: 11, of which 6 were waited for; matrix products, arithmetic and copies ran while one was open for 0% of the time, Pallas kernels for 26%

profile of v16, /device:TPU:0, one launch (start us, length us, event | category | flops | bytes accessed | tf_op | source)
XLA Modules:
  0.0 28.7 jit_solution(11601327246746283390)
XLA Ops:
  0.6 0.8 %fetch_inputs.1 = bf16[288,128]{1,0:T(8,128)(2,1)S(1)} custom-call(bf16[144,128]{1,0:T(8,128)(2,1)} %bitcast.8, bf16[144,128]{1,0:T(8,128)(2,1)} %bitcast.9), custom_call_target="tpu_custom_call" | custom-call | flops 1000000000 | tf_op jit(solution)/shard_map/fetch_inputs/pallas_call | solution.py:424
  1.4 4.1 %collective-permute-start.2 = (bf16[288,128]{1,0:T(8,128)(2,1)S(1)}, bf16[288,128]{1,0:T(8,128)(2,1)S(1)}, u32[]{:S(2)}, u32[]{:S(2)}) collective-permute-start(bf16[288,128]{1,0:T(8,128)(2,1)S(1)} %fetch_inputs.1), channel_id=1, source_target_pairs={{0,8},{2,10},{4,12},{6,14},{8,0},{10,2},{12,4},{14,6},{1,9},{3,11}... | collective-permute-start | bytes 221192 | tf_op jit(solution)/shard_map/ppermute | solution.py:435
  5.5 1.3 %collective-permute-start.1 = (bf16[288,128]{1,0:T(8,128)(2,1)S(1)}, bf16[288,128]{1,0:T(8,128)(2,1)S(1)}, u32[]{:S(2)}, u32[]{:S(2)}) collective-permute-start(bf16[288,128]{1,0:T(8,128)(2,1)S(1)} %fetch_inputs.1), channel_id=1, source_target_pairs={{0,12},{2,14},{4,8},{6,10},{8,4},{10,6},{12,0},{14,2},{1,13},{3,15... | collective-permute-start | bytes 221192 | tf_op jit(solution)/shard_map/ppermute | solution.py:435
  6.9 0.2 collective-permute-start
  7.1 1.5 %collective-permute-start.4 = (bf16[288,128]{1,0:T(8,128)(2,1)S(1)}, bf16[288,128]{1,0:T(8,128)(2,1)S(1)}, u32[]{:S(2)}, u32[]{:S(2)}) collective-permute-start(bf16[288,128]{1,0:T(8,128)(2,1)S(1)} %fetch_inputs.1), channel_id=1, source_target_pairs={{0,2},{2,0},{4,6},{6,4},{8,10},{10,8},{12,14},{14,12},{1,3},{3,1},... | collective-permute-start | bytes 221192 | tf_op jit(solution)/shard_map/ppermute | solution.py:435
  8.7 1.0 %fetch_weights.1 = (f32[4,128]{1,0:T(4,128)S(1)}, bf16[128,512]{1,0:T(8,128)(2,1)S(1)}, bf16[128,128]{1,0:T(8,128)(2,1)S(1)}, bf16[128,128]{1,0:T(8,128)(2,1)S(1)}) custom-call(f32[1,128]{1,0:T(1,128)} %bitcast.10, f32[1,128]{1,0:T(1,128)} %bitcast.11, f32[1,128]{1,0:T(1,128)} %bitcast.12, f32[1,128]{1,0:T(1,128)} %bitcast.13, bf16[128,512]{1,0:T(8,128)(2,1)} %refs_4_.1, ...), custom_call_target="tpu_custom_call" | custom-call | flops 1000000000 | tf_op jit(solution)/shard_map/fetch_weights/pallas_call | solution.py:424
  9.7 0.7 %collective-permute-done.2 = bf16[288,128]{1,0:T(8,128)(2,1)S(1)} collective-permute-done((bf16[288,128]{1,0:T(8,128)(2,1)S(1)}, bf16[288,128]{1,0:T(8,128)(2,1)S(1)}, u32[]{:S(2)}, u32[]{:S(2)}) %collective-permute-start.2) | collective-permute-done | bytes 73760 | tf_op jit(solution)/shard_map/ppermute | solution.py:435
  10.4 1.6 %collective-permute-done.1 = bf16[288,128]{1,0:T(8,128)(2,1)S(1)} collective-permute-done((bf16[288,128]{1,0:T(8,128)(2,1)S(1)}, bf16[288,128]{1,0:T(8,128)(2,1)S(1)}, u32[]{:S(2)}, u32[]{:S(2)}) %collective-permute-start.1) | collective-permute-done | bytes 73760 | tf_op jit(solution)/shard_map/ppermute | solution.py:435
  12.0 0.2 collective-permute-done
  12.2 1.8 %collective-permute-start.5 = (bf16[432,128]{1,0:T(8,128)(2,1)S(1)}, bf16[432,128]{1,0:T(8,128)(2,1)S(1)}, u32[]{:S(2)}, u32[]{:S(2)}) collective-permute-start(bf16[432,128]{1,0:T(8,128)(2,1)S(1)} %pad_maximum_fusion.refs_1_), channel_id=1, source_target_pairs={{0,2},{2,0},{4,6},{6,4},{8,10},{10,8},{12,14},{14,12},{1,3},{3,1},... | collective-permute-start | bytes 331784 | tf_op jit(solution)/shard_map/ppermute | solution.py:435
  14.0 0.6 %own_edges.2 = (bf16[864,128]{1,0:T(8,128)(2,1)S(1)}, bf16[576,128]{1,0:T(8,128)(2,1)S(1)}, f32[576,128]{1,0:T(8,128)S(1)}, f32[576,128]{1,0:T(8,128)S(1)}, f32[...) custom-call(f32[4,128]{1,0:T(4,128)S(1)} %get-tuple-element.48.params, ...), custom_call_target="tpu_custom_call" | custom-call | flops 10000000000 | tf_op jit(solution)/shard_map/own_edges/pallas_call | solution.py:424
  14.7 0.1 collective-permute-start.3
  14.8 0.4 %collective-permute-start.7 = (bf16[432,128]{1,0:T(8,128)(2,1)S(1)}, bf16[432,128]{1,0:T(8,128)(2,1)S(1)}, u32[]{:S(2)}, u32[]{:S(2)}) collective-permute-start(bf16[432,128]{1,0:T(8,128)(2,1)S(1)} %pad_maximum_fusion.1.refs_3_), channel_id=1, source_target_pairs={{0,2},{2,0},{4,6},{6,4},{8,10},{10,8},{12,14},{14,12},{1,3},{3,1},... | collective-permute-start | bytes 331784 | tf_op jit(solution)/shard_map/ppermute | solution.py:435
  15.1 0.0 collective-permute-done.4
  15.1 1.9 %collective-permute-done.5.refs_1_ = bf16[432,128]{1,0:T(8,128)(2,1)S(1)} collective-permute-done((bf16[432,128]{1,0:T(8,128)(2,1)S(1)}, bf16[432,128]{1,0:T(8,128)(2,1)S(1)}, u32[]{:S(2)}, u32[]{:S(2)}) %collective-permute-start.5) | collective-permute-done | bytes 110624 | tf_op jit(solution)/shard_map/ppermute | solution.py:435
  17.0 0.6 %own_edges.3 = (bf16[864,128]{1,0:T(8,128)(2,1)S(1)}, bf16[576,128]{1,0:T(8,128)(2,1)S(1)}, f32[576,128]{1,0:T(8,128)S(1)}, f32[576,128]{1,0:T(8,128)S(1)}, f32[...) custom-call(f32[4,128]{1,0:T(4,128)S(1)} %get-tuple-element.48.params, ...), custom_call_target="tpu_custom_call" | custom-call | flops 10000000000 | tf_op jit(solution)/shard_map/own_edges/pallas_call | solution.py:424
  17.7 0.1 collective-permute-start.6
  17.8 1.0 %own_triangle.1.more = f32[1152,128]{1,0:T(8,128)S(1)} custom-call(f32[576,128]{1,0:T(8,128)S(1)} %get-tuple-element.55.left_0.refs_2_, f32[576,128]{1,0:T(8,128)S(1)} %get-tuple-element.56.left_1.refs_3_, f32[576,128]{1,0:T(8,128)S(1)} %get-tuple-element.57.right_0.refs_4_, f32[576,128]{1,0:T(8,128)S(1)} %get-tuple-element.58.right_1.refs_5_), custom_call_target="tpu_custom_call" | custom-call | flops 10000000000 | tf_op jit(solution)/shard_map/own_triangle/pallas_call | solution.py:424
  18.8 0.0 collective-permute-done.3.edges_0
  18.8 0.4 %collective-permute-done.6.edges_1 = bf16[864,128]{1,0:T(8,128)(2,1)S(1)} collective-permute-done((bf16[864,128]{1,0:T(8,128)(2,1)S(1)}, bf16[864,128]{1,0:T(8,128)(2,1)S(1)}, u32[]{:S(2)}, u32[]{:S(2)}) %collective-permute-start.6) | collective-permute-done | bytes 221216 | tf_op jit(solution)/shard_map/ppermute | solution.py:438
  19.2 1.1 %mate_triangle.1.tri = f32[1152,128]{1,0:T(8,128)S(1)} custom-call(bf16[864,128]{1,0:T(8,128)(2,1)S(1)} %collective-permute-done.3.edges_0, bf16[864,128]{1,0:T(8,128)(2,1)S(1)} %collective-permute-done.6.edges_1, f32[1152,128]{1,0:T(8,128)S(1)} %own_triangle.1.more), custom_call_target="tpu_custom_call" | custom-call | flops 1000000000 | tf_op jit(solution)/shard_map/mate_triangle/pallas_call | solution.py:424
  20.3 0.0 collective-permute-done.7.refs_5_
  20.3 0.9 %cells.1 = (bf16[144,128]{1,0:T(8,128)(2,1)S(1)}, bf16[1152,128]{1,0:T(8,128)(2,1)S(1)}, bf16[1152,128]{1,0:T(8,128)(2,1)S(1)}, bf16[1152,128]{1,0:T(8,128)(2,1)S(1)}, bf16[1152,128]{1,0:T(8,128)(2,1)S(1)}) custom-call(f32[4,128]{1,0:T(4,128)S(1)} %get-tuple-element.48.params, f32[1152,128]{1,0:T(8,128)S(1)} %mate_triangle.1.tri, ...), custom_call_target="tpu_custom_call" | custom-call | flops 2000000000 | tf_op jit(solution)/shard_map/cells/pallas_call | solution.py:424
  21.2 0.2 collective-permute-start.8
  21.4 2.1 %early.1 = (f32[1152,128]{1,0:T(8,128)S(1)}, f32[1152,128]{1,0:T(8,128)S(1)}, bf16[1152,128]{1,0:T(8,128)(2,1)S(1)}, f32[1152,128]{1,0:T(8,128)S(1)}, f32[576,128]{1,0:T(8,128)S(1)}, /*index=5*/f32[128,256]{1,0:T(8,128)S(1)}) custom-call(bf16[1152,128]{1,0:T(8,128)(2,1)S(1)} %get-tuple-element.64.d_tri_ref, bf16[1152,128]{1,0:T(8,128)(2,1)S(1)} %get-tuple-element.65.d_gate, ...), custom_call_target="tpu_custom_call" | custom-call | flops 30000001024 | tf_op jit(solution)/shard_map/early/pallas_call | solution.py:424
  23.5 0.0 collective-permute-done.8.d_tri_ref
  23.5 2.6 %late.1 = (f32[128,512]{1,0:T(8,128)S(1)}, bf16[1152,512]{1,0:T(8,128)(2,1)S(1)}) custom-call(bf16[1152,128]{1,0:T(8,128)(2,1)S(1)} %collective-permute-done.8.d_tri_ref, f32[1152,128]{1,0:T(8,128)S(1)} %get-tuple-element.68.left, f32[1152,128]{1,0:T(8,128)S(1)} %get-tuple-element.69.right, bf16[1152,128]{1,0:T(8,128)(2,1)S(1)} %get-tuple-element.70.normed, ...), custom_call_target="tpu_custom_call" | custom-call | flops 40000000000 | tf_op jit(solution)/shard_map/late/pallas_call | solution.py:424
  26.1 0.4 %collective-permute-start.9 = (f32[128,512]{1,0:T(8,128)S(1)}, f32[128,512]{1,0:T(8,128)S(1)}, u32[]{:S(2)}, u32[]{:S(2)}) collective-permute-start(f32[128,512]{1,0:T(8,128)S(1)} %get-tuple-element.85.proj_own), channel_id=1, source_target_pairs={{0,1},{1,0},{2,3},{3,2},{4,5},{5,4},{6,7},{7,6},{8,9},{9,8},{10,11... | collective-permute-start | bytes 786440 | tf_op jit(solution)/shard_map/ppermute | solution.py:438
  26.6 0.1 collective-permute-start.10
  26.7 1.0 %outputs.1 = (bf16[144,128]{1,0:T(8,128)(2,1)}, f32[144,128]{1,0:T(8,128)}) custom-call(f32[4,128]{1,0:T(4,128)S(1)} %get-tuple-element.48.params, bf16[144,128]{1,0:T(8,128)(2,1)S(1)} %get-tuple-element.100.refs_0_.pair, bf16[1152,512]{1,0:T(8,128)(2,1)S(1)} %get-tuple-element.81.d_proj, bf16[1152,128]{1,0:T(8,128)(2,1)S(1)} %get-tuple-element.65.d_gate, ...), custom_call_target="tpu_custom_call" | custom-call | flops 10000000000 | tf_op jit(solution)/shard_map/outputs/pallas_call | solution.py:424
  27.6 0.3 collective-permute-done.10.small_mate
  27.9 0.8 %sums.1 = (f32[128,512]{1,0:T(8,128)}, f32[128,128]{1,0:T(8,128)}, f32[128,128]{1,0:T(8,128)}) custom-call(f32[128,512]{1,0:T(8,128)S(1)} %get-tuple-element.85.proj_own, f32[128,512]{1,0:T(8,128)S(1)} %collective-permute-done.9.proj_mate, f32[128,256]{1,0:T(8,128)S(1)} %get-tuple-element.87.small_own, f32[128,256]{1,0:T(8,128)S(1)} %collective-permute-done.10.small_mate), custom_call_target="tpu_custom_call" | custom-call | flops 1000000000 | tf_op jit(solution)/shard_map/sums/pallas_call | solution.py:424
  (7 shorter events, 0.1 us)
Async XLA Ops:
  1.4 9.0 %collective-permute-start.2 = (bf16[288,128]{1,0:T(8,128)(2,1)S(1)}, bf16[288,128]{1,0:T(8,128)(2,1)S(1)}, u32[]{:S(2)}, u32[]{:S(2)}) collective-permute-start(bf16[288,128]{1,0:T(8,128)(2,1)S(1)} %fetch_inputs.1), channel_id=1, source_target_pairs={{0,8},{2,10},{4,12},{6,14},{8,0},{10,2},{12,4},{14,6},{1,9},{3,11}... | collective-permute-start | bytes 221192 | tf_op jit(solution)/shard_map/ppermute | solution.py:435
  5.5 6.5 %collective-permute-start.1 = (bf16[288,128]{1,0:T(8,128)(2,1)S(1)}, bf16[288,128]{1,0:T(8,128)(2,1)S(1)}, u32[]{:S(2)}, u32[]{:S(2)}) collective-permute-start(bf16[288,128]{1,0:T(8,128)(2,1)S(1)} %fetch_inputs.1), channel_id=1, source_target_pairs={{0,12},{2,14},{4,8},{6,10},{8,4},{10,6},{12,0},{14,2},{1,13},{3,15... | collective-permute-start | bytes 221192 | tf_op jit(solution)/shard_map/ppermute | solution.py:435
  6.9 5.3 %collective-permute-start = (bf16[288,128]{1,0:T(8,128)(2,1)S(1)}, bf16[288,128]{1,0:T(8,128)(2,1)S(1)}, u32[]{:S(2)}, u32[]{:S(2)}) collective-permute-start(bf16[288,128]{1,0:T(8,128)(2,1)S(1)} %fetch_inputs.1), channel_id=1, source_target_pairs={{0,4},{2,6},{4,0},{6,2},{8,12},{10,14},{12,8},{14,10},{1,5},{3,7},... | collective-permute-start | bytes 221192 | tf_op jit(solution)/shard_map/ppermute | solution.py:435
  7.1 8.0 %collective-permute-start.4 = (bf16[288,128]{1,0:T(8,128)(2,1)S(1)}, bf16[288,128]{1,0:T(8,128)(2,1)S(1)}, u32[]{:S(2)}, u32[]{:S(2)}) collective-permute-start(bf16[288,128]{1,0:T(8,128)(2,1)S(1)} %fetch_inputs.1), channel_id=1, source_target_pairs={{0,2},{2,0},{4,6},{6,4},{8,10},{10,8},{12,14},{14,12},{1,3},{3,1},... | collective-permute-start | bytes 221192 | tf_op jit(solution)/shard_map/ppermute | solution.py:435
  12.2 4.8 %collective-permute-start.5 = (bf16[432,128]{1,0:T(8,128)(2,1)S(1)}, bf16[432,128]{1,0:T(8,128)(2,1)S(1)}, u32[]{:S(2)}, u32[]{:S(2)}) collective-permute-start(bf16[432,128]{1,0:T(8,128)(2,1)S(1)} %pad_maximum_fusion.refs_1_), channel_id=1, source_target_pairs={{0,2},{2,0},{4,6},{6,4},{8,10},{10,8},{12,14},{14,12},{1,3},{3,1},... | collective-permute-start | bytes 331784 | tf_op jit(solution)/shard_map/ppermute | solution.py:435
  14.7 4.1 %collective-permute-start.3 = (bf16[864,128]{1,0:T(8,128)(2,1)S(1)}, bf16[864,128]{1,0:T(8,128)(2,1)S(1)}, u32[]{:S(2)}, u32[]{:S(2)}) collective-permute-start(bf16[864,128]{1,0:T(8,128)(2,1)S(1)} %get-tuple-element.53), channel_id=1, source_target_pairs={{0,1},{1,0},{2,3},{3,2},{4,5},{5,4},{6,7},{7,6},{8,9},{9,8},{10,11... | collective-permute-start | bytes 663560 | tf_op jit(solution)/shard_map/ppermute | solution.py:438
  14.8 5.5 %collective-permute-start.7 = (bf16[432,128]{1,0:T(8,128)(2,1)S(1)}, bf16[432,128]{1,0:T(8,128)(2,1)S(1)}, u32[]{:S(2)}, u32[]{:S(2)}) collective-permute-start(bf16[432,128]{1,0:T(8,128)(2,1)S(1)} %pad_maximum_fusion.1.refs_3_), channel_id=1, source_target_pairs={{0,2},{2,0},{4,6},{6,4},{8,10},{10,8},{12,14},{14,12},{1,3},{3,1},... | collective-permute-start | bytes 331784 | tf_op jit(solution)/shard_map/ppermute | solution.py:435
  17.7 1.5 %collective-permute-start.6 = (bf16[864,128]{1,0:T(8,128)(2,1)S(1)}, bf16[864,128]{1,0:T(8,128)(2,1)S(1)}, u32[]{:S(2)}, u32[]{:S(2)}) collective-permute-start(bf16[864,128]{1,0:T(8,128)(2,1)S(1)} %get-tuple-element.54), channel_id=1, source_target_pairs={{0,1},{1,0},{2,3},{3,2},{4,5},{5,4},{6,7},{7,6},{8,9},{9,8},{10,11... | collective-permute-start | bytes 663560 | tf_op jit(solution)/shard_map/ppermute | solution.py:438
  21.2 2.3 %collective-permute-start.8 = (bf16[1152,128]{1,0:T(8,128)(2,1)S(1)}, bf16[1152,128]{1,0:T(8,128)(2,1)S(1)}, u32[]{:S(2)}, u32[]{:S(2)}) collective-permute-start(bf16[1152,128]{1,0:T(8,128)(2,1)S(1)} %get-tuple-element.64.d_tri_ref), channel_id=1, source_target_pairs={{0,1},{1,0},{2,3},{3,2},{4,5},{5,4},{6,7},{7,6},{8,9},{9,8},{10,11... | collective-permute-start | bytes 884744 | tf_op jit(solution)/shard_map/ppermute | solution.py:438
  26.1 1.8 %collective-permute-start.9 = (f32[128,512]{1,0:T(8,128)S(1)}, f32[128,512]{1,0:T(8,128)S(1)}, u32[]{:S(2)}, u32[]{:S(2)}) collective-permute-start(f32[128,512]{1,0:T(8,128)S(1)} %get-tuple-element.85.proj_own), channel_id=1, source_target_pairs={{0,1},{1,0},{2,3},{3,2},{4,5},{5,4},{6,7},{7,6},{8,9},{9,8},{10,11... | collective-permute-start | bytes 786440 | tf_op jit(solution)/shard_map/ppermute | solution.py:438
  26.6 1.4 %collective-permute-start.10 = (f32[128,256]{1,0:T(8,128)S(1)}, f32[128,256]{1,0:T(8,128)S(1)}, u32[]{:S(2)}, u32[]{:S(2)}) collective-permute-start(f32[128,256]{1,0:T(8,128)S(1)} %get-tuple-element.87.small_own), channel_id=1, source_target_pairs={{0,1},{1,0},{2,3},{3,2},{4,5},{5,4},{6,7},{7,6},{8,9},{9,8},{10,11... | collective-permute-start | bytes 393224 | tf_op jit(solution)/shard_map/ppermute | solution.py:438

commit v17 on v16

--- a/solution.py
+++ b/solution.py
@@ -153,7 +153,22 @@
             tri[tile(p * cells + t * 8), :] = value
 
 
-def own_triangle_kernel(sizes, left_0, left_1, right_0, right_1, tri, picked):
+def own_triangle_kernel(
+    sizes,
+    left_0,
+    left_1,
+    right_0,
+    right_1,
+    normed_0,
+    normed_1,
+    gate_weight,
+    tri,
+    gate_0,
+    gate_1,
+    picked,
+):
+    gate_0[...] = sigmoid(dot(normed_0[...], gate_weight[...]))
+    gate_1[...] = sigmoid(dot(normed_1[...], gate_weight[...]))
     rights = (right_0, right_1)
     triangle_half(
         sizes,
@@ -184,13 +199,12 @@
     sizes,
     params,
     tri,
-    gate_weight,
     out_weight,
     *refs,
 ):
     rows, cols, groups = sizes
     cells = rows * cols
-    normed, cots, (block_out, d_tri, d_gate, tri_norm_out, d_update_out) = (
+    gates, cots, (block_out, d_tri, d_gate, tri_norm_out, d_update_out) = (
         refs[:2],
         refs[2:6],
         refs[6:],
@@ -205,7 +219,7 @@
         tri_norm = tri_f.astype(BF16)
         update = dot(tri_norm, out_weight[...])
         n, s, _ = chunk[0]
-        out_gate = sigmoid(dot(normed[n][s * cells : (s + 4) * cells, :], gate_weight[...]))
+        out_gate = gates[n][s * cells : (s + 4) * cells, :]
         if first == 0:
             block_out[...] = (out_gate[:cells] * update[:cells]).astype(BF16)
         cot = jnp.concatenate([cots[2 * n + min(s, 1)][max(s - 1, 0) * cells : max(s, 1) * cells, :] for n, s, _ in chunk], axis=0)
@@ -497,19 +511,28 @@
     left, left_gate, left_value = ([o[n] for o in own] for n in (1, 2, 3))
     right, right_gate, right_value = ([o[n] for o in own] for n in (4, 5, 6))
     outs, picked, half_left = [(full, F32)], ((cols * cols, hidden), F32), ((every // 2, hidden), F32)
-    tri = call(own_triangle_kernel, outs, *left, *right, scratch=[picked], micros=10, name="own_triangle")
+    tri, *gates = call(
+        own_triangle_kernel,
+        outs + [((every // 2, channels), F32)] * 2,
+        *left,
+        *right,
+        *normed,
+        gate_weight,
+        scratch=[picked],
+        micros=10,
+        name="own_triangle",
+    )
     scratch = [picked, half_left, half_left]
 
-    args = (mate_0, mate_1, *tri)
+    args = (mate_0, mate_1, tri)
     (tri,) = call(mate_triangle_kernel, outs, *args, scratch=scratch, name="mate_triangle")
     block_out, d_tri, d_gate, tri_norm, d_update = call(
         cells_kernel,
         [((cells, channels), BF16)] + [(full, BF16)] * 4,
         params,
         tri,
-        gate_weight,
         out_weight,
-        *normed,
+        *gates,
         *cots,
         micros=2,
         name="cells",

time: 28.9 us -> 29.2 us (1.010)
  Pallas kernels: 12.5 us -> 12.9 us
    pallas_call x11, Pallas kernels: 12.5 us -> 12.9 us  [call(): pl.pallas_call(functools.partial(kernel, sizes), out_shape=[jax.ShapeDtyp...]
  transfers between devices with their start and end apart: 11 -> 11, of which waited for: 6 -> 6; matrix products, arithmetic and copies ran while one was open for 0% -> 0% of each run, Pallas kernels for 26% -> 27%
where the time goes in v17:
time: 29.2 us; the launch traced here: 29 us
  Pallas kernels  12.9 us (44%)
  starting transfers between devices  10.4 us (36%)
  waiting for transfers between devices  4.89 us (17%)
  between operations  0.77 us (3%)
    pallas_call x11, Pallas kernels, call(): pl.pallas_call(functools.partial(kernel, sizes), out_shape=[jax.ShapeDtyp...  12.9 us
    ppermute x6, starting transfers between devices, across(): return lax.ppermute(value, 'row', [(i, i ^ mask) for i in range(groups)])  9.36 us
    ppermute x6, waiting for transfers between devices, across(): return lax.ppermute(value, 'row', [(i, i ^ mask) for i in range(groups)])  4.39 us
    ppermute x5, starting transfers between devices, over(): return lax.ppermute(value, 'col', SWAP)  1.05 us
  transfers between devices with their start and end apart: 11, of which 6 were waited for; matrix products, arithmetic and copies ran while one was open for 0% of the time, Pallas kernels for 27%

profile of v17, /device:TPU:0, one launch (start us, length us, event | category | flops | bytes accessed | tf_op | source)
XLA Modules:
  0.0 29.0 jit_solution(2966914100888304261)
XLA Ops:
  0.6 0.8 %fetch_inputs.1 = bf16[288,128]{1,0:T(8,128)(2,1)S(1)} custom-call(bf16[144,128]{1,0:T(8,128)(2,1)} %bitcast.8, bf16[144,128]{1,0:T(8,128)(2,1)} %bitcast.9), custom_call_target="tpu_custom_call" | custom-call | flops 1000000000 | tf_op jit(solution)/shard_map/fetch_inputs/pallas_call | solution.py:438
  1.4 4.1 %collective-permute-start.2 = (bf16[288,128]{1,0:T(8,128)(2,1)S(1)}, bf16[288,128]{1,0:T(8,128)(2,1)S(1)}, u32[]{:S(2)}, u32[]{:S(2)}) collective-permute-start(bf16[288,128]{1,0:T(8,128)(2,1)S(1)} %fetch_inputs.1), channel_id=1, source_target_pairs={{0,8},{2,10},{4,12},{6,14},{8,0},{10,2},{12,4},{14,6},{1,9},{3,11}... | collective-permute-start | bytes 221192 | tf_op jit(solution)/shard_map/ppermute | solution.py:449
  5.5 1.3 %collective-permute-start.1 = (bf16[288,128]{1,0:T(8,128)(2,1)S(1)}, bf16[288,128]{1,0:T(8,128)(2,1)S(1)}, u32[]{:S(2)}, u32[]{:S(2)}) collective-permute-start(bf16[288,128]{1,0:T(8,128)(2,1)S(1)} %fetch_inputs.1), channel_id=1, source_target_pairs={{0,12},{2,14},{4,8},{6,10},{8,4},{10,6},{12,0},{14,2},{1,13},{3,15... | collective-permute-start | bytes 221192 | tf_op jit(solution)/shard_map/ppermute | solution.py:449
  6.9 0.2 collective-permute-start
  7.1 1.5 %collective-permute-start.4 = (bf16[288,128]{1,0:T(8,128)(2,1)S(1)}, bf16[288,128]{1,0:T(8,128)(2,1)S(1)}, u32[]{:S(2)}, u32[]{:S(2)}) collective-permute-start(bf16[288,128]{1,0:T(8,128)(2,1)S(1)} %fetch_inputs.1), channel_id=1, source_target_pairs={{0,2},{2,0},{4,6},{6,4},{8,10},{10,8},{12,14},{14,12},{1,3},{3,1},... | collective-permute-start | bytes 221192 | tf_op jit(solution)/shard_map/ppermute | solution.py:449
  8.7 1.0 %fetch_weights.1 = (f32[4,128]{1,0:T(4,128)S(1)}, bf16[128,512]{1,0:T(8,128)(2,1)S(1)}, bf16[128,128]{1,0:T(8,128)(2,1)S(1)}, bf16[128,128]{1,0:T(8,128)(2,1)S(1)}) custom-call(f32[1,128]{1,0:T(1,128)} %bitcast.10, f32[1,128]{1,0:T(1,128)} %bitcast.11, f32[1,128]{1,0:T(1,128)} %bitcast.12, f32[1,128]{1,0:T(1,128)} %bitcast.13, bf16[128,512]{1,0:T(8,128)(2,1)} %refs_4_.1, ...), custom_call_target="tpu_custom_call" | custom-call | flops 1000000000 | tf_op jit(solution)/shard_map/fetch_weights/pallas_call | solution.py:438
  9.7 0.7 %collective-permute-done.2 = bf16[288,128]{1,0:T(8,128)(2,1)S(1)} collective-permute-done((bf16[288,128]{1,0:T(8,128)(2,1)S(1)}, bf16[288,128]{1,0:T(8,128)(2,1)S(1)}, u32[]{:S(2)}, u32[]{:S(2)}) %collective-permute-start.2) | collective-permute-done | bytes 73760 | tf_op jit(solution)/shard_map/ppermute | solution.py:449
  10.4 1.6 %collective-permute-done.1 = bf16[288,128]{1,0:T(8,128)(2,1)S(1)} collective-permute-done((bf16[288,128]{1,0:T(8,128)(2,1)S(1)}, bf16[288,128]{1,0:T(8,128)(2,1)S(1)}, u32[]{:S(2)}, u32[]{:S(2)}) %collective-permute-start.1) | collective-permute-done | bytes 73760 | tf_op jit(solution)/shard_map/ppermute | solution.py:449
  12.0 0.2 collective-permute-done
  12.2 1.8 %collective-permute-start.5 = (bf16[432,128]{1,0:T(8,128)(2,1)S(1)}, bf16[432,128]{1,0:T(8,128)(2,1)S(1)}, u32[]{:S(2)}, u32[]{:S(2)}) collective-permute-start(bf16[432,128]{1,0:T(8,128)(2,1)S(1)} %pad_maximum_fusion.refs_1_), channel_id=1, source_target_pairs={{0,2},{2,0},{4,6},{6,4},{8,10},{10,8},{12,14},{14,12},{1,3},{3,1},... | collective-permute-start | bytes 331784 | tf_op jit(solution)/shard_map/ppermute | solution.py:449
  14.0 0.6 %own_edges.2 = (bf16[864,128]{1,0:T(8,128)(2,1)S(1)}, bf16[576,128]{1,0:T(8,128)(2,1)S(1)}, f32[576,128]{1,0:T(8,128)S(1)}, f32[576,128]{1,0:T(8,128)S(1)}, f32[...) custom-call(f32[4,128]{1,0:T(4,128)S(1)} %get-tuple-element.51.params, ...), custom_call_target="tpu_custom_call" | custom-call | flops 10000000000 | tf_op jit(solution)/shard_map/own_edges/pallas_call | solution.py:438
  14.7 0.1 collective-permute-start.3
  14.8 0.4 %collective-permute-start.7 = (bf16[432,128]{1,0:T(8,128)(2,1)S(1)}, bf16[432,128]{1,0:T(8,128)(2,1)S(1)}, u32[]{:S(2)}, u32[]{:S(2)}) collective-permute-start(bf16[432,128]{1,0:T(8,128)(2,1)S(1)} %pad_maximum_fusion.1.refs_3_), channel_id=1, source_target_pairs={{0,2},{2,0},{4,6},{6,4},{8,10},{10,8},{12,14},{14,12},{1,3},{3,1},... | collective-permute-start | bytes 331784 | tf_op jit(solution)/shard_map/ppermute | solution.py:449
  15.1 0.0 collective-permute-done.4
  15.1 1.9 %collective-permute-done.5.refs_1_ = bf16[432,128]{1,0:T(8,128)(2,1)S(1)} collective-permute-done((bf16[432,128]{1,0:T(8,128)(2,1)S(1)}, bf16[432,128]{1,0:T(8,128)(2,1)S(1)}, u32[]{:S(2)}, u32[]{:S(2)}) %collective-permute-start.5) | collective-permute-done | bytes 110624 | tf_op jit(solution)/shard_map/ppermute | solution.py:449
  17.0 0.6 %own_edges.3 = (bf16[864,128]{1,0:T(8,128)(2,1)S(1)}, bf16[576,128]{1,0:T(8,128)(2,1)S(1)}, f32[576,128]{1,0:T(8,128)S(1)}, f32[576,128]{1,0:T(8,128)S(1)}, f32[...) custom-call(f32[4,128]{1,0:T(4,128)S(1)} %get-tuple-element.51.params, ...), custom_call_target="tpu_custom_call" | custom-call | flops 10000000000 | tf_op jit(solution)/shard_map/own_edges/pallas_call | solution.py:438
  17.7 0.1 collective-permute-start.6
  17.8 1.2 %own_triangle.1 = (f32[1152,128]{1,0:T(8,128)S(1)}, f32[576,128]{1,0:T(8,128)S(1)}, f32[576,128]{1,0:T(8,128)S(1)}) custom-call(f32[576,128]{1,0:T(8,128)S(1)} %get-tuple-element.58.left_0.refs_2_, f32[576,128]{1,0:T(8,128)S(1)} %get-tuple-element.59.left_1.refs_3_, f32[576,128]{1,0:T(8,128)S(1)} %get-tuple-element.60.right_0.refs_4_, ...), custom_call_target="tpu_custom_call" | custom-call | flops 10000000000 | tf_op jit(solution)/shard_map/own_triangle/pallas_call | solution.py:438
  19.0 0.0 collective-permute-done.3.edges_0
  19.0 0.2 collective-permute-done.6.edges_1
  19.2 1.1 %mate_triangle.1.tri = f32[1152,128]{1,0:T(8,128)S(1)} custom-call(bf16[864,128]{1,0:T(8,128)(2,1)S(1)} %collective-permute-done.3.edges_0, bf16[864,128]{1,0:T(8,128)(2,1)S(1)} %collective-permute-done.6.edges_1, f32[1152,128]{1,0:T(8,128)S(1)} %get-tuple-element.65.more), custom_call_target="tpu_custom_call" | custom-call | flops 1000000000 | tf_op jit(solution)/shard_map/mate_triangle/pallas_call | solution.py:438
  20.3 1.0 %cells.1 = (bf16[144,128]{1,0:T(8,128)(2,1)S(1)}, bf16[1152,128]{1,0:T(8,128)(2,1)S(1)}, bf16[1152,128]{1,0:T(8,128)(2,1)S(1)}, bf16[1152,128]{1,0:T(8,128)(2,1)S(1)}, bf16[1152,128]{1,0:T(8,128)(2,1)S(1)}) custom-call(f32[4,128]{1,0:T(4,128)S(1)} %get-tuple-element.51.params, f32[1152,128]{1,0:T(8,128)S(1)} %mate_triangle.1.tri, ...), custom_call_target="tpu_custom_call" | custom-call | flops 2000000000 | tf_op jit(solution)/shard_map/cells/pallas_call | solution.py:438
  21.3 0.3 %collective-permute-start.8 = (bf16[1152,128]{1,0:T(8,128)(2,1)S(1)}, bf16[1152,128]{1,0:T(8,128)(2,1)S(1)}, u32[]{:S(2)}, u32[]{:S(2)}) collective-permute-start(bf16[1152,128]{1,0:T(8,128)(2,1)S(1)} %get-tuple-element.70.d_tri_ref), channel_id=1, source_target_pairs={{0,1},{1,0},{2,3},{3,2},{4,5},{5,4},{6,7},{7,6},{8,9},{9,8},{10,11... | collective-permute-start | bytes 884744 | tf_op jit(solution)/shard_map/ppermute | solution.py:452
  21.7 2.1 %early.1 = (f32[1152,128]{1,0:T(8,128)S(1)}, f32[1152,128]{1,0:T(8,128)S(1)}, bf16[1152,128]{1,0:T(8,128)(2,1)S(1)}, f32[1152,128]{1,0:T(8,128)S(1)}, f32[576,128]{1,0:T(8,128)S(1)}, /*index=5*/f32[128,256]{1,0:T(8,128)S(1)}) custom-call(bf16[1152,128]{1,0:T(8,128)(2,1)S(1)} %get-tuple-element.70.d_tri_ref, bf16[1152,128]{1,0:T(8,128)(2,1)S(1)} %get-tuple-element.71.d_gate, ...), custom_call_target="tpu_custom_call" | custom-call | flops 30000001024 | tf_op jit(solution)/shard_map/early/pallas_call | solution.py:438
  23.8 0.0 collective-permute-done.8.d_tri_ref
  23.8 2.6 %late.1 = (f32[128,512]{1,0:T(8,128)S(1)}, bf16[1152,512]{1,0:T(8,128)(2,1)S(1)}) custom-call(bf16[1152,128]{1,0:T(8,128)(2,1)S(1)} %collective-permute-done.8.d_tri_ref, f32[1152,128]{1,0:T(8,128)S(1)} %get-tuple-element.74.left, f32[1152,128]{1,0:T(8,128)S(1)} %get-tuple-element.75.right, bf16[1152,128]{1,0:T(8,128)(2,1)S(1)} %get-tuple-element.76.normed, ...), custom_call_target="tpu_custom_call" | custom-call | flops 40000000000 | tf_op jit(solution)/shard_map/late/pallas_call | solution.py:438
  26.5 0.3 %collective-permute-start.9 = (f32[128,512]{1,0:T(8,128)S(1)}, f32[128,512]{1,0:T(8,128)S(1)}, u32[]{:S(2)}, u32[]{:S(2)}) collective-permute-start(f32[128,512]{1,0:T(8,128)S(1)} %get-tuple-element.91.proj_own), channel_id=1, source_target_pairs={{0,1},{1,0},{2,3},{3,2},{4,5},{5,4},{6,7},{7,6},{8,9},{9,8},{10,11... | collective-permute-start | bytes 786440 | tf_op jit(solution)/shard_map/ppermute | solution.py:452
  26.8 0.3 collective-permute-start.10
  27.0 1.0 %outputs.1 = (bf16[144,128]{1,0:T(8,128)(2,1)}, f32[144,128]{1,0:T(8,128)}) custom-call(f32[4,128]{1,0:T(4,128)S(1)} %get-tuple-element.51.params, bf16[144,128]{1,0:T(8,128)(2,1)S(1)} %get-tuple-element.106.refs_0_.pair, bf16[1152,512]{1,0:T(8,128)(2,1)S(1)} %get-tuple-element.87.d_proj, bf16[1152,128]{1,0:T(8,128)(2,1)S(1)} %get-tuple-element.71.d_gate, ...), custom_call_target="tpu_custom_call" | custom-call | flops 10000000000 | tf_op jit(solution)/shard_map/outputs/pallas_call | solution.py:438
  28.0 0.3 collective-permute-done.10.small_mate
  28.3 0.0 collective-permute-done.9.proj_mate
  28.3 0.8 %sums.1 = (f32[128,512]{1,0:T(8,128)}, f32[128,128]{1,0:T(8,128)}, f32[128,128]{1,0:T(8,128)}) custom-call(f32[128,512]{1,0:T(8,128)S(1)} %get-tuple-element.91.proj_own, f32[128,512]{1,0:T(8,128)S(1)} %collective-permute-done.9.proj_mate, f32[128,256]{1,0:T(8,128)S(1)} %get-tuple-element.93.small_own, f32[128,256]{1,0:T(8,128)S(1)} %collective-permute-done.10.small_mate), custom_call_target="tpu_custom_call" | custom-call | flops 1000000000 | tf_op jit(solution)/shard_map/sums/pallas_call | solution.py:438
  (7 shorter events, 0.1 us)
Async XLA Ops:
  1.4 9.0 %collective-permute-start.2 = (bf16[288,128]{1,0:T(8,128)(2,1)S(1)}, bf16[288,128]{1,0:T(8,128)(2,1)S(1)}, u32[]{:S(2)}, u32[]{:S(2)}) collective-permute-start(bf16[288,128]{1,0:T(8,128)(2,1)S(1)} %fetch_inputs.1), channel_id=1, source_target_pairs={{0,8},{2,10},{4,12},{6,14},{8,0},{10,2},{12,4},{14,6},{1,9},{3,11}... | collective-permute-start | bytes 221192 | tf_op jit(solution)/shard_map/ppermute | solution.py:449
  5.5 6.5 %collective-permute-start.1 = (bf16[288,128]{1,0:T(8,128)(2,1)S(1)}, bf16[288,128]{1,0:T(8,128)(2,1)S(1)}, u32[]{:S(2)}, u32[]{:S(2)}) collective-permute-start(bf16[288,128]{1,0:T(8,128)(2,1)S(1)} %fetch_inputs.1), channel_id=1, source_target_pairs={{0,12},{2,14},{4,8},{6,10},{8,4},{10,6},{12,0},{14,2},{1,13},{3,15... | collective-permute-start | bytes 221192 | tf_op jit(solution)/shard_map/ppermute | solution.py:449
  6.9 5.3 %collective-permute-start = (bf16[288,128]{1,0:T(8,128)(2,1)S(1)}, bf16[288,128]{1,0:T(8,128)(2,1)S(1)}, u32[]{:S(2)}, u32[]{:S(2)}) collective-permute-start(bf16[288,128]{1,0:T(8,128)(2,1)S(1)} %fetch_inputs.1), channel_id=1, source_target_pairs={{0,4},{2,6},{4,0},{6,2},{8,12},{10,14},{12,8},{14,10},{1,5},{3,7},... | collective-permute-start | bytes 221192 | tf_op jit(solution)/shard_map/ppermute | solution.py:449
  7.1 8.0 %collective-permute-start.4 = (bf16[288,128]{1,0:T(8,128)(2,1)S(1)}, bf16[288,128]{1,0:T(8,128)(2,1)S(1)}, u32[]{:S(2)}, u32[]{:S(2)}) collective-permute-start(bf16[288,128]{1,0:T(8,128)(2,1)S(1)} %fetch_inputs.1), channel_id=1, source_target_pairs={{0,2},{2,0},{4,6},{6,4},{8,10},{10,8},{12,14},{14,12},{1,3},{3,1},... | collective-permute-start | bytes 221192 | tf_op jit(solution)/shard_map/ppermute | solution.py:449
  12.2 4.8 %collective-permute-start.5 = (bf16[432,128]{1,0:T(8,128)(2,1)S(1)}, bf16[432,128]{1,0:T(8,128)(2,1)S(1)}, u32[]{:S(2)}, u32[]{:S(2)}) collective-permute-start(bf16[432,128]{1,0:T(8,128)(2,1)S(1)} %pad_maximum_fusion.refs_1_), channel_id=1, source_target_pairs={{0,2},{2,0},{4,6},{6,4},{8,10},{10,8},{12,14},{14,12},{1,3},{3,1},... | collective-permute-start | bytes 331784 | tf_op jit(solution)/shard_map/ppermute | solution.py:449
  14.7 4.3 %collective-permute-start.3 = (bf16[864,128]{1,0:T(8,128)(2,1)S(1)}, bf16[864,128]{1,0:T(8,128)(2,1)S(1)}, u32[]{:S(2)}, u32[]{:S(2)}) collective-permute-start(bf16[864,128]{1,0:T(8,128)(2,1)S(1)} %get-tuple-element.56), channel_id=1, source_target_pairs={{0,1},{1,0},{2,3},{3,2},{4,5},{5,4},{6,7},{7,6},{8,9},{9,8},{10,11... | collective-permute-start | bytes 663560 | tf_op jit(solution)/shard_map/ppermute | solution.py:452
  14.8 5.5 %collective-permute-start.7 = (bf16[432,128]{1,0:T(8,128)(2,1)S(1)}, bf16[432,128]{1,0:T(8,128)(2,1)S(1)}, u32[]{:S(2)}, u32[]{:S(2)}) collective-permute-start(bf16[432,128]{1,0:T(8,128)(2,1)S(1)} %pad_maximum_fusion.1.refs_3_), channel_id=1, source_target_pairs={{0,2},{2,0},{4,6},{6,4},{8,10},{10,8},{12,14},{14,12},{1,3},{3,1},... | collective-permute-start | bytes 331784 | tf_op jit(solution)/shard_map/ppermute | solution.py:449
  17.7 1.5 %collective-permute-start.6 = (bf16[864,128]{1,0:T(8,128)(2,1)S(1)}, bf16[864,128]{1,0:T(8,128)(2,1)S(1)}, u32[]{:S(2)}, u32[]{:S(2)}) collective-permute-start(bf16[864,128]{1,0:T(8,128)(2,1)S(1)} %get-tuple-element.57), channel_id=1, source_target_pairs={{0,1},{1,0},{2,3},{3,2},{4,5},{5,4},{6,7},{7,6},{8,9},{9,8},{10,11... | collective-permute-start | bytes 663560 | tf_op jit(solution)/shard_map/ppermute | solution.py:452
  21.3 2.5 %collective-permute-start.8 = (bf16[1152,128]{1,0:T(8,128)(2,1)S(1)}, bf16[1152,128]{1,0:T(8,128)(2,1)S(1)}, u32[]{:S(2)}, u32[]{:S(2)}) collective-permute-start(bf16[1152,128]{1,0:T(8,128)(2,1)S(1)} %get-tuple-element.70.d_tri_ref), channel_id=1, source_target_pairs={{0,1},{1,0},{2,3},{3,2},{4,5},{5,4},{6,7},{7,6},{8,9},{9,8},{10,11... | collective-permute-start | bytes 884744 | tf_op jit(solution)/shard_map/ppermute | solution.py:452
  26.5 1.8 %collective-permute-start.9 = (f32[128,512]{1,0:T(8,128)S(1)}, f32[128,512]{1,0:T(8,128)S(1)}, u32[]{:S(2)}, u32[]{:S(2)}) collective-permute-start(f32[128,512]{1,0:T(8,128)S(1)} %get-tuple-element.91.proj_own), channel_id=1, source_target_pairs={{0,1},{1,0},{2,3},{3,2},{4,5},{5,4},{6,7},{7,6},{8,9},{9,8},{10,11... | collective-permute-start | bytes 786440 | tf_op jit(solution)/shard_map/ppermute | solution.py:452
  26.8 1.5 %collective-permute-start.10 = (f32[128,256]{1,0:T(8,128)S(1)}, f32[128,256]{1,0:T(8,128)S(1)}, u32[]{:S(2)}, u32[]{:S(2)}) collective-permute-start(f32[128,256]{1,0:T(8,128)S(1)} %get-tuple-element.93.small_own), channel_id=1, source_target_pairs={{0,1},{1,0},{2,3},{3,2},{4,5},{5,4},{6,7},{7,6},{8,9},{9,8},{10,11... | collective-permute-start | bytes 393224 | tf_op jit(solution)/shard_map/ppermute | solution.py:452
